TPU v7x, 256 devices: a whole 4x4x8 slice. The times are simulated.
256 devices in a mesh: tm: 32 (over x, z), chan: 4 (over y), clip: 2 (over core).
Axes of the slice: x: 4, y: 4, z: 8, core: 2. Of those that a mesh axis runs over, the one named last changes fastest.
Arguments:
- frames: bfloat16 [2048, 16, 16, 256], P(('clip', 'tm')), parts along dimension 0, may hold values from -6 to 6
- intervals: float32 [2048], P(('clip', 'tm')), parts along dimension 0, may hold values from 0.35 to 924.6
- decay_rates: float32 [256], P('chan'), may hold values from 0.00016276042 to 0.03448276
- in_kernel: bfloat16 [3, 3, 256, 256], P(None, None, None, 'chan'), may hold values from -0.125 to 0.125
- out_kernel: bfloat16 [3, 3, 256, 256], P(None, None, 'chan'), may hold values from -0.125 to 0.125
- skip_gain: float32 [256], replicated, may hold values from 0.5 to 1.5
Outputs:
- readout: bfloat16 [2048, 16, 16, 256], P(('clip', 'tm'), 'chan'), parts along dimension 0
There are 2 independent parts, one for each index of `clip`. A program takes and returns all parts, laid end to end along the dimension named above; an argument that names none is the same for every part. Nothing has to cross between parts.
All inputs are finite; a program needn't handle non-finite values.
Results may differ from a plain program's by a relative error of at most 0.019.
Values may be sent and summed in bfloat16 or wider, within the bound.
No kernel may reach another device: no remote copies, remote signals or barrier semaphores. Data moves between devices by JAX's collectives and lax.ppermute only.
A program may use at most 128 MiB of HBM per device.

v0:
```python
import jax
import jax.numpy as jnp
from jax import lax
from jax.sharding import PartitionSpec as P


def entering(array, axis, combine, identity):
    length, position = (lax.axis_size(axis), lax.axis_index(axis))
    everything = jax.tree.map(
        lambda part, kind: lax.all_gather(part.astype(kind), axis),
        array,
        (jnp.bfloat16, jnp.bfloat16),
    )
    start = jax.tree.map(
        lambda part, zero: jnp.broadcast_to(jnp.asarray(zero, part.dtype), part.shape),
        array,
        identity,
    )

    def hop(k, before):
        reached = k < position
        new = combine(
            before, jax.tree.map(lambda part, own: part[k].astype(own.dtype), everything, array)
        )
        return jax.tree.map(lambda a, b: jnp.where(reached, a, b), new, before)

    return lax.fori_loop(0, length, hop, start)


def convolve(volume, kernel, padding):
    return lax.conv_general_dilated(
        volume,
        kernel,
        (1, 1),
        padding,
        dimension_numbers=("NHWC", "HWIO", "NHWC"),
        preferred_element_type=jnp.float32,
    )


def combine(earlier_part, later_part):
    return (earlier_part[0] * later_part[0], later_part[0] * earlier_part[1] + later_part[1])


def recur(drives, intervals, decay_rates):
    scaled = intervals[:, None] * decay_rates[None, :]
    gain_rows = jnp.sqrt(-jnp.expm1(-2.0 * scaled))
    elapsed = jnp.cumsum(intervals)
    frame_index = jnp.arange(intervals.shape[0])
    causal = (frame_index[:, None] >= frame_index[None, :])[:, :, None]
    elapsed_gap = elapsed[:, None] - elapsed[None, :]
    exponent = jnp.where(causal, -elapsed_gap[:, :, None] * decay_rates[None, None, :], 0.0)
    weights = jnp.where(causal, jnp.exp(exponent), 0.0)
    local_states = jnp.einsum(
        "tsp,shwp->thwp",
        weights,
        gain_rows[:, None, None, :] * drives,
        precision=lax.Precision.HIGHEST,
    )
    inflow = jnp.exp(-elapsed[:, None] * decay_rates[None, :])
    block_decay = inflow[-1]
    block_end = local_states[-1]
    identity = (jnp.ones_like(block_decay), jnp.zeros_like(block_end))
    unused, incoming = entering((block_decay, block_end), "tm", combine, identity)
    return local_states + inflow[:, None, None, :] * incoming[None]


def local(frames, intervals, decay_rates, in_kernel, out_kernel, skip_gain):
    row_count = frames.shape[1] // lax.axis_size("chan")
    chan_index = lax.axis_index("chan")
    own_rows = lax.dynamic_slice_in_dim(frames, chan_index * row_count, row_count, 1)
    skipped = skip_gain * own_rows.astype(jnp.float32)
    drives = convolve(frames, in_kernel, "SAME")
    states = recur(drives, intervals, decay_rates).astype(jnp.bfloat16)
    partial_value = convolve(states, out_kernel, "SAME")
    summed = lax.psum_scatter(
        partial_value.astype(jnp.bfloat16), "chan", scatter_dimension=1, tiled=True
    ).astype(jnp.float32)
    return (summed + skipped).astype(jnp.bfloat16)


def solution(mesh):
    placed = (
        P(("clip", "tm"), None, None, None),
        P(("clip", "tm")),
        P("chan"),
        P(None, None, None, "chan"),
        P(None, None, "chan", None),
        P(),
    )
    return jax.shard_map(
        local,
        mesh=mesh,
        in_specs=placed,
        out_specs=P(("clip", "tm"), "chan", None, None),
        check_vma=False,
    )
```

profile of v0, /device:TPU:32, one launch (start us, length us, event | category | flops | bytes accessed | tf_op | source)
XLA Modules:
  0.0 240.3 jit_solution(16136287342210356566)
XLA Ops:
  6.5 0.8 copy.26
  8.4 13.5 %convolution_multiply_fusion = f32[32,16,16,64]{3,0,2,1:T(8,128)} fusion(bf16[3,3,256,64]{2,3,1,0:T(8,128)(2,1)} %param.11, f32[32,64]{1,0:T(8,128)S(1)} %get-tuple-element.139, bf16[32,16,16,256]{3,2,1,0:T(8,128)(2,1)} %param.8), kind=kOutput, calls=%fused_computation.9 | convolution fusion | flops 2219311104 | bytes 6594560 | tf_op jit(solution)/shard_map/conv_general_dilated | solution.py:31
  21.8 9.1 %copy.27 = f32[32,16,16,64]{0,2,1,3:T(8,128)} copy(f32[32,16,16,64]{3,0,2,1:T(8,128)} %convolution_multiply_fusion) | data formatting | bytes 4194304 | tf_op jit(solution)/shard_map/mul | solution.py:57
  30.9 9.8 %convolution_bitcast_fusion = f32[32,16,16,64]{0,2,1,3:T(8,128)S(1)} fusion(f32[32,16,16,64]{0,2,1,3:T(8,128)} %copy.27, f32[64]{0:T(128)S(1)} %copy-done.2, f32[32,32]{1,0:T(8,128)S(1)} %subtract_negate_fusion, pred[32,32]{1,0:T(8,128)(4,1)S(1)} %iota_compare_fusion), kind=kOutput, calls=%fused_computation.7 | convolution fusion | flops 201523200 | bytes 4199680 | tf_op jit(solution)/shard_map/tsp,shwp->thwp/dot_general | solution.py:54
  40.7 3.2 %copy-done.1 = f32[32,16,16,64]{0,2,1,3:T(8,128)} copy-done((f32[32,16,16,64]{0,2,1,3:T(8,128)}, f32[32,16,16,64]{0,2,1,3:T(8,128)S(1)}, u32[]{:S(2)}) %copy-start.1) | copy-done | bytes 2097176
  43.9 3.3 %slice.16 = bf16[1,16,16,64]{0,2,1,3:T(8,128)(2,1)} slice(f32[32,16,16,64]{0,2,1,3:T(8,128)S(1)} %convolution_bitcast_fusion), slice={[31:32], [0:16], [0:16], [0:64]} | slice | bytes 65536 | tf_op jit(solution)/shard_map/slice | solution.py:62
  47.2 6.6 %copy.29 = bf16[1,16,16,64]{3,2,1,0:T(8,128)(2,1)} copy(bf16[1,16,16,64]{0,2,1,3:T(8,128)(2,1)} %slice.16) | data formatting | bytes 65536 | tf_op jit(solution)/shard_map/slice | solution.py:62
  54.0 40.2 %all-gather = bf16[32,1,64]{2,1,0:T(2,128)(2,1)S(1)} all-gather(bf16[1,1,64]{2,1,0:T(2,128)(2,1)S(1)} %fusion.15), channel_id=1, replica_groups=mesh['tm'=32,'chan'=4,'clip'=2] {'tm'}, dimensions={0}, use_global_device_ids=true | all-gather | bytes 4224 | tf_op jit(solution)/shard_map/all_gather | solution.py:10
  94.2 39.3 %all-gather.3.cloned.1.call-done = bf16[32,16,16,64]{3,2,1,0:T(8,128)(2,1)} async-done(((bf16[1,16,16,64]{3,2,1,0:T(8,128)(2,1)}), bf16[32,16,16,64]{3,2,1,0:T(8,128)(2,1)}) %all-gather.3.cloned.1.call-update) | async-done | bytes 1048592 | tf_op jit(solution)/shard_map/all_gather | solution.py:10
  133.5 30.2 %while.14 = (s32[]{:T(128)}, f32[16,16,64]{2,1,0:T(8,128)S(1)}, s32[]{:T(128)}, bf16[32,64]{1,0:T(8,128)(2,1)S(1)}, bf16[32,16,16,64]{3,2,1,0:T(8,128)(2,1)}, /*index=5*/s32[]{:T(128)}, s32[]{:T(128)}) while((s32[]{:T(128)}, f32[16,16,64]{2,1,0:T(8,128)S(1)}, s32[]{:T(128)}, bf16[32,64]{1,0:T(8,128)(2,1)S(1)}, ...), condition=%wide.region_2.3_spmd.clone, body=%wide.region_1.2_spmd.clone.sunk | while | flops 81988 | bytes 164585 | solution.py:27
  133.5 0.9 fusion.22
  134.5 0.9 fusion.22
  135.4 0.9 fusion.22
  136.4 0.9 fusion.22
  137.3 0.9 fusion.22
  138.3 0.9 fusion.22
  139.2 0.9 fusion.22
  140.1 0.9 fusion.22
  141.1 0.9 fusion.22
  142.0 0.9 fusion.22
  143.0 0.9 fusion.22
  143.9 0.9 fusion.22
  144.9 0.9 fusion.22
  145.8 0.9 fusion.22
  146.8 0.9 fusion.22
  147.7 0.9 fusion.22
  148.6 0.9 fusion.22
  149.6 0.9 fusion.22
  150.5 0.9 fusion.22
  151.5 0.9 fusion.22
  152.4 0.9 fusion.22
  153.4 0.9 fusion.22
  154.3 0.9 fusion.22
  155.2 0.9 fusion.22
  156.2 0.9 fusion.22
  157.1 0.9 fusion.22
  158.1 0.9 fusion.22
  159.0 0.9 fusion.22
  160.0 0.9 fusion.22
  160.9 0.9 fusion.22
  161.9 0.9 fusion.22
  162.8 0.9 fusion.22
  164.0 5.2 %add_convert_fusion = bf16[32,16,16,64]{0,2,1,3:T(8,128)(2,1)S(1)} fusion(f32[32,16,16,64]{0,2,1,3:T(8,128)} %copy-done.1, f32[16,16,64]{1,0,2:T(8,128)S(1)} %copy.30, f32[32,64]{0,1:T(8,128)S(1)} %copy.28), kind=kLoop, calls=%fused_computation.4 | loop fusion | flops 1572864 | bytes 3219456 | tf_op jit(solution)/shard_map/convert_element_type | solution.py:74
  169.2 13.0 %fusion.3 = bf16[32,16,16,256]{3,0,2,1:T(8,128)(2,1)} fusion(bf16[3,3,64,256]{3,2,1,0:T(8,128)(2,1)S(1)} %copy-done, bf16[32,16,16,64]{0,2,1,3:T(8,128)(2,1)S(1)} %add_convert_fusion), kind=kOutput, calls=%fused_computation.8 | convolution fusion | flops 2220883968 | bytes 5537792 | tf_op jit(solution)/shard_map/conv_general_dilated | solution.py:31
  182.2 6.5 %copy.25 = bf16[32,16,16,256]{3,0,2,1:T(8,128)(2,1)} copy(bf16[32,16,16,256]{3,2,1,0:T(8,128)(2,1)} %param.8) | data formatting | bytes 8388608 | tf_op args[0]
  188.8 41.2 %reduce-scatter.2.cloned.1.call-done = bf16[32,4,16,256]{3,0,2,1:T(8,128)(2,1)} async-done(((bf16[32,16,16,256]{3,0,2,1:T(8,128)(2,1)}), bf16[32,4,16,256]{3,0,2,1:T(8,128)(2,1)}) %reduce-scatter.2.cloned.1.call-update) | async-done | bytes 1048592 | tf_op jit(solution)/shard_map/reduce_scatter | solution.py:76
  230.0 1.9 add_convert_fusion.1
  231.9 1.6 copy.33
  (54 shorter events, 1.8 us)
Async XLA Ops:
  6.5 162.7 %copy-start = (bf16[3,3,64,256]{3,2,1,0:T(8,128)(2,1)S(1)}, bf16[3,3,64,256]{3,2,1,0:T(8,128)(2,1)}, u32[]{:S(2)}) copy-start(bf16[3,3,64,256]{3,2,1,0:T(8,128)(2,1)} %param.12) | copy-start | bytes 884740
  6.5 127.0 %all-gather.3.cloned.1.call-start = ((), (), s32[]{:S(2)}) async-start(), calls=%async_computation.1 | async-start | bytes 2162688 | tf_op jit(solution)/shard_map/all_gather | solution.py:10
  21.8 9.1 %copy-start.2 = (f32[64]{0:T(128)S(1)}, f32[64]{0:T(128)}, u32[]{:S(2)}) copy-start(f32[64]{0:T(128)} %param.10) | copy-start | bytes 772
  40.7 3.2 %copy-start.1 = (f32[32,16,16,64]{0,2,1,3:T(8,128)}, f32[32,16,16,64]{0,2,1,3:T(8,128)S(1)}, u32[]{:S(2)}) copy-start(f32[32,16,16,64]{0,2,1,3:T(8,128)S(1)} %convolution_bitcast_fusion) | copy-start | bytes 6291460
  53.9 176.1 %reduce-scatter.2.cloned.1.call-start = ((), (), s32[]{:S(2)}) async-start(), calls=%async_computation.2 | async-start | bytes 5242880 | tf_op jit(solution)/shard_map/reduce_scatter | solution.py:76
  182.2 47.7 %copy-start.3 = (f32[256]{0:T(256)S(1)}, f32[256]{0:T(256)}, u32[]{:S(2)}) copy-start(f32[256]{0:T(256)} %param.13) | copy-start | bytes 3076
Sparse Core Ops, SparseCore 0:
  54.0 79.5 all-gather.2
  182.4 47.5 reduce-scatter.1
where the time goes:
time: 243 us; the launch traced here: 240 us
  waiting for transfers between devices  80.5 us (33%)
  blocking collectives  40.2 us (17%)
  other arithmetic  37.5 us (15%)
  matrix products  36.2 us (15%)
  local copies, waits for them, and re-layouts  31.4 us (13%)
  between operations  13.5 us (6%)
    reduce_scatter x1, waiting for transfers between devices, local(): lax.psum_scatter(partial_value.astype(jnp.bfloat16), 'chan', scatter_dime...  41.2 us
    all_gather x1, blocking collectives, entering(): lax.all_gather(part.astype(kind), axis)  40.2 us
    all_gather x1, waiting for transfers between devices, entering(): lax.all_gather(part.astype(kind), axis)  39.3 us
    select_n x32, other arithmetic, hop(): return jax.tree.map(lambda a, b: jnp.where(reached, a, b), new, before)  28.9 us
    conv_general_dilated x2, matrix products, convolve(): lax.conv_general_dilated(volume, kernel, (1, 1), padding, dimension_numbe...  26.4 us
    slice x2, local copies, waits for them, and re-layouts, recur(): block_end = local_states[-1]  9.89 us
    dot_general x1, matrix products, recur(): jnp.einsum('tsp,shwp->thwp', weights, gain_rows[:, None, None, :] * drive...  9.8 us
    unnamed x11, local copies, waits for them, and re-layouts  9.77 us
  transfers between devices with their start and end apart: 2, of which 2 were waited for; matrix products, arithmetic and copies ran while one was open for 3% of the time, Pallas kernels for 0%

commit v1 on v0

v1 whole, which is shorter than its diff:
```python
import functools

import jax
import jax.numpy as jnp
from jax import lax
from jax.experimental import pallas as pl
from jax.experimental.pallas import tpu as pltpu
from jax.sharding import PartitionSpec as P

F32 = jnp.float32
BF16 = jnp.bfloat16
FRAMES = 32
HALF = 16
ROWS = 16
WIDE = 16
CH = 256
OWN = 64
LANES = 128
CHANS = 4
ZS = 8
XS = 4
WINDOW = 6
STEP = 2
CHUNKS = HALF // STEP


def split3(value):
    high = value.astype(BF16)
    rest = value - high.astype(F32)
    middle = rest.astype(BF16)
    low = (rest - middle.astype(F32)).astype(BF16)
    return high, middle, low


def join3(block, start):
    parts = block.astype(F32)
    return parts[start : start + 1] + parts[start + 1 : start + 2] + parts[start + 2 : start + 3]


def low_half(shape):
    return lax.broadcasted_iota(jnp.int32, shape, len(shape) - 1) < OWN


def swap_halves(value):
    return pltpu.roll(value, OWN, value.ndim - 1)


def doubled(rates):
    row = jnp.concatenate([rates, rates], axis=1)
    return row


def table(low_values, high_values):
    row = lax.broadcasted_iota(jnp.int32, (HALF, LANES), 0)
    low = low_half((HALF, LANES))
    result = jnp.zeros((HALF, LANES), F32)
    for t in range(HALF):
        result = jnp.where(row == t, jnp.where(low, low_values[t], high_values[t]), result)
    return result


def spread(target, index, lanes, rows):
    for t in range(HALF):
        target[index, t, :, lanes] = jnp.broadcast_to(rows[t : t + 1], (WIDE, LANES))


def one_minus_exp(value):
    series = value * (
        1.0 - value * (0.5 - value * (1.0 / 6 - value * (1.0 / 24 - value * (1.0 / 120))))
    )
    return jnp.where(value < 0.125, series, 1.0 - jnp.exp(-value))


def running(values):
    sums = [values[0]]
    for value in values[1:]:
        sums.append(sums[-1] + value)
    return sums


def drive_kernel(
    place, intervals, rates, kernel_t, frames,
    own, one, two, three, message,
    padded, weights, factors, state, kept, load_sem, store_sem,
):
    windows = (own, one, two, three)

    def load(chunk, half):
        start = half * HALF + chunk * STEP
        return pltpu.make_async_copy(
            frames.at[pl.ds(start, STEP)],
            padded.at[pl.ds(start, STEP), pl.ds(1, ROWS)],
            load_sem.at[chunk, half],
        )

    def store(chunk, step):
        first = CHANS * lax.rem(place[0] + step, CHANS)
        return pltpu.make_async_copy(
            kept.at[pl.ds(chunk * STEP, STEP), pl.ds(first, WINDOW)],
            windows[step].at[pl.ds(chunk * STEP, STEP)],
            store_sem.at[chunk, step],
        )

    for chunk in range(CHUNKS):
        load(chunk, 0).start()
        load(chunk, 1).start()

    empty = jnp.zeros((FRAMES, 1, WIDE, CH), BF16)
    padded[:, 0:1] = empty
    padded[:, ROWS + 1 : ROWS + 2] = empty
    empty = jnp.zeros((HALF, 1, WIDE, LANES), BF16)
    kept[:, 0:1] = empty
    kept[:, ROWS + 1 : ROWS + 2] = empty
    nothing = jnp.zeros((CH, OWN), BF16)
    for i in range(3):
        tap = [kernel_t[3 * i + j].astype(F32).T.astype(BF16) for j in range(3)]
        weights[0, CH * i : CH * (i + 1), :] = jnp.concatenate([tap[0], tap[1], tap[2], nothing], 1)
        weights[1, CH * i : CH * (i + 1), :] = jnp.concatenate([tap[1], tap[0], nothing, tap[2]], 1)

    values = [intervals[t] for t in range(FRAMES)]
    rate = doubled(rates[...])
    scaled = table(values[:HALF], values[HALF:]) * rate
    spread(factors, 0, slice(None), jnp.exp(-scaled))
    spread(factors, 1, slice(None), jnp.sqrt(one_minus_exp(2.0 * scaled)))
    state[...] = jnp.zeros_like(state)

    def advance(chunk, carry):
        start = pl.multiple_of(chunk * STEP, STEP)

        def product(half):
            block = padded[pl.ds(half * HALF + start, STEP)]
            taps = [block[:, i : i + ROWS].reshape(STEP * ROWS * WIDE, CH) for i in range(3)]
            return jnp.dot(
                jnp.concatenate(taps, axis=1), weights[half], preferred_element_type=F32
            )

        load(chunk, 0).wait()
        load(chunk, 1).wait()
        first, second = product(0), product(1)
        low = low_half((STEP * ROWS * WIDE, LANES))
        left = jnp.where(low, first[:, :LANES], second[:, :LANES])
        centre = swap_halves(jnp.where(low, second[:, :LANES], first[:, :LANES]))
        right = first[:, LANES:] + second[:, LANES:]
        shape = (STEP * ROWS, WIDE, LANES)
        column = lax.broadcasted_iota(jnp.int32, shape, 1)
        left = jnp.where(column == 0, 0.0, pltpu.roll(left.reshape(shape), 1, 1))
        right = jnp.where(column == WIDE - 1, 0.0, pltpu.roll(right.reshape(shape), WIDE - 1, 1))
        drives = (left + centre.reshape(shape) + right).reshape(STEP, ROWS, WIDE, LANES)
        carried = state[...]
        for step in range(STEP):
            decay, gain = factors[0, start + step], factors[1, start + step]
            carried = decay * carried + gain * drives[step]
            kept[start + step, 1 : ROWS + 1] = carried.astype(BF16)
        state[...] = carried
        for step in range(CHANS):
            store(chunk, step).start()
        return carry

    lax.fori_loop(0, CHUNKS, advance, 0)

    late = functools.reduce(lambda a, b: a + b, values[HALF:])
    total = functools.reduce(lambda a, b: a + b, values[:HALF]) + late
    carried = state[...]
    end = carried + jnp.exp(-late * rate).reshape(1, 1, LANES) * swap_halves(carried)
    other = swap_halves(end)
    low = low_half((ROWS // 2, WIDE, LANES))
    packed = jnp.where(low, other[: ROWS // 2], end[ROWS // 2 :]).astype(BF16)
    row = lax.broadcasted_iota(jnp.int32, (WIDE, LANES), 0)
    pieces = split3(jnp.full((WIDE, LANES), total, F32))
    extra = jnp.where(row == 0, pieces[0].astype(F32), jnp.where(row == 1, pieces[1].astype(F32), pieces[2].astype(F32))).astype(BF16)
    for z in range(ZS):
        message[z, : ROWS // 2] = packed
        message[z, ROWS // 2] = extra
    for chunk in range(CHUNKS):
        for step in range(CHANS):
            store(chunk, step).wait()


def relay_kernel(place, rates, received, message):
    x, z = place[1], place[2]
    rate = doubled(rates[...])
    total = jnp.zeros((ROWS // 2, WIDE, LANES), F32)
    before = total
    elapsed = jnp.zeros((1, LANES), F32)
    elapsed_before = elapsed
    for other in range(ZS):
        mine = z == other
        before = jnp.where(mine, total, before)
        elapsed_before = jnp.where(mine, elapsed, elapsed_before)
        spent = join3(received[other, ROWS // 2], 0)
        decay = jnp.exp(-spent * rate).reshape(1, 1, LANES)
        total = decay * total + received[other, : ROWS // 2].astype(F32)
        elapsed = elapsed + spent

    low = low_half((WIDE, LANES))
    blank = jnp.zeros((WIDE, LANES), F32)

    def rows_of(value):
        swapped = swap_halves(value)
        top = [jnp.where(low, value[r], swapped[r]) for r in range(ROWS // 2)]
        bottom = [jnp.where(low, swapped[r], value[r]) for r in range(ROWS // 2)]
        return [blank] + top + bottom + [blank]

    totals, befores = rows_of(total), rows_of(before)
    row = lax.broadcasted_iota(jnp.int32, (WIDE, LANES), 0)
    extra = blank
    pieces = split3(elapsed) + split3(elapsed_before) + split3(rate)
    for index, piece in enumerate(pieces):
        extra = jnp.where(row == index, piece.astype(F32), extra)
    extra = extra.astype(BF16)
    for chan in range(CHANS):
        for q in range(WINDOW // 2):
            here = CHANS * chan + q
            there = here + WINDOW // 2
            later = jnp.where(low, totals[here], totals[there]).astype(BF16)
            level = jnp.where(low, befores[here], befores[there]).astype(BF16)
            for to in range(XS):
                message[to * CHANS + chan, q] = jnp.where(x == to, level, later)
        for to in range(XS):
            message[to * CHANS + chan, WINDOW // 2] = extra


OUT_STEP = 8
OUT_CHUNKS = FRAMES // OUT_STEP


def readout_kernel(
    place, intervals, skip_gain, received, own, one, two, three, out_kernel, frames,
    result,
    weights, direct, states, written, flows, base, load_sem, store_sem,
):
    chan, x = place[0], place[1]
    blocks = (own, one, two, three)

    def fetch(step):
        return pltpu.make_async_copy(
            out_kernel.at[lax.rem(chan + CHANS - step, CHANS)],
            weights.at[:, pl.ds(OWN * step, OWN)],
            load_sem.at[step],
        )

    def fetch_direct():
        return pltpu.make_async_copy(
            frames.at[:, pl.ds(CHANS * chan, CHANS)], direct, load_sem.at[CHANS]
        )

    def store(chunk):
        part = pl.ds(chunk * OUT_STEP, OUT_STEP)
        return pltpu.make_async_copy(written.at[part], result.at[part], store_sem.at[chunk])

    for step in range(CHANS):
        fetch(step).start()
    fetch_direct().start()

    low = low_half((WIDE, LANES))
    rates, entering = [], []
    for step in range(CHANS):
        source = lax.rem(chan + CHANS - step, CHANS)
        level = received[x * CHANS + source]
        rate = join3(level[WINDOW // 2], 6)
        spent = join3(level[WINDOW // 2], 3)
        total = jnp.zeros((WINDOW // 2, WIDE, LANES), F32)
        for other in range(XS - 1):
            earlier = received[other * CHANS + source]
            decay = jnp.exp(-join3(earlier[WINDOW // 2], 0) * rate).reshape(1, 1, LANES)
            added = decay * total + earlier[: WINDOW // 2].astype(F32)
            total = jnp.where(other < x, added, total)
        decay = jnp.exp(-spent * rate).reshape(1, 1, LANES)
        total = level[: WINDOW // 2].astype(F32) + decay * total
        swapped = swap_halves(total)
        rates.append(rate)
        entering.append(
            [jnp.where(low, total[r], swapped[r]) for r in range(WINDOW // 2)]
            + [jnp.where(low, swapped[r], total[r]) for r in range(WINDOW // 2)]
        )

    values = [intervals[t] for t in range(FRAMES)]
    first, second = running(values[:HALF]), running(values[HALF:])
    first_table, second_table = table(first, first), table(second, second)
    low_row = low_half((1, LANES))

    def halves(t, pair):
        a = blocks[2 * pair][t].astype(F32)
        b = blocks[2 * pair + 1][t].astype(F32)
        low = low_half(a.shape)
        return jnp.where(low, a, swap_halves(b)), jnp.where(low, swap_halves(a), b)

    for pair in range(2):
        rate = jnp.where(low_row, rates[2 * pair], rates[2 * pair + 1])
        part = slice(LANES * pair, LANES * (pair + 1))
        inflow = jnp.exp(-first_table * rate)
        spread(flows, 0, part, inflow)
        spread(flows, 1, part, jnp.exp(-second_table * rate))
        last = halves(HALF - 1, pair)[0]
        for r in range(WINDOW):
            arriving = jnp.where(low, entering[2 * pair][r], entering[2 * pair + 1][r])
            base[0, r, :, part] = arriving
            base[1, r, :, part] = inflow[HALF - 1 :] * arriving + last[r]

    def fill(t, carry):
        for pair in range(2):
            part = slice(LANES * pair, LANES * (pair + 1))
            for half, local in enumerate(halves(t, pair)):
                flow = flows[half, t, :, part]
                full = local + flow * base[half, :, :, part]
                states[half * HALF + t, :, :, part] = full.astype(BF16)
        return carry

    lax.fori_loop(0, HALF, fill, 0)
    for step in range(CHANS):
        fetch(step).wait()
    fetch_direct().wait()

    def convolve(chunk, carry):
        start = pl.multiple_of(chunk * OUT_STEP, OUT_STEP)
        size = OUT_STEP * CHANS * WIDE
        block = states[pl.ds(start, OUT_STEP)]
        taps = [block[:, i : i + CHANS].reshape(size, CH) for i in range(3)]
        operand = jnp.concatenate(taps, axis=1)
        shape = (OUT_STEP * CHANS, WIDE, CH)
        column = lax.broadcasted_iota(jnp.int32, shape, 1)
        parts = []
        for j in range(3):
            weight = jnp.concatenate([weights[3 * i + j] for i in range(3)], axis=0)
            parts.append(jnp.dot(operand, weight, preferred_element_type=F32).reshape(shape))
        total = parts[1]
        total += jnp.where(column == 0, 0.0, pltpu.roll(parts[0], 1, 1))
        total += jnp.where(column == WIDE - 1, 0.0, pltpu.roll(parts[2], WIDE - 1, 1))
        passed = direct[pl.ds(start, OUT_STEP)].astype(F32).reshape(shape)
        total += skip_gain[...].reshape(1, 1, CH) * passed
        written[pl.ds(start, OUT_STEP)] = total.astype(BF16).reshape(OUT_STEP, CHANS, WIDE, CH)
        store(chunk).start()
        return carry

    lax.fori_loop(0, OUT_CHUNKS, convolve, 0)
    for chunk in range(OUT_CHUNKS):
        store(chunk).wait()


def in_vmem():
    return pl.BlockSpec(memory_space=pltpu.VMEM)


def in_smem():
    return pl.BlockSpec(memory_space=pltpu.SMEM)


def anywhere():
    return pl.BlockSpec(memory_space=pl.ANY)


def drive(place, intervals, rates, kernel_t, frames):
    window = jax.ShapeDtypeStruct((HALF, WINDOW, WIDE, LANES), BF16)
    return pl.pallas_call(
        drive_kernel,
        out_shape=[window] * CHANS
        + [jax.ShapeDtypeStruct((ZS, ROWS // 2 + 1, WIDE, LANES), BF16)],
        in_specs=[in_smem(), in_smem(), in_vmem(), in_vmem(), anywhere()],
        out_specs=[anywhere()] * CHANS + [in_vmem()],
        scratch_shapes=[
            pltpu.VMEM((FRAMES, ROWS + 2, WIDE, CH), BF16),
            pltpu.VMEM((2, 3 * CH, CH), BF16),
            pltpu.VMEM((2, HALF, WIDE, LANES), F32),
            pltpu.VMEM((ROWS, WIDE, LANES), F32),
            pltpu.VMEM((HALF, ROWS + 2, WIDE, LANES), BF16),
            pltpu.SemaphoreType.DMA((CHUNKS, 2)),
            pltpu.SemaphoreType.DMA((CHUNKS, CHANS)),
        ],
        compiler_params=pltpu.CompilerParams(vmem_limit_bytes=32 << 20),
        name="drive",
    )(place, intervals, rates, kernel_t, frames)


def relay(place, rates, received):
    return pl.pallas_call(
        relay_kernel,
        out_shape=jax.ShapeDtypeStruct((XS * CHANS, WINDOW // 2 + 1, WIDE, LANES), BF16),
        in_specs=[in_smem(), in_vmem(), in_vmem()],
        out_specs=in_vmem(),
        compiler_params=pltpu.CompilerParams(vmem_limit_bytes=16 << 20),
        name="relay",
    )(place, rates, received)


def read_out(place, intervals, skip_gain, received, blocks, out_kernel, frames):
    return pl.pallas_call(
        readout_kernel,
        out_shape=jax.ShapeDtypeStruct((FRAMES, CHANS, WIDE, CH), BF16),
        in_specs=[in_smem(), in_smem(), in_vmem(), in_vmem()]
        + [in_vmem()] * CHANS
        + [anywhere(), anywhere()],
        out_specs=anywhere(),
        scratch_shapes=[
            pltpu.VMEM((9, CHANS * OWN, CH), BF16),
            pltpu.VMEM((FRAMES, CHANS, WIDE, CH), BF16),
            pltpu.VMEM((FRAMES, WINDOW, WIDE, CH), BF16),
            pltpu.VMEM((FRAMES, CHANS, WIDE, CH), BF16),
            pltpu.VMEM((2, HALF, WIDE, CH), F32),
            pltpu.VMEM((2, WINDOW, WIDE, CH), F32),
            pltpu.SemaphoreType.DMA((CHANS + 1,)),
            pltpu.SemaphoreType.DMA((OUT_CHUNKS,)),
        ],
        compiler_params=pltpu.CompilerParams(vmem_limit_bytes=32 << 20),
        name="read_out",
    )(place, intervals, skip_gain, received, *blocks, out_kernel, frames)


def local(frames, intervals, decay_rates, in_kernel, out_kernel, skip_gain):
    place = jnp.stack([lax.axis_index(name) for name in ("chan", "x", "z")]).astype(jnp.int32)
    rates = decay_rates.reshape(1, OWN)
    kernel_t = jnp.transpose(in_kernel.reshape(9, CH, OWN), (0, 2, 1))
    gathered = lax.all_gather(out_kernel.reshape(9, OWN, CH), "chan")
    *windows, message = drive(place, intervals, rates, kernel_t, frames)
    arrived = lax.all_to_all(message, "z", 0, 0)
    blocks = [windows[0]]
    for step in range(1, CHANS):
        route = [(c, (c + step) % CHANS) for c in range(CHANS)]
        blocks.append(lax.ppermute(windows[step], "chan", route))
    onward = relay(place, rates, arrived)
    onward = lax.all_to_all(onward, ("x", "chan"), 0, 0)
    return read_out(place, intervals, skip_gain.reshape(1, CH), onward, blocks, gathered, frames)


def solution(mesh):
    whole = jax.sharding.Mesh(
        mesh.devices.reshape(XS, ZS, CHANS, 2), ("x", "z", "chan", "clip")
    )
    time = ("clip", "x", "z")
    placed = (
        P(time, None, None, None),
        P(time),
        P("chan"),
        P(None, None, None, "chan"),
        P(None, None, "chan", None),
        P(),
    )
    return jax.shard_map(
        local,
        mesh=whole,
        in_specs=placed,
        out_specs=P(time, "chan", None, None),
        check_vma=False,
    )
```

time: 243 us -> 75.1 us (0.31)
  waiting for transfers between devices: 80.5 us -> 14.5 us
  blocking collectives: 40.2 us -> 0 us
  other arithmetic: 37.5 us -> 0.08 us
  matrix products: 36.2 us -> 0 us
  local copies, waits for them, and re-layouts: 31.4 us -> 7.93 us
  starting transfers between devices: 0.04 us -> 21.4 us
  Pallas kernels: 0 us -> 17.1 us
    reduce_scatter x1 -> x0, waiting for transfers between devices: 41.2 us -> none  [local(): lax.psum_scatter(partial_value.astype(jnp.bfloat16), 'chan', scatter_dime...]
    all_gather x1 -> x0, blocking collectives: 40.2 us -> none  [entering(): lax.all_gather(part.astype(kind), axis)]
    all_gather x1, waiting for transfers between devices: 39.3 us -> 0.01 us  [local(): gathered = lax.all_gather(out_kernel.reshape(9, OWN, CH), 'chan')]
    select_n x32 -> x0, other arithmetic: 28.9 us -> none  [hop(): return jax.tree.map(lambda a, b: jnp.where(reached, a, b), new, before)]
    conv_general_dilated x2 -> x0, matrix products: 26.4 us -> none  [convolve(): lax.conv_general_dilated(volume, kernel, (1, 1), padding, dimension_numbe...]
    pallas_call x0 -> x3, Pallas kernels: none -> 17.1 us  [the longest x1 9.06 us: drive(): pl.pallas_call(drive_kernel, out_shape=[window] * CHANS + [jax.ShapeDtype...]
    all_to_all x0 -> x2, starting transfers between devices: none -> 15.6 us  [the longest x1 8.58 us: local(): arrived = lax.all_to_all(message, 'z', 0, 0)]
    slice x2 -> x0, local copies, waits for them, and re-layouts: 9.89 us -> none  [recur(): block_end = local_states[-1]]
  transfers between devices with their start and end apart: 2 -> 6, of which waited for: 2 -> 3; matrix products, arithmetic and copies ran while one was open for 3% -> 0% of each run, Pallas kernels for 0% -> 14%
where the time goes in v1:
time: 75.1 us; the launch traced here: 74.5 us
  starting transfers between devices  21.4 us (28%)
  Pallas kernels  17.1 us (23%)
  waiting for transfers between devices  14.5 us (19%)
  between operations  13.5 us (18%)
  local copies, waits for them, and re-layouts  7.93 us (11%)
    pallas_call x1, Pallas kernels, drive(): pl.pallas_call(drive_kernel, out_shape=[window] * CHANS + [jax.ShapeDtype...  9.06 us
    all_to_all x1, starting transfers between devices, local(): arrived = lax.all_to_all(message, 'z', 0, 0)  8.58 us
    unnamed x18, local copies, waits for them, and re-layouts  7.93 us
    ppermute x3, waiting for transfers between devices, local(): blocks.append(lax.ppermute(windows[step], 'chan', route))  7.06 us
    all_to_all x1, starting transfers between devices, local(): onward = lax.all_to_all(onward, ('x', 'chan'), 0, 0)  7.03 us
    pallas_call x1, Pallas kernels, read_out(): pl.pallas_call(readout_kernel, out_shape=jax.ShapeDtypeStruct((FRAMES, CH...  6.57 us
    ppermute x3, starting transfers between devices, local(): blocks.append(lax.ppermute(windows[step], 'chan', route))  5.83 us
    all_to_all x1, waiting for transfers between devices, local(): arrived = lax.all_to_all(message, 'z', 0, 0)  5.3 us
  transfers between devices with their start and end apart: 6, of which 3 were waited for; matrix products, arithmetic and copies ran while one was open for 0% of the time, Pallas kernels for 14%

profile of v1, /device:TPU:32, one launch (start us, length us, event | category | flops | bytes accessed | tf_op | source)
XLA Modules:
  0.0 74.5 jit_solution(18148090252540552054)
XLA Ops:
  6.5 0.0 copy-start.5
  6.5 0.0 copy-start.7
  6.5 0.0 copy-start.8
  6.5 0.0 all-gather.2.cloned.1.call-start
  6.5 0.7 all-gather.2.cloned.1.call-update
  7.3 0.1 pad_add_fusion.place
  7.3 0.0 copy-start
  7.3 2.2 %copy-done = bf16[32,16,16,256]{3,2,1,0:T(8,128)(2,1)S(1)} copy-done((bf16[32,16,16,256]{3,2,1,0:T(8,128)(2,1)S(1)}, bf16[32,16,16,256]{3,2,1,0:T(8,128)(2,1)}, u32[]{:S(2)}) %copy-start) | copy-done | bytes 4194328
  9.5 0.0 copy-start.3
  9.5 1.0 %copy-done.3 = bf16[3,3,256,64]{2,3,1,0:T(8,128)(2,1)S(1)} copy-done((bf16[3,3,256,64]{2,3,1,0:T(8,128)(2,1)S(1)}, bf16[3,3,256,64]{2,3,1,0:T(8,128)(2,1)}, u32[]{:S(2)}) %copy-start.3) | copy-done | bytes 294936
  10.5 0.0 copy-start.4
  10.5 0.7 copy-done.4
  11.2 0.0 copy-start.6
  11.2 0.7 copy-done.6
  11.8 9.1 %drive.1 = (bf16[16,6,16,128]{3,2,1,0:T(8,128)(2,1)S(1)}, bf16[16,6,16,128]{3,2,1,0:T(8,128)(2,1)S(1)}, bf16[16,6,16,128]{3,2,1,0:T(8,128)(2,1)S(1)}, bf16[16,6,...) custom-call(s32[3]{0:T(128)S(1)} %pad_add_fusion.place, f32[32]{0:T(128)S(1)} %copy-done.4, f32[1,64]{1,0:T(1,128)S(1)} %bitcast.10, ...), custom_call_target="tpu_custom_call" | custom-call | tf_op jit(solution)/shard_map/drive/pallas_call | solution.py:354
  20.9 8.6 %all-to-all-start = ((bf16[8,9,16,128]{3,2,1,0:T(8,128)(2,1)}), bf16[8,9,16,128]{3,2,1,0:T(8,128)(2,1)S(1)}, u32[]{:S(2)}, u32[]{:S(2)}) async-start(bf16[8,9,16,128]{3,2,1,0:T(8,128)(2,1)} %get-tuple-element.10), calls=%async_computation | async-start | bytes 589824 | tf_op jit(solution)/shard_map/all_to_all | solution.py:414
  29.5 1.6 %collective-permute-start = (bf16[16,6,16,128]{3,2,1,0:T(8,128)(2,1)S(1)}, bf16[16,6,16,128]{3,2,1,0:T(8,128)(2,1)S(1)}, u32[]{:S(2)}, u32[]{:S(2)}) collective-permute-start(bf16[16,6,16,128]{3,2,1,0:T(8,128)(2,1)S(1)} %get-tuple-element.12), channel_id=1, source_target_pairs={{0,2},{2,4},{4,6},{6,0},{1,3},{3,5},{5,7},{7,1},{8,10},{10,12},{12... | collective-permute-start | bytes 1179656 | tf_op jit(solution)/shard_map/ppermute | solution.py:418
  31.0 2.9 %collective-permute-start.1 = (bf16[16,6,16,128]{3,2,1,0:T(8,128)(2,1)S(1)}, bf16[16,6,16,128]{3,2,1,0:T(8,128)(2,1)S(1)}, u32[]{:S(2)}, u32[]{:S(2)}) collective-permute-start(bf16[16,6,16,128]{3,2,1,0:T(8,128)(2,1)S(1)} %get-tuple-element.13), channel_id=1, source_target_pairs={{0,4},{2,6},{4,0},{6,2},{1,5},{3,7},{5,1},{7,3},{8,12},{10,14},{12... | collective-permute-start | bytes 1179656 | tf_op jit(solution)/shard_map/ppermute | solution.py:418
  33.9 1.3 %collective-permute-start.2 = (bf16[16,6,16,128]{3,2,1,0:T(8,128)(2,1)S(1)}, bf16[16,6,16,128]{3,2,1,0:T(8,128)(2,1)S(1)}, u32[]{:S(2)}, u32[]{:S(2)}) collective-permute-start(bf16[16,6,16,128]{3,2,1,0:T(8,128)(2,1)S(1)} %get-tuple-element.14), channel_id=1, source_target_pairs={{0,6},{2,0},{4,2},{6,4},{1,7},{3,1},{5,3},{7,5},{8,14},{10,8},{12,... | collective-permute-start | bytes 1179656 | tf_op jit(solution)/shard_map/ppermute | solution.py:418
  35.3 5.3 %all-to-all-done.received = bf16[8,9,16,128]{3,2,1,0:T(8,128)(2,1)S(1)} async-done(((bf16[8,9,16,128]{3,2,1,0:T(8,128)(2,1)}), bf16[8,9,16,128]{3,2,1,0:T(8,128)(2,1)S(1)}, u32[]{:S(2)}, u32[]{:S(2)}) %all-to-all-start) | async-done | bytes 294944 | tf_op jit(solution)/shard_map/all_to_all | solution.py:414
  40.6 0.0 copy-done.7
  40.6 1.5 %relay.1 = bf16[16,4,16,128]{3,2,1,0:T(8,128)(2,1)} custom-call(s32[3]{0:T(128)S(1)} %pad_add_fusion.place, f32[1,64]{1,0:T(1,128)S(1)} %bitcast.11, bf16[8,9,16,128]{3,2,1,0:T(8,128)(2,1)S(1)} %all-to-all-done.received), custom_call_target="tpu_custom_call" | custom-call | tf_op jit(solution)/shard_map/relay/pallas_call | solution.py:375
  42.1 7.0 %all-to-all-start.1 = ((bf16[16,4,16,128]{3,2,1,0:T(8,128)(2,1)}), bf16[16,4,16,128]{3,2,1,0:T(8,128)(2,1)S(1)}, u32[]{:S(2)}, u32[]{:S(2)}) async-start(bf16[16,4,16,128]{3,2,1,0:T(8,128)(2,1)} %relay.1), calls=%async_computation.1 | async-start | bytes 524288 | tf_op jit(solution)/shard_map/all_to_all | solution.py:420
  49.1 0.0 collective-permute-done.one
  49.1 7.1 %collective-permute-done.1.two = bf16[16,6,16,128]{3,2,1,0:T(8,128)(2,1)S(1)} collective-permute-done((bf16[16,6,16,128]{3,2,1,0:T(8,128)(2,1)S(1)}, bf16[16,6,16,128]{3,2,1,0:T(8,128)(2,1)S(1)}, u32[]{:S(2)}, u32[]{:S(2)}) %collective-permute-start.1) | collective-permute-done | bytes 393248 | tf_op jit(solution)/shard_map/ppermute | solution.py:418
  56.2 0.0 collective-permute-done.2.three
  56.2 1.4 %all-to-all-done.1.received = bf16[16,4,16,128]{3,2,1,0:T(8,128)(2,1)S(1)} async-done(((bf16[16,4,16,128]{3,2,1,0:T(8,128)(2,1)}), bf16[16,4,16,128]{3,2,1,0:T(8,128)(2,1)S(1)}, u32[]{:S(2)}, u32[]{:S(2)}) %all-to-all-start.1) | async-done | bytes 262176 | tf_op jit(solution)/shard_map/all_to_all | solution.py:420
  57.6 0.0 all-gather.2.cloned.1.call-done.out_kernel
  57.6 0.0 copy-done.5
  57.6 0.0 copy-done.8
  57.6 0.0 copy-start.1
  57.6 2.2 %copy-done.1 = bf16[32,16,16,256]{3,2,1,0:T(8,128)(2,1)S(1)} copy-done((bf16[32,16,16,256]{3,2,1,0:T(8,128)(2,1)S(1)}, bf16[32,16,16,256]{3,2,1,0:T(8,128)(2,1)}, u32[]{:S(2)}) %copy-start.1) | copy-done | bytes 4194328
  59.8 0.0 copy-start.2
  59.8 1.3 %copy-done.2 = bf16[4,9,64,256]{3,2,1,0:T(8,128)(2,1)S(1)} copy-done((bf16[4,9,64,256]{3,2,1,0:T(8,128)(2,1)S(1)}, bf16[4,9,64,256]{3,2,1,0:T(8,128)(2,1)}, u32[]{:S(2)}) %copy-start.2) | copy-done | bytes 1179672
  61.0 6.6 %read_out.1 = bf16[32,4,16,256]{3,2,1,0:T(8,128)(2,1)} custom-call(s32[3]{0:T(128)S(1)} %pad_add_fusion.place, f32[32]{0:T(128)S(1)} %copy-done.5, f32[1,256]{1,0:T(1,128)S(1)} %bitcast.12, bf16[16,4,16,128]{3,2,1,0:T(8,128)(2,1)S(1)} %all-to-all-done.1.received, bf16[16,6,16,128]{3,2,1,0:T(8,128)(2,1)S(1)} %get-tuple-element.11.own, ...), custom_call_target="tpu_custom_call" | custom-call | tf_op jit(solution)/shard_map/read_out/pallas_call | solution.py:386
Async XLA Ops:
  6.5 51.0 %copy-start.5 = (f32[32]{0:T(128)S(1)}, f32[32]{0:T(128)}, u32[]{:S(2)}) copy-start(f32[32]{0:T(128)} %intervals.3) | copy-start | bytes 388
  6.5 34.0 %copy-start.7 = (f32[64]{0:T(128)S(1)}, f32[64]{0:T(128)}, u32[]{:S(2)}) copy-start(f32[64]{0:T(128)} %param.8) | copy-start | bytes 772
  6.5 51.0 %copy-start.8 = (f32[256]{0:T(256)S(1)}, f32[256]{0:T(256)}, u32[]{:S(2)}) copy-start(f32[256]{0:T(256)} %param.11) | copy-start | bytes 3076
  6.5 51.0 %all-gather.2.cloned.1.call-start = ((), (), s32[]{:S(2)}) async-start(), calls=%async_computation.2 | async-start | bytes 1474560 | tf_op jit(solution)/shard_map/all_gather | solution.py:412
  7.3 2.2 %copy-start = (bf16[32,16,16,256]{3,2,1,0:T(8,128)(2,1)S(1)}, bf16[32,16,16,256]{3,2,1,0:T(8,128)(2,1)}, u32[]{:S(2)}) copy-start(bf16[32,16,16,256]{3,2,1,0:T(8,128)(2,1)} %frames.3) | copy-start | bytes 12582916
  9.5 1.0 %copy-start.3 = (bf16[3,3,256,64]{2,3,1,0:T(8,128)(2,1)S(1)}, bf16[3,3,256,64]{2,3,1,0:T(8,128)(2,1)}, u32[]{:S(2)}) copy-start(bf16[3,3,256,64]{2,3,1,0:T(8,128)(2,1)} %param.9) | copy-start | bytes 884740
  10.5 0.7 copy-start.4
  11.2 0.7 copy-start.6
  20.9 19.7 %all-to-all-start = ((bf16[8,9,16,128]{3,2,1,0:T(8,128)(2,1)}), bf16[8,9,16,128]{3,2,1,0:T(8,128)(2,1)S(1)}, u32[]{:S(2)}, u32[]{:S(2)}) async-start(bf16[8,9,16,128]{3,2,1,0:T(8,128)(2,1)} %get-tuple-element.10), calls=%async_computation | async-start | bytes 589824 | tf_op jit(solution)/shard_map/all_to_all | solution.py:414
  29.5 19.6 %collective-permute-start = (bf16[16,6,16,128]{3,2,1,0:T(8,128)(2,1)S(1)}, bf16[16,6,16,128]{3,2,1,0:T(8,128)(2,1)S(1)}, u32[]{:S(2)}, u32[]{:S(2)}) collective-permute-start(bf16[16,6,16,128]{3,2,1,0:T(8,128)(2,1)S(1)} %get-tuple-element.12), channel_id=1, source_target_pairs={{0,2},{2,4},{4,6},{6,0},{1,3},{3,5},{5,7},{7,1},{8,10},{10,12},{12... | collective-permute-start | bytes 1179656 | tf_op jit(solution)/shard_map/ppermute | solution.py:418
  31.0 25.1 %collective-permute-start.1 = (bf16[16,6,16,128]{3,2,1,0:T(8,128)(2,1)S(1)}, bf16[16,6,16,128]{3,2,1,0:T(8,128)(2,1)S(1)}, u32[]{:S(2)}, u32[]{:S(2)}) collective-permute-start(bf16[16,6,16,128]{3,2,1,0:T(8,128)(2,1)S(1)} %get-tuple-element.13), channel_id=1, source_target_pairs={{0,4},{2,6},{4,0},{6,2},{1,5},{3,7},{5,1},{7,3},{8,12},{10,14},{12... | collective-permute-start | bytes 1179656 | tf_op jit(solution)/shard_map/ppermute | solution.py:418
  33.9 22.2 %collective-permute-start.2 = (bf16[16,6,16,128]{3,2,1,0:T(8,128)(2,1)S(1)}, bf16[16,6,16,128]{3,2,1,0:T(8,128)(2,1)S(1)}, u32[]{:S(2)}, u32[]{:S(2)}) collective-permute-start(bf16[16,6,16,128]{3,2,1,0:T(8,128)(2,1)S(1)} %get-tuple-element.14), channel_id=1, source_target_pairs={{0,6},{2,0},{4,2},{6,4},{1,7},{3,1},{5,3},{7,5},{8,14},{10,8},{12,... | collective-permute-start | bytes 1179656 | tf_op jit(solution)/shard_map/ppermute | solution.py:418
  42.1 15.5 %all-to-all-start.1 = ((bf16[16,4,16,128]{3,2,1,0:T(8,128)(2,1)}), bf16[16,4,16,128]{3,2,1,0:T(8,128)(2,1)S(1)}, u32[]{:S(2)}, u32[]{:S(2)}) async-start(bf16[16,4,16,128]{3,2,1,0:T(8,128)(2,1)} %relay.1), calls=%async_computation.1 | async-start | bytes 524288 | tf_op jit(solution)/shard_map/all_to_all | solution.py:420
  57.6 2.2 %copy-start.1 = (bf16[32,16,16,256]{3,2,1,0:T(8,128)(2,1)S(1)}, bf16[32,16,16,256]{3,2,1,0:T(8,128)(2,1)}, u32[]{:S(2)}) copy-start(bf16[32,16,16,256]{3,2,1,0:T(8,128)(2,1)} %frames.3) | copy-start | bytes 12582916
  59.8 1.3 %copy-start.2 = (bf16[4,9,64,256]{3,2,1,0:T(8,128)(2,1)S(1)}, bf16[4,9,64,256]{3,2,1,0:T(8,128)(2,1)}, u32[]{:S(2)}) copy-start(bf16[4,9,64,256]{3,2,1,0:T(8,128)(2,1)} %all-gather.2.cloned.1.call-done.out_kernel) | copy-start | bytes 3538948
Sparse Core Ops, SparseCore 0:
  9.2 38.2 all-gather.1

commit v2 on v1

--- a/solution.py
+++ b/solution.py
@@ -79,11 +79,20 @@
 
 
 def drive_kernel(
-    place, intervals, rates, kernel_t, frames,
+    place, intervals_far, rates_far, kernel_far, frames,
     own, one, two, three, message,
-    padded, weights, factors, state, kept, load_sem, store_sem,
+    intervals, rates, kernel_t, padded, weights, factors, state, kept,
+    load_sem, store_sem, small_sem,
 ):
     windows = (own, one, two, three)
+    small = [
+        pltpu.make_async_copy(source, target, small_sem.at[index])
+        for index, (source, target) in enumerate(
+            ((kernel_far, kernel_t), (intervals_far, intervals), (rates_far, rates))
+        )
+    ]
+    for copy in small:
+        copy.start()
 
     def load(chunk, half):
         start = half * HALF + chunk * STEP
@@ -112,6 +121,8 @@
     kept[:, 0:1] = empty
     kept[:, ROWS + 1 : ROWS + 2] = empty
     nothing = jnp.zeros((CH, OWN), BF16)
+    for copy in small:
+        copy.wait()
     for i in range(3):
         tap = [kernel_t[3 * i + j].astype(F32).T.astype(BF16) for j in range(3)]
         weights[0, CH * i : CH * (i + 1), :] = jnp.concatenate([tap[0], tap[1], tap[2], nothing], 1)
@@ -176,8 +187,11 @@
             store(chunk, step).wait()
 
 
-def relay_kernel(place, rates, received, message):
+def relay_kernel(place, rates_far, received, message, rates, small_sem):
     x, z = place[1], place[2]
+    copy = pltpu.make_async_copy(rates_far, rates, small_sem)
+    copy.start()
+    copy.wait()
     rate = doubled(rates[...])
     total = jnp.zeros((ROWS // 2, WIDE, LANES), F32)
     before = total
@@ -225,16 +239,25 @@
 
 
 def readout_kernel(
-    place, intervals, skip_gain, received, own, one, two, three, out_kernel, frames,
+    place, intervals_far, gain_far, received, own, one, two, three,
+    kernel_own, kernel_one, kernel_two, kernel_three, frames,
     result,
-    weights, direct, states, written, flows, base, load_sem, store_sem,
+    intervals, skip_gain, weights, direct, states, written, flows, base,
+    load_sem, store_sem, small_sem,
 ):
+    small = [
+        pltpu.make_async_copy(intervals_far, intervals, small_sem.at[0]),
+        pltpu.make_async_copy(gain_far, skip_gain, small_sem.at[1]),
+    ]
+    for copy in small:
+        copy.start()
+    kernels = (kernel_own, kernel_one, kernel_two, kernel_three)
     chan, x = place[0], place[1]
     blocks = (own, one, two, three)
 
     def fetch(step):
         return pltpu.make_async_copy(
-            out_kernel.at[lax.rem(chan + CHANS - step, CHANS)],
+            kernels[step],
             weights.at[:, pl.ds(OWN * step, OWN)],
             load_sem.at[step],
         )
@@ -274,6 +297,8 @@
             + [jnp.where(low, swapped[r], total[r]) for r in range(WINDOW // 2)]
         )
 
+    for copy in small:
+        copy.wait()
     values = [intervals[t] for t in range(FRAMES)]
     first, second = running(values[:HALF]), running(values[HALF:])
     first_table, second_table = table(first, first), table(second, second)
@@ -349,15 +374,22 @@
     return pl.BlockSpec(memory_space=pl.ANY)
 
 
+def far():
+    return pl.BlockSpec(memory_space=pltpu.HBM)
+
+
 def drive(place, intervals, rates, kernel_t, frames):
     window = jax.ShapeDtypeStruct((HALF, WINDOW, WIDE, LANES), BF16)
     return pl.pallas_call(
         drive_kernel,
         out_shape=[window] * CHANS
         + [jax.ShapeDtypeStruct((ZS, ROWS // 2 + 1, WIDE, LANES), BF16)],
-        in_specs=[in_smem(), in_smem(), in_vmem(), in_vmem(), anywhere()],
+        in_specs=[in_smem(), far(), far(), far(), far()],
         out_specs=[anywhere()] * CHANS + [in_vmem()],
         scratch_shapes=[
+            pltpu.SMEM((FRAMES,), F32),
+            pltpu.VMEM((1, OWN), F32),
+            pltpu.VMEM((9, OWN, CH), BF16),
             pltpu.VMEM((FRAMES, ROWS + 2, WIDE, CH), BF16),
             pltpu.VMEM((2, 3 * CH, CH), BF16),
             pltpu.VMEM((2, HALF, WIDE, LANES), F32),
@@ -365,8 +397,9 @@
             pltpu.VMEM((HALF, ROWS + 2, WIDE, LANES), BF16),
             pltpu.SemaphoreType.DMA((CHUNKS, 2)),
             pltpu.SemaphoreType.DMA((CHUNKS, CHANS)),
+            pltpu.SemaphoreType.DMA((3,)),
         ],
-        compiler_params=pltpu.CompilerParams(vmem_limit_bytes=32 << 20),
+        compiler_params=pltpu.CompilerParams(vmem_limit_bytes=62 << 20),
         name="drive",
     )(place, intervals, rates, kernel_t, frames)
 
@@ -375,22 +408,27 @@
     return pl.pallas_call(
         relay_kernel,
         out_shape=jax.ShapeDtypeStruct((XS * CHANS, WINDOW // 2 + 1, WIDE, LANES), BF16),
-        in_specs=[in_smem(), in_vmem(), in_vmem()],
+        in_specs=[in_smem(), far(), in_vmem()],
         out_specs=in_vmem(),
+        scratch_shapes=[pltpu.VMEM((1, OWN), F32), pltpu.SemaphoreType.DMA],
         compiler_params=pltpu.CompilerParams(vmem_limit_bytes=16 << 20),
         name="relay",
     )(place, rates, received)
 
 
-def read_out(place, intervals, skip_gain, received, blocks, out_kernel, frames):
+def read_out(place, intervals, skip_gain, received, blocks, kernels, frames):
     return pl.pallas_call(
         readout_kernel,
         out_shape=jax.ShapeDtypeStruct((FRAMES, CHANS, WIDE, CH), BF16),
-        in_specs=[in_smem(), in_smem(), in_vmem(), in_vmem()]
+        in_specs=[in_smem(), far(), far(), in_vmem()]
         + [in_vmem()] * CHANS
-        + [anywhere(), anywhere()],
+        + [far()]
+        + [anywhere()] * (CHANS - 1)
+        + [far()],
         out_specs=anywhere(),
         scratch_shapes=[
+            pltpu.SMEM((FRAMES,), F32),
+            pltpu.VMEM((1, CH), F32),
             pltpu.VMEM((9, CHANS * OWN, CH), BF16),
             pltpu.VMEM((FRAMES, CHANS, WIDE, CH), BF16),
             pltpu.VMEM((FRAMES, WINDOW, WIDE, CH), BF16),
@@ -399,26 +437,29 @@
             pltpu.VMEM((2, WINDOW, WIDE, CH), F32),
             pltpu.SemaphoreType.DMA((CHANS + 1,)),
             pltpu.SemaphoreType.DMA((OUT_CHUNKS,)),
+            pltpu.SemaphoreType.DMA((2,)),
         ],
-        compiler_params=pltpu.CompilerParams(vmem_limit_bytes=32 << 20),
+        compiler_params=pltpu.CompilerParams(vmem_limit_bytes=62 << 20),
         name="read_out",
-    )(place, intervals, skip_gain, received, *blocks, out_kernel, frames)
+    )(place, intervals, skip_gain, received, *blocks, *kernels, frames)
 
 
 def local(frames, intervals, decay_rates, in_kernel, out_kernel, skip_gain):
     place = jnp.stack([lax.axis_index(name) for name in ("chan", "x", "z")]).astype(jnp.int32)
     rates = decay_rates.reshape(1, OWN)
     kernel_t = jnp.transpose(in_kernel.reshape(9, CH, OWN), (0, 2, 1))
-    gathered = lax.all_gather(out_kernel.reshape(9, OWN, CH), "chan")
+    kernels = [out_kernel.reshape(9, OWN, CH)]
+    kernels += [around(kernels[0], step) for step in range(1, CHANS)]
     *windows, message = drive(place, intervals, rates, kernel_t, frames)
     arrived = lax.all_to_all(message, "z", 0, 0)
-    blocks = [windows[0]]
-    for step in range(1, CHANS):
-        route = [(c, (c + step) % CHANS) for c in range(CHANS)]
-        blocks.append(lax.ppermute(windows[step], "chan", route))
+    blocks = [windows[0]] + [around(windows[step], step) for step in range(1, CHANS)]
     onward = relay(place, rates, arrived)
     onward = lax.all_to_all(onward, ("x", "chan"), 0, 0)
-    return read_out(place, intervals, skip_gain.reshape(1, CH), onward, blocks, gathered, frames)
+    return read_out(place, intervals, skip_gain.reshape(1, CH), onward, blocks, kernels, frames)
+
+
+def around(value, step):
+    return lax.ppermute(value, "chan", [(c, (c + step) % CHANS) for c in range(CHANS)])
 
 
 def solution(mesh):

time: 75.1 us -> 67.6 us (0.900)
  between operations: 13.5 us -> 0.08 us
  local copies, waits for them, and re-layouts: 7.93 us -> 1.06 us
  starting transfers between devices: 21.4 us -> 26.8 us
  waiting for transfers between devices: 14.5 us -> 18.6 us
  Pallas kernels: 17.1 us -> 19.9 us
    ppermute x3 -> x6, waiting for transfers between devices: 7.06 us -> 18.5 us  [around(): lax.ppermute(value, 'chan', [(c, (c + step) % CHANS) for c in range(CHANS)])]
    unnamed x18 -> x20, local copies, waits for them, and re-layouts: 7.93 us -> 1.06 us
    all_to_all x1, waiting for transfers between devices: 5.3 us -> 0.01 us  [local(): arrived = lax.all_to_all(message, 'z', 0, 0)]
    ppermute x3 -> x6, starting transfers between devices: 5.83 us -> 9.18 us  [around(): lax.ppermute(value, 'chan', [(c, (c + step) % CHANS) for c in range(CHANS)])]
    all_to_all x1, starting transfers between devices: 7.03 us -> 9 us  [local(): onward = lax.all_to_all(onward, ('x', 'chan'), 0, 0)]
    pallas_call x1, Pallas kernels: 6.57 us -> 8.06 us  [read_out(): pl.pallas_call(readout_kernel, out_shape=jax.ShapeDtypeStruct((FRAMES, CH...]
    all_to_all x1, waiting for transfers between devices: 1.4 us -> 0.13 us  [local(): onward = lax.all_to_all(onward, ('x', 'chan'), 0, 0)]
    pallas_call x1, Pallas kernels: 9.06 us -> 10.3 us  [drive(): pl.pallas_call(drive_kernel, out_shape=[window] * CHANS + [jax.ShapeDtype...]
  transfers between devices with their start and end apart: 6 -> 8, of which waited for: 3 -> 4; matrix products, arithmetic and copies ran while one was open for 0% -> 0% of each run, Pallas kernels for 14% -> 2%
where the time goes in v2:
time: 67.6 us; the launch traced here: 67 us
  starting transfers between devices  26.8 us (40%)
  Pallas kernels  19.9 us (29%)
  waiting for transfers between devices  18.6 us (28%)
  local copies, waits for them, and re-layouts  1.06 us (2%)
    ppermute x6, waiting for transfers between devices, around(): lax.ppermute(value, 'chan', [(c, (c + step) % CHANS) for c in range(CHANS)])  18.5 us
    pallas_call x1, Pallas kernels, drive(): pl.pallas_call(drive_kernel, out_shape=[window] * CHANS + [jax.ShapeDtype...  10.3 us
    ppermute x6, starting transfers between devices, around(): lax.ppermute(value, 'chan', [(c, (c + step) % CHANS) for c in range(CHANS)])  9.18 us
    all_to_all x1, starting transfers between devices, local(): onward = lax.all_to_all(onward, ('x', 'chan'), 0, 0)  9 us
    all_to_all x1, starting transfers between devices, local(): arrived = lax.all_to_all(message, 'z', 0, 0)  8.58 us
    pallas_call x1, Pallas kernels, read_out(): pl.pallas_call(readout_kernel, out_shape=jax.ShapeDtypeStruct((FRAMES, CH...  8.06 us
    pallas_call x1, Pallas kernels, relay(): pl.pallas_call(relay_kernel, out_shape=jax.ShapeDtypeStruct((XS * CHANS,...  1.48 us
  transfers between devices with their start and end apart: 8, of which 4 were waited for; matrix products, arithmetic and copies ran while one was open for 0% of the time, Pallas kernels for 2%

profile of v2, /device:TPU:32, one launch (start us, length us, event | category | flops | bytes accessed | tf_op | source)
XLA Modules:
  0.0 67.0 jit_solution(15300313266624752920)
XLA Ops:
  0.0 0.0 copy-start.1
  0.0 0.0 copy-start.6
  0.0 0.7 pad_add_fusion.place
  0.7 0.0 copy-start
  0.7 10.3 %drive.1 = (bf16[16,6,16,128]{3,2,1,0:T(8,128)(2,1)}, bf16[16,6,16,128]{3,2,1,0:T(8,128)(2,1)}, bf16[16,6,16,128]{3,2,1,0:T(8,128)(2,1)}, bf16[16,6,16,128]{3,2,1,0:T(8,128)(2,1)}, bf16[8,9,16,128]{3,2,1,0:T(8,128)(2,1)}) custom-call(s32[3]{0:T(128)} %pad_add_fusion.place, f32[32]{0:T(128)} %intervals_far.3, f32[1,64]{1,0:T(1,128)} %bitcast.9, ...), custom_call_target="tpu_custom_call" | custom-call | tf_op jit(solution)/shard_map/drive/pallas_call | solution.py:383
  11.0 8.6 %all-to-all-start = ((bf16[8,9,16,128]{3,2,1,0:T(8,128)(2,1)}), bf16[8,9,16,128]{3,2,1,0:T(8,128)(2,1)S(1)}, u32[]{:S(2)}, u32[]{:S(2)}) async-start(bf16[8,9,16,128]{3,2,1,0:T(8,128)(2,1)} %get-tuple-element.10), calls=%async_computation | async-start | bytes 589824 | tf_op jit(solution)/shard_map/all_to_all | solution.py:454
  19.6 0.0 copy-done.6
  19.6 3.0 %collective-permute-start.5 = (bf16[9,64,256]{2,1,0:T(8,128)(2,1)S(1)}, bf16[9,64,256]{2,1,0:T(8,128)(2,1)S(1)}, u32[]{:S(2)}, u32[]{:S(2)}) collective-permute-start(bf16[9,64,256]{2,1,0:T(8,128)(2,1)S(1)} %bitcast.12), channel_id=1, source_target_pairs={{0,6},{2,0},{4,2},{6,4},{1,7},{3,1},{5,3},{7,5},{8,14},{10,8},{12,... | collective-permute-start | bytes 884744 | tf_op jit(solution)/shard_map/ppermute | solution.py:462
  22.6 0.0 collective-permute-start
  22.6 2.2 %collective-permute-start.1 = (bf16[16,6,16,128]{3,2,1,0:T(8,128)(2,1)}, bf16[16,6,16,128]{3,2,1,0:T(8,128)(2,1)S(1)}, u32[]{:S(2)}, u32[]{:S(2)}) collective-permute-start(bf16[16,6,16,128]{3,2,1,0:T(8,128)(2,1)} %get-tuple-element.13), channel_id=1, source_target_pairs={{0,4},{2,6},{4,0},{6,2},{1,5},{3,7},{5,1},{7,3},{8,12},{10,14},{12... | collective-permute-start | bytes 1179656 | tf_op jit(solution)/shard_map/ppermute | solution.py:462
  24.8 1.1 %collective-permute-start.2 = (bf16[16,6,16,128]{3,2,1,0:T(8,128)(2,1)}, bf16[16,6,16,128]{3,2,1,0:T(8,128)(2,1)S(1)}, u32[]{:S(2)}, u32[]{:S(2)}) collective-permute-start(bf16[16,6,16,128]{3,2,1,0:T(8,128)(2,1)} %get-tuple-element.14), channel_id=1, source_target_pairs={{0,6},{2,0},{4,2},{6,4},{1,7},{3,1},{5,3},{7,5},{8,14},{10,8},{12,... | collective-permute-start | bytes 1179656 | tf_op jit(solution)/shard_map/ppermute | solution.py:462
  25.9 2.9 %collective-permute-start.4 = (bf16[9,64,256]{2,1,0:T(8,128)(2,1)S(1)}, bf16[9,64,256]{2,1,0:T(8,128)(2,1)S(1)}, u32[]{:S(2)}, u32[]{:S(2)}) collective-permute-start(bf16[9,64,256]{2,1,0:T(8,128)(2,1)S(1)} %bitcast.13), channel_id=1, source_target_pairs={{0,4},{2,6},{4,0},{6,2},{1,5},{3,7},{5,1},{7,3},{8,12},{10,14},{12... | collective-permute-start | bytes 884744 | tf_op jit(solution)/shard_map/ppermute | solution.py:462
  28.8 9.7 %collective-permute-done.5.kernel_three = bf16[9,64,256]{2,1,0:T(8,128)(2,1)S(1)} collective-permute-done((bf16[9,64,256]{2,1,0:T(8,128)(2,1)S(1)}, bf16[9,64,256]{2,1,0:T(8,128)(2,1)S(1)}, u32[]{:S(2)}, u32[]{:S(2)}) %collective-permute-start.5) | collective-permute-done | bytes 294944 | tf_op jit(solution)/shard_map/ppermute | solution.py:462
  38.5 0.0 copy-start.7
  38.5 0.0 collective-permute-start.3
  38.5 0.0 all-to-all-done.received
  38.5 0.0 copy-done.1
  38.5 0.0 copy-done
  38.5 1.5 %relay.1 = bf16[16,4,16,128]{3,2,1,0:T(8,128)(2,1)} custom-call(s32[3]{0:T(128)S(1)} %copy-done, f32[1,64]{1,0:T(1,128)S(1)} %bitcast.10, bf16[8,9,16,128]{3,2,1,0:T(8,128)(2,1)S(1)} %all-to-all-done.received), custom_call_target="tpu_custom_call" | custom-call | tf_op jit(solution)/shard_map/relay/pallas_call | solution.py:408
  40.0 9.0 %all-to-all-start.1 = ((bf16[16,4,16,128]{3,2,1,0:T(8,128)(2,1)}), bf16[16,4,16,128]{3,2,1,0:T(8,128)(2,1)S(1)}, u32[]{:S(2)}, u32[]{:S(2)}) async-start(bf16[16,4,16,128]{3,2,1,0:T(8,128)(2,1)} %relay.1), calls=%async_computation.1 | async-start | bytes 524288 | tf_op jit(solution)/shard_map/all_to_all | solution.py:457
  49.0 1.9 %collective-permute-done.4.kernel_two = bf16[9,64,256]{2,1,0:T(8,128)(2,1)S(1)} collective-permute-done((bf16[9,64,256]{2,1,0:T(8,128)(2,1)S(1)}, bf16[9,64,256]{2,1,0:T(8,128)(2,1)S(1)}, u32[]{:S(2)}, u32[]{:S(2)}) %collective-permute-start.4) | collective-permute-done | bytes 294944 | tf_op jit(solution)/shard_map/ppermute | solution.py:462
  50.9 0.0 copy-start.8
  50.9 6.8 %collective-permute-done.3.kernel_one = bf16[9,64,256]{2,1,0:T(8,128)(2,1)S(1)} collective-permute-done((bf16[9,64,256]{2,1,0:T(8,128)(2,1)S(1)}, bf16[9,64,256]{2,1,0:T(8,128)(2,1)S(1)}, u32[]{:S(2)}, u32[]{:S(2)}) %collective-permute-start.3) | collective-permute-done | bytes 294944 | tf_op jit(solution)/shard_map/ppermute | solution.py:462
  57.7 0.0 copy-start.9
  57.7 0.0 collective-permute-done.one
  57.7 0.0 copy-start.3
  57.7 0.0 collective-permute-done.1.two
  57.7 0.0 copy-start.4
  57.8 0.0 collective-permute-done.2.three
  57.8 0.0 copy-start.5
  57.8 0.1 all-to-all-done.1.received
  57.9 0.0 copy-done.8
  57.9 0.0 copy-start.2
  57.9 0.5 copy-done.9
  58.4 0.0 copy-done.7
  58.4 0.1 copy-done.3
  58.6 0.1 copy-done.4
  58.7 0.1 copy-done.5
  58.9 0.1 copy-done.2
  59.0 8.1 %read_out.1 = bf16[32,4,16,256]{3,2,1,0:T(8,128)(2,1)} custom-call(s32[3]{0:T(128)} %pad_add_fusion.place, f32[32]{0:T(128)} %intervals_far.3, f32[1,256]{1,0:T(1,128)} %bitcast.16, bf16[16,4,16,128]{3,2,1,0:T(8,128)(2,1)} %copy-done.2, bf16[16,6,16,128]{3,2,1,0:T(8,128)(2,1)} %get-tuple-element.11.own, bf16[16,6,16,128]{3,2,1,0:T(8,128)(2,1)} %copy-done.3, ...), custom_call_target="tpu_custom_call" | custom-call | tf_op jit(solution)/shard_map/read_out/pallas_call | solution.py:420
Async XLA Ops:
  0.0 38.5 %copy-start.1 = (f32[64]{0:T(128)S(1)}, f32[64]{0:T(128)}, u32[]{:S(2)}) copy-start(f32[64]{0:T(128)} %param.8) | copy-start | bytes 772
  0.0 19.6 %copy-start.6 = (bf16[3,3,64,256]{3,2,1,0:T(8,128)(2,1)S(1)}, bf16[3,3,64,256]{3,2,1,0:T(8,128)(2,1)}, u32[]{:S(2)}) copy-start(bf16[3,3,64,256]{3,2,1,0:T(8,128)(2,1)} %param.10) | copy-start | bytes 884740
  0.7 37.8 %copy-start = (s32[3]{0:T(128)S(1)}, s32[3]{0:T(128)}, u32[]{:S(2)}) copy-start(s32[3]{0:T(128)} %pad_add_fusion.place) | copy-start | bytes 40
  11.0 27.5 %all-to-all-start = ((bf16[8,9,16,128]{3,2,1,0:T(8,128)(2,1)}), bf16[8,9,16,128]{3,2,1,0:T(8,128)(2,1)S(1)}, u32[]{:S(2)}, u32[]{:S(2)}) async-start(bf16[8,9,16,128]{3,2,1,0:T(8,128)(2,1)} %get-tuple-element.10), calls=%async_computation | async-start | bytes 589824 | tf_op jit(solution)/shard_map/all_to_all | solution.py:454
  19.6 18.9 %collective-permute-start.5 = (bf16[9,64,256]{2,1,0:T(8,128)(2,1)S(1)}, bf16[9,64,256]{2,1,0:T(8,128)(2,1)S(1)}, u32[]{:S(2)}, u32[]{:S(2)}) collective-permute-start(bf16[9,64,256]{2,1,0:T(8,128)(2,1)S(1)} %bitcast.12), channel_id=1, source_target_pairs={{0,6},{2,0},{4,2},{6,4},{1,7},{3,1},{5,3},{7,5},{8,14},{10,8},{12,... | collective-permute-start | bytes 884744 | tf_op jit(solution)/shard_map/ppermute | solution.py:462
  22.6 35.1 %collective-permute-start = (bf16[16,6,16,128]{3,2,1,0:T(8,128)(2,1)}, bf16[16,6,16,128]{3,2,1,0:T(8,128)(2,1)S(1)}, u32[]{:S(2)}, u32[]{:S(2)}) collective-permute-start(bf16[16,6,16,128]{3,2,1,0:T(8,128)(2,1)} %get-tuple-element.12), channel_id=1, source_target_pairs={{0,2},{2,4},{4,6},{6,0},{1,3},{3,5},{5,7},{7,1},{8,10},{10,12},{12... | collective-permute-start | bytes 1179656 | tf_op jit(solution)/shard_map/ppermute | solution.py:462
  22.6 35.1 %collective-permute-start.1 = (bf16[16,6,16,128]{3,2,1,0:T(8,128)(2,1)}, bf16[16,6,16,128]{3,2,1,0:T(8,128)(2,1)S(1)}, u32[]{:S(2)}, u32[]{:S(2)}) collective-permute-start(bf16[16,6,16,128]{3,2,1,0:T(8,128)(2,1)} %get-tuple-element.13), channel_id=1, source_target_pairs={{0,4},{2,6},{4,0},{6,2},{1,5},{3,7},{5,1},{7,3},{8,12},{10,14},{12... | collective-permute-start | bytes 1179656 | tf_op jit(solution)/shard_map/ppermute | solution.py:462
  24.8 33.0 %collective-permute-start.2 = (bf16[16,6,16,128]{3,2,1,0:T(8,128)(2,1)}, bf16[16,6,16,128]{3,2,1,0:T(8,128)(2,1)S(1)}, u32[]{:S(2)}, u32[]{:S(2)}) collective-permute-start(bf16[16,6,16,128]{3,2,1,0:T(8,128)(2,1)} %get-tuple-element.14), channel_id=1, source_target_pairs={{0,6},{2,0},{4,2},{6,4},{1,7},{3,1},{5,3},{7,5},{8,14},{10,8},{12,... | collective-permute-start | bytes 1179656 | tf_op jit(solution)/shard_map/ppermute | solution.py:462
  25.9 25.0 %collective-permute-start.4 = (bf16[9,64,256]{2,1,0:T(8,128)(2,1)S(1)}, bf16[9,64,256]{2,1,0:T(8,128)(2,1)S(1)}, u32[]{:S(2)}, u32[]{:S(2)}) collective-permute-start(bf16[9,64,256]{2,1,0:T(8,128)(2,1)S(1)} %bitcast.13), channel_id=1, source_target_pairs={{0,4},{2,6},{4,0},{6,2},{1,5},{3,7},{5,1},{7,3},{8,12},{10,14},{12... | collective-permute-start | bytes 884744 | tf_op jit(solution)/shard_map/ppermute | solution.py:462
  38.5 20.0 %copy-start.7 = (bf16[9,64,256]{2,1,0:T(8,128)(2,1)}, bf16[9,64,256]{2,1,0:T(8,128)(2,1)S(1)}, u32[]{:S(2)}) copy-start(bf16[9,64,256]{2,1,0:T(8,128)(2,1)S(1)} %collective-permute-done.5.kernel_three) | copy-start | bytes 884740
  38.5 19.2 %collective-permute-start.3 = (bf16[9,64,256]{2,1,0:T(8,128)(2,1)S(1)}, bf16[9,64,256]{2,1,0:T(8,128)(2,1)S(1)}, u32[]{:S(2)}, u32[]{:S(2)}) collective-permute-start(bf16[9,64,256]{2,1,0:T(8,128)(2,1)S(1)} %bitcast.14), channel_id=1, source_target_pairs={{0,2},{2,4},{4,6},{6,0},{1,3},{3,5},{5,7},{7,1},{8,10},{10,12},{12... | collective-permute-start | bytes 884744 | tf_op jit(solution)/shard_map/ppermute | solution.py:462
  40.0 17.9 %all-to-all-start.1 = ((bf16[16,4,16,128]{3,2,1,0:T(8,128)(2,1)}), bf16[16,4,16,128]{3,2,1,0:T(8,128)(2,1)S(1)}, u32[]{:S(2)}, u32[]{:S(2)}) async-start(bf16[16,4,16,128]{3,2,1,0:T(8,128)(2,1)} %relay.1), calls=%async_computation.1 | async-start | bytes 524288 | tf_op jit(solution)/shard_map/all_to_all | solution.py:457
  50.9 7.0 %copy-start.8 = (bf16[9,64,256]{2,1,0:T(8,128)(2,1)}, bf16[9,64,256]{2,1,0:T(8,128)(2,1)S(1)}, u32[]{:S(2)}) copy-start(bf16[9,64,256]{2,1,0:T(8,128)(2,1)S(1)} %collective-permute-done.4.kernel_two) | copy-start | bytes 884740
  57.7 0.7 %copy-start.9 = (bf16[9,64,256]{2,1,0:T(8,128)(2,1)}, bf16[9,64,256]{2,1,0:T(8,128)(2,1)S(1)}, u32[]{:S(2)}) copy-start(bf16[9,64,256]{2,1,0:T(8,128)(2,1)S(1)} %collective-permute-done.3.kernel_one) | copy-start | bytes 884740
  57.7 0.9 %copy-start.3 = (bf16[16,6,16,128]{3,2,1,0:T(8,128)(2,1)}, bf16[16,6,16,128]{3,2,1,0:T(8,128)(2,1)S(1)}, u32[]{:S(2)}) copy-start(bf16[16,6,16,128]{3,2,1,0:T(8,128)(2,1)S(1)} %collective-permute-done.one) | copy-start | bytes 1179652
  57.7 1.0 %copy-start.4 = (bf16[16,6,16,128]{3,2,1,0:T(8,128)(2,1)}, bf16[16,6,16,128]{3,2,1,0:T(8,128)(2,1)S(1)}, u32[]{:S(2)}) copy-start(bf16[16,6,16,128]{3,2,1,0:T(8,128)(2,1)S(1)} %collective-permute-done.1.two) | copy-start | bytes 1179652
  57.8 1.1 %copy-start.5 = (bf16[16,6,16,128]{3,2,1,0:T(8,128)(2,1)}, bf16[16,6,16,128]{3,2,1,0:T(8,128)(2,1)S(1)}, u32[]{:S(2)}) copy-start(bf16[16,6,16,128]{3,2,1,0:T(8,128)(2,1)S(1)} %collective-permute-done.2.three) | copy-start | bytes 1179652
  57.9 1.0 %copy-start.2 = (bf16[16,4,16,128]{3,2,1,0:T(8,128)(2,1)}, bf16[16,4,16,128]{3,2,1,0:T(8,128)(2,1)S(1)}, u32[]{:S(2)}) copy-start(bf16[16,4,16,128]{3,2,1,0:T(8,128)(2,1)S(1)} %all-to-all-done.1.received) | copy-start | bytes 786436

commit v3 on v2

--- a/solution.py
+++ b/solution.py
@@ -71,6 +71,12 @@
     return jnp.where(value < 0.125, series, 1.0 - jnp.exp(-value))
 
 
+def beside(left, centre, right):
+    column = lax.broadcasted_iota(jnp.int32, centre.shape, 1)
+    total = centre + jnp.where(column == 0, 0.0, pltpu.roll(left, 1, 1))
+    return total + jnp.where(column == WIDE - 1, 0.0, pltpu.roll(right, WIDE - 1, 1))
+
+
 def running(values):
     sums = [values[0]]
     for value in values[1:]:
@@ -79,12 +85,10 @@
 
 
 def drive_kernel(
-    place, intervals_far, rates_far, kernel_far, frames,
-    own, one, two, three, message,
-    intervals, rates, kernel_t, padded, weights, factors, state, kept,
-    load_sem, store_sem, small_sem,
+    intervals_far, rates_far, kernel_far, frames,
+    message,
+    intervals, rates, kernel_t, padded, weights, factors, state, load_sem, small_sem,
 ):
-    windows = (own, one, two, three)
     small = [
         pltpu.make_async_copy(source, target, small_sem.at[index])
         for index, (source, target) in enumerate(
@@ -102,14 +106,6 @@
             load_sem.at[chunk, half],
         )
 
-    def store(chunk, step):
-        first = CHANS * lax.rem(place[0] + step, CHANS)
-        return pltpu.make_async_copy(
-            kept.at[pl.ds(chunk * STEP, STEP), pl.ds(first, WINDOW)],
-            windows[step].at[pl.ds(chunk * STEP, STEP)],
-            store_sem.at[chunk, step],
-        )
-
     for chunk in range(CHUNKS):
         load(chunk, 0).start()
         load(chunk, 1).start()
@@ -117,9 +113,6 @@
     empty = jnp.zeros((FRAMES, 1, WIDE, CH), BF16)
     padded[:, 0:1] = empty
     padded[:, ROWS + 1 : ROWS + 2] = empty
-    empty = jnp.zeros((HALF, 1, WIDE, LANES), BF16)
-    kept[:, 0:1] = empty
-    kept[:, ROWS + 1 : ROWS + 2] = empty
     nothing = jnp.zeros((CH, OWN), BF16)
     for copy in small:
         copy.wait()
@@ -153,18 +146,13 @@
         centre = swap_halves(jnp.where(low, second[:, :LANES], first[:, :LANES]))
         right = first[:, LANES:] + second[:, LANES:]
         shape = (STEP * ROWS, WIDE, LANES)
-        column = lax.broadcasted_iota(jnp.int32, shape, 1)
-        left = jnp.where(column == 0, 0.0, pltpu.roll(left.reshape(shape), 1, 1))
-        right = jnp.where(column == WIDE - 1, 0.0, pltpu.roll(right.reshape(shape), WIDE - 1, 1))
-        drives = (left + centre.reshape(shape) + right).reshape(STEP, ROWS, WIDE, LANES)
+        drives = beside(left.reshape(shape), centre.reshape(shape), right.reshape(shape))
+        drives = drives.reshape(STEP, ROWS, WIDE, LANES)
         carried = state[...]
         for step in range(STEP):
             decay, gain = factors[0, start + step], factors[1, start + step]
             carried = decay * carried + gain * drives[step]
-            kept[start + step, 1 : ROWS + 1] = carried.astype(BF16)
         state[...] = carried
-        for step in range(CHANS):
-            store(chunk, step).start()
         return carry
 
     lax.fori_loop(0, CHUNKS, advance, 0)
@@ -178,16 +166,96 @@
     packed = jnp.where(low, other[: ROWS // 2], end[ROWS // 2 :]).astype(BF16)
     row = lax.broadcasted_iota(jnp.int32, (WIDE, LANES), 0)
     pieces = split3(jnp.full((WIDE, LANES), total, F32))
-    extra = jnp.where(row == 0, pieces[0].astype(F32), jnp.where(row == 1, pieces[1].astype(F32), pieces[2].astype(F32))).astype(BF16)
+    extra = jnp.zeros((WIDE, LANES), F32)
+    for index, piece in enumerate(pieces):
+        extra = jnp.where(row == index, piece.astype(F32), extra)
+    extra = extra.astype(BF16)
     for z in range(ZS):
         message[z, : ROWS // 2] = packed
         message[z, ROWS // 2] = extra
-    for chunk in range(CHUNKS):
-        for step in range(CHANS):
-            store(chunk, step).wait()
-
-
-def relay_kernel(place, rates_far, received, message, rates, small_sem):
+
+
+WINDOW_STEP = 4
+WINDOW_CHUNKS = FRAMES // WINDOW_STEP
+TALL = 12
+
+
+def window_kernel(
+    place, kernel_own, kernel_one, kernel_two, kernel_three, frames,
+    drives, token,
+    rows, weights, written, load_sem, kernel_sem, store_sem,
+):
+    chan = place[0]
+    kernels = (kernel_own, kernel_one, kernel_two, kernel_three)
+    source = jnp.clip(CHANS * chan - 2, 0, 8)
+    target = source - CHANS * chan + 4
+
+    def load(chunk):
+        part = pl.ds(chunk * WINDOW_STEP, WINDOW_STEP)
+        return pltpu.make_async_copy(
+            frames.at[part, pl.ds(source, 8)], rows.at[part, pl.ds(target, 8)], load_sem.at[chunk]
+        )
+
+    def fetch(step):
+        return pltpu.make_async_copy(
+            kernels[step], weights.at[:, pl.ds(OWN * step, OWN)], kernel_sem.at[step]
+        )
+
+    def store(chunk):
+        part = pl.ds(chunk * WINDOW_STEP, WINDOW_STEP)
+        return pltpu.make_async_copy(written.at[part], drives.at[part], store_sem.at[chunk])
+
+    token[...] = jnp.zeros_like(token)
+    for step in range(CHANS):
+        fetch(step).start()
+    for chunk in range(WINDOW_CHUNKS):
+        load(chunk).start()
+    empty = jnp.zeros((FRAMES, 2, WIDE, CH), BF16)
+
+    @pl.when(chan == 0)
+    def _():
+        rows[:, 2:4] = empty
+
+    @pl.when(chan == CHANS - 1)
+    def _():
+        rows[:, 8:10] = empty
+
+    for step in range(CHANS):
+        fetch(step).wait()
+
+    def convolve(chunk, carry):
+        load(chunk).wait()
+        start = pl.multiple_of(chunk * WINDOW_STEP, WINDOW_STEP)
+        block = rows[pl.ds(start, WINDOW_STEP)]
+        size = WINDOW_STEP * WINDOW * WIDE
+        taps = [block[:, 2 + i : 2 + i + WINDOW].reshape(size, CH) for i in range(3)]
+        operand = jnp.concatenate(taps, axis=1)
+        shape = (WINDOW_STEP * WINDOW, WIDE, CH)
+        parts = []
+        for j in range(3):
+            weight = jnp.concatenate([weights[3 * i + j] for i in range(3)], axis=1)
+            parts.append(
+                lax.dot_general(
+                    operand, weight, (((1,), (1,)), ((), ())), preferred_element_type=F32
+                ).reshape(shape)
+            )
+        total = beside(*parts).reshape(WINDOW_STEP, WINDOW, WIDE, CH)
+        for r in range(WINDOW):
+            kept = total[:, r]
+            if r == 0:
+                kept = jnp.where(chan == 0, 0.0, kept)
+            if r == WINDOW - 1:
+                kept = jnp.where(chan == CHANS - 1, 0.0, kept)
+            written[pl.ds(start, WINDOW_STEP), r] = kept.astype(BF16)
+        store(chunk).start()
+        return carry
+
+    lax.fori_loop(0, WINDOW_CHUNKS, convolve, 0)
+    for chunk in range(WINDOW_CHUNKS):
+        store(chunk).wait()
+
+
+def relay_kernel(place, rates_far, received, token, message, rates, small_sem):
     x, z = place[1], place[2]
     copy = pltpu.make_async_copy(rates_far, rates, small_sem)
     copy.start()
@@ -239,11 +307,11 @@
 
 
 def readout_kernel(
-    place, intervals_far, gain_far, received, own, one, two, three,
+    place, intervals_far, gain_far, received, drives_far,
     kernel_own, kernel_one, kernel_two, kernel_three, frames,
     result,
-    intervals, skip_gain, weights, direct, states, written, flows, base,
-    load_sem, store_sem, small_sem,
+    intervals, skip_gain, weights, direct, drives, states, written, factors, state,
+    load_sem, drive_sem, store_sem, small_sem,
 ):
     small = [
         pltpu.make_async_copy(intervals_far, intervals, small_sem.at[0]),
@@ -253,13 +321,10 @@
         copy.start()
     kernels = (kernel_own, kernel_one, kernel_two, kernel_three)
     chan, x = place[0], place[1]
-    blocks = (own, one, two, three)
 
     def fetch(step):
         return pltpu.make_async_copy(
-            kernels[step],
-            weights.at[:, pl.ds(OWN * step, OWN)],
-            load_sem.at[step],
+            kernels[step], weights.at[:, pl.ds(OWN * step, OWN)], load_sem.at[step]
         )
 
     def fetch_direct():
@@ -267,10 +332,16 @@
             frames.at[:, pl.ds(CHANS * chan, CHANS)], direct, load_sem.at[CHANS]
         )
 
+    def load(chunk):
+        part = pl.ds(chunk * OUT_STEP, OUT_STEP)
+        return pltpu.make_async_copy(drives_far.at[part], drives.at[part], drive_sem.at[chunk])
+
     def store(chunk):
         part = pl.ds(chunk * OUT_STEP, OUT_STEP)
         return pltpu.make_async_copy(written.at[part], result.at[part], store_sem.at[chunk])
 
+    for chunk in range(OUT_CHUNKS):
+        load(chunk).start()
     for step in range(CHANS):
         fetch(step).start()
     fetch_direct().start()
@@ -300,59 +371,43 @@
     for copy in small:
         copy.wait()
     values = [intervals[t] for t in range(FRAMES)]
-    first, second = running(values[:HALF]), running(values[HALF:])
-    first_table, second_table = table(first, first), table(second, second)
     low_row = low_half((1, LANES))
-
-    def halves(t, pair):
-        a = blocks[2 * pair][t].astype(F32)
-        b = blocks[2 * pair + 1][t].astype(F32)
-        low = low_half(a.shape)
-        return jnp.where(low, a, swap_halves(b)), jnp.where(low, swap_halves(a), b)
-
     for pair in range(2):
         rate = jnp.where(low_row, rates[2 * pair], rates[2 * pair + 1])
         part = slice(LANES * pair, LANES * (pair + 1))
-        inflow = jnp.exp(-first_table * rate)
-        spread(flows, 0, part, inflow)
-        spread(flows, 1, part, jnp.exp(-second_table * rate))
-        last = halves(HALF - 1, pair)[0]
+        for half in range(2):
+            some = values[HALF * half : HALF * (half + 1)]
+            scaled = table(some, some) * rate
+            rest = pl.ds(HALF * half, HALF)
+            spread(factors.at[:, rest], 0, part, jnp.exp(-scaled))
+            spread(factors.at[:, rest], 1, part, jnp.sqrt(one_minus_exp(2.0 * scaled)))
         for r in range(WINDOW):
-            arriving = jnp.where(low, entering[2 * pair][r], entering[2 * pair + 1][r])
-            base[0, r, :, part] = arriving
-            base[1, r, :, part] = inflow[HALF - 1 :] * arriving + last[r]
-
-    def fill(t, carry):
-        for pair in range(2):
-            part = slice(LANES * pair, LANES * (pair + 1))
-            for half, local in enumerate(halves(t, pair)):
-                flow = flows[half, t, :, part]
-                full = local + flow * base[half, :, :, part]
-                states[half * HALF + t, :, :, part] = full.astype(BF16)
-        return carry
-
-    lax.fori_loop(0, HALF, fill, 0)
+            state[r, :, part] = jnp.where(low, entering[2 * pair][r], entering[2 * pair + 1][r])
+
     for step in range(CHANS):
         fetch(step).wait()
     fetch_direct().wait()
 
     def convolve(chunk, carry):
         start = pl.multiple_of(chunk * OUT_STEP, OUT_STEP)
+        load(chunk).wait()
+        carried = state[...]
+        for step in range(OUT_STEP):
+            decay, gain = factors[0, start + step], factors[1, start + step]
+            carried = decay * carried + gain * drives[start + step].astype(F32)
+            states[start + step] = carried.astype(BF16)
+        state[...] = carried
         size = OUT_STEP * CHANS * WIDE
         block = states[pl.ds(start, OUT_STEP)]
         taps = [block[:, i : i + CHANS].reshape(size, CH) for i in range(3)]
         operand = jnp.concatenate(taps, axis=1)
         shape = (OUT_STEP * CHANS, WIDE, CH)
-        column = lax.broadcasted_iota(jnp.int32, shape, 1)
         parts = []
         for j in range(3):
             weight = jnp.concatenate([weights[3 * i + j] for i in range(3)], axis=0)
             parts.append(jnp.dot(operand, weight, preferred_element_type=F32).reshape(shape))
-        total = parts[1]
-        total += jnp.where(column == 0, 0.0, pltpu.roll(parts[0], 1, 1))
-        total += jnp.where(column == WIDE - 1, 0.0, pltpu.roll(parts[2], WIDE - 1, 1))
         passed = direct[pl.ds(start, OUT_STEP)].astype(F32).reshape(shape)
-        total += skip_gain[...].reshape(1, 1, CH) * passed
+        total = beside(*parts) + skip_gain[...].reshape(1, 1, CH) * passed
         written[pl.ds(start, OUT_STEP)] = total.astype(BF16).reshape(OUT_STEP, CHANS, WIDE, CH)
         store(chunk).start()
         return carry
@@ -374,18 +429,18 @@
     return pl.BlockSpec(memory_space=pl.ANY)
 
 
-def far():
-    return pl.BlockSpec(memory_space=pltpu.HBM)
-
-
-def drive(place, intervals, rates, kernel_t, frames):
-    window = jax.ShapeDtypeStruct((HALF, WINDOW, WIDE, LANES), BF16)
+def cost(microseconds):
+    return pl.CostEstimate(
+        flops=int(microseconds * 1.1e9), bytes_accessed=1 << 20, transcendentals=0
+    )
+
+
+def drive(intervals, rates, kernel_t, frames):
     return pl.pallas_call(
         drive_kernel,
-        out_shape=[window] * CHANS
-        + [jax.ShapeDtypeStruct((ZS, ROWS // 2 + 1, WIDE, LANES), BF16)],
-        in_specs=[in_smem(), far(), far(), far(), far()],
-        out_specs=[anywhere()] * CHANS + [in_vmem()],
+        out_shape=jax.ShapeDtypeStruct((ZS, ROWS // 2 + 1, WIDE, LANES), BF16),
+        in_specs=[anywhere()] * 4,
+        out_specs=in_vmem(),
         scratch_shapes=[
             pltpu.SMEM((FRAMES,), F32),
             pltpu.VMEM((1, OWN), F32),
@@ -394,37 +449,56 @@
             pltpu.VMEM((2, 3 * CH, CH), BF16),
             pltpu.VMEM((2, HALF, WIDE, LANES), F32),
             pltpu.VMEM((ROWS, WIDE, LANES), F32),
-            pltpu.VMEM((HALF, ROWS + 2, WIDE, LANES), BF16),
             pltpu.SemaphoreType.DMA((CHUNKS, 2)),
-            pltpu.SemaphoreType.DMA((CHUNKS, CHANS)),
             pltpu.SemaphoreType.DMA((3,)),
         ],
         compiler_params=pltpu.CompilerParams(vmem_limit_bytes=62 << 20),
+        cost_estimate=cost(8),
         name="drive",
-    )(place, intervals, rates, kernel_t, frames)
-
-
-def relay(place, rates, received):
+    )(intervals, rates, kernel_t, frames)
+
+
+def window(place, kernels, frames):
+    return pl.pallas_call(
+        window_kernel,
+        out_shape=[
+            jax.ShapeDtypeStruct((FRAMES, WINDOW, WIDE, CH), BF16),
+            jax.ShapeDtypeStruct((8, LANES), F32),
+        ],
+        in_specs=[in_smem()] + [anywhere()] * (CHANS + 1),
+        out_specs=[anywhere(), in_vmem()],
+        scratch_shapes=[
+            pltpu.VMEM((FRAMES, TALL, WIDE, CH), BF16),
+            pltpu.VMEM((9, CHANS * OWN, CH), BF16),
+            pltpu.VMEM((FRAMES, WINDOW, WIDE, CH), BF16),
+            pltpu.SemaphoreType.DMA((WINDOW_CHUNKS,)),
+            pltpu.SemaphoreType.DMA((CHANS,)),
+            pltpu.SemaphoreType.DMA((WINDOW_CHUNKS,)),
+        ],
+        compiler_params=pltpu.CompilerParams(vmem_limit_bytes=61 << 20),
+        cost_estimate=cost(6),
+        name="window",
+    )(place, *kernels, frames)
+
+
+def relay(place, rates, received, token):
     return pl.pallas_call(
         relay_kernel,
         out_shape=jax.ShapeDtypeStruct((XS * CHANS, WINDOW // 2 + 1, WIDE, LANES), BF16),
-        in_specs=[in_smem(), far(), in_vmem()],
+        in_specs=[in_smem(), anywhere(), in_vmem(), anywhere()],
         out_specs=in_vmem(),
         scratch_shapes=[pltpu.VMEM((1, OWN), F32), pltpu.SemaphoreType.DMA],
         compiler_params=pltpu.CompilerParams(vmem_limit_bytes=16 << 20),
+        cost_estimate=cost(1),
         name="relay",
-    )(place, rates, received)
-
-
-def read_out(place, intervals, skip_gain, received, blocks, kernels, frames):
+    )(place, rates, received, token)
+
+
+def read_out(place, intervals, skip_gain, received, drives, kernels, frames):
     return pl.pallas_call(
         readout_kernel,
         out_shape=jax.ShapeDtypeStruct((FRAMES, CHANS, WIDE, CH), BF16),
-        in_specs=[in_smem(), far(), far(), in_vmem()]
-        + [in_vmem()] * CHANS
-        + [far()]
-        + [anywhere()] * (CHANS - 1)
-        + [far()],
+        in_specs=[in_smem(), anywhere(), anywhere(), in_vmem()] + [anywhere()] * (CHANS + 2),
         out_specs=anywhere(),
         scratch_shapes=[
             pltpu.SMEM((FRAMES,), F32),
@@ -432,34 +506,40 @@
             pltpu.VMEM((9, CHANS * OWN, CH), BF16),
             pltpu.VMEM((FRAMES, CHANS, WIDE, CH), BF16),
             pltpu.VMEM((FRAMES, WINDOW, WIDE, CH), BF16),
+            pltpu.VMEM((FRAMES, WINDOW, WIDE, CH), BF16),
             pltpu.VMEM((FRAMES, CHANS, WIDE, CH), BF16),
-            pltpu.VMEM((2, HALF, WIDE, CH), F32),
-            pltpu.VMEM((2, WINDOW, WIDE, CH), F32),
+            pltpu.VMEM((2, FRAMES, WIDE, CH), F32),
+            pltpu.VMEM((WINDOW, WIDE, CH), F32),
             pltpu.SemaphoreType.DMA((CHANS + 1,)),
+            pltpu.SemaphoreType.DMA((OUT_CHUNKS,)),
             pltpu.SemaphoreType.DMA((OUT_CHUNKS,)),
             pltpu.SemaphoreType.DMA((2,)),
         ],
-        compiler_params=pltpu.CompilerParams(vmem_limit_bytes=62 << 20),
+        compiler_params=pltpu.CompilerParams(vmem_limit_bytes=61 << 20),
+        cost_estimate=cost(6),
         name="read_out",
-    )(place, intervals, skip_gain, received, *blocks, *kernels, frames)
+    )(place, intervals, skip_gain, received, drives, *kernels, frames)
+
+
+def around(value):
+    routes = [[(c, (c + step) % CHANS) for c in range(CHANS)] for step in range(1, CHANS)]
+    return [value] + [lax.ppermute(value, "chan", route) for route in routes]
 
 
 def local(frames, intervals, decay_rates, in_kernel, out_kernel, skip_gain):
     place = jnp.stack([lax.axis_index(name) for name in ("chan", "x", "z")]).astype(jnp.int32)
     rates = decay_rates.reshape(1, OWN)
     kernel_t = jnp.transpose(in_kernel.reshape(9, CH, OWN), (0, 2, 1))
-    kernels = [out_kernel.reshape(9, OWN, CH)]
-    kernels += [around(kernels[0], step) for step in range(1, CHANS)]
-    *windows, message = drive(place, intervals, rates, kernel_t, frames)
+    in_kernels = around(kernel_t)
+    out_kernels = around(out_kernel.reshape(9, OWN, CH))
+    message = drive(intervals, rates, kernel_t, frames)
     arrived = lax.all_to_all(message, "z", 0, 0)
-    blocks = [windows[0]] + [around(windows[step], step) for step in range(1, CHANS)]
-    onward = relay(place, rates, arrived)
+    drives, token = window(place, in_kernels, frames)
+    onward = relay(place, rates, arrived, token)
     onward = lax.all_to_all(onward, ("x", "chan"), 0, 0)
-    return read_out(place, intervals, skip_gain.reshape(1, CH), onward, blocks, kernels, frames)
-
-
-def around(value, step):
-    return lax.ppermute(value, "chan", [(c, (c + step) % CHANS) for c in range(CHANS)])
+    return read_out(
+        place, intervals, skip_gain.reshape(1, CH), onward, drives, out_kernels, frames
+    )
 
 
 def solution(mesh):

time: 67.6 us -> 63.2 us (0.935)
  waiting for transfers between devices: 18.6 us -> 8.43 us
  Pallas kernels: 19.9 us -> 26.6 us
  starting transfers between devices: 26.8 us -> 24.3 us
  local copies, waits for them, and re-layouts: 1.06 us -> 2.8 us
    ppermute x6, waiting for transfers between devices: 18.5 us -> 0.02 us  [around(): return [value] + [lax.ppermute(value, 'chan', route) for route in routes]]
    all_to_all x1, waiting for transfers between devices: 0.13 us -> 8.41 us  [local(): onward = lax.all_to_all(onward, ('x', 'chan'), 0, 0)]
    pallas_call x1 -> x2, Pallas kernels: 10.3 us -> 18 us  [the longest x1 9.27 us: window(): pl.pallas_call(window_kernel, out_shape=[jax.ShapeDtypeStruct((FRAMES, WI...]
    all_to_all x1, starting transfers between devices: 9 us -> 7.07 us  [local(): onward = lax.all_to_all(onward, ('x', 'chan'), 0, 0)]
    unnamed x20 -> x22, local copies, waits for them, and re-layouts: 1.06 us -> 2.8 us
    pallas_call x1, Pallas kernels: 8.06 us -> 7.07 us  [read_out(): pl.pallas_call(readout_kernel, out_shape=jax.ShapeDtypeStruct((FRAMES, CH...]
  transfers between devices with their start and end apart: 8 -> 8, of which waited for: 4 -> 1; matrix products, arithmetic and copies ran while one was open for 0% -> 1% of each run, Pallas kernels for 2% -> 31%
where the time goes in v3:
time: 63.2 us; the launch traced here: 62.9 us
  Pallas kernels  26.6 us (42%)
  starting transfers between devices  24.3 us (38%)
  waiting for transfers between devices  8.43 us (13%)
  local copies, waits for them, and re-layouts  2.8 us (4%)
    pallas_call x1, Pallas kernels, window(): pl.pallas_call(window_kernel, out_shape=[jax.ShapeDtypeStruct((FRAMES, WI...  9.27 us
    pallas_call x1, Pallas kernels, drive(): pl.pallas_call(drive_kernel, out_shape=jax.ShapeDtypeStruct((ZS, ROWS //...  8.74 us
    ppermute x6, starting transfers between devices, around(): return [value] + [lax.ppermute(value, 'chan', route) for route in routes]  8.65 us
    all_to_all x1, starting transfers between devices, local(): arrived = lax.all_to_all(message, 'z', 0, 0)  8.58 us
    all_to_all x1, waiting for transfers between devices, local(): onward = lax.all_to_all(onward, ('x', 'chan'), 0, 0)  8.41 us
    pallas_call x1, Pallas kernels, read_out(): pl.pallas_call(readout_kernel, out_shape=jax.ShapeDtypeStruct((FRAMES, CH...  7.07 us
    all_to_all x1, starting transfers between devices, local(): onward = lax.all_to_all(onward, ('x', 'chan'), 0, 0)  7.07 us
    unnamed x22, local copies, waits for them, and re-layouts  2.8 us
  transfers between devices with their start and end apart: 8, of which 1 were waited for; matrix products, arithmetic and copies ran while one was open for 1% of the time, Pallas kernels for 31%

profile of v3, /device:TPU:32, one launch (start us, length us, event | category | flops | bytes accessed | tf_op | source)
XLA Modules:
  0.0 62.9 jit_solution(7242362836578381821)
XLA Ops:
  0.0 3.0 %collective-permute-start.2 = (bf16[9,64,256]{2,1,0:T(8,128)(2,1)}, bf16[9,64,256]{2,1,0:T(8,128)(2,1)S(1)}, u32[]{:S(2)}, u32[]{:S(2)}) collective-permute-start(bf16[9,64,256]{2,1,0:T(8,128)(2,1)} %bitcast.11), channel_id=1, source_target_pairs={{0,6},{2,0},{4,2},{6,4},{1,7},{3,1},{5,3},{7,5},{8,14},{10,8},{12,... | collective-permute-start | bytes 884744 | tf_op jit(solution)/shard_map/ppermute | solution.py:526
  3.0 0.6 %collective-permute-start.1 = (bf16[9,64,256]{2,1,0:T(8,128)(2,1)}, bf16[9,64,256]{2,1,0:T(8,128)(2,1)S(1)}, u32[]{:S(2)}, u32[]{:S(2)}) collective-permute-start(bf16[9,64,256]{2,1,0:T(8,128)(2,1)} %bitcast.12), channel_id=1, source_target_pairs={{0,4},{2,6},{4,0},{6,2},{1,5},{3,7},{5,1},{7,3},{8,12},{10,14},{12... | collective-permute-start | bytes 884744 | tf_op jit(solution)/shard_map/ppermute | solution.py:526
  3.6 1.0 %collective-permute-start = (bf16[9,64,256]{2,1,0:T(8,128)(2,1)}, bf16[9,64,256]{2,1,0:T(8,128)(2,1)S(1)}, u32[]{:S(2)}, u32[]{:S(2)}) collective-permute-start(bf16[9,64,256]{2,1,0:T(8,128)(2,1)} %bitcast.13), channel_id=1, source_target_pairs={{0,2},{2,4},{4,6},{6,0},{1,3},{3,5},{5,7},{7,1},{8,10},{10,12},{12... | collective-permute-start | bytes 884744 | tf_op jit(solution)/shard_map/ppermute | solution.py:526
  4.6 2.3 %collective-permute-start.5 = (bf16[9,64,256]{2,1,0:T(8,128)(2,1)}, bf16[9,64,256]{2,1,0:T(8,128)(2,1)S(1)}, u32[]{:S(2)}, u32[]{:S(2)}) collective-permute-start(bf16[9,64,256]{2,1,0:T(8,128)(2,1)} %bitcast.16), channel_id=1, source_target_pairs={{0,6},{2,0},{4,2},{6,4},{1,7},{3,1},{5,3},{7,5},{8,14},{10,8},{12,... | collective-permute-start | bytes 884744 | tf_op jit(solution)/shard_map/ppermute | solution.py:526
  6.9 1.7 %collective-permute-start.4 = (bf16[9,64,256]{2,1,0:T(8,128)(2,1)}, bf16[9,64,256]{2,1,0:T(8,128)(2,1)S(1)}, u32[]{:S(2)}, u32[]{:S(2)}) collective-permute-start(bf16[9,64,256]{2,1,0:T(8,128)(2,1)} %bitcast.17), channel_id=1, source_target_pairs={{0,4},{2,6},{4,0},{6,2},{1,5},{3,7},{5,1},{7,3},{8,12},{10,14},{12... | collective-permute-start | bytes 884744 | tf_op jit(solution)/shard_map/ppermute | solution.py:526
  8.6 0.0 copy-start.4
  8.6 8.7 %drive.1 = bf16[8,9,16,128]{3,2,1,0:T(8,128)(2,1)} custom-call(f32[32]{0:T(128)} %intervals_far.3, f32[1,64]{1,0:T(1,128)} %bitcast.9, bf16[9,64,256]{2,1,0:T(8,128)(2,1)} %bitcast.14, bf16[32,16,16,256]{3,2,1,0:T(8,128)(2,1)} %frames.5), custom_call_target="tpu_custom_call" | custom-call | flops 8800000000 | bytes 1048576 | tf_op jit(solution)/shard_map/drive/pallas_call | solution.py:439
  17.3 8.6 %all-to-all-start = ((bf16[8,9,16,128]{3,2,1,0:T(8,128)(2,1)}), bf16[8,9,16,128]{3,2,1,0:T(8,128)(2,1)S(1)}, u32[]{:S(2)}, u32[]{:S(2)}) async-start(bf16[8,9,16,128]{3,2,1,0:T(8,128)(2,1)} %drive.1), calls=%async_computation | async-start | bytes 589824 | tf_op jit(solution)/shard_map/all_to_all | solution.py:536
  25.9 0.6 pad_add_fusion.place
  26.5 0.0 copy-start
  26.5 0.0 copy-start.1
  26.5 0.0 collective-permute-done.2.kernel_three
  26.5 0.0 copy-done.4
  26.5 0.0 copy-start.7
  26.5 0.1 collective-permute-start.3
  26.6 0.0 collective-permute-done.1.kernel_two
  26.6 0.0 copy-start.8
  26.6 0.0 collective-permute-done.kernel_one
  26.6 0.6 copy-done.7
  27.2 0.1 copy-done.8
  27.3 0.0 copy-start.9
  27.3 0.7 %copy-done.9 = bf16[9,64,256]{2,1,0:T(8,128)(2,1)} copy-done((bf16[9,64,256]{2,1,0:T(8,128)(2,1)}, bf16[9,64,256]{2,1,0:T(8,128)(2,1)S(1)}, u32[]{:S(2)}) %copy-start.9) | copy-done | bytes 294936
  28.0 9.3 %window.1 = (bf16[32,6,16,256]{3,2,1,0:T(8,128)(2,1)}, f32[8,128]{1,0:T(8,128)}) custom-call(s32[3]{0:T(128)} %pad_add_fusion.place, bf16[9,64,256]{2,1,0:T(8,128)(2,1)} %bitcast.15, bf16[9,64,256]{2,1,0:T(8,128)(2,1)} %copy-done.9, bf16[9,64,256]{2,1,0:T(8,128)(2,1)} %copy-done.8, bf16[9,64,256]{2,1,0:T(8,128)(2,1)} %copy-done.7, ...), custom_call_target="tpu_custom_call" | custom-call | flops 6600000000 | bytes 1048576 | tf_op jit(solution)/shard_map/window/pallas_call | solution.py:462
  37.3 0.0 all-to-all-done.received
  37.3 0.0 copy-done
  37.3 0.0 copy-done.1
  37.4 0.0 copy-start.2
  37.4 0.7 %copy-done.2 = f32[8,128]{1,0:T(8,128)S(1)} copy-done((f32[8,128]{1,0:T(8,128)S(1)}, f32[8,128]{1,0:T(8,128)}, u32[]{:S(2)}) %copy-start.2) | copy-done | bytes 4120
  38.0 1.5 %relay.1 = bf16[16,4,16,128]{3,2,1,0:T(8,128)(2,1)} custom-call(s32[3]{0:T(128)S(1)} %copy-done, f32[1,64]{1,0:T(1,128)S(1)} %bitcast.10, bf16[8,9,16,128]{3,2,1,0:T(8,128)(2,1)S(1)} %all-to-all-done.received, f32[8,128]{1,0:T(8,128)S(1)} %copy-done.2), custom_call_target="tpu_custom_call" | custom-call | flops 1100000000 | bytes 1048576 | tf_op jit(solution)/shard_map/relay/pallas_call | solution.py:485
  39.5 7.1 %all-to-all-start.1 = ((bf16[16,4,16,128]{3,2,1,0:T(8,128)(2,1)}), bf16[16,4,16,128]{3,2,1,0:T(8,128)(2,1)S(1)}, u32[]{:S(2)}, u32[]{:S(2)}) async-start(bf16[16,4,16,128]{3,2,1,0:T(8,128)(2,1)} %relay.1), calls=%async_computation.1 | async-start | bytes 524288 | tf_op jit(solution)/shard_map/all_to_all | solution.py:539
  46.6 0.0 collective-permute-done.5.kernel_three
  46.6 0.0 copy-start.5
  46.6 0.0 collective-permute-done.4.kernel_two
  46.6 0.0 copy-start.6
  46.6 0.0 collective-permute-done.3.kernel_one
  46.7 0.0 copy-start.10
  46.7 8.4 %all-to-all-done.1.received = bf16[16,4,16,128]{3,2,1,0:T(8,128)(2,1)S(1)} async-done(((bf16[16,4,16,128]{3,2,1,0:T(8,128)(2,1)}), bf16[16,4,16,128]{3,2,1,0:T(8,128)(2,1)S(1)}, u32[]{:S(2)}, u32[]{:S(2)}) %all-to-all-start.1) | async-done | bytes 262176 | tf_op jit(solution)/shard_map/all_to_all | solution.py:539
  55.1 0.0 copy-start.3
  55.1 0.0 copy-done.5
  55.1 0.0 copy-done.6
  55.1 0.0 copy-done.10
  55.1 0.7 %copy-done.3 = bf16[16,4,16,128]{3,2,1,0:T(8,128)(2,1)} copy-done((bf16[16,4,16,128]{3,2,1,0:T(8,128)(2,1)}, bf16[16,4,16,128]{3,2,1,0:T(8,128)(2,1)S(1)}, u32[]{:S(2)}) %copy-start.3) | copy-done | bytes 262168
  55.8 7.1 %read_out.1 = bf16[32,4,16,256]{3,2,1,0:T(8,128)(2,1)} custom-call(s32[3]{0:T(128)} %pad_add_fusion.place, f32[32]{0:T(128)} %intervals_far.3, f32[1,256]{1,0:T(1,128)} %bitcast.20, bf16[16,4,16,128]{3,2,1,0:T(8,128)(2,1)} %copy-done.3, bf16[32,6,16,256]{3,2,1,0:T(8,128)(2,1)} %get-tuple-element.8.drives_far, bf16[9,64,256]{2,1,0:T(8,128)(2,1)} %bitcast.18, ...), custom_call_target="tpu_custom_call" | custom-call | flops 6600000000 | bytes 1048576 | tf_op jit(solution)/shard_map/read_out/pallas_call | solution.py:498
Async XLA Ops:
  0.0 26.5 %collective-permute-start.2 = (bf16[9,64,256]{2,1,0:T(8,128)(2,1)}, bf16[9,64,256]{2,1,0:T(8,128)(2,1)S(1)}, u32[]{:S(2)}, u32[]{:S(2)}) collective-permute-start(bf16[9,64,256]{2,1,0:T(8,128)(2,1)} %bitcast.11), channel_id=1, source_target_pairs={{0,6},{2,0},{4,2},{6,4},{1,7},{3,1},{5,3},{7,5},{8,14},{10,8},{12,... | collective-permute-start | bytes 884744 | tf_op jit(solution)/shard_map/ppermute | solution.py:526
  3.0 23.6 %collective-permute-start.1 = (bf16[9,64,256]{2,1,0:T(8,128)(2,1)}, bf16[9,64,256]{2,1,0:T(8,128)(2,1)S(1)}, u32[]{:S(2)}, u32[]{:S(2)}) collective-permute-start(bf16[9,64,256]{2,1,0:T(8,128)(2,1)} %bitcast.12), channel_id=1, source_target_pairs={{0,4},{2,6},{4,0},{6,2},{1,5},{3,7},{5,1},{7,3},{8,12},{10,14},{12... | collective-permute-start | bytes 884744 | tf_op jit(solution)/shard_map/ppermute | solution.py:526
  3.6 23.0 %collective-permute-start = (bf16[9,64,256]{2,1,0:T(8,128)(2,1)}, bf16[9,64,256]{2,1,0:T(8,128)(2,1)S(1)}, u32[]{:S(2)}, u32[]{:S(2)}) collective-permute-start(bf16[9,64,256]{2,1,0:T(8,128)(2,1)} %bitcast.13), channel_id=1, source_target_pairs={{0,2},{2,4},{4,6},{6,0},{1,3},{3,5},{5,7},{7,1},{8,10},{10,12},{12... | collective-permute-start | bytes 884744 | tf_op jit(solution)/shard_map/ppermute | solution.py:526
  4.6 42.0 %collective-permute-start.5 = (bf16[9,64,256]{2,1,0:T(8,128)(2,1)}, bf16[9,64,256]{2,1,0:T(8,128)(2,1)S(1)}, u32[]{:S(2)}, u32[]{:S(2)}) collective-permute-start(bf16[9,64,256]{2,1,0:T(8,128)(2,1)} %bitcast.16), channel_id=1, source_target_pairs={{0,6},{2,0},{4,2},{6,4},{1,7},{3,1},{5,3},{7,5},{8,14},{10,8},{12,... | collective-permute-start | bytes 884744 | tf_op jit(solution)/shard_map/ppermute | solution.py:526
  6.9 39.7 %collective-permute-start.4 = (bf16[9,64,256]{2,1,0:T(8,128)(2,1)}, bf16[9,64,256]{2,1,0:T(8,128)(2,1)S(1)}, u32[]{:S(2)}, u32[]{:S(2)}) collective-permute-start(bf16[9,64,256]{2,1,0:T(8,128)(2,1)} %bitcast.17), channel_id=1, source_target_pairs={{0,4},{2,6},{4,0},{6,2},{1,5},{3,7},{5,1},{7,3},{8,12},{10,14},{12... | collective-permute-start | bytes 884744 | tf_op jit(solution)/shard_map/ppermute | solution.py:526
  8.6 17.9 %copy-start.4 = (bf16[3,3,64,256]{3,2,1,0:T(8,128)(2,1)S(1)}, bf16[3,3,64,256]{3,2,1,0:T(8,128)(2,1)}, u32[]{:S(2)}) copy-start(bf16[3,3,64,256]{3,2,1,0:T(8,128)(2,1)} %param.10) | copy-start | bytes 884740
  17.3 20.0 %all-to-all-start = ((bf16[8,9,16,128]{3,2,1,0:T(8,128)(2,1)}), bf16[8,9,16,128]{3,2,1,0:T(8,128)(2,1)S(1)}, u32[]{:S(2)}, u32[]{:S(2)}) async-start(bf16[8,9,16,128]{3,2,1,0:T(8,128)(2,1)} %drive.1), calls=%async_computation | async-start | bytes 589824 | tf_op jit(solution)/shard_map/all_to_all | solution.py:536
  26.5 10.8 %copy-start = (s32[3]{0:T(128)S(1)}, s32[3]{0:T(128)}, u32[]{:S(2)}) copy-start(s32[3]{0:T(128)} %pad_add_fusion.place) | copy-start | bytes 40
  26.5 10.8 %copy-start.1 = (f32[64]{0:T(128)S(1)}, f32[64]{0:T(128)}, u32[]{:S(2)}) copy-start(f32[64]{0:T(128)} %param.8) | copy-start | bytes 772
  26.5 0.7 %copy-start.7 = (bf16[9,64,256]{2,1,0:T(8,128)(2,1)}, bf16[9,64,256]{2,1,0:T(8,128)(2,1)S(1)}, u32[]{:S(2)}) copy-start(bf16[9,64,256]{2,1,0:T(8,128)(2,1)S(1)} %collective-permute-done.2.kernel_three) | copy-start | bytes 884740
  26.5 20.1 %collective-permute-start.3 = (bf16[9,64,256]{2,1,0:T(8,128)(2,1)S(1)}, bf16[9,64,256]{2,1,0:T(8,128)(2,1)S(1)}, u32[]{:S(2)}, u32[]{:S(2)}) collective-permute-start(bf16[9,64,256]{2,1,0:T(8,128)(2,1)S(1)} %bitcast.19), channel_id=1, source_target_pairs={{0,2},{2,4},{4,6},{6,0},{1,3},{3,5},{5,7},{7,1},{8,10},{10,12},{12... | collective-permute-start | bytes 884744 | tf_op jit(solution)/shard_map/ppermute | solution.py:526
  26.6 0.7 %copy-start.8 = (bf16[9,64,256]{2,1,0:T(8,128)(2,1)}, bf16[9,64,256]{2,1,0:T(8,128)(2,1)S(1)}, u32[]{:S(2)}) copy-start(bf16[9,64,256]{2,1,0:T(8,128)(2,1)S(1)} %collective-permute-done.1.kernel_two) | copy-start | bytes 884740
  27.3 0.7 %copy-start.9 = (bf16[9,64,256]{2,1,0:T(8,128)(2,1)}, bf16[9,64,256]{2,1,0:T(8,128)(2,1)S(1)}, u32[]{:S(2)}) copy-start(bf16[9,64,256]{2,1,0:T(8,128)(2,1)S(1)} %collective-permute-done.kernel_one) | copy-start | bytes 884740
  37.4 0.7 %copy-start.2 = (f32[8,128]{1,0:T(8,128)S(1)}, f32[8,128]{1,0:T(8,128)}, u32[]{:S(2)}) copy-start(f32[8,128]{1,0:T(8,128)} %get-tuple-element.7.token) | copy-start | bytes 12292
  39.5 15.5 %all-to-all-start.1 = ((bf16[16,4,16,128]{3,2,1,0:T(8,128)(2,1)}), bf16[16,4,16,128]{3,2,1,0:T(8,128)(2,1)S(1)}, u32[]{:S(2)}, u32[]{:S(2)}) async-start(bf16[16,4,16,128]{3,2,1,0:T(8,128)(2,1)} %relay.1), calls=%async_computation.1 | async-start | bytes 524288 | tf_op jit(solution)/shard_map/all_to_all | solution.py:539
  46.6 8.5 %copy-start.5 = (bf16[9,64,256]{2,1,0:T(8,128)(2,1)}, bf16[9,64,256]{2,1,0:T(8,128)(2,1)S(1)}, u32[]{:S(2)}) copy-start(bf16[9,64,256]{2,1,0:T(8,128)(2,1)S(1)} %collective-permute-done.5.kernel_three) | copy-start | bytes 884740
  46.6 8.4 %copy-start.6 = (bf16[9,64,256]{2,1,0:T(8,128)(2,1)}, bf16[9,64,256]{2,1,0:T(8,128)(2,1)S(1)}, u32[]{:S(2)}) copy-start(bf16[9,64,256]{2,1,0:T(8,128)(2,1)S(1)} %collective-permute-done.4.kernel_two) | copy-start | bytes 884740
  46.7 8.4 %copy-start.10 = (bf16[9,64,256]{2,1,0:T(8,128)(2,1)}, bf16[9,64,256]{2,1,0:T(8,128)(2,1)S(1)}, u32[]{:S(2)}) copy-start(bf16[9,64,256]{2,1,0:T(8,128)(2,1)S(1)} %collective-permute-done.3.kernel_one) | copy-start | bytes 884740
  55.1 0.7 %copy-start.3 = (bf16[16,4,16,128]{3,2,1,0:T(8,128)(2,1)}, bf16[16,4,16,128]{3,2,1,0:T(8,128)(2,1)S(1)}, u32[]{:S(2)}) copy-start(bf16[16,4,16,128]{3,2,1,0:T(8,128)(2,1)S(1)} %all-to-all-done.1.received) | copy-start | bytes 786436

commit v4 on v3

--- a/solution.py
+++ b/solution.py
@@ -20,7 +20,7 @@
 ZS = 8
 XS = 4
 WINDOW = 6
-STEP = 2
+STEP = 4
 CHUNKS = HALF // STEP
 
 
@@ -175,7 +175,11 @@
         message[z, ROWS // 2] = extra
 
 
-WINDOW_STEP = 4
+def whole(kernels, tap):
+    return jnp.concatenate([kernel[tap] for kernel in kernels], axis=0)
+
+
+WINDOW_STEP = 8
 WINDOW_CHUNKS = FRAMES // WINDOW_STEP
 TALL = 12
 
@@ -183,7 +187,7 @@
 def window_kernel(
     place, kernel_own, kernel_one, kernel_two, kernel_three, frames,
     drives, token,
-    rows, weights, written, load_sem, kernel_sem, store_sem,
+    rows, written, load_sem, store_sem,
 ):
     chan = place[0]
     kernels = (kernel_own, kernel_one, kernel_two, kernel_three)
@@ -196,18 +200,11 @@
             frames.at[part, pl.ds(source, 8)], rows.at[part, pl.ds(target, 8)], load_sem.at[chunk]
         )
 
-    def fetch(step):
-        return pltpu.make_async_copy(
-            kernels[step], weights.at[:, pl.ds(OWN * step, OWN)], kernel_sem.at[step]
-        )
-
     def store(chunk):
         part = pl.ds(chunk * WINDOW_STEP, WINDOW_STEP)
         return pltpu.make_async_copy(written.at[part], drives.at[part], store_sem.at[chunk])
 
     token[...] = jnp.zeros_like(token)
-    for step in range(CHANS):
-        fetch(step).start()
     for chunk in range(WINDOW_CHUNKS):
         load(chunk).start()
     empty = jnp.zeros((FRAMES, 2, WIDE, CH), BF16)
@@ -219,9 +216,6 @@
     @pl.when(chan == CHANS - 1)
     def _():
         rows[:, 8:10] = empty
-
-    for step in range(CHANS):
-        fetch(step).wait()
 
     def convolve(chunk, carry):
         load(chunk).wait()
@@ -233,7 +227,7 @@
         shape = (WINDOW_STEP * WINDOW, WIDE, CH)
         parts = []
         for j in range(3):
-            weight = jnp.concatenate([weights[3 * i + j] for i in range(3)], axis=1)
+            weight = jnp.concatenate([whole(kernels, 3 * i + j) for i in range(3)], axis=1)
             parts.append(
                 lax.dot_general(
                     operand, weight, (((1,), (1,)), ((), ())), preferred_element_type=F32
@@ -310,7 +304,7 @@
     place, intervals_far, gain_far, received, drives_far,
     kernel_own, kernel_one, kernel_two, kernel_three, frames,
     result,
-    intervals, skip_gain, weights, direct, drives, states, written, factors, state,
+    intervals, skip_gain, direct, drives, states, written, factors, state,
     load_sem, drive_sem, store_sem, small_sem,
 ):
     small = [
@@ -322,17 +316,13 @@
     kernels = (kernel_own, kernel_one, kernel_two, kernel_three)
     chan, x = place[0], place[1]
 
-    def fetch(step):
+    def load(chunk):
+        part = pl.ds(chunk * OUT_STEP, OUT_STEP)
         return pltpu.make_async_copy(
-            kernels[step], weights.at[:, pl.ds(OWN * step, OWN)], load_sem.at[step]
+            frames.at[part, pl.ds(CHANS * chan, CHANS)], direct.at[part], load_sem.at[chunk]
         )
 
-    def fetch_direct():
-        return pltpu.make_async_copy(
-            frames.at[:, pl.ds(CHANS * chan, CHANS)], direct, load_sem.at[CHANS]
-        )
-
-    def load(chunk):
+    def arrive(chunk):
         part = pl.ds(chunk * OUT_STEP, OUT_STEP)
         return pltpu.make_async_copy(drives_far.at[part], drives.at[part], drive_sem.at[chunk])
 
@@ -341,10 +331,8 @@
         return pltpu.make_async_copy(written.at[part], result.at[part], store_sem.at[chunk])
 
     for chunk in range(OUT_CHUNKS):
+        arrive(chunk).start()
         load(chunk).start()
-    for step in range(CHANS):
-        fetch(step).start()
-    fetch_direct().start()
 
     low = low_half((WIDE, LANES))
     rates, entering = [], []
@@ -384,13 +372,9 @@
         for r in range(WINDOW):
             state[r, :, part] = jnp.where(low, entering[2 * pair][r], entering[2 * pair + 1][r])
 
-    for step in range(CHANS):
-        fetch(step).wait()
-    fetch_direct().wait()
-
     def convolve(chunk, carry):
         start = pl.multiple_of(chunk * OUT_STEP, OUT_STEP)
-        load(chunk).wait()
+        arrive(chunk).wait()
         carried = state[...]
         for step in range(OUT_STEP):
             decay, gain = factors[0, start + step], factors[1, start + step]
@@ -404,8 +388,9 @@
         shape = (OUT_STEP * CHANS, WIDE, CH)
         parts = []
         for j in range(3):
-            weight = jnp.concatenate([weights[3 * i + j] for i in range(3)], axis=0)
+            weight = jnp.concatenate([whole(kernels, 3 * i + j) for i in range(3)], axis=0)
             parts.append(jnp.dot(operand, weight, preferred_element_type=F32).reshape(shape))
+        load(chunk).wait()
         passed = direct[pl.ds(start, OUT_STEP)].astype(F32).reshape(shape)
         total = beside(*parts) + skip_gain[...].reshape(1, 1, CH) * passed
         written[pl.ds(start, OUT_STEP)] = total.astype(BF16).reshape(OUT_STEP, CHANS, WIDE, CH)
@@ -452,10 +437,29 @@
             pltpu.SemaphoreType.DMA((CHUNKS, 2)),
             pltpu.SemaphoreType.DMA((3,)),
         ],
-        compiler_params=pltpu.CompilerParams(vmem_limit_bytes=62 << 20),
+        compiler_params=pltpu.CompilerParams(vmem_limit_bytes=60 << 20),
         cost_estimate=cost(8),
         name="drive",
     )(intervals, rates, kernel_t, frames)
+
+
+def hold_kernel(value, one, two, three, result, sem):
+    copy = pltpu.make_async_copy(value, result, sem)
+    copy.start()
+    copy.wait()
+
+
+def hold(value, others):
+    return pl.pallas_call(
+        hold_kernel,
+        out_shape=jax.ShapeDtypeStruct(value.shape, value.dtype),
+        in_specs=[anywhere()] * (1 + len(others)),
+        out_specs=anywhere(),
+        scratch_shapes=[pltpu.SemaphoreType.DMA],
+        compiler_params=pltpu.CompilerParams(vmem_limit_bytes=16 << 20),
+        cost_estimate=cost(1),
+        name="hold",
+    )(value, *others)
 
 
 def window(place, kernels, frames):
@@ -465,17 +469,15 @@
             jax.ShapeDtypeStruct((FRAMES, WINDOW, WIDE, CH), BF16),
             jax.ShapeDtypeStruct((8, LANES), F32),
         ],
-        in_specs=[in_smem()] + [anywhere()] * (CHANS + 1),
+        in_specs=[in_smem()] + [in_vmem()] * CHANS + [anywhere()],
         out_specs=[anywhere(), in_vmem()],
         scratch_shapes=[
             pltpu.VMEM((FRAMES, TALL, WIDE, CH), BF16),
-            pltpu.VMEM((9, CHANS * OWN, CH), BF16),
             pltpu.VMEM((FRAMES, WINDOW, WIDE, CH), BF16),
             pltpu.SemaphoreType.DMA((WINDOW_CHUNKS,)),
-            pltpu.SemaphoreType.DMA((CHANS,)),
             pltpu.SemaphoreType.DMA((WINDOW_CHUNKS,)),
         ],
-        compiler_params=pltpu.CompilerParams(vmem_limit_bytes=61 << 20),
+        compiler_params=pltpu.CompilerParams(vmem_limit_bytes=52 << 20),
         cost_estimate=cost(6),
         name="window",
     )(place, *kernels, frames)
@@ -498,24 +500,25 @@
     return pl.pallas_call(
         readout_kernel,
         out_shape=jax.ShapeDtypeStruct((FRAMES, CHANS, WIDE, CH), BF16),
-        in_specs=[in_smem(), anywhere(), anywhere(), in_vmem()] + [anywhere()] * (CHANS + 2),
+        in_specs=[in_smem(), anywhere(), anywhere(), in_vmem(), anywhere()]
+        + [in_vmem()] * CHANS
+        + [anywhere()],
         out_specs=anywhere(),
         scratch_shapes=[
             pltpu.SMEM((FRAMES,), F32),
             pltpu.VMEM((1, CH), F32),
-            pltpu.VMEM((9, CHANS * OWN, CH), BF16),
             pltpu.VMEM((FRAMES, CHANS, WIDE, CH), BF16),
             pltpu.VMEM((FRAMES, WINDOW, WIDE, CH), BF16),
             pltpu.VMEM((FRAMES, WINDOW, WIDE, CH), BF16),
             pltpu.VMEM((FRAMES, CHANS, WIDE, CH), BF16),
             pltpu.VMEM((2, FRAMES, WIDE, CH), F32),
             pltpu.VMEM((WINDOW, WIDE, CH), F32),
-            pltpu.SemaphoreType.DMA((CHANS + 1,)),
+            pltpu.SemaphoreType.DMA((OUT_CHUNKS,)),
             pltpu.SemaphoreType.DMA((OUT_CHUNKS,)),
             pltpu.SemaphoreType.DMA((OUT_CHUNKS,)),
             pltpu.SemaphoreType.DMA((2,)),
         ],
-        compiler_params=pltpu.CompilerParams(vmem_limit_bytes=61 << 20),
+        compiler_params=pltpu.CompilerParams(vmem_limit_bytes=52 << 20),
         cost_estimate=cost(6),
         name="read_out",
     )(place, intervals, skip_gain, received, drives, *kernels, frames)
@@ -531,8 +534,8 @@
     rates = decay_rates.reshape(1, OWN)
     kernel_t = jnp.transpose(in_kernel.reshape(9, CH, OWN), (0, 2, 1))
     in_kernels = around(kernel_t)
-    out_kernels = around(out_kernel.reshape(9, OWN, CH))
     message = drive(intervals, rates, kernel_t, frames)
+    out_kernels = around(hold(out_kernel.reshape(9, OWN, CH), in_kernels[1:]))
     arrived = lax.all_to_all(message, "z", 0, 0)
     drives, token = window(place, in_kernels, frames)
     onward = relay(place, rates, arrived, token)

time: 63.2 us -> 55.8 us (0.88)
  Pallas kernels: 26.6 us -> 22.4 us
  local copies, waits for them, and re-layouts: 2.8 us -> 0.03 us
    unnamed x22 -> x10, local copies, waits for them, and re-layouts: 2.8 us -> 0.03 us
    pallas_call x1, Pallas kernels: 9.27 us -> 6.9 us  [window(): pl.pallas_call(window_kernel, out_shape=[jax.ShapeDtypeStruct((FRAMES, WI...]
    pallas_call x1, Pallas kernels: 8.74 us -> 7.64 us  [drive(): pl.pallas_call(drive_kernel, out_shape=jax.ShapeDtypeStruct((ZS, ROWS //...]
    pallas_call x1, Pallas kernels: 7.07 us -> 6.3 us  [read_out(): pl.pallas_call(readout_kernel, out_shape=jax.ShapeDtypeStruct((FRAMES, CH...]
  transfers between devices with their start and end apart: 8 -> 8, of which waited for: 1 -> 1; matrix products, arithmetic and copies ran while one was open for 1% -> 0% of each run, Pallas kernels for 31% -> 29%
where the time goes in v4:
time: 55.8 us; the launch traced here: 55.5 us
  starting transfers between devices  24.4 us (44%)
  Pallas kernels  22.4 us (40%)
  waiting for transfers between devices  8.46 us (15%)
    all_to_all x1, starting transfers between devices, local(): arrived = lax.all_to_all(message, 'z', 0, 0)  8.71 us
    ppermute x6, starting transfers between devices, around(): return [value] + [lax.ppermute(value, 'chan', route) for route in routes]  8.65 us
    all_to_all x1, waiting for transfers between devices, local(): onward = lax.all_to_all(onward, ('x', 'chan'), 0, 0)  8.44 us
    pallas_call x1, Pallas kernels, drive(): pl.pallas_call(drive_kernel, out_shape=jax.ShapeDtypeStruct((ZS, ROWS //...  7.64 us
    all_to_all x1, starting transfers between devices, local(): onward = lax.all_to_all(onward, ('x', 'chan'), 0, 0)  7.08 us
    pallas_call x1, Pallas kernels, window(): pl.pallas_call(window_kernel, out_shape=[jax.ShapeDtypeStruct((FRAMES, WI...  6.9 us
    pallas_call x1, Pallas kernels, read_out(): pl.pallas_call(readout_kernel, out_shape=jax.ShapeDtypeStruct((FRAMES, CH...  6.3 us
    pallas_call x1, Pallas kernels, relay(): pl.pallas_call(relay_kernel, out_shape=jax.ShapeDtypeStruct((XS * CHANS,...  1.49 us
  transfers between devices with their start and end apart: 8, of which 1 were waited for; matrix products, arithmetic and copies ran while one was open for 0% of the time, Pallas kernels for 29%

profile of v4, /device:TPU:32, one launch (start us, length us, event | category | flops | bytes accessed | tf_op | source)
XLA Modules:
  0.0 55.5 jit_solution(5745869974139636831)
XLA Ops:
  0.0 3.0 %collective-permute-start.2 = (bf16[9,64,256]{2,1,0:T(8,128)(2,1)}, bf16[9,64,256]{2,1,0:T(8,128)(2,1)S(1)}, u32[]{:S(2)}, u32[]{:S(2)}) collective-permute-start(bf16[9,64,256]{2,1,0:T(8,128)(2,1)} %bitcast.10), channel_id=1, source_target_pairs={{0,6},{2,0},{4,2},{6,4},{1,7},{3,1},{5,3},{7,5},{8,14},{10,8},{12,... | collective-permute-start | bytes 884744 | tf_op jit(solution)/shard_map/ppermute | solution.py:529
  3.0 0.6 %collective-permute-start.1 = (bf16[9,64,256]{2,1,0:T(8,128)(2,1)}, bf16[9,64,256]{2,1,0:T(8,128)(2,1)S(1)}, u32[]{:S(2)}, u32[]{:S(2)}) collective-permute-start(bf16[9,64,256]{2,1,0:T(8,128)(2,1)} %bitcast.11), channel_id=1, source_target_pairs={{0,4},{2,6},{4,0},{6,2},{1,5},{3,7},{5,1},{7,3},{8,12},{10,14},{12... | collective-permute-start | bytes 884744 | tf_op jit(solution)/shard_map/ppermute | solution.py:529
  3.6 1.0 %collective-permute-start = (bf16[9,64,256]{2,1,0:T(8,128)(2,1)}, bf16[9,64,256]{2,1,0:T(8,128)(2,1)S(1)}, u32[]{:S(2)}, u32[]{:S(2)}) collective-permute-start(bf16[9,64,256]{2,1,0:T(8,128)(2,1)} %bitcast.12), channel_id=1, source_target_pairs={{0,2},{2,4},{4,6},{6,0},{1,3},{3,5},{5,7},{7,1},{8,10},{10,12},{12... | collective-permute-start | bytes 884744 | tf_op jit(solution)/shard_map/ppermute | solution.py:529
  4.6 0.0 copy-start
  4.6 7.6 %drive.1 = bf16[8,9,16,128]{3,2,1,0:T(8,128)(2,1)} custom-call(f32[32]{0:T(128)} %intervals_far.3, f32[1,64]{1,0:T(1,128)} %bitcast.16, bf16[9,64,256]{2,1,0:T(8,128)(2,1)} %bitcast.13, bf16[32,16,16,256]{3,2,1,0:T(8,128)(2,1)} %frames.5), custom_call_target="tpu_custom_call" | custom-call | flops 8800000000 | bytes 1048576 | tf_op jit(solution)/shard_map/drive/pallas_call | solution.py:424
  12.3 0.0 copy-start.1
  12.3 8.7 %all-to-all-start = ((bf16[8,9,16,128]{3,2,1,0:T(8,128)(2,1)}), bf16[8,9,16,128]{3,2,1,0:T(8,128)(2,1)S(1)}, u32[]{:S(2)}, u32[]{:S(2)}) async-start(bf16[8,9,16,128]{3,2,1,0:T(8,128)(2,1)} %drive.1), calls=%async_computation | async-start | bytes 589824 | tf_op jit(solution)/shard_map/all_to_all | solution.py:539
  21.0 0.1 pad_add_fusion.place
  21.1 0.0 collective-permute-done.2.kernel_three.three
  21.1 0.0 collective-permute-done.1.kernel_two.two
  21.1 0.0 collective-permute-done.kernel_one.one
  21.1 0.0 copy-done
  21.1 0.1 hold.1.kernel_own
  21.2 0.0 copy-start.3
  21.2 2.3 %collective-permute-start.5 = (bf16[9,64,256]{2,1,0:T(8,128)(2,1)S(1)}, bf16[9,64,256]{2,1,0:T(8,128)(2,1)S(1)}, u32[]{:S(2)}, u32[]{:S(2)}) collective-permute-start(bf16[9,64,256]{2,1,0:T(8,128)(2,1)S(1)} %hold.1.kernel_own), channel_id=1, source_target_pairs={{0,6},{2,0},{4,2},{6,4},{1,7},{3,1},{5,3},{7,5},{8,14},{10,8},{12,... | collective-permute-start | bytes 884744 | tf_op jit(solution)/shard_map/ppermute | solution.py:529
  23.5 1.7 %collective-permute-start.4 = (bf16[9,64,256]{2,1,0:T(8,128)(2,1)S(1)}, bf16[9,64,256]{2,1,0:T(8,128)(2,1)S(1)}, u32[]{:S(2)}, u32[]{:S(2)}) collective-permute-start(bf16[9,64,256]{2,1,0:T(8,128)(2,1)S(1)} %hold.1.kernel_own), channel_id=1, source_target_pairs={{0,4},{2,6},{4,0},{6,2},{1,5},{3,7},{5,1},{7,3},{8,12},{10,14},{12... | collective-permute-start | bytes 884744 | tf_op jit(solution)/shard_map/ppermute | solution.py:529
  25.2 0.0 collective-permute-start.3
  25.2 0.0 copy-done.1
  25.2 6.9 %window.1 = (bf16[32,6,16,256]{3,2,1,0:T(8,128)(2,1)}, f32[8,128]{1,0:T(8,128)S(1)}) custom-call(s32[3]{0:T(128)S(1)} %pad_add_fusion.place, bf16[9,64,256]{2,1,0:T(8,128)(2,1)S(1)} %bitcast.14, bf16[9,64,256]{2,1,0:T(8,128)(2,1)S(1)} %collective-permute-done.kernel_one.one, bf16[9,64,256]{2,1,0:T(8,128)(2,1)S(1)} %collective-permute-done.1.kernel_two.two, ...), custom_call_target="tpu_custom_call" | custom-call | flops 6600000000 | bytes 1048576 | tf_op jit(solution)/shard_map/window/pallas_call | solution.py:466
  32.1 0.0 copy-start.2
  32.1 0.0 copy-start.4
  32.2 0.0 all-to-all-done.received
  32.2 0.0 copy-done.3
  32.2 1.5 %relay.1 = bf16[16,4,16,128]{3,2,1,0:T(8,128)(2,1)} custom-call(s32[3]{0:T(128)S(1)} %pad_add_fusion.place, f32[1,64]{1,0:T(1,128)S(1)} %bitcast.17, bf16[8,9,16,128]{3,2,1,0:T(8,128)(2,1)S(1)} %all-to-all-done.received, f32[8,128]{1,0:T(8,128)S(1)} %get-tuple-element.7.token), custom_call_target="tpu_custom_call" | custom-call | flops 1100000000 | bytes 1048576 | tf_op jit(solution)/shard_map/relay/pallas_call | solution.py:487
  33.7 7.1 %all-to-all-start.1 = ((bf16[16,4,16,128]{3,2,1,0:T(8,128)(2,1)}), bf16[16,4,16,128]{3,2,1,0:T(8,128)(2,1)S(1)}, u32[]{:S(2)}, u32[]{:S(2)}) async-start(bf16[16,4,16,128]{3,2,1,0:T(8,128)(2,1)} %relay.1), calls=%async_computation.1 | async-start | bytes 524288 | tf_op jit(solution)/shard_map/all_to_all | solution.py:542
  40.8 0.0 collective-permute-done.5.kernel_three
  40.8 0.0 collective-permute-done.4.kernel_two
  40.8 0.0 collective-permute-done.3.kernel_one
  40.8 8.4 %all-to-all-done.1.received = bf16[16,4,16,128]{3,2,1,0:T(8,128)(2,1)S(1)} async-done(((bf16[16,4,16,128]{3,2,1,0:T(8,128)(2,1)}), bf16[16,4,16,128]{3,2,1,0:T(8,128)(2,1)S(1)}, u32[]{:S(2)}, u32[]{:S(2)}) %all-to-all-start.1) | async-done | bytes 262176 | tf_op jit(solution)/shard_map/all_to_all | solution.py:542
  49.2 0.0 copy-done.2
  49.2 0.0 copy-done.4
  49.2 6.3 %read_out.1 = bf16[32,4,16,256]{3,2,1,0:T(8,128)(2,1)} custom-call(s32[3]{0:T(128)S(1)} %pad_add_fusion.place, f32[32]{0:T(128)S(1)} %copy-done.4, f32[1,256]{1,0:T(1,128)S(1)} %bitcast.15, bf16[16,4,16,128]{3,2,1,0:T(8,128)(2,1)S(1)} %all-to-all-done.1.received, bf16[32,6,16,256]{3,2,1,0:T(8,128)(2,1)} %get-tuple-element.8.drives_far, ...), custom_call_target="tpu_custom_call" | custom-call | flops 6600000000 | bytes 1048576 | tf_op jit(solution)/shard_map/read_out/pallas_call | solution.py:500
Async XLA Ops:
  0.0 21.1 %collective-permute-start.2 = (bf16[9,64,256]{2,1,0:T(8,128)(2,1)}, bf16[9,64,256]{2,1,0:T(8,128)(2,1)S(1)}, u32[]{:S(2)}, u32[]{:S(2)}) collective-permute-start(bf16[9,64,256]{2,1,0:T(8,128)(2,1)} %bitcast.10), channel_id=1, source_target_pairs={{0,6},{2,0},{4,2},{6,4},{1,7},{3,1},{5,3},{7,5},{8,14},{10,8},{12,... | collective-permute-start | bytes 884744 | tf_op jit(solution)/shard_map/ppermute | solution.py:529
  3.0 18.1 %collective-permute-start.1 = (bf16[9,64,256]{2,1,0:T(8,128)(2,1)}, bf16[9,64,256]{2,1,0:T(8,128)(2,1)S(1)}, u32[]{:S(2)}, u32[]{:S(2)}) collective-permute-start(bf16[9,64,256]{2,1,0:T(8,128)(2,1)} %bitcast.11), channel_id=1, source_target_pairs={{0,4},{2,6},{4,0},{6,2},{1,5},{3,7},{5,1},{7,3},{8,12},{10,14},{12... | collective-permute-start | bytes 884744 | tf_op jit(solution)/shard_map/ppermute | solution.py:529
  3.6 17.4 %collective-permute-start = (bf16[9,64,256]{2,1,0:T(8,128)(2,1)}, bf16[9,64,256]{2,1,0:T(8,128)(2,1)S(1)}, u32[]{:S(2)}, u32[]{:S(2)}) collective-permute-start(bf16[9,64,256]{2,1,0:T(8,128)(2,1)} %bitcast.12), channel_id=1, source_target_pairs={{0,2},{2,4},{4,6},{6,0},{1,3},{3,5},{5,7},{7,1},{8,10},{10,12},{12... | collective-permute-start | bytes 884744 | tf_op jit(solution)/shard_map/ppermute | solution.py:529
  4.6 16.5 %copy-start = (bf16[3,3,64,256]{3,2,1,0:T(8,128)(2,1)S(1)}, bf16[3,3,64,256]{3,2,1,0:T(8,128)(2,1)}, u32[]{:S(2)}) copy-start(bf16[3,3,64,256]{3,2,1,0:T(8,128)(2,1)} %param.10) | copy-start | bytes 884740
  12.3 13.0 %copy-start.1 = (bf16[3,3,256,64]{2,3,1,0:T(8,128)(2,1)S(1)}, bf16[3,3,256,64]{2,3,1,0:T(8,128)(2,1)}, u32[]{:S(2)}) copy-start(bf16[3,3,256,64]{2,3,1,0:T(8,128)(2,1)} %param.9) | copy-start | bytes 884740
  12.3 19.9 %all-to-all-start = ((bf16[8,9,16,128]{3,2,1,0:T(8,128)(2,1)}), bf16[8,9,16,128]{3,2,1,0:T(8,128)(2,1)S(1)}, u32[]{:S(2)}, u32[]{:S(2)}) async-start(bf16[8,9,16,128]{3,2,1,0:T(8,128)(2,1)} %drive.1), calls=%async_computation | async-start | bytes 589824 | tf_op jit(solution)/shard_map/all_to_all | solution.py:539
  21.2 11.0 %copy-start.3 = (f32[64]{0:T(128)S(1)}, f32[64]{0:T(128)}, u32[]{:S(2)}) copy-start(f32[64]{0:T(128)} %param.8) | copy-start | bytes 772
  21.2 19.6 %collective-permute-start.5 = (bf16[9,64,256]{2,1,0:T(8,128)(2,1)S(1)}, bf16[9,64,256]{2,1,0:T(8,128)(2,1)S(1)}, u32[]{:S(2)}, u32[]{:S(2)}) collective-permute-start(bf16[9,64,256]{2,1,0:T(8,128)(2,1)S(1)} %hold.1.kernel_own), channel_id=1, source_target_pairs={{0,6},{2,0},{4,2},{6,4},{1,7},{3,1},{5,3},{7,5},{8,14},{10,8},{12,... | collective-permute-start | bytes 884744 | tf_op jit(solution)/shard_map/ppermute | solution.py:529
  23.5 17.2 %collective-permute-start.4 = (bf16[9,64,256]{2,1,0:T(8,128)(2,1)S(1)}, bf16[9,64,256]{2,1,0:T(8,128)(2,1)S(1)}, u32[]{:S(2)}, u32[]{:S(2)}) collective-permute-start(bf16[9,64,256]{2,1,0:T(8,128)(2,1)S(1)} %hold.1.kernel_own), channel_id=1, source_target_pairs={{0,4},{2,6},{4,0},{6,2},{1,5},{3,7},{5,1},{7,3},{8,12},{10,14},{12... | collective-permute-start | bytes 884744 | tf_op jit(solution)/shard_map/ppermute | solution.py:529
  25.2 15.6 %collective-permute-start.3 = (bf16[9,64,256]{2,1,0:T(8,128)(2,1)S(1)}, bf16[9,64,256]{2,1,0:T(8,128)(2,1)S(1)}, u32[]{:S(2)}, u32[]{:S(2)}) collective-permute-start(bf16[9,64,256]{2,1,0:T(8,128)(2,1)S(1)} %hold.1.kernel_own), channel_id=1, source_target_pairs={{0,2},{2,4},{4,6},{6,0},{1,3},{3,5},{5,7},{7,1},{8,10},{10,12},{12... | collective-permute-start | bytes 884744 | tf_op jit(solution)/shard_map/ppermute | solution.py:529
  32.1 17.1 %copy-start.2 = (f32[256]{0:T(256)S(1)}, f32[256]{0:T(256)}, u32[]{:S(2)}) copy-start(f32[256]{0:T(256)} %param.11) | copy-start | bytes 3076
  32.1 17.1 %copy-start.4 = (f32[32]{0:T(128)S(1)}, f32[32]{0:T(128)}, u32[]{:S(2)}) copy-start(f32[32]{0:T(128)} %intervals_far.3) | copy-start | bytes 388
  33.7 15.6 %all-to-all-start.1 = ((bf16[16,4,16,128]{3,2,1,0:T(8,128)(2,1)}), bf16[16,4,16,128]{3,2,1,0:T(8,128)(2,1)S(1)}, u32[]{:S(2)}, u32[]{:S(2)}) async-start(bf16[16,4,16,128]{3,2,1,0:T(8,128)(2,1)} %relay.1), calls=%async_computation.1 | async-start | bytes 524288 | tf_op jit(solution)/shard_map/all_to_all | solution.py:542

commit v5 on v4

--- a/solution.py
+++ b/solution.py
@@ -21,7 +21,8 @@
 XS = 4
 WINDOW = 6
 STEP = 4
-CHUNKS = HALF // STEP
+PIECES = ((0, 4), (4, 4), (8, 4), (12, 4))
+CHUNKS = len(PIECES)
 
 
 def split3(value):
@@ -86,7 +87,7 @@
 
 def drive_kernel(
     intervals_far, rates_far, kernel_far, frames,
-    message,
+    message, token,
     intervals, rates, kernel_t, padded, weights, factors, state, load_sem, small_sem,
 ):
     small = [
@@ -97,18 +98,19 @@
     ]
     for copy in small:
         copy.start()
+    token[...] = jnp.zeros_like(token)
 
     def load(chunk, half):
-        start = half * HALF + chunk * STEP
+        first, size = PIECES[chunk]
+        part = pl.ds(half * HALF + first, size)
         return pltpu.make_async_copy(
-            frames.at[pl.ds(start, STEP)],
-            padded.at[pl.ds(start, STEP), pl.ds(1, ROWS)],
+            frames.at[part],
+            padded.at[part, pl.ds(1, ROWS)],
             load_sem.at[chunk, half],
         )
 
-    for chunk in range(CHUNKS):
-        load(chunk, 0).start()
-        load(chunk, 1).start()
+    load(0, 0).start()
+    load(0, 1).start()
 
     empty = jnp.zeros((FRAMES, 1, WIDE, CH), BF16)
     padded[:, 0:1] = empty
@@ -116,6 +118,9 @@
     nothing = jnp.zeros((CH, OWN), BF16)
     for copy in small:
         copy.wait()
+    for chunk in range(1, CHUNKS):
+        load(chunk, 0).start()
+        load(chunk, 1).start()
     for i in range(3):
         tap = [kernel_t[3 * i + j].astype(F32).T.astype(BF16) for j in range(3)]
         weights[0, CH * i : CH * (i + 1), :] = jnp.concatenate([tap[0], tap[1], tap[2], nothing], 1)
@@ -128,34 +133,40 @@
     spread(factors, 1, slice(None), jnp.sqrt(one_minus_exp(2.0 * scaled)))
     state[...] = jnp.zeros_like(state)
 
-    def advance(chunk, carry):
-        start = pl.multiple_of(chunk * STEP, STEP)
-
-        def product(half):
-            block = padded[pl.ds(half * HALF + start, STEP)]
-            taps = [block[:, i : i + ROWS].reshape(STEP * ROWS * WIDE, CH) for i in range(3)]
-            return jnp.dot(
-                jnp.concatenate(taps, axis=1), weights[half], preferred_element_type=F32
-            )
-
+    def products(chunk):
         load(chunk, 0).wait()
         load(chunk, 1).wait()
-        first, second = product(0), product(1)
-        low = low_half((STEP * ROWS * WIDE, LANES))
+        begin, size = PIECES[chunk]
+        both = []
+        for half in range(2):
+            block = padded[pl.ds(half * HALF + begin, size)]
+            taps = [block[:, i : i + ROWS].reshape(size * ROWS * WIDE, CH) for i in range(3)]
+            both.append(
+                jnp.dot(jnp.concatenate(taps, axis=1), weights[half], preferred_element_type=F32)
+            )
+        return both
+
+    def advance(chunk, first, second):
+        begin, size = PIECES[chunk]
+        low = low_half((size * ROWS * WIDE, LANES))
         left = jnp.where(low, first[:, :LANES], second[:, :LANES])
         centre = swap_halves(jnp.where(low, second[:, :LANES], first[:, :LANES]))
         right = first[:, LANES:] + second[:, LANES:]
-        shape = (STEP * ROWS, WIDE, LANES)
+        shape = (size * ROWS, WIDE, LANES)
         drives = beside(left.reshape(shape), centre.reshape(shape), right.reshape(shape))
-        drives = drives.reshape(STEP, ROWS, WIDE, LANES)
+        drives = drives.reshape(size, ROWS, WIDE, LANES)
         carried = state[...]
-        for step in range(STEP):
-            decay, gain = factors[0, start + step], factors[1, start + step]
-            carried = decay * carried + gain * drives[step]
+        for step in range(size):
+            now = begin + step
+            carried = factors[0, now] * carried + factors[1, now] * drives[step]
         state[...] = carried
-        return carry
-
-    lax.fori_loop(0, CHUNKS, advance, 0)
+
+    waiting = products(0)
+    for chunk in range(CHUNKS):
+        ready = waiting
+        if chunk + 1 < CHUNKS:
+            waiting = products(chunk + 1)
+        advance(chunk, *ready)
 
     late = functools.reduce(lambda a, b: a + b, values[HALF:])
     total = functools.reduce(lambda a, b: a + b, values[:HALF]) + late
@@ -175,8 +186,9 @@
         message[z, ROWS // 2] = extra
 
 
-def whole(kernels, tap):
-    return jnp.concatenate([kernel[tap] for kernel in kernels], axis=0)
+def whole(own, pairs, use_left, tap):
+    parts = [own[tap]] + [jnp.where(use_left, left[tap], right[tap]) for left, right in pairs]
+    return jnp.concatenate(parts, axis=0)
 
 
 WINDOW_STEP = 8
@@ -185,12 +197,12 @@
 
 
 def window_kernel(
-    place, kernel_own, kernel_one, kernel_two, kernel_three, frames,
-    drives, token,
-    rows, written, load_sem, store_sem,
+    place, kernel_own, *rest
 ):
-    chan = place[0]
-    kernels = (kernel_own, kernel_one, kernel_two, kernel_three)
+    direct, swapped = rest[: CHANS - 1], rest[CHANS - 1 : 2 * CHANS - 2]
+    (frames, drives, token, rows, written, load_sem, store_sem) = rest[2 * CHANS - 2 :]
+    pairs = list(zip(direct, swapped))
+    chan, first = place[0], place[3] == 0
     source = jnp.clip(CHANS * chan - 2, 0, 8)
     target = source - CHANS * chan + 4
 
@@ -227,7 +239,7 @@
         shape = (WINDOW_STEP * WINDOW, WIDE, CH)
         parts = []
         for j in range(3):
-            weight = jnp.concatenate([whole(kernels, 3 * i + j) for i in range(3)], axis=1)
+            weight = jnp.concatenate([whole(kernel_own, pairs, first, 3 * i + j) for i in range(3)], axis=1)
             parts.append(
                 lax.dot_general(
                     operand, weight, (((1,), (1,)), ((), ())), preferred_element_type=F32
@@ -249,11 +261,8 @@
         store(chunk).wait()
 
 
-def relay_kernel(place, rates_far, received, token, message, rates, small_sem):
+def relay_kernel(place, rates, received, token, message):
     x, z = place[1], place[2]
-    copy = pltpu.make_async_copy(rates_far, rates, small_sem)
-    copy.start()
-    copy.wait()
     rate = doubled(rates[...])
     total = jnp.zeros((ROWS // 2, WIDE, LANES), F32)
     before = total
@@ -301,20 +310,17 @@
 
 
 def readout_kernel(
-    place, intervals_far, gain_far, received, drives_far,
-    kernel_own, kernel_one, kernel_two, kernel_three, frames,
-    result,
-    intervals, skip_gain, direct, drives, states, written, factors, state,
-    load_sem, drive_sem, store_sem, small_sem,
+    place, intervals_far, skip_gain, received, drives_far, kernel_own, *rest
 ):
-    small = [
-        pltpu.make_async_copy(intervals_far, intervals, small_sem.at[0]),
-        pltpu.make_async_copy(gain_far, skip_gain, small_sem.at[1]),
-    ]
+    pairs = list(zip(rest[: CHANS - 1], rest[CHANS - 1 : 2 * CHANS - 2]))
+    (
+        frames, result, intervals, direct, drives, states, written, factors, state,
+        load_sem, drive_sem, store_sem, small_sem,
+    ) = rest[2 * CHANS - 2 :]
+    small = [pltpu.make_async_copy(intervals_far, intervals, small_sem)]
     for copy in small:
         copy.start()
-    kernels = (kernel_own, kernel_one, kernel_two, kernel_three)
-    chan, x = place[0], place[1]
+    chan, x, second = place[0], place[1], place[3] == 1
 
     def load(chunk):
         part = pl.ds(chunk * OUT_STEP, OUT_STEP)
@@ -388,7 +394,7 @@
         shape = (OUT_STEP * CHANS, WIDE, CH)
         parts = []
         for j in range(3):
-            weight = jnp.concatenate([whole(kernels, 3 * i + j) for i in range(3)], axis=0)
+            weight = jnp.concatenate([whole(kernel_own, pairs, second, 3 * i + j) for i in range(3)], axis=0)
             parts.append(jnp.dot(operand, weight, preferred_element_type=F32).reshape(shape))
         load(chunk).wait()
         passed = direct[pl.ds(start, OUT_STEP)].astype(F32).reshape(shape)
@@ -423,9 +429,12 @@
 def drive(intervals, rates, kernel_t, frames):
     return pl.pallas_call(
         drive_kernel,
-        out_shape=jax.ShapeDtypeStruct((ZS, ROWS // 2 + 1, WIDE, LANES), BF16),
+        out_shape=[
+            jax.ShapeDtypeStruct((ZS, ROWS // 2 + 1, WIDE, LANES), BF16),
+            jax.ShapeDtypeStruct((8, LANES), F32),
+        ],
         in_specs=[anywhere()] * 4,
-        out_specs=in_vmem(),
+        out_specs=[in_vmem()] * 2,
         scratch_shapes=[
             pltpu.SMEM((FRAMES,), F32),
             pltpu.VMEM((1, OWN), F32),
@@ -443,33 +452,31 @@
     )(intervals, rates, kernel_t, frames)
 
 
-def hold_kernel(value, one, two, three, result, sem):
-    copy = pltpu.make_async_copy(value, result, sem)
-    copy.start()
-    copy.wait()
-
-
-def hold(value, others):
+def hold_kernel(*refs):
+    del refs
+
+
+def hold(values, other):
     return pl.pallas_call(
         hold_kernel,
-        out_shape=jax.ShapeDtypeStruct(value.shape, value.dtype),
-        in_specs=[anywhere()] * (1 + len(others)),
-        out_specs=anywhere(),
-        scratch_shapes=[pltpu.SemaphoreType.DMA],
+        out_shape=[jax.ShapeDtypeStruct(value.shape, value.dtype) for value in values],
+        in_specs=[anywhere()] * (len(values) + 1),
+        out_specs=[anywhere()] * len(values),
+        input_output_aliases={index: index for index in range(len(values))},
         compiler_params=pltpu.CompilerParams(vmem_limit_bytes=16 << 20),
-        cost_estimate=cost(1),
+        cost_estimate=cost(0),
         name="hold",
-    )(value, *others)
-
-
-def window(place, kernels, frames):
+    )(*values, other)
+
+
+def window(place, own, direct, swapped, frames):
     return pl.pallas_call(
         window_kernel,
         out_shape=[
             jax.ShapeDtypeStruct((FRAMES, WINDOW, WIDE, CH), BF16),
             jax.ShapeDtypeStruct((8, LANES), F32),
         ],
-        in_specs=[in_smem()] + [in_vmem()] * CHANS + [anywhere()],
+        in_specs=[in_smem()] + [in_vmem()] * (2 * CHANS - 1) + [anywhere()],
         out_specs=[anywhere(), in_vmem()],
         scratch_shapes=[
             pltpu.VMEM((FRAMES, TALL, WIDE, CH), BF16),
@@ -477,36 +484,34 @@
             pltpu.SemaphoreType.DMA((WINDOW_CHUNKS,)),
             pltpu.SemaphoreType.DMA((WINDOW_CHUNKS,)),
         ],
-        compiler_params=pltpu.CompilerParams(vmem_limit_bytes=52 << 20),
-        cost_estimate=cost(6),
+        compiler_params=pltpu.CompilerParams(vmem_limit_bytes=51 << 20),
+        cost_estimate=cost(1),
         name="window",
-    )(place, *kernels, frames)
+    )(place, own, *direct, *swapped, frames)
 
 
 def relay(place, rates, received, token):
     return pl.pallas_call(
         relay_kernel,
         out_shape=jax.ShapeDtypeStruct((XS * CHANS, WINDOW // 2 + 1, WIDE, LANES), BF16),
-        in_specs=[in_smem(), anywhere(), in_vmem(), anywhere()],
+        in_specs=[in_smem(), in_vmem(), in_vmem(), anywhere()],
         out_specs=in_vmem(),
-        scratch_shapes=[pltpu.VMEM((1, OWN), F32), pltpu.SemaphoreType.DMA],
         compiler_params=pltpu.CompilerParams(vmem_limit_bytes=16 << 20),
         cost_estimate=cost(1),
         name="relay",
     )(place, rates, received, token)
 
 
-def read_out(place, intervals, skip_gain, received, drives, kernels, frames):
+def read_out(place, intervals, skip_gain, received, drives, own, direct, swapped, frames):
     return pl.pallas_call(
         readout_kernel,
         out_shape=jax.ShapeDtypeStruct((FRAMES, CHANS, WIDE, CH), BF16),
-        in_specs=[in_smem(), anywhere(), anywhere(), in_vmem(), anywhere()]
-        + [in_vmem()] * CHANS
+        in_specs=[in_smem(), anywhere(), in_vmem(), in_vmem(), anywhere()]
+        + [in_vmem()] * (2 * CHANS - 1)
         + [anywhere()],
         out_specs=anywhere(),
         scratch_shapes=[
             pltpu.SMEM((FRAMES,), F32),
-            pltpu.VMEM((1, CH), F32),
             pltpu.VMEM((FRAMES, CHANS, WIDE, CH), BF16),
             pltpu.VMEM((FRAMES, WINDOW, WIDE, CH), BF16),
             pltpu.VMEM((FRAMES, WINDOW, WIDE, CH), BF16),
@@ -516,33 +521,35 @@
             pltpu.SemaphoreType.DMA((OUT_CHUNKS,)),
             pltpu.SemaphoreType.DMA((OUT_CHUNKS,)),
             pltpu.SemaphoreType.DMA((OUT_CHUNKS,)),
-            pltpu.SemaphoreType.DMA((2,)),
+            pltpu.SemaphoreType.DMA,
         ],
         compiler_params=pltpu.CompilerParams(vmem_limit_bytes=52 << 20),
         cost_estimate=cost(6),
         name="read_out",
-    )(place, intervals, skip_gain, received, drives, *kernels, frames)
+    )(place, intervals, skip_gain, received, drives, own, *direct, *swapped, frames)
 
 
 def around(value):
     routes = [[(c, (c + step) % CHANS) for c in range(CHANS)] for step in range(1, CHANS)]
-    return [value] + [lax.ppermute(value, "chan", route) for route in routes]
+    return [lax.ppermute(value, "chan", route) for route in routes]
 
 
 def local(frames, intervals, decay_rates, in_kernel, out_kernel, skip_gain):
-    place = jnp.stack([lax.axis_index(name) for name in ("chan", "x", "z")]).astype(jnp.int32)
+    axes = ("chan", "x", "z", "clip")
+    place = jnp.stack([lax.axis_index(name) for name in axes]).astype(jnp.int32)
     rates = decay_rates.reshape(1, OWN)
     kernel_t = jnp.transpose(in_kernel.reshape(9, CH, OWN), (0, 2, 1))
-    in_kernels = around(kernel_t)
-    message = drive(intervals, rates, kernel_t, frames)
-    out_kernels = around(hold(out_kernel.reshape(9, OWN, CH), in_kernels[1:]))
+    out_own = out_kernel.reshape(9, OWN, CH)
+    direct = around(jnp.where(lax.axis_index("clip") == 0, kernel_t, out_own))
+    message, done = drive(intervals, rates, kernel_t, frames)
+    direct = hold(direct, done)
+    swapped = [lax.ppermute(piece, "clip", [(0, 1), (1, 0)]) for piece in direct]
     arrived = lax.all_to_all(message, "z", 0, 0)
-    drives, token = window(place, in_kernels, frames)
+    drives, token = window(place, kernel_t, direct, swapped, frames)
     onward = relay(place, rates, arrived, token)
     onward = lax.all_to_all(onward, ("x", "chan"), 0, 0)
-    return read_out(
-        place, intervals, skip_gain.reshape(1, CH), onward, drives, out_kernels, frames
-    )
+    skip = skip_gain.reshape(1, CH)
+    return read_out(place, intervals, skip, onward, drives, out_own, direct, swapped, frames)
 
 
 def solution(mesh):

time: 55.8 us -> 53.8 us (0.964)
  blocking collectives: 0 us -> 14.5 us
  starting transfers between devices: 24.4 us -> 13.8 us
  waiting for transfers between devices: 8.46 us -> 2.03 us
  Pallas kernels: 22.4 us -> 21.1 us
  other arithmetic: 0.08 us -> 1.16 us
  local copies, waits for them, and re-layouts: 0.03 us -> 0.7 us
    all_to_all x0 -> x1, blocking collectives: none -> 14.5 us  [local(): onward = lax.all_to_all(onward, ('x', 'chan'), 0, 0)]
    all_to_all x1 -> x0, waiting for transfers between devices: 8.44 us -> none  [local(): onward = lax.all_to_all(onward, ('x', 'chan'), 0, 0)]
    all_to_all x1 -> x0, starting transfers between devices: 7.08 us -> none  [local(): onward = lax.all_to_all(onward, ('x', 'chan'), 0, 0)]
    ppermute x6, starting transfers between devices: 8.65 us -> 5.2 us  [the longest x3 4.69 us: around(): return [lax.ppermute(value, 'chan', route) for route in routes]]
    ppermute x6, waiting for transfers between devices: 0.02 us -> 1.83 us  [the longest x3 1.83 us: local(): lax.ppermute(piece, 'clip', [(0, 1), (1, 0)])]
    pallas_call x2, Pallas kernels: 7.71 us -> 6.47 us  [the longest x1 6.47 us: drive(): pl.pallas_call(drive_kernel, out_shape=[jax.ShapeDtypeStruct((ZS, ROWS //...]
    select_n x0 -> x1, other arithmetic: none -> 1.08 us  [local(): direct = around(jnp.where(lax.axis_index('clip') == 0, kernel_t, out_own))]
    pallas_call x1, Pallas kernels: 1.49 us -> 0.77 us  [relay(): pl.pallas_call(relay_kernel, out_shape=jax.ShapeDtypeStruct((XS * CHANS,...]
  transfers between devices with their start and end apart: 8 -> 7, of which waited for: 1 -> 4; matrix products, arithmetic and copies ran while one was open for 0% -> 0% of each run, Pallas kernels for 29% -> 25%
where the time goes in v5:
time: 53.8 us; the launch traced here: 53.4 us
  Pallas kernels  21.1 us (39%)
  blocking collectives  14.5 us (27%)
  starting transfers between devices  13.8 us (26%)
  waiting for transfers between devices  2.03 us (4%)
  other arithmetic  1.16 us (2%)
  local copies, waits for them, and re-layouts  0.7 us (1%)
    all_to_all x1, blocking collectives, local(): onward = lax.all_to_all(onward, ('x', 'chan'), 0, 0)  14.5 us
    all_to_all x1, starting transfers between devices, local(): arrived = lax.all_to_all(message, 'z', 0, 0)  8.58 us
    pallas_call x1, Pallas kernels, window(): pl.pallas_call(window_kernel, out_shape=[jax.ShapeDtypeStruct((FRAMES, WI...  6.95 us
    pallas_call x1, Pallas kernels, read_out(): pl.pallas_call(readout_kernel, out_shape=jax.ShapeDtypeStruct((FRAMES, CH...  6.89 us
    pallas_call x1, Pallas kernels, drive(): pl.pallas_call(drive_kernel, out_shape=[jax.ShapeDtypeStruct((ZS, ROWS //...  6.47 us
    ppermute x3, starting transfers between devices, around(): return [lax.ppermute(value, 'chan', route) for route in routes]  4.69 us
    ppermute x3, waiting for transfers between devices, local(): lax.ppermute(piece, 'clip', [(0, 1), (1, 0)])  1.83 us
    select_n x1, other arithmetic, local(): direct = around(jnp.where(lax.axis_index('clip') == 0, kernel_t, out_own))  1.08 us
  transfers between devices with their start and end apart: 7, of which 4 were waited for; matrix products, arithmetic and copies ran while one was open for 0% of the time, Pallas kernels for 25%

profile of v5, /device:TPU:32, one launch (start us, length us, event | category | flops | bytes accessed | tf_op | source)
XLA Modules:
  0.0 53.4 jit_solution(1067243735586581477)
XLA Ops:
  0.0 1.1 %broadcast_select_fusion = bf16[9,64,256]{2,1,0:T(8,128)(2,1)S(1)} fusion(pred[]{:T(512)S(6)} %eq.3, bf16[3,3,64,256]{3,2,1,0:T(8,128)(2,1)} %param.10, bf16[3,3,256,64]{2,3,1,0:T(8,128)(2,1)} %param.9), kind=kLoop, calls=%fused_computation | loop fusion | flops 147456 | bytes 884737 | tf_op jit(solution)/shard_map/jit(_where)/select_n | solution.py:543
  1.1 3.1 %collective-permute-start.2 = (bf16[9,64,256]{2,1,0:T(8,128)(2,1)S(1)}, bf16[9,64,256]{2,1,0:T(8,128)(2,1)S(1)}, u32[]{:S(2)}, u32[]{:S(2)}) collective-permute-start(bf16[9,64,256]{2,1,0:T(8,128)(2,1)S(1)} %broadcast_select_fusion), channel_id=1, source_target_pairs={{0,6},{2,0},{4,2},{6,4},{1,7},{3,1},{5,3},{7,5},{8,14},{10,8},{12,... | collective-permute-start | bytes 884744 | tf_op jit(solution)/shard_map/ppermute | solution.py:534
  4.2 0.6 %collective-permute-start.1 = (bf16[9,64,256]{2,1,0:T(8,128)(2,1)S(1)}, bf16[9,64,256]{2,1,0:T(8,128)(2,1)S(1)}, u32[]{:S(2)}, u32[]{:S(2)}) collective-permute-start(bf16[9,64,256]{2,1,0:T(8,128)(2,1)S(1)} %broadcast_select_fusion), channel_id=1, source_target_pairs={{0,4},{2,6},{4,0},{6,2},{1,5},{3,7},{5,1},{7,3},{8,12},{10,14},{12... | collective-permute-start | bytes 884744 | tf_op jit(solution)/shard_map/ppermute | solution.py:534
  4.8 1.0 %collective-permute-start = (bf16[9,64,256]{2,1,0:T(8,128)(2,1)S(1)}, bf16[9,64,256]{2,1,0:T(8,128)(2,1)S(1)}, u32[]{:S(2)}, u32[]{:S(2)}) collective-permute-start(bf16[9,64,256]{2,1,0:T(8,128)(2,1)S(1)} %broadcast_select_fusion), channel_id=1, source_target_pairs={{0,2},{2,4},{4,6},{6,0},{1,3},{3,5},{5,7},{7,1},{8,10},{10,12},{12... | collective-permute-start | bytes 884744 | tf_op jit(solution)/shard_map/ppermute | solution.py:534
  5.8 0.0 copy-start
  5.8 6.5 %drive.1 = (bf16[8,9,16,128]{3,2,1,0:T(8,128)(2,1)}, f32[8,128]{1,0:T(8,128)}) custom-call(f32[32]{0:T(128)} %intervals_far.3, f32[1,64]{1,0:T(1,128)} %bitcast.16, bf16[9,64,256]{2,1,0:T(8,128)(2,1)} %bitcast.12, bf16[32,16,16,256]{3,2,1,0:T(8,128)(2,1)} %rest_6_.3), custom_call_target="tpu_custom_call" | custom-call | flops 8800000000 | bytes 1048576 | tf_op jit(solution)/shard_map/drive/pallas_call | solution.py:430
  12.3 0.0 copy-start.6
  12.3 8.6 %all-to-all-start = ((bf16[8,9,16,128]{3,2,1,0:T(8,128)(2,1)}), bf16[8,9,16,128]{3,2,1,0:T(8,128)(2,1)S(1)}, u32[]{:S(2)}, u32[]{:S(2)}) async-start(bf16[8,9,16,128]{3,2,1,0:T(8,128)(2,1)} %get-tuple-element.12), calls=%async_computation | async-start | bytes 589824 | tf_op jit(solution)/shard_map/all_to_all | solution.py:547
  20.9 0.0 collective-permute-done.2.refs_2_
  20.9 0.0 collective-permute-done.1.refs_1_
  20.9 0.0 collective-permute-done.refs_0_
  20.9 0.0 copy-start.4
  20.9 0.7 %copy-done.4 = f32[8,128]{1,0:T(8,128)S(1)} copy-done((f32[8,128]{1,0:T(8,128)S(1)}, f32[8,128]{1,0:T(8,128)}, u32[]{:S(2)}) %copy-start.4) | copy-done | bytes 4120
  21.6 0.0 collective-permute-start.3
  21.6 0.5 collective-permute-start.4
  22.1 0.0 collective-permute-start.5
  22.1 0.1 pad_add_fusion.place
  22.1 0.0 copy-start.3
  22.1 0.0 copy-start.5
  22.1 0.0 copy-start.7
  22.1 1.0 %collective-permute-done.3.rest_3_ = bf16[9,64,256]{2,1,0:T(8,128)(2,1)S(1)} collective-permute-done((bf16[9,64,256]{2,1,0:T(8,128)(2,1)S(1)}, bf16[9,64,256]{2,1,0:T(8,128)(2,1)S(1)}, u32[]{:S(2)}, u32[]{:S(2)}) %collective-permute-start.3) | collective-permute-done | bytes 294944 | tf_op jit(solution)/shard_map/ppermute | solution.py:546
  23.1 0.4 collective-permute-done.4.rest_4_
  23.6 0.0 copy-start.1
  23.6 0.4 collective-permute-done.5.rest_5_
  24.0 0.0 copy-done
  24.0 0.0 copy-start.2
  24.0 6.9 %window.1 = (bf16[32,6,16,256]{3,2,1,0:T(8,128)(2,1)}, f32[8,128]{1,0:T(8,128)S(1)}) custom-call(s32[4]{0:T(128)S(1)} %pad_add_fusion.place, bf16[9,64,256]{2,1,0:T(8,128)(2,1)S(1)} %bitcast.13, bf16[9,64,256]{2,1,0:T(8,128)(2,1)S(1)} %get-tuple-element.14.rest_0_, bf16[9,64,256]{2,1,0:T(8,128)(2,1)S(1)} %get-tuple-element.15.rest_1_, ...), custom_call_target="tpu_custom_call" | custom-call | flops 1100000000 | bytes 1048576 | tf_op jit(solution)/shard_map/window/pallas_call | solution.py:473
  30.9 0.2 all-to-all-done.received
  31.1 0.0 copy-done.6
  31.1 0.8 %relay.1 = bf16[16,4,16,128]{3,2,1,0:T(8,128)(2,1)S(1)} custom-call(s32[4]{0:T(128)S(1)} %pad_add_fusion.place, f32[1,64]{1,0:T(1,128)S(1)} %bitcast.17, bf16[8,9,16,128]{3,2,1,0:T(8,128)(2,1)S(1)} %all-to-all-done.received, f32[8,128]{1,0:T(8,128)S(1)} %get-tuple-element.17.token), custom_call_target="tpu_custom_call" | custom-call | flops 1100000000 | bytes 1048576 | tf_op jit(solution)/shard_map/relay/pallas_call | solution.py:494
  31.9 0.0 copy-done.1
  31.9 0.0 copy-done.2
  31.9 14.5 %all_to_all.10.received = bf16[16,4,16,128]{3,2,1,0:T(8,128)(2,1)S(1)} all-to-all(bf16[16,4,16,128]{3,2,1,0:T(8,128)(2,1)S(1)} %relay.1), channel_id=1, replica_groups=mesh['x'=4,'z'=8,'chan'=4,'clip'=2] {'x','chan'}, dimensions={0} | all-to-all | bytes 524288 | tf_op jit(solution)/shard_map/all_to_all | solution.py:550
  46.5 0.0 copy-done.3
  46.5 0.0 copy-done.5
  46.5 0.0 copy-done.7
  46.5 6.9 %read_out.1 = bf16[32,4,16,256]{3,2,1,0:T(8,128)(2,1)} custom-call(s32[4]{0:T(128)S(1)} %pad_add_fusion.place, f32[32]{0:T(128)S(1)} %copy-done.7, f32[1,256]{1,0:T(1,128)S(1)} %bitcast.15, bf16[16,4,16,128]{3,2,1,0:T(8,128)(2,1)S(1)} %all_to_all.10.received, bf16[32,6,16,256]{3,2,1,0:T(8,128)(2,1)} %get-tuple-element.18.drives_far, ...), custom_call_target="tpu_custom_call" | custom-call | flops 6600000000 | bytes 1048576 | tf_op jit(solution)/shard_map/read_out/pallas_call | solution.py:506
  (1 shorter events, 0.0 us)
Async XLA Ops:
  1.1 19.8 %collective-permute-start.2 = (bf16[9,64,256]{2,1,0:T(8,128)(2,1)S(1)}, bf16[9,64,256]{2,1,0:T(8,128)(2,1)S(1)}, u32[]{:S(2)}, u32[]{:S(2)}) collective-permute-start(bf16[9,64,256]{2,1,0:T(8,128)(2,1)S(1)} %broadcast_select_fusion), channel_id=1, source_target_pairs={{0,6},{2,0},{4,2},{6,4},{1,7},{3,1},{5,3},{7,5},{8,14},{10,8},{12,... | collective-permute-start | bytes 884744 | tf_op jit(solution)/shard_map/ppermute | solution.py:534
  4.2 16.7 %collective-permute-start.1 = (bf16[9,64,256]{2,1,0:T(8,128)(2,1)S(1)}, bf16[9,64,256]{2,1,0:T(8,128)(2,1)S(1)}, u32[]{:S(2)}, u32[]{:S(2)}) collective-permute-start(bf16[9,64,256]{2,1,0:T(8,128)(2,1)S(1)} %broadcast_select_fusion), channel_id=1, source_target_pairs={{0,4},{2,6},{4,0},{6,2},{1,5},{3,7},{5,1},{7,3},{8,12},{10,14},{12... | collective-permute-start | bytes 884744 | tf_op jit(solution)/shard_map/ppermute | solution.py:534
  4.8 16.1 %collective-permute-start = (bf16[9,64,256]{2,1,0:T(8,128)(2,1)S(1)}, bf16[9,64,256]{2,1,0:T(8,128)(2,1)S(1)}, u32[]{:S(2)}, u32[]{:S(2)}) collective-permute-start(bf16[9,64,256]{2,1,0:T(8,128)(2,1)S(1)} %broadcast_select_fusion), channel_id=1, source_target_pairs={{0,2},{2,4},{4,6},{6,0},{1,3},{3,5},{5,7},{7,1},{8,10},{10,12},{12... | collective-permute-start | bytes 884744 | tf_op jit(solution)/shard_map/ppermute | solution.py:534
  5.8 18.2 %copy-start = (bf16[3,3,256,64]{2,3,1,0:T(8,128)(2,1)S(1)}, bf16[3,3,256,64]{2,3,1,0:T(8,128)(2,1)}, u32[]{:S(2)}) copy-start(bf16[3,3,256,64]{2,3,1,0:T(8,128)(2,1)} %param.9) | copy-start | bytes 884740
  12.3 18.9 %copy-start.6 = (f32[64]{0:T(128)S(1)}, f32[64]{0:T(128)}, u32[]{:S(2)}) copy-start(f32[64]{0:T(128)} %param.8) | copy-start | bytes 772
  12.3 18.9 %all-to-all-start = ((bf16[8,9,16,128]{3,2,1,0:T(8,128)(2,1)}), bf16[8,9,16,128]{3,2,1,0:T(8,128)(2,1)S(1)}, u32[]{:S(2)}, u32[]{:S(2)}) async-start(bf16[8,9,16,128]{3,2,1,0:T(8,128)(2,1)} %get-tuple-element.12), calls=%async_computation | async-start | bytes 589824 | tf_op jit(solution)/shard_map/all_to_all | solution.py:547
  20.9 0.7 %copy-start.4 = (f32[8,128]{1,0:T(8,128)S(1)}, f32[8,128]{1,0:T(8,128)}, u32[]{:S(2)}) copy-start(f32[8,128]{1,0:T(8,128)} %get-tuple-element.13.refs_3_) | copy-start | bytes 12292
  21.6 1.6 %collective-permute-start.3 = (bf16[9,64,256]{2,1,0:T(8,128)(2,1)S(1)}, bf16[9,64,256]{2,1,0:T(8,128)(2,1)S(1)}, u32[]{:S(2)}, u32[]{:S(2)}) collective-permute-start(bf16[9,64,256]{2,1,0:T(8,128)(2,1)S(1)} %get-tuple-element.14.rest_0_), channel_id=1, source_target_pairs={{0,1},{1,0},{2,3},{3,2},{4,5},{5,4},{6,7},{7,6},{8,9},{9,8},{10,11... | collective-permute-start | bytes 884744 | tf_op jit(solution)/shard_map/ppermute | solution.py:546
  21.6 2.0 %collective-permute-start.4 = (bf16[9,64,256]{2,1,0:T(8,128)(2,1)S(1)}, bf16[9,64,256]{2,1,0:T(8,128)(2,1)S(1)}, u32[]{:S(2)}, u32[]{:S(2)}) collective-permute-start(bf16[9,64,256]{2,1,0:T(8,128)(2,1)S(1)} %get-tuple-element.15.rest_1_), channel_id=1, source_target_pairs={{0,1},{1,0},{2,3},{3,2},{4,5},{5,4},{6,7},{7,6},{8,9},{9,8},{10,11... | collective-permute-start | bytes 884744 | tf_op jit(solution)/shard_map/ppermute | solution.py:546
  22.1 1.9 %collective-permute-start.5 = (bf16[9,64,256]{2,1,0:T(8,128)(2,1)S(1)}, bf16[9,64,256]{2,1,0:T(8,128)(2,1)S(1)}, u32[]{:S(2)}, u32[]{:S(2)}) collective-permute-start(bf16[9,64,256]{2,1,0:T(8,128)(2,1)S(1)} %get-tuple-element.16.rest_2_), channel_id=1, source_target_pairs={{0,1},{1,0},{2,3},{3,2},{4,5},{5,4},{6,7},{7,6},{8,9},{9,8},{10,11... | collective-permute-start | bytes 884744 | tf_op jit(solution)/shard_map/ppermute | solution.py:546
  22.1 24.3 %copy-start.3 = (bf16[3,3,64,256]{3,2,1,0:T(8,128)(2,1)S(1)}, bf16[3,3,64,256]{3,2,1,0:T(8,128)(2,1)}, u32[]{:S(2)}) copy-start(bf16[3,3,64,256]{3,2,1,0:T(8,128)(2,1)} %param.10) | copy-start | bytes 884740
  22.1 24.3 %copy-start.5 = (f32[256]{0:T(256)S(1)}, f32[256]{0:T(256)}, u32[]{:S(2)}) copy-start(f32[256]{0:T(256)} %param.11) | copy-start | bytes 3076
  22.1 24.3 %copy-start.7 = (f32[32]{0:T(128)S(1)}, f32[32]{0:T(128)}, u32[]{:S(2)}) copy-start(f32[32]{0:T(128)} %intervals_far.3) | copy-start | bytes 388
  23.6 8.4 %copy-start.1 = (bf16[9,64,256]{2,1,0:T(8,128)(2,1)}, bf16[9,64,256]{2,1,0:T(8,128)(2,1)S(1)}, u32[]{:S(2)}) copy-start(bf16[9,64,256]{2,1,0:T(8,128)(2,1)S(1)} %collective-permute-done.4.rest_4_) | copy-start | bytes 884740
  24.0 7.9 %copy-start.2 = (bf16[9,64,256]{2,1,0:T(8,128)(2,1)}, bf16[9,64,256]{2,1,0:T(8,128)(2,1)S(1)}, u32[]{:S(2)}) copy-start(bf16[9,64,256]{2,1,0:T(8,128)(2,1)S(1)} %collective-permute-done.5.rest_5_) | copy-start | bytes 884740

commit v6 on v5

--- a/solution.py
+++ b/solution.py
@@ -87,7 +87,7 @@
 
 def drive_kernel(
     intervals_far, rates_far, kernel_far, frames,
-    message, token,
+    message,
     intervals, rates, kernel_t, padded, weights, factors, state, load_sem, small_sem,
 ):
     small = [
@@ -98,7 +98,6 @@
     ]
     for copy in small:
         copy.start()
-    token[...] = jnp.zeros_like(token)
 
     def load(chunk, half):
         first, size = PIECES[chunk]
@@ -186,40 +185,44 @@
         message[z, ROWS // 2] = extra
 
 
-def whole(own, pairs, use_left, tap):
-    parts = [own[tap]] + [jnp.where(use_left, left[tap], right[tap]) for left, right in pairs]
-    return jnp.concatenate(parts, axis=0)
-
-
 WINDOW_STEP = 8
-WINDOW_CHUNKS = FRAMES // WINDOW_STEP
+WINDOW_CHUNKS = HALF // WINDOW_STEP
 TALL = 12
 
 
-def window_kernel(
-    place, kernel_own, *rest
-):
-    direct, swapped = rest[: CHANS - 1], rest[CHANS - 1 : 2 * CHANS - 2]
-    (frames, drives, token, rows, written, load_sem, store_sem) = rest[2 * CHANS - 2 :]
-    pairs = list(zip(direct, swapped))
+def assemble(target, own, pairs, use_left):
+    def tap(index, carry):
+        parts = [own[index]]
+        parts += [jnp.where(use_left, left[index], right[index]) for left, right in pairs]
+        target[index] = jnp.concatenate(parts, axis=0)
+        return carry
+
+    lax.fori_loop(0, 9, tap, 0)
+
+
+def window_kernel(half, place, own, *rest):
+    others = CHANS - 1
+    pairs = list(zip(rest[:others], rest[others : 2 * others]))
+    frames, out_own, _, drives, result = rest[2 * others : 2 * others + 5]
+    weights, rows, written, load_sem, store_sem = rest[2 * others + 5 :]
     chan, first = place[0], place[3] == 0
     source = jnp.clip(CHANS * chan - 2, 0, 8)
     target = source - CHANS * chan + 4
 
     def load(chunk):
         part = pl.ds(chunk * WINDOW_STEP, WINDOW_STEP)
+        where = pl.ds(half * HALF + chunk * WINDOW_STEP, WINDOW_STEP)
         return pltpu.make_async_copy(
-            frames.at[part, pl.ds(source, 8)], rows.at[part, pl.ds(target, 8)], load_sem.at[chunk]
+            frames.at[where, pl.ds(source, 8)], rows.at[part, pl.ds(target, 8)], load_sem.at[chunk]
         )
 
     def store(chunk):
         part = pl.ds(chunk * WINDOW_STEP, WINDOW_STEP)
         return pltpu.make_async_copy(written.at[part], drives.at[part], store_sem.at[chunk])
 
-    token[...] = jnp.zeros_like(token)
     for chunk in range(WINDOW_CHUNKS):
         load(chunk).start()
-    empty = jnp.zeros((FRAMES, 2, WIDE, CH), BF16)
+    empty = jnp.zeros((HALF, 2, WIDE, CH), BF16)
 
     @pl.when(chan == 0)
     def _():
@@ -228,6 +231,12 @@
     @pl.when(chan == CHANS - 1)
     def _():
         rows[:, 8:10] = empty
+
+    assemble(weights, own, pairs, first)
+    if half == 0:
+        result[...] = jnp.zeros_like(result)
+    else:
+        assemble(result, out_own, pairs, jnp.logical_not(first))
 
     def convolve(chunk, carry):
         load(chunk).wait()
@@ -237,13 +246,12 @@
         taps = [block[:, 2 + i : 2 + i + WINDOW].reshape(size, CH) for i in range(3)]
         operand = jnp.concatenate(taps, axis=1)
         shape = (WINDOW_STEP * WINDOW, WIDE, CH)
+        dims = (((1,), (1,)), ((), ()))
         parts = []
         for j in range(3):
-            weight = jnp.concatenate([whole(kernel_own, pairs, first, 3 * i + j) for i in range(3)], axis=1)
+            weight = jnp.concatenate([weights[3 * i + j] for i in range(3)], axis=1)
             parts.append(
-                lax.dot_general(
-                    operand, weight, (((1,), (1,)), ((), ())), preferred_element_type=F32
-                ).reshape(shape)
+                lax.dot_general(operand, weight, dims, preferred_element_type=F32).reshape(shape)
             )
         total = beside(*parts).reshape(WINDOW_STEP, WINDOW, WIDE, CH)
         for r in range(WINDOW):
@@ -261,8 +269,9 @@
         store(chunk).wait()
 
 
-def relay_kernel(place, rates, received, token, message):
+def relay_kernel(place, rates, received, token, message, done):
     x, z = place[1], place[2]
+    done[...] = jnp.zeros_like(done)
     rate = doubled(rates[...])
     total = jnp.zeros((ROWS // 2, WIDE, LANES), F32)
     before = total
@@ -310,17 +319,15 @@
 
 
 def readout_kernel(
-    place, intervals_far, skip_gain, received, drives_far, kernel_own, *rest
+    place, intervals_far, skip_gain, received, early_drives, late_drives, weights, frames,
+    result,
+    intervals, direct, drives, states, written, factors, state,
+    load_sem, drive_sem, store_sem, small_sem,
 ):
-    pairs = list(zip(rest[: CHANS - 1], rest[CHANS - 1 : 2 * CHANS - 2]))
-    (
-        frames, result, intervals, direct, drives, states, written, factors, state,
-        load_sem, drive_sem, store_sem, small_sem,
-    ) = rest[2 * CHANS - 2 :]
     small = [pltpu.make_async_copy(intervals_far, intervals, small_sem)]
     for copy in small:
         copy.start()
-    chan, x, second = place[0], place[1], place[3] == 1
+    chan, x = place[0], place[1]
 
     def load(chunk):
         part = pl.ds(chunk * OUT_STEP, OUT_STEP)
@@ -328,16 +335,17 @@
             frames.at[part, pl.ds(CHANS * chan, CHANS)], direct.at[part], load_sem.at[chunk]
         )
 
-    def arrive(chunk):
+    def arrive(chunk, source=early_drives):
         part = pl.ds(chunk * OUT_STEP, OUT_STEP)
-        return pltpu.make_async_copy(drives_far.at[part], drives.at[part], drive_sem.at[chunk])
+        where = pl.ds(chunk % (HALF // OUT_STEP) * OUT_STEP, OUT_STEP)
+        return pltpu.make_async_copy(source.at[where], drives.at[part], drive_sem.at[chunk])
 
     def store(chunk):
         part = pl.ds(chunk * OUT_STEP, OUT_STEP)
         return pltpu.make_async_copy(written.at[part], result.at[part], store_sem.at[chunk])
 
     for chunk in range(OUT_CHUNKS):
-        arrive(chunk).start()
+        arrive(chunk, late_drives if chunk * OUT_STEP >= HALF else early_drives).start()
         load(chunk).start()
 
     low = low_half((WIDE, LANES))
@@ -394,7 +402,7 @@
         shape = (OUT_STEP * CHANS, WIDE, CH)
         parts = []
         for j in range(3):
-            weight = jnp.concatenate([whole(kernel_own, pairs, second, 3 * i + j) for i in range(3)], axis=0)
+            weight = jnp.concatenate([weights[3 * i + j] for i in range(3)], axis=0)
             parts.append(jnp.dot(operand, weight, preferred_element_type=F32).reshape(shape))
         load(chunk).wait()
         passed = direct[pl.ds(start, OUT_STEP)].astype(F32).reshape(shape)
@@ -429,12 +437,9 @@
 def drive(intervals, rates, kernel_t, frames):
     return pl.pallas_call(
         drive_kernel,
-        out_shape=[
-            jax.ShapeDtypeStruct((ZS, ROWS // 2 + 1, WIDE, LANES), BF16),
-            jax.ShapeDtypeStruct((8, LANES), F32),
-        ],
+        out_shape=jax.ShapeDtypeStruct((ZS, ROWS // 2 + 1, WIDE, LANES), BF16),
         in_specs=[anywhere()] * 4,
-        out_specs=[in_vmem()] * 2,
+        out_specs=in_vmem(),
         scratch_shapes=[
             pltpu.SMEM((FRAMES,), F32),
             pltpu.VMEM((1, OWN), F32),
@@ -452,63 +457,53 @@
     )(intervals, rates, kernel_t, frames)
 
 
-def hold_kernel(*refs):
-    del refs
-
-
-def hold(values, other):
+def window(half, place, own, direct, swapped, frames, out_own, after):
+    token = jax.ShapeDtypeStruct((8, LANES), F32)
+    laid = jax.ShapeDtypeStruct((9, CHANS * OWN, CH), BF16)
     return pl.pallas_call(
-        hold_kernel,
-        out_shape=[jax.ShapeDtypeStruct(value.shape, value.dtype) for value in values],
-        in_specs=[anywhere()] * (len(values) + 1),
-        out_specs=[anywhere()] * len(values),
-        input_output_aliases={index: index for index in range(len(values))},
-        compiler_params=pltpu.CompilerParams(vmem_limit_bytes=16 << 20),
-        cost_estimate=cost(0),
-        name="hold",
-    )(*values, other)
-
-
-def window(place, own, direct, swapped, frames):
-    return pl.pallas_call(
-        window_kernel,
+        functools.partial(window_kernel, half),
         out_shape=[
-            jax.ShapeDtypeStruct((FRAMES, WINDOW, WIDE, CH), BF16),
-            jax.ShapeDtypeStruct((8, LANES), F32),
+            jax.ShapeDtypeStruct((HALF, WINDOW, WIDE, CH), BF16),
+            token if half == 0 else laid,
         ],
-        in_specs=[in_smem()] + [in_vmem()] * (2 * CHANS - 1) + [anywhere()],
+        in_specs=[in_smem()]
+        + [in_vmem()] * (2 * CHANS - 1)
+        + [anywhere(), anywhere() if half == 0 else in_vmem(), anywhere()],
         out_specs=[anywhere(), in_vmem()],
         scratch_shapes=[
-            pltpu.VMEM((FRAMES, TALL, WIDE, CH), BF16),
-            pltpu.VMEM((FRAMES, WINDOW, WIDE, CH), BF16),
+            pltpu.VMEM((9, CHANS * OWN, CH), BF16),
+            pltpu.VMEM((HALF, TALL, WIDE, CH), BF16),
+            pltpu.VMEM((HALF, WINDOW, WIDE, CH), BF16),
             pltpu.SemaphoreType.DMA((WINDOW_CHUNKS,)),
             pltpu.SemaphoreType.DMA((WINDOW_CHUNKS,)),
         ],
         compiler_params=pltpu.CompilerParams(vmem_limit_bytes=51 << 20),
-        cost_estimate=cost(1),
+        cost_estimate=cost(1 if half == 0 else 3),
         name="window",
-    )(place, own, *direct, *swapped, frames)
+    )(place, own, *direct, *swapped, frames, out_own, after)
 
 
 def relay(place, rates, received, token):
     return pl.pallas_call(
         relay_kernel,
-        out_shape=jax.ShapeDtypeStruct((XS * CHANS, WINDOW // 2 + 1, WIDE, LANES), BF16),
+        out_shape=[
+            jax.ShapeDtypeStruct((XS * CHANS, WINDOW // 2 + 1, WIDE, LANES), BF16),
+            jax.ShapeDtypeStruct((8, LANES), F32),
+        ],
         in_specs=[in_smem(), in_vmem(), in_vmem(), anywhere()],
-        out_specs=in_vmem(),
+        out_specs=[in_vmem()] * 2,
         compiler_params=pltpu.CompilerParams(vmem_limit_bytes=16 << 20),
         cost_estimate=cost(1),
         name="relay",
     )(place, rates, received, token)
 
 
-def read_out(place, intervals, skip_gain, received, drives, own, direct, swapped, frames):
+def read_out(place, intervals, skip_gain, received, early, late, weights, frames):
     return pl.pallas_call(
         readout_kernel,
         out_shape=jax.ShapeDtypeStruct((FRAMES, CHANS, WIDE, CH), BF16),
-        in_specs=[in_smem(), anywhere(), in_vmem(), in_vmem(), anywhere()]
-        + [in_vmem()] * (2 * CHANS - 1)
-        + [anywhere()],
+        in_specs=[in_smem(), anywhere(), in_vmem(), in_vmem(), anywhere(), anywhere()]
+        + [in_vmem(), anywhere()],
         out_specs=anywhere(),
         scratch_shapes=[
             pltpu.SMEM((FRAMES,), F32),
@@ -523,10 +518,10 @@
             pltpu.SemaphoreType.DMA((OUT_CHUNKS,)),
             pltpu.SemaphoreType.DMA,
         ],
-        compiler_params=pltpu.CompilerParams(vmem_limit_bytes=52 << 20),
+        compiler_params=pltpu.CompilerParams(vmem_limit_bytes=53 << 20),
         cost_estimate=cost(6),
         name="read_out",
-    )(place, intervals, skip_gain, received, drives, own, *direct, *swapped, frames)
+    )(place, intervals, skip_gain, received, early, late, weights, frames)
 
 
 def around(value):
@@ -541,15 +536,15 @@
     kernel_t = jnp.transpose(in_kernel.reshape(9, CH, OWN), (0, 2, 1))
     out_own = out_kernel.reshape(9, OWN, CH)
     direct = around(jnp.where(lax.axis_index("clip") == 0, kernel_t, out_own))
-    message, done = drive(intervals, rates, kernel_t, frames)
-    direct = hold(direct, done)
+    message = drive(intervals, rates, kernel_t, frames)
     swapped = [lax.ppermute(piece, "clip", [(0, 1), (1, 0)]) for piece in direct]
     arrived = lax.all_to_all(message, "z", 0, 0)
-    drives, token = window(place, kernel_t, direct, swapped, frames)
-    onward = relay(place, rates, arrived, token)
-    onward = lax.all_to_all(onward, ("x", "chan"), 0, 0)
+    early, done = window(0, place, kernel_t, direct, swapped, frames, out_own, place)
+    onward, done = relay(place, rates, arrived, done)
+    received = lax.all_to_all(onward, ("x", "chan"), 0, 0)
+    late, weights = window(1, place, kernel_t, direct, swapped, frames, out_own, done)
     skip = skip_gain.reshape(1, CH)
-    return read_out(place, intervals, skip, onward, drives, out_own, direct, swapped, frames)
+    return read_out(place, intervals, skip, received, early, late, weights, frames)
 
 
 def solution(mesh):

time: 53.8 us -> 54.8 us (1.019)
  blocking collectives: 14.5 us -> 0 us
  starting transfers between devices: 13.8 us -> 20 us
  waiting for transfers between devices: 2.03 us -> 7.75 us
  Pallas kernels: 21.1 us -> 25.2 us
  local copies, waits for them, and re-layouts: 0.7 us -> 0.03 us
    all_to_all x1 -> x0, blocking collectives: 14.5 us -> none  [local(): onward = lax.all_to_all(onward, ('x', 'chan'), 0, 0)]
    all_to_all x0 -> x1, starting transfers between devices: none -> 6.11 us  [local(): received = lax.all_to_all(onward, ('x', 'chan'), 0, 0)]
    pallas_call x4, Pallas kernels: 14.2 us -> 18.2 us  [the longest x2 10.3 us: window(): pl.pallas_call(functools.partial(window_kernel, half), out_shape=[jax.Sha...]
    all_to_all x1, waiting for transfers between devices: 0.19 us -> 3.23 us  [local(): arrived = lax.all_to_all(message, 'z', 0, 0)]
    all_to_all x0 -> x1, waiting for transfers between devices: none -> 2.78 us  [local(): received = lax.all_to_all(onward, ('x', 'chan'), 0, 0)]
    unnamed x16 -> x10, local copies, waits for them, and re-layouts: 0.7 us -> 0.03 us
  transfers between devices with their start and end apart: 7 -> 8, of which waited for: 4 -> 5; matrix products, arithmetic and copies ran while one was open for 0% -> 0% of each run, Pallas kernels for 25% -> 31%
where the time goes in v6:
time: 54.8 us; the launch traced here: 54.2 us
  Pallas kernels  25.2 us (46%)
  starting transfers between devices  20 us (36%)
  waiting for transfers between devices  7.75 us (14%)
  other arithmetic  1.16 us (2%)
    pallas_call x2, Pallas kernels, window(): pl.pallas_call(functools.partial(window_kernel, half), out_shape=[jax.Sha...  10.3 us
    all_to_all x1, starting transfers between devices, local(): arrived = lax.all_to_all(message, 'z', 0, 0)  8.58 us
    pallas_call x1, Pallas kernels, read_out(): pl.pallas_call(readout_kernel, out_shape=jax.ShapeDtypeStruct((FRAMES, CH...  7.03 us
    pallas_call x1, Pallas kernels, drive(): pl.pallas_call(drive_kernel, out_shape=jax.ShapeDtypeStruct((ZS, ROWS //...  6.48 us
    all_to_all x1, starting transfers between devices, local(): received = lax.all_to_all(onward, ('x', 'chan'), 0, 0)  6.11 us
    ppermute x3, starting transfers between devices, around(): return [lax.ppermute(value, 'chan', route) for route in routes]  4.69 us
    all_to_all x1, waiting for transfers between devices, local(): arrived = lax.all_to_all(message, 'z', 0, 0)  3.23 us
    all_to_all x1, waiting for transfers between devices, local(): received = lax.all_to_all(onward, ('x', 'chan'), 0, 0)  2.78 us
  transfers between devices with their start and end apart: 8, of which 5 were waited for; matrix products, arithmetic and copies ran while one was open for 0% of the time, Pallas kernels for 31%

profile of v6, /device:TPU:32, one launch (start us, length us, event | category | flops | bytes accessed | tf_op | source)
XLA Modules:
  0.0 54.2 jit_solution(15831152120077202884)
XLA Ops:
  0.0 1.1 %broadcast_select_fusion = bf16[9,64,256]{2,1,0:T(8,128)(2,1)S(1)} fusion(pred[]{:T(512)S(6)} %eq.3, bf16[3,3,64,256]{3,2,1,0:T(8,128)(2,1)} %param.10, bf16[3,3,256,64]{2,3,1,0:T(8,128)(2,1)} %param.9), kind=kLoop, calls=%fused_computation | loop fusion | flops 147456 | bytes 884737 | tf_op jit(solution)/shard_map/jit(_where)/select_n | solution.py:538
  1.1 3.1 %collective-permute-start.2 = (bf16[9,64,256]{2,1,0:T(8,128)(2,1)S(1)}, bf16[9,64,256]{2,1,0:T(8,128)(2,1)S(1)}, u32[]{:S(2)}, u32[]{:S(2)}) collective-permute-start(bf16[9,64,256]{2,1,0:T(8,128)(2,1)S(1)} %broadcast_select_fusion), channel_id=1, source_target_pairs={{0,6},{2,0},{4,2},{6,4},{1,7},{3,1},{5,3},{7,5},{8,14},{10,8},{12,... | collective-permute-start | bytes 884744 | tf_op jit(solution)/shard_map/ppermute | solution.py:529
  4.2 0.6 %collective-permute-start.1 = (bf16[9,64,256]{2,1,0:T(8,128)(2,1)S(1)}, bf16[9,64,256]{2,1,0:T(8,128)(2,1)S(1)}, u32[]{:S(2)}, u32[]{:S(2)}) collective-permute-start(bf16[9,64,256]{2,1,0:T(8,128)(2,1)S(1)} %broadcast_select_fusion), channel_id=1, source_target_pairs={{0,4},{2,6},{4,0},{6,2},{1,5},{3,7},{5,1},{7,3},{8,12},{10,14},{12... | collective-permute-start | bytes 884744 | tf_op jit(solution)/shard_map/ppermute | solution.py:529
  4.8 1.0 %collective-permute-start = (bf16[9,64,256]{2,1,0:T(8,128)(2,1)S(1)}, bf16[9,64,256]{2,1,0:T(8,128)(2,1)S(1)}, u32[]{:S(2)}, u32[]{:S(2)}) collective-permute-start(bf16[9,64,256]{2,1,0:T(8,128)(2,1)S(1)} %broadcast_select_fusion), channel_id=1, source_target_pairs={{0,2},{2,4},{4,6},{6,0},{1,3},{3,5},{5,7},{7,1},{8,10},{10,12},{12... | collective-permute-start | bytes 884744 | tf_op jit(solution)/shard_map/ppermute | solution.py:529
  5.8 0.0 copy-start
  5.8 0.0 copy-start.1
  5.8 6.5 %drive.1 = bf16[8,9,16,128]{3,2,1,0:T(8,128)(2,1)} custom-call(f32[32]{0:T(128)} %intervals_far.3, f32[1,64]{1,0:T(1,128)} %bitcast.18, bf16[9,64,256]{2,1,0:T(8,128)(2,1)} %bitcast.12, bf16[32,16,16,256]{3,2,1,0:T(8,128)(2,1)} %frames.3), custom_call_target="tpu_custom_call" | custom-call | flops 8800000000 | bytes 1048576 | tf_op jit(solution)/shard_map/drive/pallas_call | solution.py:438
  12.3 0.0 copy-start.3
  12.3 8.6 %all-to-all-start = ((bf16[8,9,16,128]{3,2,1,0:T(8,128)(2,1)}), bf16[8,9,16,128]{3,2,1,0:T(8,128)(2,1)S(1)}, u32[]{:S(2)}, u32[]{:S(2)}) async-start(bf16[8,9,16,128]{3,2,1,0:T(8,128)(2,1)} %drive.1), calls=%async_computation | async-start | bytes 589824 | tf_op jit(solution)/shard_map/all_to_all | solution.py:541
  20.9 0.0 collective-permute-done.2.rest_2_
  20.9 0.0 collective-permute-start.5
  20.9 0.0 collective-permute-done.1.rest_1_
  20.9 0.5 collective-permute-start.4
  21.4 0.0 collective-permute-done.rest_0_
  21.4 0.1 collective-permute-start.3
  21.5 0.1 pad_add_fusion.place.rest_8_
  21.6 0.9 %collective-permute-done.5.rest_5_ = bf16[9,64,256]{2,1,0:T(8,128)(2,1)S(1)} collective-permute-done((bf16[9,64,256]{2,1,0:T(8,128)(2,1)S(1)}, bf16[9,64,256]{2,1,0:T(8,128)(2,1)S(1)}, u32[]{:S(2)}, u32[]{:S(2)}) %collective-permute-start.5) | collective-permute-done | bytes 294944 | tf_op jit(solution)/shard_map/ppermute | solution.py:540
  22.5 0.4 collective-permute-done.4.rest_4_
  22.9 0.4 collective-permute-done.3.rest_3_
  23.3 0.0 copy-done
  23.3 0.0 copy-done.1
  23.3 4.6 %window.2 = (bf16[16,6,16,256]{3,2,1,0:T(8,128)(2,1)}, f32[8,128]{1,0:T(8,128)S(1)}) custom-call(s32[4]{0:T(128)S(1)} %pad_add_fusion.place.rest_8_, bf16[9,64,256]{2,1,0:T(8,128)(2,1)S(1)} %bitcast.13, bf16[9,64,256]{2,1,0:T(8,128)(2,1)S(1)} %collective-permute-done.rest_0_, bf16[9,64,256]{2,1,0:T(8,128)(2,1)S(1)} %collective-permute-done.1.rest_1_, ...), custom_call_target="tpu_custom_call" | custom-call | flops 1100000000 | bytes 1048576 | tf_op jit(solution)/shard_map/window/pallas_call | solution.py:463
  27.9 3.2 %all-to-all-done.received = bf16[8,9,16,128]{3,2,1,0:T(8,128)(2,1)S(1)} async-done(((bf16[8,9,16,128]{3,2,1,0:T(8,128)(2,1)}), bf16[8,9,16,128]{3,2,1,0:T(8,128)(2,1)S(1)}, u32[]{:S(2)}, u32[]{:S(2)}) %all-to-all-start) | async-done | bytes 294944 | tf_op jit(solution)/shard_map/all_to_all | solution.py:541
  31.1 0.0 copy-done.3
  31.2 1.5 %relay.1 = (bf16[16,4,16,128]{3,2,1,0:T(8,128)(2,1)}, f32[8,128]{1,0:T(8,128)S(1)}) custom-call(s32[4]{0:T(128)S(1)} %pad_add_fusion.place.rest_8_, f32[1,64]{1,0:T(1,128)S(1)} %bitcast.19, bf16[8,9,16,128]{3,2,1,0:T(8,128)(2,1)S(1)} %all-to-all-done.received, f32[8,128]{1,0:T(8,128)S(1)} %get-tuple-element.11.token), custom_call_target="tpu_custom_call" | custom-call | flops 1100000000 | bytes 1048576 | tf_op jit(solution)/shard_map/relay/pallas_call | solution.py:487
  32.6 6.1 %all-to-all-start.1 = ((bf16[16,4,16,128]{3,2,1,0:T(8,128)(2,1)}), bf16[16,4,16,128]{3,2,1,0:T(8,128)(2,1)S(1)}, u32[]{:S(2)}, u32[]{:S(2)}) async-start(bf16[16,4,16,128]{3,2,1,0:T(8,128)(2,1)} %get-tuple-element.12), calls=%async_computation.1 | async-start | bytes 524288 | tf_op jit(solution)/shard_map/all_to_all | solution.py:544
  38.7 0.0 copy-start.2
  38.8 0.0 copy-start.4
  38.8 5.7 %window.3 = (bf16[16,6,16,256]{3,2,1,0:T(8,128)(2,1)}, bf16[9,256,256]{2,1,0:T(8,128)(2,1)}) custom-call(s32[4]{0:T(128)S(1)} %pad_add_fusion.place.rest_8_, bf16[9,64,256]{2,1,0:T(8,128)(2,1)S(1)} %bitcast.14, bf16[9,64,256]{2,1,0:T(8,128)(2,1)S(1)} %collective-permute-done.rest_0_, bf16[9,64,256]{2,1,0:T(8,128)(2,1)S(1)} %collective-permute-done.1.rest_1_, ...), custom_call_target="tpu_custom_call" | custom-call | flops 3300000000 | bytes 1048576 | tf_op jit(solution)/shard_map/window/pallas_call | solution.py:463
  44.4 2.8 %all-to-all-done.1.received = bf16[16,4,16,128]{3,2,1,0:T(8,128)(2,1)S(1)} async-done(((bf16[16,4,16,128]{3,2,1,0:T(8,128)(2,1)}), bf16[16,4,16,128]{3,2,1,0:T(8,128)(2,1)S(1)}, u32[]{:S(2)}, u32[]{:S(2)}) %all-to-all-start.1) | async-done | bytes 262176 | tf_op jit(solution)/shard_map/all_to_all | solution.py:544
  47.2 0.0 copy-done.2
  47.2 0.0 copy-done.4
  47.2 7.0 %read_out.1 = bf16[32,4,16,256]{3,2,1,0:T(8,128)(2,1)} custom-call(s32[4]{0:T(128)S(1)} %pad_add_fusion.place.rest_8_, f32[32]{0:T(128)S(1)} %copy-done.4, f32[1,256]{1,0:T(1,128)S(1)} %bitcast.17, bf16[16,4,16,128]{3,2,1,0:T(8,128)(2,1)S(1)} %all-to-all-done.1.received, bf16[16,6,16,256]{3,2,1,0:T(8,128)(2,1)} %get-tuple-element.13.early_drives, ...), custom_call_target="tpu_custom_call" | custom-call | flops 6600000000 | bytes 1048576 | tf_op jit(solution)/shard_map/read_out/pallas_call | solution.py:502
Async XLA Ops:
  1.1 19.8 %collective-permute-start.2 = (bf16[9,64,256]{2,1,0:T(8,128)(2,1)S(1)}, bf16[9,64,256]{2,1,0:T(8,128)(2,1)S(1)}, u32[]{:S(2)}, u32[]{:S(2)}) collective-permute-start(bf16[9,64,256]{2,1,0:T(8,128)(2,1)S(1)} %broadcast_select_fusion), channel_id=1, source_target_pairs={{0,6},{2,0},{4,2},{6,4},{1,7},{3,1},{5,3},{7,5},{8,14},{10,8},{12,... | collective-permute-start | bytes 884744 | tf_op jit(solution)/shard_map/ppermute | solution.py:529
  4.2 16.7 %collective-permute-start.1 = (bf16[9,64,256]{2,1,0:T(8,128)(2,1)S(1)}, bf16[9,64,256]{2,1,0:T(8,128)(2,1)S(1)}, u32[]{:S(2)}, u32[]{:S(2)}) collective-permute-start(bf16[9,64,256]{2,1,0:T(8,128)(2,1)S(1)} %broadcast_select_fusion), channel_id=1, source_target_pairs={{0,4},{2,6},{4,0},{6,2},{1,5},{3,7},{5,1},{7,3},{8,12},{10,14},{12... | collective-permute-start | bytes 884744 | tf_op jit(solution)/shard_map/ppermute | solution.py:529
  4.8 16.6 %collective-permute-start = (bf16[9,64,256]{2,1,0:T(8,128)(2,1)S(1)}, bf16[9,64,256]{2,1,0:T(8,128)(2,1)S(1)}, u32[]{:S(2)}, u32[]{:S(2)}) collective-permute-start(bf16[9,64,256]{2,1,0:T(8,128)(2,1)S(1)} %broadcast_select_fusion), channel_id=1, source_target_pairs={{0,2},{2,4},{4,6},{6,0},{1,3},{3,5},{5,7},{7,1},{8,10},{10,12},{12... | collective-permute-start | bytes 884744 | tf_op jit(solution)/shard_map/ppermute | solution.py:529
  5.8 17.5 %copy-start = (bf16[3,3,256,64]{2,3,1,0:T(8,128)(2,1)S(1)}, bf16[3,3,256,64]{2,3,1,0:T(8,128)(2,1)}, u32[]{:S(2)}) copy-start(bf16[3,3,256,64]{2,3,1,0:T(8,128)(2,1)} %param.9) | copy-start | bytes 884740
  5.8 17.5 %copy-start.1 = (bf16[3,3,64,256]{3,2,1,0:T(8,128)(2,1)S(1)}, bf16[3,3,64,256]{3,2,1,0:T(8,128)(2,1)}, u32[]{:S(2)}) copy-start(bf16[3,3,64,256]{3,2,1,0:T(8,128)(2,1)} %param.10) | copy-start | bytes 884740
  12.3 18.9 %copy-start.3 = (f32[64]{0:T(128)S(1)}, f32[64]{0:T(128)}, u32[]{:S(2)}) copy-start(f32[64]{0:T(128)} %param.8) | copy-start | bytes 772
  12.3 18.9 %all-to-all-start = ((bf16[8,9,16,128]{3,2,1,0:T(8,128)(2,1)}), bf16[8,9,16,128]{3,2,1,0:T(8,128)(2,1)S(1)}, u32[]{:S(2)}, u32[]{:S(2)}) async-start(bf16[8,9,16,128]{3,2,1,0:T(8,128)(2,1)} %drive.1), calls=%async_computation | async-start | bytes 589824 | tf_op jit(solution)/shard_map/all_to_all | solution.py:541
  20.9 1.6 %collective-permute-start.5 = (bf16[9,64,256]{2,1,0:T(8,128)(2,1)S(1)}, bf16[9,64,256]{2,1,0:T(8,128)(2,1)S(1)}, u32[]{:S(2)}, u32[]{:S(2)}) collective-permute-start(bf16[9,64,256]{2,1,0:T(8,128)(2,1)S(1)} %collective-permute-done.2.rest_2_), channel_id=1, source_target_pairs={{0,1},{1,0},{2,3},{3,2},{4,5},{5,4},{6,7},{7,6},{8,9},{9,8},{10,11... | collective-permute-start | bytes 884744 | tf_op jit(solution)/shard_map/ppermute | solution.py:540
  20.9 2.0 %collective-permute-start.4 = (bf16[9,64,256]{2,1,0:T(8,128)(2,1)S(1)}, bf16[9,64,256]{2,1,0:T(8,128)(2,1)S(1)}, u32[]{:S(2)}, u32[]{:S(2)}) collective-permute-start(bf16[9,64,256]{2,1,0:T(8,128)(2,1)S(1)} %collective-permute-done.1.rest_1_), channel_id=1, source_target_pairs={{0,1},{1,0},{2,3},{3,2},{4,5},{5,4},{6,7},{7,6},{8,9},{9,8},{10,11... | collective-permute-start | bytes 884744 | tf_op jit(solution)/shard_map/ppermute | solution.py:540
  21.4 1.9 %collective-permute-start.3 = (bf16[9,64,256]{2,1,0:T(8,128)(2,1)S(1)}, bf16[9,64,256]{2,1,0:T(8,128)(2,1)S(1)}, u32[]{:S(2)}, u32[]{:S(2)}) collective-permute-start(bf16[9,64,256]{2,1,0:T(8,128)(2,1)S(1)} %collective-permute-done.rest_0_), channel_id=1, source_target_pairs={{0,1},{1,0},{2,3},{3,2},{4,5},{5,4},{6,7},{7,6},{8,9},{9,8},{10,11... | collective-permute-start | bytes 884744 | tf_op jit(solution)/shard_map/ppermute | solution.py:540
  32.6 14.6 %all-to-all-start.1 = ((bf16[16,4,16,128]{3,2,1,0:T(8,128)(2,1)}), bf16[16,4,16,128]{3,2,1,0:T(8,128)(2,1)S(1)}, u32[]{:S(2)}, u32[]{:S(2)}) async-start(bf16[16,4,16,128]{3,2,1,0:T(8,128)(2,1)} %get-tuple-element.12), calls=%async_computation.1 | async-start | bytes 524288 | tf_op jit(solution)/shard_map/all_to_all | solution.py:544
  38.7 8.5 %copy-start.2 = (f32[256]{0:T(256)S(1)}, f32[256]{0:T(256)}, u32[]{:S(2)}) copy-start(f32[256]{0:T(256)} %param.11) | copy-start | bytes 3076
  38.8 8.5 %copy-start.4 = (f32[32]{0:T(128)S(1)}, f32[32]{0:T(128)}, u32[]{:S(2)}) copy-start(f32[32]{0:T(128)} %intervals_far.3) | copy-start | bytes 388

commit v7 on v6

--- a/solution.py
+++ b/solution.py
@@ -186,34 +186,33 @@
 
 
 WINDOW_STEP = 8
-WINDOW_CHUNKS = HALF // WINDOW_STEP
+WINDOW_CHUNKS = FRAMES // WINDOW_STEP
 TALL = 12
 
 
-def assemble(target, own, pairs, use_left):
+def assemble(target, own, near, swapped, far, first):
     def tap(index, carry):
-        parts = [own[index]]
-        parts += [jnp.where(use_left, left[index], right[index]) for left, right in pairs]
-        target[index] = jnp.concatenate(parts, axis=0)
+        left = jnp.where(first, near[index], swapped[index])
+        right = jnp.where(first, swapped[index], near[index])
+        target[index] = jnp.concatenate([own[index], left, far[index], right], axis=0)
         return carry
 
     lax.fori_loop(0, 9, tap, 0)
 
 
-def window_kernel(half, place, own, *rest):
-    others = CHANS - 1
-    pairs = list(zip(rest[:others], rest[others : 2 * others]))
-    frames, out_own, _, drives, result = rest[2 * others : 2 * others + 5]
-    weights, rows, written, load_sem, store_sem = rest[2 * others + 5 :]
+def window_kernel(
+    place, own, near, swapped, far, frames,
+    drives, token,
+    weights, rows, written, load_sem, store_sem,
+):
     chan, first = place[0], place[3] == 0
     source = jnp.clip(CHANS * chan - 2, 0, 8)
     target = source - CHANS * chan + 4
 
     def load(chunk):
         part = pl.ds(chunk * WINDOW_STEP, WINDOW_STEP)
-        where = pl.ds(half * HALF + chunk * WINDOW_STEP, WINDOW_STEP)
         return pltpu.make_async_copy(
-            frames.at[where, pl.ds(source, 8)], rows.at[part, pl.ds(target, 8)], load_sem.at[chunk]
+            frames.at[part, pl.ds(source, 8)], rows.at[part, pl.ds(target, 8)], load_sem.at[chunk]
         )
 
     def store(chunk):
@@ -222,7 +221,7 @@
 
     for chunk in range(WINDOW_CHUNKS):
         load(chunk).start()
-    empty = jnp.zeros((HALF, 2, WIDE, CH), BF16)
+    empty = jnp.zeros((FRAMES, 2, WIDE, CH), BF16)
 
     @pl.when(chan == 0)
     def _():
@@ -232,11 +231,8 @@
     def _():
         rows[:, 8:10] = empty
 
-    assemble(weights, own, pairs, first)
-    if half == 0:
-        result[...] = jnp.zeros_like(result)
-    else:
-        assemble(result, out_own, pairs, jnp.logical_not(first))
+    token[...] = jnp.zeros_like(token)
+    assemble(weights, own, near, swapped, far, first)
 
     def convolve(chunk, carry):
         load(chunk).wait()
@@ -319,7 +315,7 @@
 
 
 def readout_kernel(
-    place, intervals_far, skip_gain, received, early_drives, late_drives, weights, frames,
+    place, intervals_far, skip_gain, received, drives_far, weights, frames,
     result,
     intervals, direct, drives, states, written, factors, state,
     load_sem, drive_sem, store_sem, small_sem,
@@ -335,17 +331,16 @@
             frames.at[part, pl.ds(CHANS * chan, CHANS)], direct.at[part], load_sem.at[chunk]
         )
 
-    def arrive(chunk, source=early_drives):
+    def arrive(chunk):
         part = pl.ds(chunk * OUT_STEP, OUT_STEP)
-        where = pl.ds(chunk % (HALF // OUT_STEP) * OUT_STEP, OUT_STEP)
-        return pltpu.make_async_copy(source.at[where], drives.at[part], drive_sem.at[chunk])
+        return pltpu.make_async_copy(drives_far.at[part], drives.at[part], drive_sem.at[chunk])
 
     def store(chunk):
         part = pl.ds(chunk * OUT_STEP, OUT_STEP)
         return pltpu.make_async_copy(written.at[part], result.at[part], store_sem.at[chunk])
 
     for chunk in range(OUT_CHUNKS):
-        arrive(chunk, late_drives if chunk * OUT_STEP >= HALF else early_drives).start()
+        arrive(chunk).start()
         load(chunk).start()
 
     low = low_half((WIDE, LANES))
@@ -457,30 +452,62 @@
     )(intervals, rates, kernel_t, frames)
 
 
-def window(half, place, own, direct, swapped, frames, out_own, after):
-    token = jax.ShapeDtypeStruct((8, LANES), F32)
-    laid = jax.ShapeDtypeStruct((9, CHANS * OWN, CH), BF16)
+def window(place, own, near, swapped, far, frames):
     return pl.pallas_call(
-        functools.partial(window_kernel, half),
+        window_kernel,
         out_shape=[
-            jax.ShapeDtypeStruct((HALF, WINDOW, WIDE, CH), BF16),
-            token if half == 0 else laid,
+            jax.ShapeDtypeStruct((FRAMES, WINDOW, WIDE, CH), BF16),
+            jax.ShapeDtypeStruct((8, LANES), F32),
         ],
-        in_specs=[in_smem()]
-        + [in_vmem()] * (2 * CHANS - 1)
-        + [anywhere(), anywhere() if half == 0 else in_vmem(), anywhere()],
+        in_specs=[in_smem()] + [in_vmem()] * CHANS + [anywhere()],
         out_specs=[anywhere(), in_vmem()],
         scratch_shapes=[
             pltpu.VMEM((9, CHANS * OWN, CH), BF16),
-            pltpu.VMEM((HALF, TALL, WIDE, CH), BF16),
-            pltpu.VMEM((HALF, WINDOW, WIDE, CH), BF16),
+            pltpu.VMEM((FRAMES, TALL, WIDE, CH), BF16),
+            pltpu.VMEM((FRAMES, WINDOW, WIDE, CH), BF16),
             pltpu.SemaphoreType.DMA((WINDOW_CHUNKS,)),
             pltpu.SemaphoreType.DMA((WINDOW_CHUNKS,)),
         ],
-        compiler_params=pltpu.CompilerParams(vmem_limit_bytes=51 << 20),
-        cost_estimate=cost(1 if half == 0 else 3),
+        compiler_params=pltpu.CompilerParams(vmem_limit_bytes=52 << 20),
+        cost_estimate=cost(1),
         name="window",
-    )(place, own, *direct, *swapped, frames, out_own, after)
+    )(place, own, near, swapped, far, frames)
+
+
+def lay_kernel(place, own, near, swapped, far, result):
+    assemble(result, own, near, swapped, far, place[3] == 0)
+
+
+def lay(place, own, near, swapped, far):
+    return pl.pallas_call(
+        lay_kernel,
+        out_shape=jax.ShapeDtypeStruct((9, CHANS * OWN, CH), BF16),
+        in_specs=[in_smem()] + [in_vmem()] * CHANS,
+        out_specs=in_vmem(),
+        compiler_params=pltpu.CompilerParams(vmem_limit_bytes=16 << 20),
+        cost_estimate=cost(1),
+        name="lay",
+    )(place, own, near, swapped, far)
+
+
+def hold_kernel(value, *refs):
+    result, sem = refs[-2:]
+    copy = pltpu.make_async_copy(value, result, sem)
+    copy.start()
+    copy.wait()
+
+
+def hold(value, others):
+    return pl.pallas_call(
+        hold_kernel,
+        out_shape=jax.ShapeDtypeStruct(value.shape, value.dtype),
+        in_specs=[anywhere()] * (1 + len(others)),
+        out_specs=anywhere(),
+        scratch_shapes=[pltpu.SemaphoreType.DMA],
+        compiler_params=pltpu.CompilerParams(vmem_limit_bytes=16 << 20),
+        cost_estimate=cost(1),
+        name="hold",
+    )(value, *others)
 
 
 def relay(place, rates, received, token):
@@ -498,12 +525,11 @@
     )(place, rates, received, token)
 
 
-def read_out(place, intervals, skip_gain, received, early, late, weights, frames):
+def read_out(place, intervals, skip_gain, received, drives, weights, frames):
     return pl.pallas_call(
         readout_kernel,
         out_shape=jax.ShapeDtypeStruct((FRAMES, CHANS, WIDE, CH), BF16),
-        in_specs=[in_smem(), anywhere(), in_vmem(), in_vmem(), anywhere(), anywhere()]
-        + [in_vmem(), anywhere()],
+        in_specs=[in_smem(), anywhere(), in_vmem(), in_vmem(), anywhere(), in_vmem(), anywhere()],
         out_specs=anywhere(),
         scratch_shapes=[
             pltpu.SMEM((FRAMES,), F32),
@@ -518,15 +544,41 @@
             pltpu.SemaphoreType.DMA((OUT_CHUNKS,)),
             pltpu.SemaphoreType.DMA,
         ],
-        compiler_params=pltpu.CompilerParams(vmem_limit_bytes=53 << 20),
+        compiler_params=pltpu.CompilerParams(vmem_limit_bytes=52 << 20),
         cost_estimate=cost(6),
         name="read_out",
-    )(place, intervals, skip_gain, received, early, late, weights, frames)
+    )(place, intervals, skip_gain, received, drives, weights, frames)
 
 
 def around(value):
-    routes = [[(c, (c + step) % CHANS) for c in range(CHANS)] for step in range(1, CHANS)]
-    return [lax.ppermute(value, "chan", route) for route in routes]
+    near = [
+        (2 * c + core, 2 * ((c + step) % CHANS) + core)
+        for c in range(CHANS)
+        for core, step in ((0, 1), (1, CHANS - 1))
+    ]
+    far = [(c, (c + 2) % CHANS) for c in range(CHANS)]
+    return lax.ppermute(value, ("chan", "clip"), near), lax.ppermute(value, "chan", far)
+
+
+def after_kernel(*refs):
+    del refs
+
+
+def after(value, other):
+    return pl.pallas_call(
+        after_kernel,
+        out_shape=jax.ShapeDtypeStruct(value.shape, value.dtype),
+        in_specs=[anywhere()] * 2,
+        out_specs=anywhere(),
+        input_output_aliases={0: 0},
+        compiler_params=pltpu.CompilerParams(vmem_limit_bytes=16 << 20),
+        cost_estimate=cost(0),
+        name="after",
+    )(value, other)
+
+
+def swap(value):
+    return lax.ppermute(value, "clip", [(0, 1), (1, 0)])
 
 
 def local(frames, intervals, decay_rates, in_kernel, out_kernel, skip_gain):
@@ -535,16 +587,17 @@
     rates = decay_rates.reshape(1, OWN)
     kernel_t = jnp.transpose(in_kernel.reshape(9, CH, OWN), (0, 2, 1))
     out_own = out_kernel.reshape(9, OWN, CH)
-    direct = around(jnp.where(lax.axis_index("clip") == 0, kernel_t, out_own))
+    in_near, in_far = around(kernel_t)
     message = drive(intervals, rates, kernel_t, frames)
-    swapped = [lax.ppermute(piece, "clip", [(0, 1), (1, 0)]) for piece in direct]
     arrived = lax.all_to_all(message, "z", 0, 0)
-    early, done = window(0, place, kernel_t, direct, swapped, frames, out_own, place)
+    out_near, out_far = around(hold(out_own, (in_near, in_far)))
+    drives, done = window(place, kernel_t, in_near, swap(in_near), in_far, frames)
     onward, done = relay(place, rates, arrived, done)
+    out_near = after(out_near, done)
     received = lax.all_to_all(onward, ("x", "chan"), 0, 0)
-    late, weights = window(1, place, kernel_t, direct, swapped, frames, out_own, done)
+    weights = lay(place, out_own, out_near, swap(out_near), out_far)
     skip = skip_gain.reshape(1, CH)
-    return read_out(place, intervals, skip, received, early, late, weights, frames)
+    return read_out(place, intervals, skip, received, drives, weights, frames)
 
 
 def solution(mesh):

time: 54.8 us -> 54.4 us (level)
  starting transfers between devices: 20 us -> 24 us
  Pallas kernels: 25.2 us -> 21.8 us
  other arithmetic: 1.16 us -> 0.08 us
    all_to_all x1, waiting for transfers between devices: 2.78 us -> 7.97 us  [local(): received = lax.all_to_all(onward, ('x', 'chan'), 0, 0)]
    all_to_all x1, waiting for transfers between devices: 3.23 us -> 0.01 us  [local(): arrived = lax.all_to_all(message, 'z', 0, 0)]
    ppermute x6, starting transfers between devices: 5.29 us -> 8.19 us  [the longest x2 7.23 us: around(): lax.ppermute(value, 'chan', far)]
    pallas_call x2 -> x4, Pallas kernels: 10.3 us -> 7.63 us  [the longest x1 6.9 us: window(): pl.pallas_call(window_kernel, out_shape=[jax.ShapeDtypeStruct((FRAMES, WI...]
    ppermute x6, waiting for transfers between devices: 1.74 us -> 0.02 us  [the longest x2 0.01 us: around(): lax.ppermute(value, ('chan', 'clip'), near)]
    all_to_all x1, starting transfers between devices: 6.11 us -> 7.24 us  [local(): received = lax.all_to_all(onward, ('x', 'chan'), 0, 0)]
    select_n x1 -> x0, other arithmetic: 1.08 us -> none  [local(): direct = around(jnp.where(lax.axis_index('clip') == 0, kernel_t, out_own))]
    pallas_call x1, Pallas kernels: 7.03 us -> 6.29 us  [read_out(): pl.pallas_call(readout_kernel, out_shape=jax.ShapeDtypeStruct((FRAMES, CH...]
  transfers between devices with their start and end apart: 8 -> 8, of which waited for: 5 -> 1; matrix products, arithmetic and copies ran while one was open for 0% -> 0% of each run, Pallas kernels for 31% -> 29%
where the time goes in v7:
time: 54.4 us; the launch traced here: 54.1 us
  starting transfers between devices  24 us (44%)
  Pallas kernels  21.8 us (40%)
  waiting for transfers between devices  7.99 us (15%)
    all_to_all x1, starting transfers between devices, local(): arrived = lax.all_to_all(message, 'z', 0, 0)  8.58 us
    all_to_all x1, waiting for transfers between devices, local(): received = lax.all_to_all(onward, ('x', 'chan'), 0, 0)  7.97 us
    all_to_all x1, starting transfers between devices, local(): received = lax.all_to_all(onward, ('x', 'chan'), 0, 0)  7.24 us
    ppermute x2, starting transfers between devices, around(): lax.ppermute(value, 'chan', far)  7.23 us
    pallas_call x1, Pallas kernels, window(): pl.pallas_call(window_kernel, out_shape=[jax.ShapeDtypeStruct((FRAMES, WI...  6.9 us
    pallas_call x1, Pallas kernels, drive(): pl.pallas_call(drive_kernel, out_shape=jax.ShapeDtypeStruct((ZS, ROWS //...  6.46 us
    pallas_call x1, Pallas kernels, read_out(): pl.pallas_call(readout_kernel, out_shape=jax.ShapeDtypeStruct((FRAMES, CH...  6.29 us
    pallas_call x1, Pallas kernels, relay(): pl.pallas_call(relay_kernel, out_shape=[jax.ShapeDtypeStruct((XS * CHANS,...  1.47 us
  transfers between devices with their start and end apart: 8, of which 1 were waited for; matrix products, arithmetic and copies ran while one was open for 0% of the time, Pallas kernels for 29%

profile of v7, /device:TPU:32, one launch (start us, length us, event | category | flops | bytes accessed | tf_op | source)
XLA Modules:
  0.0 54.1 jit_solution(15986200465046472097)
XLA Ops:
  0.0 3.2 %collective-permute-start.2 = (bf16[9,64,256]{2,1,0:T(8,128)(2,1)}, bf16[9,64,256]{2,1,0:T(8,128)(2,1)S(1)}, u32[]{:S(2)}, u32[]{:S(2)}) collective-permute-start(bf16[9,64,256]{2,1,0:T(8,128)(2,1)} %bitcast.10), channel_id=1, source_target_pairs={{0,4},{2,6},{4,0},{6,2},{1,5},{3,7},{5,1},{7,3},{8,12},{10,14},{12... | collective-permute-start | bytes 884744 | tf_op jit(solution)/shard_map/ppermute | solution.py:560
  3.2 0.7 %collective-permute-start = (bf16[9,64,256]{2,1,0:T(8,128)(2,1)}, bf16[9,64,256]{2,1,0:T(8,128)(2,1)S(1)}, u32[]{:S(2)}, u32[]{:S(2)}) collective-permute-start(bf16[9,64,256]{2,1,0:T(8,128)(2,1)} %bitcast.11), channel_id=1, source_target_pairs={{0,2},{1,7},{2,4},{3,1},{4,6},{5,3},{6,0},{7,5},{8,10},{9,15},{10,... | collective-permute-start | bytes 884744 | tf_op jit(solution)/shard_map/ppermute | solution.py:560
  3.9 0.0 copy-start.1
  3.9 6.5 %drive.1 = bf16[8,9,16,128]{3,2,1,0:T(8,128)(2,1)} custom-call(f32[32]{0:T(128)} %intervals_far.3, f32[1,64]{1,0:T(1,128)} %bitcast.17, bf16[9,64,256]{2,1,0:T(8,128)(2,1)} %bitcast.12, bf16[32,16,16,256]{3,2,1,0:T(8,128)(2,1)} %frames.5), custom_call_target="tpu_custom_call" | custom-call | flops 8800000000 | bytes 1048576 | tf_op jit(solution)/shard_map/drive/pallas_call | solution.py:433
  10.3 8.6 %all-to-all-start = ((bf16[8,9,16,128]{3,2,1,0:T(8,128)(2,1)}), bf16[8,9,16,128]{3,2,1,0:T(8,128)(2,1)S(1)}, u32[]{:S(2)}, u32[]{:S(2)}) async-start(bf16[8,9,16,128]{3,2,1,0:T(8,128)(2,1)} %drive.1), calls=%async_computation | async-start | bytes 589824 | tf_op jit(solution)/shard_map/all_to_all | solution.py:592
  18.9 0.0 collective-permute-done.near.refs_0_
  18.9 0.0 collective-permute-start.1
  18.9 0.0 collective-permute-done.2.far.refs_1_
  19.0 0.0 copy-done.1
  19.0 0.0 copy-start
  19.0 0.1 hold.1
  19.1 0.1 collective-permute-start.3
  19.2 0.1 pad_add_fusion.place
  19.2 0.0 copy-start.3
  19.2 4.0 %collective-permute-start.5 = (bf16[9,64,256]{2,1,0:T(8,128)(2,1)S(1)}, bf16[9,64,256]{2,1,0:T(8,128)(2,1)S(1)}, u32[]{:S(2)}, u32[]{:S(2)}) collective-permute-start(bf16[9,64,256]{2,1,0:T(8,128)(2,1)S(1)} %hold.1), channel_id=1, source_target_pairs={{0,4},{2,6},{4,0},{6,2},{1,5},{3,7},{5,1},{7,3},{8,12},{10,14},{12... | collective-permute-start | bytes 884744 | tf_op jit(solution)/shard_map/ppermute | solution.py:560
  23.3 0.0 collective-permute-done.1.swapped
  23.3 0.0 copy-done
  23.3 6.9 %window.1 = (bf16[32,6,16,256]{3,2,1,0:T(8,128)(2,1)}, f32[8,128]{1,0:T(8,128)S(1)}) custom-call(s32[4]{0:T(128)S(1)} %pad_add_fusion.place, bf16[9,64,256]{2,1,0:T(8,128)(2,1)S(1)} %bitcast.13, bf16[9,64,256]{2,1,0:T(8,128)(2,1)S(1)} %collective-permute-done.near.refs_0_, bf16[9,64,256]{2,1,0:T(8,128)(2,1)S(1)} %collective-permute-done.1.swapped, ...), custom_call_target="tpu_custom_call" | custom-call | flops 1100000000 | bytes 1048576 | tf_op jit(solution)/shard_map/window/pallas_call | solution.py:456
  30.2 0.0 all-to-all-done.received
  30.2 0.0 copy-done.3
  30.2 1.5 %relay.1 = (bf16[16,4,16,128]{3,2,1,0:T(8,128)(2,1)}, f32[8,128]{1,0:T(8,128)S(1)}) custom-call(s32[4]{0:T(128)S(1)} %pad_add_fusion.place, f32[1,64]{1,0:T(1,128)S(1)} %bitcast.18, bf16[8,9,16,128]{3,2,1,0:T(8,128)(2,1)S(1)} %all-to-all-done.received, f32[8,128]{1,0:T(8,128)S(1)} %get-tuple-element.9.token), custom_call_target="tpu_custom_call" | custom-call | flops 1100000000 | bytes 1048576 | tf_op jit(solution)/shard_map/relay/pallas_call | solution.py:514
  31.7 0.0 collective-permute-done.3.refs_0_
  31.7 0.2 collective-permute-start.4
  31.9 7.2 %all-to-all-start.1 = ((bf16[16,4,16,128]{3,2,1,0:T(8,128)(2,1)}), bf16[16,4,16,128]{3,2,1,0:T(8,128)(2,1)S(1)}, u32[]{:S(2)}, u32[]{:S(2)}) async-start(bf16[16,4,16,128]{3,2,1,0:T(8,128)(2,1)} %get-tuple-element.10), calls=%async_computation.1 | async-start | bytes 524288 | tf_op jit(solution)/shard_map/all_to_all | solution.py:597
  39.1 0.0 copy-start.2
  39.1 0.0 copy-start.4
  39.1 0.0 collective-permute-done.5.far
  39.2 0.0 collective-permute-done.4.swapped
  39.2 0.7 %lay.1.weights = bf16[9,256,256]{2,1,0:T(8,128)(2,1)S(1)} custom-call(s32[4]{0:T(128)S(1)} %pad_add_fusion.place, bf16[9,64,256]{2,1,0:T(8,128)(2,1)S(1)} %bitcast.15, bf16[9,64,256]{2,1,0:T(8,128)(2,1)S(1)} %after.1.near, bf16[9,64,256]{2,1,0:T(8,128)(2,1)S(1)} %collective-permute-done.4.swapped, bf16[9,64,256]{2,1,0:T(8,128)(2,1)S(1)} %collective-permute-done.5.far), custom_call_target="tpu_custom_call" | custom-call | flops 1100000000 | bytes 1048576 | tf_op jit(solution)/shard_map/lay/pallas_call | solution.py:482
  39.8 8.0 %all-to-all-done.1.received = bf16[16,4,16,128]{3,2,1,0:T(8,128)(2,1)S(1)} async-done(((bf16[16,4,16,128]{3,2,1,0:T(8,128)(2,1)}), bf16[16,4,16,128]{3,2,1,0:T(8,128)(2,1)S(1)}, u32[]{:S(2)}, u32[]{:S(2)}) %all-to-all-start.1) | async-done | bytes 262176 | tf_op jit(solution)/shard_map/all_to_all | solution.py:597
  47.8 0.0 copy-done.2
  47.8 0.0 copy-done.4
  47.8 6.3 %read_out.1 = bf16[32,4,16,256]{3,2,1,0:T(8,128)(2,1)} custom-call(s32[4]{0:T(128)S(1)} %pad_add_fusion.place, f32[32]{0:T(128)S(1)} %copy-done.4, f32[1,256]{1,0:T(1,128)S(1)} %bitcast.16, bf16[16,4,16,128]{3,2,1,0:T(8,128)(2,1)S(1)} %all-to-all-done.1.received, bf16[32,6,16,256]{3,2,1,0:T(8,128)(2,1)} %get-tuple-element.11.drives_far, ...), custom_call_target="tpu_custom_call" | custom-call | flops 6600000000 | bytes 1048576 | tf_op jit(solution)/shard_map/read_out/pallas_call | solution.py:529
  (1 shorter events, 0.0 us)
Async XLA Ops:
  0.0 18.9 %collective-permute-start.2 = (bf16[9,64,256]{2,1,0:T(8,128)(2,1)}, bf16[9,64,256]{2,1,0:T(8,128)(2,1)S(1)}, u32[]{:S(2)}, u32[]{:S(2)}) collective-permute-start(bf16[9,64,256]{2,1,0:T(8,128)(2,1)} %bitcast.10), channel_id=1, source_target_pairs={{0,4},{2,6},{4,0},{6,2},{1,5},{3,7},{5,1},{7,3},{8,12},{10,14},{12... | collective-permute-start | bytes 884744 | tf_op jit(solution)/shard_map/ppermute | solution.py:560
  3.2 15.7 %collective-permute-start = (bf16[9,64,256]{2,1,0:T(8,128)(2,1)}, bf16[9,64,256]{2,1,0:T(8,128)(2,1)S(1)}, u32[]{:S(2)}, u32[]{:S(2)}) collective-permute-start(bf16[9,64,256]{2,1,0:T(8,128)(2,1)} %bitcast.11), channel_id=1, source_target_pairs={{0,2},{1,7},{2,4},{3,1},{4,6},{5,3},{6,0},{7,5},{8,10},{9,15},{10,... | collective-permute-start | bytes 884744 | tf_op jit(solution)/shard_map/ppermute | solution.py:560
  3.9 15.1 %copy-start.1 = (bf16[3,3,64,256]{3,2,1,0:T(8,128)(2,1)S(1)}, bf16[3,3,64,256]{3,2,1,0:T(8,128)(2,1)}, u32[]{:S(2)}) copy-start(bf16[3,3,64,256]{3,2,1,0:T(8,128)(2,1)} %param.10) | copy-start | bytes 884740
  10.3 19.8 %all-to-all-start = ((bf16[8,9,16,128]{3,2,1,0:T(8,128)(2,1)}), bf16[8,9,16,128]{3,2,1,0:T(8,128)(2,1)S(1)}, u32[]{:S(2)}, u32[]{:S(2)}) async-start(bf16[8,9,16,128]{3,2,1,0:T(8,128)(2,1)} %drive.1), calls=%async_computation | async-start | bytes 589824 | tf_op jit(solution)/shard_map/all_to_all | solution.py:592
  18.9 4.3 %collective-permute-start.1 = (bf16[9,64,256]{2,1,0:T(8,128)(2,1)S(1)}, bf16[9,64,256]{2,1,0:T(8,128)(2,1)S(1)}, u32[]{:S(2)}, u32[]{:S(2)}) collective-permute-start(bf16[9,64,256]{2,1,0:T(8,128)(2,1)S(1)} %collective-permute-done.near.refs_0_), channel_id=1, source_target_pairs={{0,1},{1,0},{2,3},{3,2},{4,5},{5,4},{6,7},{7,6},{8,9},{9,8},{10,11... | collective-permute-start | bytes 884744 | tf_op jit(solution)/shard_map/ppermute | solution.py:581
  19.0 4.3 %copy-start = (bf16[3,3,256,64]{2,3,1,0:T(8,128)(2,1)S(1)}, bf16[3,3,256,64]{2,3,1,0:T(8,128)(2,1)}, u32[]{:S(2)}) copy-start(bf16[3,3,256,64]{2,3,1,0:T(8,128)(2,1)} %param.9) | copy-start | bytes 884740
  19.1 12.6 %collective-permute-start.3 = (bf16[9,64,256]{2,1,0:T(8,128)(2,1)S(1)}, bf16[9,64,256]{2,1,0:T(8,128)(2,1)S(1)}, u32[]{:S(2)}, u32[]{:S(2)}) collective-permute-start(bf16[9,64,256]{2,1,0:T(8,128)(2,1)S(1)} %hold.1), channel_id=1, source_target_pairs={{0,2},{1,7},{2,4},{3,1},{4,6},{5,3},{6,0},{7,5},{8,10},{9,15},{10,... | collective-permute-start | bytes 884744 | tf_op jit(solution)/shard_map/ppermute | solution.py:560
  19.2 11.0 %copy-start.3 = (f32[64]{0:T(128)S(1)}, f32[64]{0:T(128)}, u32[]{:S(2)}) copy-start(f32[64]{0:T(128)} %param.8) | copy-start | bytes 772
  19.2 19.9 %collective-permute-start.5 = (bf16[9,64,256]{2,1,0:T(8,128)(2,1)S(1)}, bf16[9,64,256]{2,1,0:T(8,128)(2,1)S(1)}, u32[]{:S(2)}, u32[]{:S(2)}) collective-permute-start(bf16[9,64,256]{2,1,0:T(8,128)(2,1)S(1)} %hold.1), channel_id=1, source_target_pairs={{0,4},{2,6},{4,0},{6,2},{1,5},{3,7},{5,1},{7,3},{8,12},{10,14},{12... | collective-permute-start | bytes 884744 | tf_op jit(solution)/shard_map/ppermute | solution.py:560
  31.7 7.5 %collective-permute-start.4 = (bf16[9,64,256]{2,1,0:T(8,128)(2,1)S(1)}, bf16[9,64,256]{2,1,0:T(8,128)(2,1)S(1)}, u32[]{:S(2)}, u32[]{:S(2)}) collective-permute-start(bf16[9,64,256]{2,1,0:T(8,128)(2,1)S(1)} %after.1.near), channel_id=1, source_target_pairs={{0,1},{1,0},{2,3},{3,2},{4,5},{5,4},{6,7},{7,6},{8,9},{9,8},{10,11... | collective-permute-start | bytes 884744 | tf_op jit(solution)/shard_map/ppermute | solution.py:581
  31.9 15.9 %all-to-all-start.1 = ((bf16[16,4,16,128]{3,2,1,0:T(8,128)(2,1)}), bf16[16,4,16,128]{3,2,1,0:T(8,128)(2,1)S(1)}, u32[]{:S(2)}, u32[]{:S(2)}) async-start(bf16[16,4,16,128]{3,2,1,0:T(8,128)(2,1)} %get-tuple-element.10), calls=%async_computation.1 | async-start | bytes 524288 | tf_op jit(solution)/shard_map/all_to_all | solution.py:597
  39.1 8.7 %copy-start.2 = (f32[256]{0:T(256)S(1)}, f32[256]{0:T(256)}, u32[]{:S(2)}) copy-start(f32[256]{0:T(256)} %param.11) | copy-start | bytes 3076
  39.1 8.7 %copy-start.4 = (f32[32]{0:T(128)S(1)}, f32[32]{0:T(128)}, u32[]{:S(2)}) copy-start(f32[32]{0:T(128)} %intervals_far.3) | copy-start | bytes 388

commit v8 on v7

--- a/solution.py
+++ b/solution.py
@@ -201,7 +201,7 @@
 
 
 def window_kernel(
-    place, own, near, swapped, far, frames,
+    place, own, near, swapped, far, frames, later,
     drives, token,
     weights, rows, written, load_sem, store_sem,
 ):
@@ -265,9 +265,8 @@
         store(chunk).wait()
 
 
-def relay_kernel(place, rates, received, token, message, done):
+def relay_kernel(place, rates, received, token, later, message):
     x, z = place[1], place[2]
-    done[...] = jnp.zeros_like(done)
     rate = doubled(rates[...])
     total = jnp.zeros((ROWS // 2, WIDE, LANES), F32)
     before = total
@@ -315,15 +314,16 @@
 
 
 def readout_kernel(
-    place, intervals_far, skip_gain, received, drives_far, weights, frames,
+    place, intervals_far, skip_gain, received, drives_far,
+    own, near, swapped, far, frames,
     result,
-    intervals, direct, drives, states, written, factors, state,
+    intervals, weights, direct, drives, states, written, factors, state,
     load_sem, drive_sem, store_sem, small_sem,
 ):
     small = [pltpu.make_async_copy(intervals_far, intervals, small_sem)]
     for copy in small:
         copy.start()
-    chan, x = place[0], place[1]
+    chan, x, first = place[0], place[1], place[3] == 0
 
     def load(chunk):
         part = pl.ds(chunk * OUT_STEP, OUT_STEP)
@@ -343,6 +343,7 @@
         arrive(chunk).start()
         load(chunk).start()
 
+    assemble(weights, own, near, swapped, far, first)
     low = low_half((WIDE, LANES))
     rates, entering = [], []
     for step in range(CHANS):
@@ -452,14 +453,14 @@
     )(intervals, rates, kernel_t, frames)
 
 
-def window(place, own, near, swapped, far, frames):
+def window(place, own, near, swapped, far, frames, later):
     return pl.pallas_call(
         window_kernel,
         out_shape=[
             jax.ShapeDtypeStruct((FRAMES, WINDOW, WIDE, CH), BF16),
             jax.ShapeDtypeStruct((8, LANES), F32),
         ],
-        in_specs=[in_smem()] + [in_vmem()] * CHANS + [anywhere()],
+        in_specs=[in_smem()] + [in_vmem()] * CHANS + [anywhere()] * 2,
         out_specs=[anywhere(), in_vmem()],
         scratch_shapes=[
             pltpu.VMEM((9, CHANS * OWN, CH), BF16),
@@ -471,68 +472,32 @@
         compiler_params=pltpu.CompilerParams(vmem_limit_bytes=52 << 20),
         cost_estimate=cost(1),
         name="window",
-    )(place, own, near, swapped, far, frames)
-
-
-def lay_kernel(place, own, near, swapped, far, result):
-    assemble(result, own, near, swapped, far, place[3] == 0)
-
-
-def lay(place, own, near, swapped, far):
+    )(place, own, near, swapped, far, frames, later)
+
+
+def relay(place, rates, received, token, later):
     return pl.pallas_call(
-        lay_kernel,
-        out_shape=jax.ShapeDtypeStruct((9, CHANS * OWN, CH), BF16),
-        in_specs=[in_smem()] + [in_vmem()] * CHANS,
+        relay_kernel,
+        out_shape=jax.ShapeDtypeStruct((XS * CHANS, WINDOW // 2 + 1, WIDE, LANES), BF16),
+        in_specs=[in_smem(), in_vmem(), in_vmem(), anywhere(), anywhere()],
         out_specs=in_vmem(),
         compiler_params=pltpu.CompilerParams(vmem_limit_bytes=16 << 20),
         cost_estimate=cost(1),
-        name="lay",
-    )(place, own, near, swapped, far)
-
-
-def hold_kernel(value, *refs):
-    result, sem = refs[-2:]
-    copy = pltpu.make_async_copy(value, result, sem)
-    copy.start()
-    copy.wait()
-
-
-def hold(value, others):
-    return pl.pallas_call(
-        hold_kernel,
-        out_shape=jax.ShapeDtypeStruct(value.shape, value.dtype),
-        in_specs=[anywhere()] * (1 + len(others)),
-        out_specs=anywhere(),
-        scratch_shapes=[pltpu.SemaphoreType.DMA],
-        compiler_params=pltpu.CompilerParams(vmem_limit_bytes=16 << 20),
-        cost_estimate=cost(1),
-        name="hold",
-    )(value, *others)
-
-
-def relay(place, rates, received, token):
-    return pl.pallas_call(
-        relay_kernel,
-        out_shape=[
-            jax.ShapeDtypeStruct((XS * CHANS, WINDOW // 2 + 1, WIDE, LANES), BF16),
-            jax.ShapeDtypeStruct((8, LANES), F32),
-        ],
-        in_specs=[in_smem(), in_vmem(), in_vmem(), anywhere()],
-        out_specs=[in_vmem()] * 2,
-        compiler_params=pltpu.CompilerParams(vmem_limit_bytes=16 << 20),
-        cost_estimate=cost(1),
         name="relay",
-    )(place, rates, received, token)
-
-
-def read_out(place, intervals, skip_gain, received, drives, weights, frames):
+    )(place, rates, received, token, later)
+
+
+def read_out(place, intervals, skip_gain, received, drives, kernels, frames):
     return pl.pallas_call(
         readout_kernel,
         out_shape=jax.ShapeDtypeStruct((FRAMES, CHANS, WIDE, CH), BF16),
-        in_specs=[in_smem(), anywhere(), in_vmem(), in_vmem(), anywhere(), in_vmem(), anywhere()],
+        in_specs=[in_smem(), anywhere(), in_vmem(), in_vmem(), anywhere()]
+        + [in_vmem()] * CHANS
+        + [anywhere()],
         out_specs=anywhere(),
         scratch_shapes=[
             pltpu.SMEM((FRAMES,), F32),
+            pltpu.VMEM((9, CHANS * OWN, CH), BF16),
             pltpu.VMEM((FRAMES, CHANS, WIDE, CH), BF16),
             pltpu.VMEM((FRAMES, WINDOW, WIDE, CH), BF16),
             pltpu.VMEM((FRAMES, WINDOW, WIDE, CH), BF16),
@@ -547,34 +512,16 @@
         compiler_params=pltpu.CompilerParams(vmem_limit_bytes=52 << 20),
         cost_estimate=cost(6),
         name="read_out",
-    )(place, intervals, skip_gain, received, drives, weights, frames)
-
-
-def around(value):
-    near = [
+    )(place, intervals, skip_gain, received, drives, *kernels, frames)
+
+
+def neighbour(value):
+    route = [
         (2 * c + core, 2 * ((c + step) % CHANS) + core)
         for c in range(CHANS)
         for core, step in ((0, 1), (1, CHANS - 1))
     ]
-    far = [(c, (c + 2) % CHANS) for c in range(CHANS)]
-    return lax.ppermute(value, ("chan", "clip"), near), lax.ppermute(value, "chan", far)
-
-
-def after_kernel(*refs):
-    del refs
-
-
-def after(value, other):
-    return pl.pallas_call(
-        after_kernel,
-        out_shape=jax.ShapeDtypeStruct(value.shape, value.dtype),
-        in_specs=[anywhere()] * 2,
-        out_specs=anywhere(),
-        input_output_aliases={0: 0},
-        compiler_params=pltpu.CompilerParams(vmem_limit_bytes=16 << 20),
-        cost_estimate=cost(0),
-        name="after",
-    )(value, other)
+    return lax.ppermute(value, ("chan", "clip"), route)
 
 
 def swap(value):
@@ -587,17 +534,16 @@
     rates = decay_rates.reshape(1, OWN)
     kernel_t = jnp.transpose(in_kernel.reshape(9, CH, OWN), (0, 2, 1))
     out_own = out_kernel.reshape(9, OWN, CH)
-    in_near, in_far = around(kernel_t)
+    near, out_near = neighbour(kernel_t), neighbour(out_own)
     message = drive(intervals, rates, kernel_t, frames)
     arrived = lax.all_to_all(message, "z", 0, 0)
-    out_near, out_far = around(hold(out_own, (in_near, in_far)))
-    drives, done = window(place, kernel_t, in_near, swap(in_near), in_far, frames)
-    onward, done = relay(place, rates, arrived, done)
-    out_near = after(out_near, done)
+    pieces = (kernel_t, near, swap(near), neighbour(near))
+    out_pieces = (out_own, out_near, swap(out_near), neighbour(out_near))
+    drives, done = window(place, *pieces, frames, out_pieces[2])
+    onward = relay(place, rates, arrived, done, out_pieces[3])
     received = lax.all_to_all(onward, ("x", "chan"), 0, 0)
-    weights = lay(place, out_own, out_near, swap(out_near), out_far)
     skip = skip_gain.reshape(1, CH)
-    return read_out(place, intervals, skip, received, drives, weights, frames)
+    return read_out(place, intervals, skip, received, drives, out_pieces, frames)
 
 
 def solution(mesh):

time: 54.4 us -> 53.2 us (0.978)
  blocking collectives: 0 us -> 12.7 us
  starting transfers between devices: 24 us -> 13.7 us
  waiting for transfers between devices: 7.99 us -> 5.85 us
  Pallas kernels: 21.8 us -> 20.5 us
    all_to_all x0 -> x1, blocking collectives: none -> 12.7 us  [local(): received = lax.all_to_all(onward, ('x', 'chan'), 0, 0)]
    all_to_all x1 -> x0, waiting for transfers between devices: 7.97 us -> none  [local(): received = lax.all_to_all(onward, ('x', 'chan'), 0, 0)]
    all_to_all x1 -> x0, starting transfers between devices: 7.24 us -> none  [local(): received = lax.all_to_all(onward, ('x', 'chan'), 0, 0)]
    ppermute x4, waiting for transfers between devices: 0.01 us -> 5.84 us  [neighbour(): return lax.ppermute(value, ('chan', 'clip'), route)]
    ppermute x4, starting transfers between devices: 8.01 us -> 4.66 us  [neighbour(): return lax.ppermute(value, ('chan', 'clip'), route)]
    pallas_call x4 -> x1, Pallas kernels: 2.2 us -> 0.77 us  [relay(): pl.pallas_call(relay_kernel, out_shape=jax.ShapeDtypeStruct((XS * CHANS,...]
  transfers between devices with their start and end apart: 8 -> 7, of which waited for: 1 -> 1; matrix products, arithmetic and copies ran while one was open for 0% -> 0% of each run, Pallas kernels for 29% -> 25%
where the time goes in v8:
time: 53.2 us; the launch traced here: 52.9 us
  Pallas kernels  20.5 us (39%)
  starting transfers between devices  13.7 us (26%)
  blocking collectives  12.7 us (24%)
  waiting for transfers between devices  5.85 us (11%)
    all_to_all x1, blocking collectives, local(): received = lax.all_to_all(onward, ('x', 'chan'), 0, 0)  12.7 us
    all_to_all x1, starting transfers between devices, local(): arrived = lax.all_to_all(message, 'z', 0, 0)  8.58 us
    pallas_call x1, Pallas kernels, window(): pl.pallas_call(window_kernel, out_shape=[jax.ShapeDtypeStruct((FRAMES, WI...  6.91 us
    pallas_call x1, Pallas kernels, drive(): pl.pallas_call(drive_kernel, out_shape=jax.ShapeDtypeStruct((ZS, ROWS //...  6.46 us
    pallas_call x1, Pallas kernels, read_out(): pl.pallas_call(readout_kernel, out_shape=jax.ShapeDtypeStruct((FRAMES, CH...  6.31 us
    ppermute x4, waiting for transfers between devices, neighbour(): return lax.ppermute(value, ('chan', 'clip'), route)  5.84 us
    ppermute x4, starting transfers between devices, neighbour(): return lax.ppermute(value, ('chan', 'clip'), route)  4.66 us
  transfers between devices with their start and end apart: 7, of which 1 were waited for; matrix products, arithmetic and copies ran while one was open for 0% of the time, Pallas kernels for 25%

profile of v8, /device:TPU:32, one launch (start us, length us, event | category | flops | bytes accessed | tf_op | source)
XLA Modules:
  0.0 52.9 jit_solution(3237642587038927306)
XLA Ops:
  0.0 1.6 %collective-permute-start = (bf16[9,64,256]{2,1,0:T(8,128)(2,1)}, bf16[9,64,256]{2,1,0:T(8,128)(2,1)S(1)}, u32[]{:S(2)}, u32[]{:S(2)}) collective-permute-start(bf16[9,64,256]{2,1,0:T(8,128)(2,1)} %bitcast.10), channel_id=1, source_target_pairs={{0,2},{1,7},{2,4},{3,1},{4,6},{5,3},{6,0},{7,5},{8,10},{9,15},{10,... | collective-permute-start | bytes 884744 | tf_op jit(solution)/shard_map/ppermute | solution.py:524
  1.6 1.6 %collective-permute-start.3 = (bf16[9,64,256]{2,1,0:T(8,128)(2,1)}, bf16[9,64,256]{2,1,0:T(8,128)(2,1)S(1)}, u32[]{:S(2)}, u32[]{:S(2)}) collective-permute-start(bf16[9,64,256]{2,1,0:T(8,128)(2,1)} %bitcast.13), channel_id=1, source_target_pairs={{0,2},{1,7},{2,4},{3,1},{4,6},{5,3},{6,0},{7,5},{8,10},{9,15},{10,... | collective-permute-start | bytes 884744 | tf_op jit(solution)/shard_map/ppermute | solution.py:524
  3.2 0.0 copy-start
  3.2 6.5 %drive.1 = bf16[8,9,16,128]{3,2,1,0:T(8,128)(2,1)} custom-call(f32[32]{0:T(128)} %intervals_far.3, f32[1,64]{1,0:T(1,128)} %bitcast.16, bf16[9,64,256]{2,1,0:T(8,128)(2,1)} %bitcast.11, bf16[32,16,16,256]{3,2,1,0:T(8,128)(2,1)} %frames.5), custom_call_target="tpu_custom_call" | custom-call | flops 8800000000 | bytes 1048576 | tf_op jit(solution)/shard_map/drive/pallas_call | solution.py:434
  9.6 0.0 copy-start.3
  9.6 8.6 %all-to-all-start = ((bf16[8,9,16,128]{3,2,1,0:T(8,128)(2,1)}), bf16[8,9,16,128]{3,2,1,0:T(8,128)(2,1)S(1)}, u32[]{:S(2)}, u32[]{:S(2)}) async-start(bf16[8,9,16,128]{3,2,1,0:T(8,128)(2,1)} %drive.1), calls=%async_computation | async-start | bytes 589824 | tf_op jit(solution)/shard_map/all_to_all | solution.py:539
  18.2 0.0 collective-permute-done.near
  18.2 1.3 %collective-permute-start.2 = (bf16[9,64,256]{2,1,0:T(8,128)(2,1)S(1)}, bf16[9,64,256]{2,1,0:T(8,128)(2,1)S(1)}, u32[]{:S(2)}, u32[]{:S(2)}) collective-permute-start(bf16[9,64,256]{2,1,0:T(8,128)(2,1)S(1)} %collective-permute-done.near), channel_id=1, source_target_pairs={{0,2},{1,7},{2,4},{3,1},{4,6},{5,3},{6,0},{7,5},{8,10},{9,15},{10,... | collective-permute-start | bytes 884744 | tf_op jit(solution)/shard_map/ppermute | solution.py:524
  19.5 0.0 collective-permute-start.1
  19.5 0.0 collective-permute-done.3.near
  19.5 0.5 collective-permute-start.4
  20.0 0.2 collective-permute-start.5
  20.2 0.1 pad_add_fusion.place
  20.3 0.0 copy-start.1
  20.3 0.0 copy-start.2
  20.3 0.0 copy-start.4
  20.3 5.8 %collective-permute-done.2.far = bf16[9,64,256]{2,1,0:T(8,128)(2,1)S(1)} collective-permute-done((bf16[9,64,256]{2,1,0:T(8,128)(2,1)S(1)}, bf16[9,64,256]{2,1,0:T(8,128)(2,1)S(1)}, u32[]{:S(2)}, u32[]{:S(2)}) %collective-permute-start.2) | collective-permute-done | bytes 294944 | tf_op jit(solution)/shard_map/ppermute | solution.py:524
  26.2 0.0 collective-permute-done.1.swapped
  26.2 0.0 collective-permute-done.4.later.swapped
  26.2 0.0 copy-done
  26.2 6.9 %window.1 = (bf16[32,6,16,256]{3,2,1,0:T(8,128)(2,1)}, f32[8,128]{1,0:T(8,128)S(1)}) custom-call(s32[4]{0:T(128)S(1)} %pad_add_fusion.place, bf16[9,64,256]{2,1,0:T(8,128)(2,1)S(1)} %bitcast.12, bf16[9,64,256]{2,1,0:T(8,128)(2,1)S(1)} %collective-permute-done.near, bf16[9,64,256]{2,1,0:T(8,128)(2,1)S(1)} %collective-permute-done.1.swapped, ...), custom_call_target="tpu_custom_call" | custom-call | flops 1100000000 | bytes 1048576 | tf_op jit(solution)/shard_map/window/pallas_call | solution.py:457
  33.1 0.0 all-to-all-done.received
  33.1 0.0 collective-permute-done.5.later.far
  33.1 0.0 copy-done.3
  33.1 0.8 %relay.1 = bf16[16,4,16,128]{3,2,1,0:T(8,128)(2,1)S(1)} custom-call(s32[4]{0:T(128)S(1)} %pad_add_fusion.place, f32[1,64]{1,0:T(1,128)S(1)} %bitcast.17, bf16[8,9,16,128]{3,2,1,0:T(8,128)(2,1)S(1)} %all-to-all-done.received, f32[8,128]{1,0:T(8,128)S(1)} %get-tuple-element.7.token, bf16[9,64,256]{2,1,0:T(8,128)(2,1)S(1)} %collective-permute-done.5.later.far), custom_call_target="tpu_custom_call" | custom-call | flops 1100000000 | bytes 1048576 | tf_op jit(solution)/shard_map/relay/pallas_call | solution.py:479
  33.9 12.7 %all_to_all.10.received = bf16[16,4,16,128]{3,2,1,0:T(8,128)(2,1)S(1)} all-to-all(bf16[16,4,16,128]{3,2,1,0:T(8,128)(2,1)S(1)} %relay.1), channel_id=1, replica_groups=mesh['x'=4,'z'=8,'chan'=4,'clip'=2] {'x','chan'}, dimensions={0} | all-to-all | bytes 524288 | tf_op jit(solution)/shard_map/all_to_all | solution.py:544
  46.6 0.0 copy-done.1
  46.6 0.0 copy-done.2
  46.6 0.0 copy-done.4
  46.6 6.3 %read_out.1 = bf16[32,4,16,256]{3,2,1,0:T(8,128)(2,1)} custom-call(s32[4]{0:T(128)S(1)} %pad_add_fusion.place, f32[32]{0:T(128)S(1)} %copy-done.4, f32[1,256]{1,0:T(1,128)S(1)} %bitcast.15, bf16[16,4,16,128]{3,2,1,0:T(8,128)(2,1)S(1)} %all_to_all.10.received, bf16[32,6,16,256]{3,2,1,0:T(8,128)(2,1)} %get-tuple-element.8.drives_far, ...), custom_call_target="tpu_custom_call" | custom-call | flops 6600000000 | bytes 1048576 | tf_op jit(solution)/shard_map/read_out/pallas_call | solution.py:491
Async XLA Ops:
  0.0 18.2 %collective-permute-start = (bf16[9,64,256]{2,1,0:T(8,128)(2,1)}, bf16[9,64,256]{2,1,0:T(8,128)(2,1)S(1)}, u32[]{:S(2)}, u32[]{:S(2)}) collective-permute-start(bf16[9,64,256]{2,1,0:T(8,128)(2,1)} %bitcast.10), channel_id=1, source_target_pairs={{0,2},{1,7},{2,4},{3,1},{4,6},{5,3},{6,0},{7,5},{8,10},{9,15},{10,... | collective-permute-start | bytes 884744 | tf_op jit(solution)/shard_map/ppermute | solution.py:524
  1.6 17.9 %collective-permute-start.3 = (bf16[9,64,256]{2,1,0:T(8,128)(2,1)}, bf16[9,64,256]{2,1,0:T(8,128)(2,1)S(1)}, u32[]{:S(2)}, u32[]{:S(2)}) collective-permute-start(bf16[9,64,256]{2,1,0:T(8,128)(2,1)} %bitcast.13), channel_id=1, source_target_pairs={{0,2},{1,7},{2,4},{3,1},{4,6},{5,3},{6,0},{7,5},{8,10},{9,15},{10,... | collective-permute-start | bytes 884744 | tf_op jit(solution)/shard_map/ppermute | solution.py:524
  3.2 23.0 %copy-start = (bf16[3,3,256,64]{2,3,1,0:T(8,128)(2,1)S(1)}, bf16[3,3,256,64]{2,3,1,0:T(8,128)(2,1)}, u32[]{:S(2)}) copy-start(bf16[3,3,256,64]{2,3,1,0:T(8,128)(2,1)} %param.9) | copy-start | bytes 884740
  9.6 23.5 %copy-start.3 = (f32[64]{0:T(128)S(1)}, f32[64]{0:T(128)}, u32[]{:S(2)}) copy-start(f32[64]{0:T(128)} %param.8) | copy-start | bytes 772
  9.6 23.5 %all-to-all-start = ((bf16[8,9,16,128]{3,2,1,0:T(8,128)(2,1)}), bf16[8,9,16,128]{3,2,1,0:T(8,128)(2,1)S(1)}, u32[]{:S(2)}, u32[]{:S(2)}) async-start(bf16[8,9,16,128]{3,2,1,0:T(8,128)(2,1)} %drive.1), calls=%async_computation | async-start | bytes 589824 | tf_op jit(solution)/shard_map/all_to_all | solution.py:539
  18.2 7.9 %collective-permute-start.2 = (bf16[9,64,256]{2,1,0:T(8,128)(2,1)S(1)}, bf16[9,64,256]{2,1,0:T(8,128)(2,1)S(1)}, u32[]{:S(2)}, u32[]{:S(2)}) collective-permute-start(bf16[9,64,256]{2,1,0:T(8,128)(2,1)S(1)} %collective-permute-done.near), channel_id=1, source_target_pairs={{0,2},{1,7},{2,4},{3,1},{4,6},{5,3},{6,0},{7,5},{8,10},{9,15},{10,... | collective-permute-start | bytes 884744 | tf_op jit(solution)/shard_map/ppermute | solution.py:524
  19.5 6.7 %collective-permute-start.1 = (bf16[9,64,256]{2,1,0:T(8,128)(2,1)S(1)}, bf16[9,64,256]{2,1,0:T(8,128)(2,1)S(1)}, u32[]{:S(2)}, u32[]{:S(2)}) collective-permute-start(bf16[9,64,256]{2,1,0:T(8,128)(2,1)S(1)} %collective-permute-done.near), channel_id=1, source_target_pairs={{0,1},{1,0},{2,3},{3,2},{4,5},{5,4},{6,7},{7,6},{8,9},{9,8},{10,11... | collective-permute-start | bytes 884744 | tf_op jit(solution)/shard_map/ppermute | solution.py:528
  19.5 6.7 %collective-permute-start.4 = (bf16[9,64,256]{2,1,0:T(8,128)(2,1)S(1)}, bf16[9,64,256]{2,1,0:T(8,128)(2,1)S(1)}, u32[]{:S(2)}, u32[]{:S(2)}) collective-permute-start(bf16[9,64,256]{2,1,0:T(8,128)(2,1)S(1)} %collective-permute-done.3.near), channel_id=1, source_target_pairs={{0,1},{1,0},{2,3},{3,2},{4,5},{5,4},{6,7},{7,6},{8,9},{9,8},{10,11... | collective-permute-start | bytes 884744 | tf_op jit(solution)/shard_map/ppermute | solution.py:528
  20.0 13.1 %collective-permute-start.5 = (bf16[9,64,256]{2,1,0:T(8,128)(2,1)S(1)}, bf16[9,64,256]{2,1,0:T(8,128)(2,1)S(1)}, u32[]{:S(2)}, u32[]{:S(2)}) collective-permute-start(bf16[9,64,256]{2,1,0:T(8,128)(2,1)S(1)} %collective-permute-done.3.near), channel_id=1, source_target_pairs={{0,2},{1,7},{2,4},{3,1},{4,6},{5,3},{6,0},{7,5},{8,10},{9,15},{10,... | collective-permute-start | bytes 884744 | tf_op jit(solution)/shard_map/ppermute | solution.py:524
  20.3 26.2 %copy-start.1 = (bf16[3,3,64,256]{3,2,1,0:T(8,128)(2,1)S(1)}, bf16[3,3,64,256]{3,2,1,0:T(8,128)(2,1)}, u32[]{:S(2)}) copy-start(bf16[3,3,64,256]{3,2,1,0:T(8,128)(2,1)} %param.10) | copy-start | bytes 884740
  20.3 26.2 %copy-start.2 = (f32[256]{0:T(256)S(1)}, f32[256]{0:T(256)}, u32[]{:S(2)}) copy-start(f32[256]{0:T(256)} %param.11) | copy-start | bytes 3076
  20.3 26.2 %copy-start.4 = (f32[32]{0:T(128)S(1)}, f32[32]{0:T(128)}, u32[]{:S(2)}) copy-start(f32[32]{0:T(128)} %intervals_far.3) | copy-start | bytes 388

commit v9 on v8

--- a/solution.py
+++ b/solution.py
@@ -265,7 +265,7 @@
         store(chunk).wait()
 
 
-def relay_kernel(place, rates, received, token, later, message):
+def relay_kernel(place, rates, received, token, message):
     x, z = place[1], place[2]
     rate = doubled(rates[...])
     total = jnp.zeros((ROWS // 2, WIDE, LANES), F32)
@@ -475,16 +475,16 @@
     )(place, own, near, swapped, far, frames, later)
 
 
-def relay(place, rates, received, token, later):
+def relay(place, rates, received, token):
     return pl.pallas_call(
         relay_kernel,
         out_shape=jax.ShapeDtypeStruct((XS * CHANS, WINDOW // 2 + 1, WIDE, LANES), BF16),
-        in_specs=[in_smem(), in_vmem(), in_vmem(), anywhere(), anywhere()],
+        in_specs=[in_smem(), in_vmem(), in_vmem(), anywhere()],
         out_specs=in_vmem(),
         compiler_params=pltpu.CompilerParams(vmem_limit_bytes=16 << 20),
         cost_estimate=cost(1),
         name="relay",
-    )(place, rates, received, token, later)
+    )(place, rates, received, token)
 
 
 def read_out(place, intervals, skip_gain, received, drives, kernels, frames):
@@ -524,6 +524,23 @@
     return lax.ppermute(value, ("chan", "clip"), route)
 
 
+def after_kernel(*refs):
+    del refs
+
+
+def after(value, other):
+    return pl.pallas_call(
+        after_kernel,
+        out_shape=jax.ShapeDtypeStruct(value.shape, value.dtype),
+        in_specs=[anywhere()] * 2,
+        out_specs=anywhere(),
+        input_output_aliases={0: 0},
+        compiler_params=pltpu.CompilerParams(vmem_limit_bytes=16 << 20),
+        cost_estimate=cost(0),
+        name="after",
+    )(value, other)
+
+
 def swap(value):
     return lax.ppermute(value, "clip", [(0, 1), (1, 0)])
 
@@ -538,9 +555,12 @@
     message = drive(intervals, rates, kernel_t, frames)
     arrived = lax.all_to_all(message, "z", 0, 0)
     pieces = (kernel_t, near, swap(near), neighbour(near))
-    out_pieces = (out_own, out_near, swap(out_near), neighbour(out_near))
+    out_swapped = swap(out_near)
+    out_near = after(out_near, pieces[3])
+    out_far = neighbour(out_near)
+    out_pieces = (out_own, out_near, out_swapped, out_far)
     drives, done = window(place, *pieces, frames, out_pieces[2])
-    onward = relay(place, rates, arrived, done, out_pieces[3])
+    onward = relay(place, rates, arrived, done)
     received = lax.all_to_all(onward, ("x", "chan"), 0, 0)
     skip = skip_gain.reshape(1, CH)
     return read_out(place, intervals, skip, received, drives, out_pieces, frames)

time: 53.2 us -> 55.9 us (1.051)
  blocking collectives: 12.7 us -> 15.3 us
    all_to_all x1, blocking collectives: 12.7 us -> 15.3 us  [local(): received = lax.all_to_all(onward, ('x', 'chan'), 0, 0)]
where the time goes in v9:
time: 55.9 us; the launch traced here: 55.7 us
  Pallas kernels  20.4 us (36%)
  blocking collectives  15.3 us (27%)
  starting transfers between devices  13.7 us (25%)
  waiting for transfers between devices  6.07 us (11%)
    all_to_all x1, blocking collectives, local(): received = lax.all_to_all(onward, ('x', 'chan'), 0, 0)  15.3 us
    all_to_all x1, starting transfers between devices, local(): arrived = lax.all_to_all(message, 'z', 0, 0)  8.58 us
    pallas_call x1, Pallas kernels, window(): pl.pallas_call(window_kernel, out_shape=[jax.ShapeDtypeStruct((FRAMES, WI...  6.91 us
    pallas_call x1, Pallas kernels, drive(): pl.pallas_call(drive_kernel, out_shape=jax.ShapeDtypeStruct((ZS, ROWS //...  6.46 us
    pallas_call x1, Pallas kernels, read_out(): pl.pallas_call(readout_kernel, out_shape=jax.ShapeDtypeStruct((FRAMES, CH...  6.31 us
    ppermute x4, waiting for transfers between devices, neighbour(): return lax.ppermute(value, ('chan', 'clip'), route)  6.07 us
    ppermute x4, starting transfers between devices, neighbour(): return lax.ppermute(value, ('chan', 'clip'), route)  4.59 us
  transfers between devices with their start and end apart: 7, of which 1 were waited for; matrix products, arithmetic and copies ran while one was open for 0% of the time, Pallas kernels for 25%

profile of v9, /device:TPU:32, one launch (start us, length us, event | category | flops | bytes accessed | tf_op | source)
XLA Modules:
  0.0 55.7 jit_solution(3686389854705619368)
XLA Ops:
  0.0 1.6 %collective-permute-start = (bf16[9,64,256]{2,1,0:T(8,128)(2,1)}, bf16[9,64,256]{2,1,0:T(8,128)(2,1)S(1)}, u32[]{:S(2)}, u32[]{:S(2)}) collective-permute-start(bf16[9,64,256]{2,1,0:T(8,128)(2,1)} %bitcast.10), channel_id=1, source_target_pairs={{0,2},{1,7},{2,4},{3,1},{4,6},{5,3},{6,0},{7,5},{8,10},{9,15},{10,... | collective-permute-start | bytes 884744 | tf_op jit(solution)/shard_map/ppermute | solution.py:524
  1.6 1.6 %collective-permute-start.3 = (bf16[9,64,256]{2,1,0:T(8,128)(2,1)}, bf16[9,64,256]{2,1,0:T(8,128)(2,1)S(1)}, u32[]{:S(2)}, u32[]{:S(2)}) collective-permute-start(bf16[9,64,256]{2,1,0:T(8,128)(2,1)} %bitcast.13), channel_id=1, source_target_pairs={{0,2},{1,7},{2,4},{3,1},{4,6},{5,3},{6,0},{7,5},{8,10},{9,15},{10,... | collective-permute-start | bytes 884744 | tf_op jit(solution)/shard_map/ppermute | solution.py:524
  3.2 0.0 copy-start
  3.2 6.5 %drive.1 = bf16[8,9,16,128]{3,2,1,0:T(8,128)(2,1)} custom-call(f32[32]{0:T(128)} %intervals_far.3, f32[1,64]{1,0:T(1,128)} %bitcast.16, bf16[9,64,256]{2,1,0:T(8,128)(2,1)} %bitcast.11, bf16[32,16,16,256]{3,2,1,0:T(8,128)(2,1)} %frames.5), custom_call_target="tpu_custom_call" | custom-call | flops 8800000000 | bytes 1048576 | tf_op jit(solution)/shard_map/drive/pallas_call | solution.py:434
  9.6 0.0 copy-start.3
  9.6 8.6 %all-to-all-start = ((bf16[8,9,16,128]{3,2,1,0:T(8,128)(2,1)}), bf16[8,9,16,128]{3,2,1,0:T(8,128)(2,1)S(1)}, u32[]{:S(2)}, u32[]{:S(2)}) async-start(bf16[8,9,16,128]{3,2,1,0:T(8,128)(2,1)} %drive.1), calls=%async_computation | async-start | bytes 589824 | tf_op jit(solution)/shard_map/all_to_all | solution.py:556
  18.2 0.0 collective-permute-done.near
  18.2 1.3 %collective-permute-start.2 = (bf16[9,64,256]{2,1,0:T(8,128)(2,1)S(1)}, bf16[9,64,256]{2,1,0:T(8,128)(2,1)S(1)}, u32[]{:S(2)}, u32[]{:S(2)}) collective-permute-start(bf16[9,64,256]{2,1,0:T(8,128)(2,1)S(1)} %collective-permute-done.near), channel_id=1, source_target_pairs={{0,2},{1,7},{2,4},{3,1},{4,6},{5,3},{6,0},{7,5},{8,10},{9,15},{10,... | collective-permute-start | bytes 884744 | tf_op jit(solution)/shard_map/ppermute | solution.py:524
  19.5 0.0 collective-permute-done.3.refs_0_
  19.5 0.0 collective-permute-start.4
  19.5 0.5 collective-permute-start.1
  20.0 0.1 pad_add_fusion.place
  20.1 6.1 %collective-permute-done.2.far.refs_1_ = bf16[9,64,256]{2,1,0:T(8,128)(2,1)S(1)} collective-permute-done((bf16[9,64,256]{2,1,0:T(8,128)(2,1)S(1)}, bf16[9,64,256]{2,1,0:T(8,128)(2,1)S(1)}, u32[]{:S(2)}, u32[]{:S(2)}) %collective-permute-start.2) | collective-permute-done | bytes 294944 | tf_op jit(solution)/shard_map/ppermute | solution.py:524
  26.2 0.0 collective-permute-done.4.later.swapped
  26.2 0.0 copy-start.1
  26.2 0.0 copy-start.2
  26.2 0.0 copy-start.4
  26.2 0.1 collective-permute-start.5
  26.3 0.0 collective-permute-done.1.swapped
  26.3 0.0 copy-done
  26.3 6.9 %window.1 = (bf16[32,6,16,256]{3,2,1,0:T(8,128)(2,1)}, f32[8,128]{1,0:T(8,128)S(1)}) custom-call(s32[4]{0:T(128)S(1)} %pad_add_fusion.place, bf16[9,64,256]{2,1,0:T(8,128)(2,1)S(1)} %bitcast.12, bf16[9,64,256]{2,1,0:T(8,128)(2,1)S(1)} %collective-permute-done.near, bf16[9,64,256]{2,1,0:T(8,128)(2,1)S(1)} %collective-permute-done.1.swapped, ...), custom_call_target="tpu_custom_call" | custom-call | flops 1100000000 | bytes 1048576 | tf_op jit(solution)/shard_map/window/pallas_call | solution.py:457
  33.3 0.0 all-to-all-done.received
  33.3 0.0 copy-done.3
  33.3 0.8 %relay.1 = bf16[16,4,16,128]{3,2,1,0:T(8,128)(2,1)S(1)} custom-call(s32[4]{0:T(128)S(1)} %pad_add_fusion.place, f32[1,64]{1,0:T(1,128)S(1)} %bitcast.17, bf16[8,9,16,128]{3,2,1,0:T(8,128)(2,1)S(1)} %all-to-all-done.received, f32[8,128]{1,0:T(8,128)S(1)} %get-tuple-element.7.token), custom_call_target="tpu_custom_call" | custom-call | flops 1100000000 | bytes 1048576 | tf_op jit(solution)/shard_map/relay/pallas_call | solution.py:479
  34.0 15.3 %all_to_all.10.received = bf16[16,4,16,128]{3,2,1,0:T(8,128)(2,1)S(1)} all-to-all(bf16[16,4,16,128]{3,2,1,0:T(8,128)(2,1)S(1)} %relay.1), channel_id=1, replica_groups=mesh['x'=4,'z'=8,'chan'=4,'clip'=2] {'x','chan'}, dimensions={0} | all-to-all | bytes 524288 | tf_op jit(solution)/shard_map/all_to_all | solution.py:564
  49.3 0.0 collective-permute-done.5.far
  49.3 0.0 copy-done.1
  49.3 0.0 copy-done.2
  49.3 0.0 copy-done.4
  49.3 6.3 %read_out.1 = bf16[32,4,16,256]{3,2,1,0:T(8,128)(2,1)} custom-call(s32[4]{0:T(128)S(1)} %pad_add_fusion.place, f32[32]{0:T(128)S(1)} %copy-done.4, f32[1,256]{1,0:T(1,128)S(1)} %bitcast.15, bf16[16,4,16,128]{3,2,1,0:T(8,128)(2,1)S(1)} %all_to_all.10.received, bf16[32,6,16,256]{3,2,1,0:T(8,128)(2,1)} %get-tuple-element.8.drives_far, ...), custom_call_target="tpu_custom_call" | custom-call | flops 6600000000 | bytes 1048576 | tf_op jit(solution)/shard_map/read_out/pallas_call | solution.py:491
  (1 shorter events, 0.0 us)
Async XLA Ops:
  0.0 18.2 %collective-permute-start = (bf16[9,64,256]{2,1,0:T(8,128)(2,1)}, bf16[9,64,256]{2,1,0:T(8,128)(2,1)S(1)}, u32[]{:S(2)}, u32[]{:S(2)}) collective-permute-start(bf16[9,64,256]{2,1,0:T(8,128)(2,1)} %bitcast.10), channel_id=1, source_target_pairs={{0,2},{1,7},{2,4},{3,1},{4,6},{5,3},{6,0},{7,5},{8,10},{9,15},{10,... | collective-permute-start | bytes 884744 | tf_op jit(solution)/shard_map/ppermute | solution.py:524
  1.6 17.9 %collective-permute-start.3 = (bf16[9,64,256]{2,1,0:T(8,128)(2,1)}, bf16[9,64,256]{2,1,0:T(8,128)(2,1)S(1)}, u32[]{:S(2)}, u32[]{:S(2)}) collective-permute-start(bf16[9,64,256]{2,1,0:T(8,128)(2,1)} %bitcast.13), channel_id=1, source_target_pairs={{0,2},{1,7},{2,4},{3,1},{4,6},{5,3},{6,0},{7,5},{8,10},{9,15},{10,... | collective-permute-start | bytes 884744 | tf_op jit(solution)/shard_map/ppermute | solution.py:524
  3.2 23.2 %copy-start = (bf16[3,3,256,64]{2,3,1,0:T(8,128)(2,1)S(1)}, bf16[3,3,256,64]{2,3,1,0:T(8,128)(2,1)}, u32[]{:S(2)}) copy-start(bf16[3,3,256,64]{2,3,1,0:T(8,128)(2,1)} %param.9) | copy-start | bytes 884740
  9.6 23.6 %copy-start.3 = (f32[64]{0:T(128)S(1)}, f32[64]{0:T(128)}, u32[]{:S(2)}) copy-start(f32[64]{0:T(128)} %param.8) | copy-start | bytes 772
  9.6 23.6 %all-to-all-start = ((bf16[8,9,16,128]{3,2,1,0:T(8,128)(2,1)}), bf16[8,9,16,128]{3,2,1,0:T(8,128)(2,1)S(1)}, u32[]{:S(2)}, u32[]{:S(2)}) async-start(bf16[8,9,16,128]{3,2,1,0:T(8,128)(2,1)} %drive.1), calls=%async_computation | async-start | bytes 589824 | tf_op jit(solution)/shard_map/all_to_all | solution.py:556
  18.2 7.9 %collective-permute-start.2 = (bf16[9,64,256]{2,1,0:T(8,128)(2,1)S(1)}, bf16[9,64,256]{2,1,0:T(8,128)(2,1)S(1)}, u32[]{:S(2)}, u32[]{:S(2)}) collective-permute-start(bf16[9,64,256]{2,1,0:T(8,128)(2,1)S(1)} %collective-permute-done.near), channel_id=1, source_target_pairs={{0,2},{1,7},{2,4},{3,1},{4,6},{5,3},{6,0},{7,5},{8,10},{9,15},{10,... | collective-permute-start | bytes 884744 | tf_op jit(solution)/shard_map/ppermute | solution.py:524
  19.5 6.7 %collective-permute-start.4 = (bf16[9,64,256]{2,1,0:T(8,128)(2,1)S(1)}, bf16[9,64,256]{2,1,0:T(8,128)(2,1)S(1)}, u32[]{:S(2)}, u32[]{:S(2)}) collective-permute-start(bf16[9,64,256]{2,1,0:T(8,128)(2,1)S(1)} %collective-permute-done.3.refs_0_), channel_id=1, source_target_pairs={{0,1},{1,0},{2,3},{3,2},{4,5},{5,4},{6,7},{7,6},{8,9},{9,8},{10,11... | collective-permute-start | bytes 884744 | tf_op jit(solution)/shard_map/ppermute | solution.py:545
  19.5 6.8 %collective-permute-start.1 = (bf16[9,64,256]{2,1,0:T(8,128)(2,1)S(1)}, bf16[9,64,256]{2,1,0:T(8,128)(2,1)S(1)}, u32[]{:S(2)}, u32[]{:S(2)}) collective-permute-start(bf16[9,64,256]{2,1,0:T(8,128)(2,1)S(1)} %collective-permute-done.near), channel_id=1, source_target_pairs={{0,1},{1,0},{2,3},{3,2},{4,5},{5,4},{6,7},{7,6},{8,9},{9,8},{10,11... | collective-permute-start | bytes 884744 | tf_op jit(solution)/shard_map/ppermute | solution.py:545
  26.2 23.2 %copy-start.1 = (bf16[3,3,64,256]{3,2,1,0:T(8,128)(2,1)S(1)}, bf16[3,3,64,256]{3,2,1,0:T(8,128)(2,1)}, u32[]{:S(2)}) copy-start(bf16[3,3,64,256]{3,2,1,0:T(8,128)(2,1)} %param.10) | copy-start | bytes 884740
  26.2 23.2 %copy-start.2 = (f32[256]{0:T(256)S(1)}, f32[256]{0:T(256)}, u32[]{:S(2)}) copy-start(f32[256]{0:T(256)} %param.11) | copy-start | bytes 3076
  26.2 23.2 %copy-start.4 = (f32[32]{0:T(128)S(1)}, f32[32]{0:T(128)}, u32[]{:S(2)}) copy-start(f32[32]{0:T(128)} %intervals_far.3) | copy-start | bytes 388
  26.2 23.1 %collective-permute-start.5 = (bf16[9,64,256]{2,1,0:T(8,128)(2,1)S(1)}, bf16[9,64,256]{2,1,0:T(8,128)(2,1)S(1)}, u32[]{:S(2)}, u32[]{:S(2)}) collective-permute-start(bf16[9,64,256]{2,1,0:T(8,128)(2,1)S(1)} %after.1.near), channel_id=1, source_target_pairs={{0,2},{1,7},{2,4},{3,1},{4,6},{5,3},{6,0},{7,5},{8,10},{9,15},{10,... | collective-permute-start | bytes 884744 | tf_op jit(solution)/shard_map/ppermute | solution.py:524

commit v10 on v8

--- a/solution.py
+++ b/solution.py
@@ -524,6 +524,27 @@
     return lax.ppermute(value, ("chan", "clip"), route)
 
 
+def opposite(value):
+    return lax.ppermute(value, "chan", [(c, (c + 2) % CHANS) for c in range(CHANS)])
+
+
+def after_kernel(*refs):
+    del refs
+
+
+def after(value, other, length=2):
+    return pl.pallas_call(
+        after_kernel,
+        out_shape=jax.ShapeDtypeStruct(value.shape, value.dtype),
+        in_specs=[anywhere()] * 2,
+        out_specs=anywhere(),
+        input_output_aliases={0: 0},
+        compiler_params=pltpu.CompilerParams(vmem_limit_bytes=16 << 20),
+        cost_estimate=cost(length),
+        name="after",
+    )(value, other)
+
+
 def swap(value):
     return lax.ppermute(value, "clip", [(0, 1), (1, 0)])
 
@@ -537,9 +558,11 @@
     near, out_near = neighbour(kernel_t), neighbour(out_own)
     message = drive(intervals, rates, kernel_t, frames)
     arrived = lax.all_to_all(message, "z", 0, 0)
-    pieces = (kernel_t, near, swap(near), neighbour(near))
-    out_pieces = (out_own, out_near, swap(out_near), neighbour(out_near))
-    drives, done = window(place, *pieces, frames, out_pieces[2])
+    pieces = (kernel_t, near, swap(near), after(opposite(kernel_t), near))
+    out_swapped, out_far = swap(out_near), opposite(out_own)
+    drives, done = window(place, *pieces, frames, out_swapped)
+    out_far = after(out_far, done, 2)
+    out_pieces = (out_own, out_near, out_swapped, out_far)
     onward = relay(place, rates, arrived, done, out_pieces[3])
     received = lax.all_to_all(onward, ("x", "chan"), 0, 0)
     skip = skip_gain.reshape(1, CH)

time: 53.2 us -> 55.2 us (1.038)
  waiting for transfers between devices: 5.85 us -> 3.24 us
  starting transfers between devices: 13.7 us -> 16.2 us
  blocking collectives: 12.7 us -> 15 us
    ppermute x4 -> x2, waiting for transfers between devices: 5.84 us -> 0.7 us  [neighbour(): return lax.ppermute(value, ('chan', 'clip'), route)]
    ppermute x0 -> x2, starting transfers between devices: none -> 5.03 us  [opposite(): lax.ppermute(value, 'chan', [(c, (c + 2) % CHANS) for c in range(CHANS)])]
    ppermute x4 -> x2, starting transfers between devices: 4.66 us -> 2.25 us  [neighbour(): return lax.ppermute(value, ('chan', 'clip'), route)]
    all_to_all x1, blocking collectives: 12.7 us -> 15 us  [local(): received = lax.all_to_all(onward, ('x', 'chan'), 0, 0)]
    ppermute x2, waiting for transfers between devices: 0.01 us -> 1.3 us  [swap(): return lax.ppermute(value, 'clip', [(0, 1), (1, 0)])]
    all_to_all x1, waiting for transfers between devices: 0.01 us -> 1.24 us  [local(): arrived = lax.all_to_all(message, 'z', 0, 0)]
  transfers between devices with their start and end apart: 7 -> 7, of which waited for: 1 -> 4; matrix products, arithmetic and copies ran while one was open for 0% -> 0% of each run, Pallas kernels for 25% -> 24%
where the time goes in v10:
time: 55.2 us; the launch traced here: 54.9 us
  Pallas kernels  20.3 us (37%)
  starting transfers between devices  16.2 us (29%)
  blocking collectives  15 us (27%)
  waiting for transfers between devices  3.24 us (6%)
    all_to_all x1, blocking collectives, local(): received = lax.all_to_all(onward, ('x', 'chan'), 0, 0)  15 us
    all_to_all x1, starting transfers between devices, local(): arrived = lax.all_to_all(message, 'z', 0, 0)  8.58 us
    pallas_call x1, Pallas kernels, window(): pl.pallas_call(window_kernel, out_shape=[jax.ShapeDtypeStruct((FRAMES, WI...  6.9 us
    pallas_call x1, Pallas kernels, drive(): pl.pallas_call(drive_kernel, out_shape=jax.ShapeDtypeStruct((ZS, ROWS //...  6.42 us
    pallas_call x1, Pallas kernels, read_out(): pl.pallas_call(readout_kernel, out_shape=jax.ShapeDtypeStruct((FRAMES, CH...  6.26 us
    ppermute x2, starting transfers between devices, opposite(): lax.ppermute(value, 'chan', [(c, (c + 2) % CHANS) for c in range(CHANS)])  5.03 us
    ppermute x2, starting transfers between devices, neighbour(): return lax.ppermute(value, ('chan', 'clip'), route)  2.25 us
    ppermute x2, waiting for transfers between devices, swap(): return lax.ppermute(value, 'clip', [(0, 1), (1, 0)])  1.3 us
  transfers between devices with their start and end apart: 7, of which 4 were waited for; matrix products, arithmetic and copies ran while one was open for 0% of the time, Pallas kernels for 24%

profile of v10, /device:TPU:32, one launch (start us, length us, event | category | flops | bytes accessed | tf_op | source)
XLA Modules:
  0.0 54.9 jit_solution(2872936227777836097)
XLA Ops:
  0.0 3.2 %collective-permute-start.2 = (bf16[9,64,256]{2,1,0:T(8,128)(2,1)}, bf16[9,64,256]{2,1,0:T(8,128)(2,1)S(1)}, u32[]{:S(2)}, u32[]{:S(2)}) collective-permute-start(bf16[9,64,256]{2,1,0:T(8,128)(2,1)} %bitcast.10), channel_id=1, source_target_pairs={{0,4},{2,6},{4,0},{6,2},{1,5},{3,7},{5,1},{7,3},{8,12},{10,14},{12... | collective-permute-start | bytes 884744 | tf_op jit(solution)/shard_map/ppermute | solution.py:528
  3.2 0.7 %collective-permute-start = (bf16[9,64,256]{2,1,0:T(8,128)(2,1)}, bf16[9,64,256]{2,1,0:T(8,128)(2,1)S(1)}, u32[]{:S(2)}, u32[]{:S(2)}) collective-permute-start(bf16[9,64,256]{2,1,0:T(8,128)(2,1)} %bitcast.11), channel_id=1, source_target_pairs={{0,2},{1,7},{2,4},{3,1},{4,6},{5,3},{6,0},{7,5},{8,10},{9,15},{10,... | collective-permute-start | bytes 884744 | tf_op jit(solution)/shard_map/ppermute | solution.py:524
  3.9 1.8 %collective-permute-start.5 = (bf16[9,64,256]{2,1,0:T(8,128)(2,1)}, bf16[9,64,256]{2,1,0:T(8,128)(2,1)S(1)}, u32[]{:S(2)}, u32[]{:S(2)}) collective-permute-start(bf16[9,64,256]{2,1,0:T(8,128)(2,1)} %bitcast.14), channel_id=1, source_target_pairs={{0,4},{2,6},{4,0},{6,2},{1,5},{3,7},{5,1},{7,3},{8,12},{10,14},{12... | collective-permute-start | bytes 884744 | tf_op jit(solution)/shard_map/ppermute | solution.py:528
  5.7 1.6 %collective-permute-start.3 = (bf16[9,64,256]{2,1,0:T(8,128)(2,1)}, bf16[9,64,256]{2,1,0:T(8,128)(2,1)S(1)}, u32[]{:S(2)}, u32[]{:S(2)}) collective-permute-start(bf16[9,64,256]{2,1,0:T(8,128)(2,1)} %bitcast.15), channel_id=1, source_target_pairs={{0,2},{1,7},{2,4},{3,1},{4,6},{5,3},{6,0},{7,5},{8,10},{9,15},{10,... | collective-permute-start | bytes 884744 | tf_op jit(solution)/shard_map/ppermute | solution.py:524
  7.3 6.4 %drive.1 = bf16[8,9,16,128]{3,2,1,0:T(8,128)(2,1)} custom-call(f32[32]{0:T(128)} %intervals_far.3, f32[1,64]{1,0:T(1,128)} %bitcast.18, bf16[9,64,256]{2,1,0:T(8,128)(2,1)} %bitcast.12, bf16[32,16,16,256]{3,2,1,0:T(8,128)(2,1)} %frames.5), custom_call_target="tpu_custom_call" | custom-call | flops 8800000000 | bytes 1048576 | tf_op jit(solution)/shard_map/drive/pallas_call | solution.py:434
  13.7 8.6 %all-to-all-start = ((bf16[8,9,16,128]{3,2,1,0:T(8,128)(2,1)}), bf16[8,9,16,128]{3,2,1,0:T(8,128)(2,1)S(1)}, u32[]{:S(2)}, u32[]{:S(2)}) async-start(bf16[8,9,16,128]{3,2,1,0:T(8,128)(2,1)} %drive.1), calls=%async_computation | async-start | bytes 589824 | tf_op jit(solution)/shard_map/all_to_all | solution.py:560
  22.3 0.0 copy-start
  22.3 0.0 collective-permute-done.refs_1_.near
  22.3 0.1 collective-permute-start.1
  22.4 0.7 %collective-permute-done.3.near = bf16[9,64,256]{2,1,0:T(8,128)(2,1)S(1)} collective-permute-done((bf16[9,64,256]{2,1,0:T(8,128)(2,1)}, bf16[9,64,256]{2,1,0:T(8,128)(2,1)S(1)}, u32[]{:S(2)}, u32[]{:S(2)}) %collective-permute-start.3) | collective-permute-done | bytes 294944 | tf_op jit(solution)/shard_map/ppermute | solution.py:524
  23.1 0.2 collective-permute-start.4
  23.3 0.1 pad_add_fusion.place
  23.4 0.0 collective-permute-done.2.refs_0_
  23.4 0.6 %collective-permute-done.1.swapped = bf16[9,64,256]{2,1,0:T(8,128)(2,1)S(1)} collective-permute-done((bf16[9,64,256]{2,1,0:T(8,128)(2,1)S(1)}, bf16[9,64,256]{2,1,0:T(8,128)(2,1)S(1)}, u32[]{:S(2)}, u32[]{:S(2)}) %collective-permute-start.1) | collective-permute-done | bytes 294944 | tf_op jit(solution)/shard_map/ppermute | solution.py:549
  24.0 0.7 %collective-permute-done.4.later.swapped = bf16[9,64,256]{2,1,0:T(8,128)(2,1)S(1)} collective-permute-done((bf16[9,64,256]{2,1,0:T(8,128)(2,1)S(1)}, bf16[9,64,256]{2,1,0:T(8,128)(2,1)S(1)}, u32[]{:S(2)}, u32[]{:S(2)}) %collective-permute-start.4) | collective-permute-done | bytes 294944 | tf_op jit(solution)/shard_map/ppermute | solution.py:549
  24.7 0.0 copy-done
  24.7 6.9 %window.1 = (bf16[32,6,16,256]{3,2,1,0:T(8,128)(2,1)}, f32[8,128]{1,0:T(8,128)S(1)}) custom-call(s32[4]{0:T(128)S(1)} %pad_add_fusion.place, bf16[9,64,256]{2,1,0:T(8,128)(2,1)S(1)} %bitcast.13, bf16[9,64,256]{2,1,0:T(8,128)(2,1)S(1)} %collective-permute-done.refs_1_.near, bf16[9,64,256]{2,1,0:T(8,128)(2,1)S(1)} %collective-permute-done.1.swapped, ...), custom_call_target="tpu_custom_call" | custom-call | flops 1100000000 | bytes 1048576 | tf_op jit(solution)/shard_map/window/pallas_call | solution.py:457
  31.6 0.0 copy-start.3
  31.6 0.0 collective-permute-done.5.refs_0_
  31.6 0.0 copy-start.1
  31.6 0.0 copy-start.2
  31.7 0.0 copy-start.4
  31.7 1.2 %all-to-all-done.received = bf16[8,9,16,128]{3,2,1,0:T(8,128)(2,1)S(1)} async-done(((bf16[8,9,16,128]{3,2,1,0:T(8,128)(2,1)}), bf16[8,9,16,128]{3,2,1,0:T(8,128)(2,1)S(1)}, u32[]{:S(2)}, u32[]{:S(2)}) %all-to-all-start) | async-done | bytes 294944 | tf_op jit(solution)/shard_map/all_to_all | solution.py:560
  32.9 0.0 copy-done.3
  32.9 0.8 %relay.1 = bf16[16,4,16,128]{3,2,1,0:T(8,128)(2,1)S(1)} custom-call(s32[4]{0:T(128)S(1)} %pad_add_fusion.place, f32[1,64]{1,0:T(1,128)S(1)} %bitcast.19, bf16[8,9,16,128]{3,2,1,0:T(8,128)(2,1)S(1)} %all-to-all-done.received, f32[8,128]{1,0:T(8,128)S(1)} %get-tuple-element.7.refs_1_.token, bf16[9,64,256]{2,1,0:T(8,128)(2,1)S(1)} %after.3.later.far), custom_call_target="tpu_custom_call" | custom-call | flops 1100000000 | bytes 1048576 | tf_op jit(solution)/shard_map/relay/pallas_call | solution.py:479
  33.7 15.0 %all_to_all.10.received = bf16[16,4,16,128]{3,2,1,0:T(8,128)(2,1)S(1)} all-to-all(bf16[16,4,16,128]{3,2,1,0:T(8,128)(2,1)S(1)} %relay.1), channel_id=1, replica_groups=mesh['x'=4,'z'=8,'chan'=4,'clip'=2] {'x','chan'}, dimensions={0} | all-to-all | bytes 524288 | tf_op jit(solution)/shard_map/all_to_all | solution.py:567
  48.7 0.0 copy-done.1
  48.7 0.0 copy-done.2
  48.7 0.0 copy-done.4
  48.7 6.3 %read_out.1 = bf16[32,4,16,256]{3,2,1,0:T(8,128)(2,1)} custom-call(s32[4]{0:T(128)S(1)} %pad_add_fusion.place, f32[32]{0:T(128)S(1)} %copy-done.4, f32[1,256]{1,0:T(1,128)S(1)} %bitcast.17, bf16[16,4,16,128]{3,2,1,0:T(8,128)(2,1)S(1)} %all_to_all.10.received, bf16[32,6,16,256]{3,2,1,0:T(8,128)(2,1)} %get-tuple-element.8.drives_far, ...), custom_call_target="tpu_custom_call" | custom-call | flops 6600000000 | bytes 1048576 | tf_op jit(solution)/shard_map/read_out/pallas_call | solution.py:491
  (2 shorter events, 0.0 us)
Async XLA Ops:
  0.0 23.4 %collective-permute-start.2 = (bf16[9,64,256]{2,1,0:T(8,128)(2,1)}, bf16[9,64,256]{2,1,0:T(8,128)(2,1)S(1)}, u32[]{:S(2)}, u32[]{:S(2)}) collective-permute-start(bf16[9,64,256]{2,1,0:T(8,128)(2,1)} %bitcast.10), channel_id=1, source_target_pairs={{0,4},{2,6},{4,0},{6,2},{1,5},{3,7},{5,1},{7,3},{8,12},{10,14},{12... | collective-permute-start | bytes 884744 | tf_op jit(solution)/shard_map/ppermute | solution.py:528
  3.2 19.1 %collective-permute-start = (bf16[9,64,256]{2,1,0:T(8,128)(2,1)}, bf16[9,64,256]{2,1,0:T(8,128)(2,1)S(1)}, u32[]{:S(2)}, u32[]{:S(2)}) collective-permute-start(bf16[9,64,256]{2,1,0:T(8,128)(2,1)} %bitcast.11), channel_id=1, source_target_pairs={{0,2},{1,7},{2,4},{3,1},{4,6},{5,3},{6,0},{7,5},{8,10},{9,15},{10,... | collective-permute-start | bytes 884744 | tf_op jit(solution)/shard_map/ppermute | solution.py:524
  3.9 27.7 %collective-permute-start.5 = (bf16[9,64,256]{2,1,0:T(8,128)(2,1)}, bf16[9,64,256]{2,1,0:T(8,128)(2,1)S(1)}, u32[]{:S(2)}, u32[]{:S(2)}) collective-permute-start(bf16[9,64,256]{2,1,0:T(8,128)(2,1)} %bitcast.14), channel_id=1, source_target_pairs={{0,4},{2,6},{4,0},{6,2},{1,5},{3,7},{5,1},{7,3},{8,12},{10,14},{12... | collective-permute-start | bytes 884744 | tf_op jit(solution)/shard_map/ppermute | solution.py:528
  5.7 17.4 %collective-permute-start.3 = (bf16[9,64,256]{2,1,0:T(8,128)(2,1)}, bf16[9,64,256]{2,1,0:T(8,128)(2,1)S(1)}, u32[]{:S(2)}, u32[]{:S(2)}) collective-permute-start(bf16[9,64,256]{2,1,0:T(8,128)(2,1)} %bitcast.15), channel_id=1, source_target_pairs={{0,2},{1,7},{2,4},{3,1},{4,6},{5,3},{6,0},{7,5},{8,10},{9,15},{10,... | collective-permute-start | bytes 884744 | tf_op jit(solution)/shard_map/ppermute | solution.py:524
  13.7 19.2 %all-to-all-start = ((bf16[8,9,16,128]{3,2,1,0:T(8,128)(2,1)}), bf16[8,9,16,128]{3,2,1,0:T(8,128)(2,1)S(1)}, u32[]{:S(2)}, u32[]{:S(2)}) async-start(bf16[8,9,16,128]{3,2,1,0:T(8,128)(2,1)} %drive.1), calls=%async_computation | async-start | bytes 589824 | tf_op jit(solution)/shard_map/all_to_all | solution.py:560
  22.3 2.4 %copy-start = (bf16[3,3,256,64]{2,3,1,0:T(8,128)(2,1)S(1)}, bf16[3,3,256,64]{2,3,1,0:T(8,128)(2,1)}, u32[]{:S(2)}) copy-start(bf16[3,3,256,64]{2,3,1,0:T(8,128)(2,1)} %param.9) | copy-start | bytes 884740
  22.3 1.7 %collective-permute-start.1 = (bf16[9,64,256]{2,1,0:T(8,128)(2,1)S(1)}, bf16[9,64,256]{2,1,0:T(8,128)(2,1)S(1)}, u32[]{:S(2)}, u32[]{:S(2)}) collective-permute-start(bf16[9,64,256]{2,1,0:T(8,128)(2,1)S(1)} %collective-permute-done.refs_1_.near), channel_id=1, source_target_pairs={{0,1},{1,0},{2,3},{3,2},{4,5},{5,4},{6,7},{7,6},{8,9},{9,8},{10,11... | collective-permute-start | bytes 884744 | tf_op jit(solution)/shard_map/ppermute | solution.py:549
  23.1 1.6 %collective-permute-start.4 = (bf16[9,64,256]{2,1,0:T(8,128)(2,1)S(1)}, bf16[9,64,256]{2,1,0:T(8,128)(2,1)S(1)}, u32[]{:S(2)}, u32[]{:S(2)}) collective-permute-start(bf16[9,64,256]{2,1,0:T(8,128)(2,1)S(1)} %collective-permute-done.3.near), channel_id=1, source_target_pairs={{0,1},{1,0},{2,3},{3,2},{4,5},{5,4},{6,7},{7,6},{8,9},{9,8},{10,11... | collective-permute-start | bytes 884744 | tf_op jit(solution)/shard_map/ppermute | solution.py:549
  31.6 1.3 %copy-start.3 = (f32[64]{0:T(128)S(1)}, f32[64]{0:T(128)}, u32[]{:S(2)}) copy-start(f32[64]{0:T(128)} %param.8) | copy-start | bytes 772
  31.6 17.0 %copy-start.1 = (bf16[3,3,64,256]{3,2,1,0:T(8,128)(2,1)S(1)}, bf16[3,3,64,256]{3,2,1,0:T(8,128)(2,1)}, u32[]{:S(2)}) copy-start(bf16[3,3,64,256]{3,2,1,0:T(8,128)(2,1)} %param.10) | copy-start | bytes 884740
  31.6 17.0 %copy-start.2 = (f32[256]{0:T(256)S(1)}, f32[256]{0:T(256)}, u32[]{:S(2)}) copy-start(f32[256]{0:T(256)} %param.11) | copy-start | bytes 3076
  31.7 17.0 %copy-start.4 = (f32[32]{0:T(128)S(1)}, f32[32]{0:T(128)}, u32[]{:S(2)}) copy-start(f32[32]{0:T(128)} %intervals_far.3) | copy-start | bytes 388

commit v11 on v7

--- a/solution.py
+++ b/solution.py
@@ -315,15 +315,16 @@
 
 
 def readout_kernel(
-    place, intervals_far, skip_gain, received, drives_far, weights, frames,
+    place, intervals_far, skip_gain, received, drives_far,
+    own, near, swapped, far, frames,
     result,
-    intervals, direct, drives, states, written, factors, state,
+    intervals, weights, direct, drives, states, written, factors, state,
     load_sem, drive_sem, store_sem, small_sem,
 ):
     small = [pltpu.make_async_copy(intervals_far, intervals, small_sem)]
     for copy in small:
         copy.start()
-    chan, x = place[0], place[1]
+    chan, x, first = place[0], place[1], place[3] == 0
 
     def load(chunk):
         part = pl.ds(chunk * OUT_STEP, OUT_STEP)
@@ -343,6 +344,7 @@
         arrive(chunk).start()
         load(chunk).start()
 
+    assemble(weights, own, near, swapped, far, first)
     low = low_half((WIDE, LANES))
     rates, entering = [], []
     for step in range(CHANS):
@@ -474,22 +476,6 @@
     )(place, own, near, swapped, far, frames)
 
 
-def lay_kernel(place, own, near, swapped, far, result):
-    assemble(result, own, near, swapped, far, place[3] == 0)
-
-
-def lay(place, own, near, swapped, far):
-    return pl.pallas_call(
-        lay_kernel,
-        out_shape=jax.ShapeDtypeStruct((9, CHANS * OWN, CH), BF16),
-        in_specs=[in_smem()] + [in_vmem()] * CHANS,
-        out_specs=in_vmem(),
-        compiler_params=pltpu.CompilerParams(vmem_limit_bytes=16 << 20),
-        cost_estimate=cost(1),
-        name="lay",
-    )(place, own, near, swapped, far)
-
-
 def hold_kernel(value, *refs):
     result, sem = refs[-2:]
     copy = pltpu.make_async_copy(value, result, sem)
@@ -525,14 +511,17 @@
     )(place, rates, received, token)
 
 
-def read_out(place, intervals, skip_gain, received, drives, weights, frames):
+def read_out(place, intervals, skip_gain, received, drives, kernels, frames):
     return pl.pallas_call(
         readout_kernel,
         out_shape=jax.ShapeDtypeStruct((FRAMES, CHANS, WIDE, CH), BF16),
-        in_specs=[in_smem(), anywhere(), in_vmem(), in_vmem(), anywhere(), in_vmem(), anywhere()],
+        in_specs=[in_smem(), anywhere(), in_vmem(), in_vmem(), anywhere()]
+        + [in_vmem()] * CHANS
+        + [anywhere()],
         out_specs=anywhere(),
         scratch_shapes=[
             pltpu.SMEM((FRAMES,), F32),
+            pltpu.VMEM((9, CHANS * OWN, CH), BF16),
             pltpu.VMEM((FRAMES, CHANS, WIDE, CH), BF16),
             pltpu.VMEM((FRAMES, WINDOW, WIDE, CH), BF16),
             pltpu.VMEM((FRAMES, WINDOW, WIDE, CH), BF16),
@@ -547,7 +536,7 @@
         compiler_params=pltpu.CompilerParams(vmem_limit_bytes=52 << 20),
         cost_estimate=cost(6),
         name="read_out",
-    )(place, intervals, skip_gain, received, drives, weights, frames)
+    )(place, intervals, skip_gain, received, drives, *kernels, frames)
 
 
 def around(value):
@@ -564,7 +553,7 @@
     del refs
 
 
-def after(value, other):
+def after(value, other, length=0):
     return pl.pallas_call(
         after_kernel,
         out_shape=jax.ShapeDtypeStruct(value.shape, value.dtype),
@@ -572,7 +561,7 @@
         out_specs=anywhere(),
         input_output_aliases={0: 0},
         compiler_params=pltpu.CompilerParams(vmem_limit_bytes=16 << 20),
-        cost_estimate=cost(0),
+        cost_estimate=cost(length),
         name="after",
     )(value, other)
 
@@ -588,6 +577,7 @@
     kernel_t = jnp.transpose(in_kernel.reshape(9, CH, OWN), (0, 2, 1))
     out_own = out_kernel.reshape(9, OWN, CH)
     in_near, in_far = around(kernel_t)
+    in_far = after(in_far, in_near, 2)
     message = drive(intervals, rates, kernel_t, frames)
     arrived = lax.all_to_all(message, "z", 0, 0)
     out_near, out_far = around(hold(out_own, (in_near, in_far)))
@@ -595,9 +585,11 @@
     onward, done = relay(place, rates, arrived, done)
     out_near = after(out_near, done)
     received = lax.all_to_all(onward, ("x", "chan"), 0, 0)
-    weights = lay(place, out_own, out_near, swap(out_near), out_far)
+    received = after(received, place, 2)
+    out_far = after(out_far, done, 2)
+    kernels = (out_own, out_near, swap(out_near), out_far)
     skip = skip_gain.reshape(1, CH)
-    return read_out(place, intervals, skip, received, drives, weights, frames)
+    return read_out(place, intervals, skip, received, drives, kernels, frames)
 
 
 def solution(mesh):

time: 54.4 us -> 52.5 us (0.965)
  starting transfers between devices: 24 us -> 21.6 us
  local copies, waits for them, and re-layouts: 0.03 us -> 0.85 us
  Pallas kernels: 21.8 us -> 21.1 us
    ppermute x2, starting transfers between devices: 7.23 us -> 5.12 us  [around(): lax.ppermute(value, 'chan', far)]
    all_to_all x1, starting transfers between devices: 7.24 us -> 5.51 us  [local(): received = lax.all_to_all(onward, ('x', 'chan'), 0, 0)]
    ppermute x2, starting transfers between devices: 0.78 us -> 2.25 us  [around(): lax.ppermute(value, ('chan', 'clip'), near)]
    unnamed x10, local copies, waits for them, and re-layouts: 0.03 us -> 0.85 us
    pallas_call x1 -> x0, Pallas kernels: 0.65 us -> none  [lay(): pl.pallas_call(lay_kernel, out_shape=jax.ShapeDtypeStruct((9, CHANS * OWN...]
  transfers between devices with their start and end apart: 8 -> 8, of which waited for: 1 -> 1; matrix products, arithmetic and copies ran while one was open for 0% -> 0% of each run, Pallas kernels for 29% -> 28%
where the time goes in v11:
time: 52.5 us; the launch traced here: 52.2 us
  starting transfers between devices  21.6 us (41%)
  Pallas kernels  21.1 us (40%)
  waiting for transfers between devices  8.37 us (16%)
  local copies, waits for them, and re-layouts  0.85 us (2%)
    all_to_all x1, starting transfers between devices, local(): arrived = lax.all_to_all(message, 'z', 0, 0)  8.58 us
    all_to_all x1, waiting for transfers between devices, local(): received = lax.all_to_all(onward, ('x', 'chan'), 0, 0)  8.35 us
    pallas_call x1, Pallas kernels, window(): pl.pallas_call(window_kernel, out_shape=[jax.ShapeDtypeStruct((FRAMES, WI...  6.9 us
    pallas_call x1, Pallas kernels, drive(): pl.pallas_call(drive_kernel, out_shape=jax.ShapeDtypeStruct((ZS, ROWS //...  6.42 us
    pallas_call x1, Pallas kernels, read_out(): pl.pallas_call(readout_kernel, out_shape=jax.ShapeDtypeStruct((FRAMES, CH...  6.25 us
    all_to_all x1, starting transfers between devices, local(): received = lax.all_to_all(onward, ('x', 'chan'), 0, 0)  5.51 us
    ppermute x2, starting transfers between devices, around(): lax.ppermute(value, 'chan', far)  5.12 us
    ppermute x2, starting transfers between devices, around(): lax.ppermute(value, ('chan', 'clip'), near)  2.25 us
  transfers between devices with their start and end apart: 8, of which 1 were waited for; matrix products, arithmetic and copies ran while one was open for 0% of the time, Pallas kernels for 28%

profile of v11, /device:TPU:32, one launch (start us, length us, event | category | flops | bytes accessed | tf_op | source)
XLA Modules:
  0.0 52.2 jit_solution(15384573747737672372)
XLA Ops:
  0.0 3.2 %collective-permute-start.2 = (bf16[9,64,256]{2,1,0:T(8,128)(2,1)}, bf16[9,64,256]{2,1,0:T(8,128)(2,1)S(1)}, u32[]{:S(2)}, u32[]{:S(2)}) collective-permute-start(bf16[9,64,256]{2,1,0:T(8,128)(2,1)} %bitcast.10), channel_id=1, source_target_pairs={{0,4},{2,6},{4,0},{6,2},{1,5},{3,7},{5,1},{7,3},{8,12},{10,14},{12... | collective-permute-start | bytes 884744 | tf_op jit(solution)/shard_map/ppermute | solution.py:549
  3.2 0.7 %collective-permute-start = (bf16[9,64,256]{2,1,0:T(8,128)(2,1)}, bf16[9,64,256]{2,1,0:T(8,128)(2,1)S(1)}, u32[]{:S(2)}, u32[]{:S(2)}) collective-permute-start(bf16[9,64,256]{2,1,0:T(8,128)(2,1)} %bitcast.11), channel_id=1, source_target_pairs={{0,2},{1,7},{2,4},{3,1},{4,6},{5,3},{6,0},{7,5},{8,10},{9,15},{10,... | collective-permute-start | bytes 884744 | tf_op jit(solution)/shard_map/ppermute | solution.py:549
  3.9 6.4 %drive.1 = bf16[8,9,16,128]{3,2,1,0:T(8,128)(2,1)} custom-call(f32[32]{0:T(128)} %intervals_far.3, f32[1,64]{1,0:T(1,128)} %bitcast.17, bf16[9,64,256]{2,1,0:T(8,128)(2,1)} %bitcast.12, bf16[32,16,16,256]{3,2,1,0:T(8,128)(2,1)} %frames.5), custom_call_target="tpu_custom_call" | custom-call | flops 8800000000 | bytes 1048576 | tf_op jit(solution)/shard_map/drive/pallas_call | solution.py:435
  10.3 8.6 %all-to-all-start = ((bf16[8,9,16,128]{3,2,1,0:T(8,128)(2,1)}), bf16[8,9,16,128]{3,2,1,0:T(8,128)(2,1)S(1)}, u32[]{:S(2)}, u32[]{:S(2)}) async-start(bf16[8,9,16,128]{3,2,1,0:T(8,128)(2,1)} %drive.1), calls=%async_computation | async-start | bytes 589824 | tf_op jit(solution)/shard_map/all_to_all | solution.py:582
  18.9 0.0 copy-start.1
  18.9 0.0 copy-start
  18.9 0.0 collective-permute-done.refs_1_.near.refs_0_
  18.9 0.1 collective-permute-start.1
  19.0 0.0 collective-permute-done.2.refs_0_
  19.0 0.8 %copy-done.1 = bf16[3,3,64,256]{3,2,1,0:T(8,128)(2,1)S(1)} copy-done((bf16[3,3,64,256]{3,2,1,0:T(8,128)(2,1)S(1)}, bf16[3,3,64,256]{3,2,1,0:T(8,128)(2,1)}, u32[]{:S(2)}) %copy-start.1) | copy-done | bytes 294936
  19.8 0.0 copy-start.3
  19.8 0.1 hold.1
  19.9 1.9 %collective-permute-start.5 = (bf16[9,64,256]{2,1,0:T(8,128)(2,1)S(1)}, bf16[9,64,256]{2,1,0:T(8,128)(2,1)S(1)}, u32[]{:S(2)}, u32[]{:S(2)}) collective-permute-start(bf16[9,64,256]{2,1,0:T(8,128)(2,1)S(1)} %hold.1), channel_id=1, source_target_pairs={{0,4},{2,6},{4,0},{6,2},{1,5},{3,7},{5,1},{7,3},{8,12},{10,14},{12... | collective-permute-start | bytes 884744 | tf_op jit(solution)/shard_map/ppermute | solution.py:549
  21.8 1.6 %collective-permute-start.3 = (bf16[9,64,256]{2,1,0:T(8,128)(2,1)S(1)}, bf16[9,64,256]{2,1,0:T(8,128)(2,1)S(1)}, u32[]{:S(2)}, u32[]{:S(2)}) collective-permute-start(bf16[9,64,256]{2,1,0:T(8,128)(2,1)S(1)} %hold.1), channel_id=1, source_target_pairs={{0,2},{1,7},{2,4},{3,1},{4,6},{5,3},{6,0},{7,5},{8,10},{9,15},{10,... | collective-permute-start | bytes 884744 | tf_op jit(solution)/shard_map/ppermute | solution.py:549
  23.4 0.1 pad_add_fusion.place.refs_1_
  23.5 0.0 collective-permute-done.1.swapped
  23.5 0.0 copy-done
  23.5 6.9 %window.1 = (bf16[32,6,16,256]{3,2,1,0:T(8,128)(2,1)}, f32[8,128]{1,0:T(8,128)S(1)}) custom-call(s32[4]{0:T(128)S(1)} %pad_add_fusion.place.refs_1_, bf16[9,64,256]{2,1,0:T(8,128)(2,1)S(1)} %bitcast.13, bf16[9,64,256]{2,1,0:T(8,128)(2,1)S(1)} %collective-permute-done.refs_1_.near.refs_0_, bf16[9,64,256]{2,1,0:T(8,128)(2,1)S(1)} %collective-permute-done.1.swapped, ...), custom_call_target="tpu_custom_call" | custom-call | flops 1100000000 | bytes 1048576 | tf_op jit(solution)/shard_map/window/pallas_call | solution.py:458
  30.4 0.0 all-to-all-done.received
  30.4 0.0 copy-done.3
  30.4 1.5 %relay.1 = (bf16[16,4,16,128]{3,2,1,0:T(8,128)(2,1)}, f32[8,128]{1,0:T(8,128)S(1)}) custom-call(s32[4]{0:T(128)S(1)} %pad_add_fusion.place.refs_1_, f32[1,64]{1,0:T(1,128)S(1)} %bitcast.18, bf16[8,9,16,128]{3,2,1,0:T(8,128)(2,1)S(1)} %all-to-all-done.received, f32[8,128]{1,0:T(8,128)S(1)} %get-tuple-element.9.token), custom_call_target="tpu_custom_call" | custom-call | flops 1100000000 | bytes 1048576 | tf_op jit(solution)/shard_map/relay/pallas_call | solution.py:500
  31.9 5.5 %all-to-all-start.1 = ((bf16[16,4,16,128]{3,2,1,0:T(8,128)(2,1)}), bf16[16,4,16,128]{3,2,1,0:T(8,128)(2,1)S(1)}, u32[]{:S(2)}, u32[]{:S(2)}) async-start(bf16[16,4,16,128]{3,2,1,0:T(8,128)(2,1)} %get-tuple-element.10), calls=%async_computation.1 | async-start | bytes 524288 | tf_op jit(solution)/shard_map/all_to_all | solution.py:587
  37.4 0.0 collective-permute-done.3.refs_0_
  37.4 0.1 collective-permute-start.4
  37.5 0.0 collective-permute-done.5.refs_0_
  37.6 0.0 copy-start.2
  37.6 0.0 copy-start.4
  37.6 8.3 %all-to-all-done.1.refs_0_ = bf16[16,4,16,128]{3,2,1,0:T(8,128)(2,1)S(1)} async-done(((bf16[16,4,16,128]{3,2,1,0:T(8,128)(2,1)}), bf16[16,4,16,128]{3,2,1,0:T(8,128)(2,1)S(1)}, u32[]{:S(2)}, u32[]{:S(2)}) %all-to-all-start.1) | async-done | bytes 262176 | tf_op jit(solution)/shard_map/all_to_all | solution.py:587
  45.9 0.0 collective-permute-done.4.swapped
  45.9 0.0 copy-done.2
  45.9 0.0 copy-done.4
  45.9 6.3 %read_out.1 = bf16[32,4,16,256]{3,2,1,0:T(8,128)(2,1)} custom-call(s32[4]{0:T(128)S(1)} %pad_add_fusion.place.refs_1_, f32[32]{0:T(128)S(1)} %copy-done.4, f32[1,256]{1,0:T(1,128)S(1)} %bitcast.16, bf16[16,4,16,128]{3,2,1,0:T(8,128)(2,1)S(1)} %after.5.received, bf16[32,6,16,256]{3,2,1,0:T(8,128)(2,1)} %get-tuple-element.11.drives_far, ...), custom_call_target="tpu_custom_call" | custom-call | flops 6600000000 | bytes 1048576 | tf_op jit(solution)/shard_map/read_out/pallas_call | solution.py:515
  (4 shorter events, 0.0 us)
Async XLA Ops:
  0.0 19.0 %collective-permute-start.2 = (bf16[9,64,256]{2,1,0:T(8,128)(2,1)}, bf16[9,64,256]{2,1,0:T(8,128)(2,1)S(1)}, u32[]{:S(2)}, u32[]{:S(2)}) collective-permute-start(bf16[9,64,256]{2,1,0:T(8,128)(2,1)} %bitcast.10), channel_id=1, source_target_pairs={{0,4},{2,6},{4,0},{6,2},{1,5},{3,7},{5,1},{7,3},{8,12},{10,14},{12... | collective-permute-start | bytes 884744 | tf_op jit(solution)/shard_map/ppermute | solution.py:549
  3.2 15.7 %collective-permute-start = (bf16[9,64,256]{2,1,0:T(8,128)(2,1)}, bf16[9,64,256]{2,1,0:T(8,128)(2,1)S(1)}, u32[]{:S(2)}, u32[]{:S(2)}) collective-permute-start(bf16[9,64,256]{2,1,0:T(8,128)(2,1)} %bitcast.11), channel_id=1, source_target_pairs={{0,2},{1,7},{2,4},{3,1},{4,6},{5,3},{6,0},{7,5},{8,10},{9,15},{10,... | collective-permute-start | bytes 884744 | tf_op jit(solution)/shard_map/ppermute | solution.py:549
  10.3 20.1 %all-to-all-start = ((bf16[8,9,16,128]{3,2,1,0:T(8,128)(2,1)}), bf16[8,9,16,128]{3,2,1,0:T(8,128)(2,1)S(1)}, u32[]{:S(2)}, u32[]{:S(2)}) async-start(bf16[8,9,16,128]{3,2,1,0:T(8,128)(2,1)} %drive.1), calls=%async_computation | async-start | bytes 589824 | tf_op jit(solution)/shard_map/all_to_all | solution.py:582
  18.9 1.0 %copy-start.1 = (bf16[3,3,64,256]{3,2,1,0:T(8,128)(2,1)S(1)}, bf16[3,3,64,256]{3,2,1,0:T(8,128)(2,1)}, u32[]{:S(2)}) copy-start(bf16[3,3,64,256]{3,2,1,0:T(8,128)(2,1)} %param.10) | copy-start | bytes 884740
  18.9 4.6 %copy-start = (bf16[3,3,256,64]{2,3,1,0:T(8,128)(2,1)S(1)}, bf16[3,3,256,64]{2,3,1,0:T(8,128)(2,1)}, u32[]{:S(2)}) copy-start(bf16[3,3,256,64]{2,3,1,0:T(8,128)(2,1)} %param.9) | copy-start | bytes 884740
  18.9 4.6 %collective-permute-start.1 = (bf16[9,64,256]{2,1,0:T(8,128)(2,1)S(1)}, bf16[9,64,256]{2,1,0:T(8,128)(2,1)S(1)}, u32[]{:S(2)}, u32[]{:S(2)}) collective-permute-start(bf16[9,64,256]{2,1,0:T(8,128)(2,1)S(1)} %collective-permute-done.refs_1_.near.refs_0_), channel_id=1, source_target_pairs={{0,1},{1,0},{2,3},{3,2},{4,5},{5,4},{6,7},{7,6},{8,9},{9,8},{10,11... | collective-permute-start | bytes 884744 | tf_op jit(solution)/shard_map/ppermute | solution.py:570
  19.8 10.6 %copy-start.3 = (f32[64]{0:T(128)S(1)}, f32[64]{0:T(128)}, u32[]{:S(2)}) copy-start(f32[64]{0:T(128)} %param.8) | copy-start | bytes 772
  19.9 17.6 %collective-permute-start.5 = (bf16[9,64,256]{2,1,0:T(8,128)(2,1)S(1)}, bf16[9,64,256]{2,1,0:T(8,128)(2,1)S(1)}, u32[]{:S(2)}, u32[]{:S(2)}) collective-permute-start(bf16[9,64,256]{2,1,0:T(8,128)(2,1)S(1)} %hold.1), channel_id=1, source_target_pairs={{0,4},{2,6},{4,0},{6,2},{1,5},{3,7},{5,1},{7,3},{8,12},{10,14},{12... | collective-permute-start | bytes 884744 | tf_op jit(solution)/shard_map/ppermute | solution.py:549
  21.8 15.6 %collective-permute-start.3 = (bf16[9,64,256]{2,1,0:T(8,128)(2,1)S(1)}, bf16[9,64,256]{2,1,0:T(8,128)(2,1)S(1)}, u32[]{:S(2)}, u32[]{:S(2)}) collective-permute-start(bf16[9,64,256]{2,1,0:T(8,128)(2,1)S(1)} %hold.1), channel_id=1, source_target_pairs={{0,2},{1,7},{2,4},{3,1},{4,6},{5,3},{6,0},{7,5},{8,10},{9,15},{10,... | collective-permute-start | bytes 884744 | tf_op jit(solution)/shard_map/ppermute | solution.py:549
  31.9 14.0 %all-to-all-start.1 = ((bf16[16,4,16,128]{3,2,1,0:T(8,128)(2,1)}), bf16[16,4,16,128]{3,2,1,0:T(8,128)(2,1)S(1)}, u32[]{:S(2)}, u32[]{:S(2)}) async-start(bf16[16,4,16,128]{3,2,1,0:T(8,128)(2,1)} %get-tuple-element.10), calls=%async_computation.1 | async-start | bytes 524288 | tf_op jit(solution)/shard_map/all_to_all | solution.py:587
  37.4 8.5 %collective-permute-start.4 = (bf16[9,64,256]{2,1,0:T(8,128)(2,1)S(1)}, bf16[9,64,256]{2,1,0:T(8,128)(2,1)S(1)}, u32[]{:S(2)}, u32[]{:S(2)}) collective-permute-start(bf16[9,64,256]{2,1,0:T(8,128)(2,1)S(1)} %after.6.near), channel_id=1, source_target_pairs={{0,1},{1,0},{2,3},{3,2},{4,5},{5,4},{6,7},{7,6},{8,9},{9,8},{10,11... | collective-permute-start | bytes 884744 | tf_op jit(solution)/shard_map/ppermute | solution.py:570
  37.6 8.4 %copy-start.2 = (f32[256]{0:T(256)S(1)}, f32[256]{0:T(256)}, u32[]{:S(2)}) copy-start(f32[256]{0:T(256)} %param.11) | copy-start | bytes 3076
  37.6 8.4 %copy-start.4 = (f32[32]{0:T(128)S(1)}, f32[32]{0:T(128)}, u32[]{:S(2)}) copy-start(f32[32]{0:T(128)} %intervals_far.3) | copy-start | bytes 388

commit v12 on v11

--- a/solution.py
+++ b/solution.py
@@ -186,7 +186,7 @@
 
 
 WINDOW_STEP = 8
-WINDOW_CHUNKS = FRAMES // WINDOW_STEP
+EARLY = 24
 TALL = 12
 
 
@@ -201,27 +201,29 @@
 
 
 def window_kernel(
-    place, own, near, swapped, far, frames,
+    begin, size, place, own, near, swapped, far, frames, _,
     drives, token,
     weights, rows, written, load_sem, store_sem,
 ):
+    chunks = size // WINDOW_STEP
     chan, first = place[0], place[3] == 0
     source = jnp.clip(CHANS * chan - 2, 0, 8)
     target = source - CHANS * chan + 4
 
     def load(chunk):
         part = pl.ds(chunk * WINDOW_STEP, WINDOW_STEP)
+        where = pl.ds(begin + chunk * WINDOW_STEP, WINDOW_STEP)
         return pltpu.make_async_copy(
-            frames.at[part, pl.ds(source, 8)], rows.at[part, pl.ds(target, 8)], load_sem.at[chunk]
+            frames.at[where, pl.ds(source, 8)], rows.at[part, pl.ds(target, 8)], load_sem.at[chunk]
         )
 
     def store(chunk):
         part = pl.ds(chunk * WINDOW_STEP, WINDOW_STEP)
         return pltpu.make_async_copy(written.at[part], drives.at[part], store_sem.at[chunk])
 
-    for chunk in range(WINDOW_CHUNKS):
+    for chunk in range(chunks):
         load(chunk).start()
-    empty = jnp.zeros((FRAMES, 2, WIDE, CH), BF16)
+    empty = jnp.zeros((size, 2, WIDE, CH), BF16)
 
     @pl.when(chan == 0)
     def _():
@@ -238,8 +240,8 @@
         load(chunk).wait()
         start = pl.multiple_of(chunk * WINDOW_STEP, WINDOW_STEP)
         block = rows[pl.ds(start, WINDOW_STEP)]
-        size = WINDOW_STEP * WINDOW * WIDE
-        taps = [block[:, 2 + i : 2 + i + WINDOW].reshape(size, CH) for i in range(3)]
+        pixels = WINDOW_STEP * WINDOW * WIDE
+        taps = [block[:, 2 + i : 2 + i + WINDOW].reshape(pixels, CH) for i in range(3)]
         operand = jnp.concatenate(taps, axis=1)
         shape = (WINDOW_STEP * WINDOW, WIDE, CH)
         dims = (((1,), (1,)), ((), ()))
@@ -260,8 +262,8 @@
         store(chunk).start()
         return carry
 
-    lax.fori_loop(0, WINDOW_CHUNKS, convolve, 0)
-    for chunk in range(WINDOW_CHUNKS):
+    lax.fori_loop(0, chunks, convolve, 0)
+    for chunk in range(chunks):
         store(chunk).wait()
 
 
@@ -315,7 +317,7 @@
 
 
 def readout_kernel(
-    place, intervals_far, skip_gain, received, drives_far,
+    place, intervals_far, skip_gain, received, early, late,
     own, near, swapped, far, frames,
     result,
     intervals, weights, direct, drives, states, written, factors, state,
@@ -332,16 +334,24 @@
             frames.at[part, pl.ds(CHANS * chan, CHANS)], direct.at[part], load_sem.at[chunk]
         )
 
-    def arrive(chunk):
+    def arrive(chunk, source=early, skipped=0):
         part = pl.ds(chunk * OUT_STEP, OUT_STEP)
-        return pltpu.make_async_copy(drives_far.at[part], drives.at[part], drive_sem.at[chunk])
+        where = pl.ds(chunk * OUT_STEP - skipped, OUT_STEP)
+        return pltpu.make_async_copy(source.at[where], drives.at[part], drive_sem.at[chunk])
+
+    def arrived(chunk):
+        part = drives.at[pl.ds(chunk * OUT_STEP, OUT_STEP)]
+        return pltpu.make_async_copy(part, part, drive_sem.at[chunk])
 
     def store(chunk):
         part = pl.ds(chunk * OUT_STEP, OUT_STEP)
         return pltpu.make_async_copy(written.at[part], result.at[part], store_sem.at[chunk])
 
     for chunk in range(OUT_CHUNKS):
-        arrive(chunk).start()
+        if chunk * OUT_STEP < EARLY:
+            arrive(chunk).start()
+        else:
+            arrive(chunk, late, EARLY).start()
         load(chunk).start()
 
     assemble(weights, own, near, swapped, far, first)
@@ -385,7 +395,7 @@
 
     def convolve(chunk, carry):
         start = pl.multiple_of(chunk * OUT_STEP, OUT_STEP)
-        arrive(chunk).wait()
+        arrived(chunk).wait()
         carried = state[...]
         for step in range(OUT_STEP):
             decay, gain = factors[0, start + step], factors[1, start + step]
@@ -454,26 +464,27 @@
     )(intervals, rates, kernel_t, frames)
 
 
-def window(place, own, near, swapped, far, frames):
+def window(begin, size, place, own, near, swapped, far, frames, later):
+    chunks = size // WINDOW_STEP
     return pl.pallas_call(
-        window_kernel,
+        functools.partial(window_kernel, begin, size),
         out_shape=[
-            jax.ShapeDtypeStruct((FRAMES, WINDOW, WIDE, CH), BF16),
+            jax.ShapeDtypeStruct((size, WINDOW, WIDE, CH), BF16),
             jax.ShapeDtypeStruct((8, LANES), F32),
         ],
-        in_specs=[in_smem()] + [in_vmem()] * CHANS + [anywhere()],
+        in_specs=[in_smem()] + [in_vmem()] * CHANS + [anywhere()] * 2,
         out_specs=[anywhere(), in_vmem()],
         scratch_shapes=[
             pltpu.VMEM((9, CHANS * OWN, CH), BF16),
-            pltpu.VMEM((FRAMES, TALL, WIDE, CH), BF16),
-            pltpu.VMEM((FRAMES, WINDOW, WIDE, CH), BF16),
-            pltpu.SemaphoreType.DMA((WINDOW_CHUNKS,)),
-            pltpu.SemaphoreType.DMA((WINDOW_CHUNKS,)),
+            pltpu.VMEM((size, TALL, WIDE, CH), BF16),
+            pltpu.VMEM((size, WINDOW, WIDE, CH), BF16),
+            pltpu.SemaphoreType.DMA((chunks,)),
+            pltpu.SemaphoreType.DMA((chunks,)),
         ],
         compiler_params=pltpu.CompilerParams(vmem_limit_bytes=52 << 20),
         cost_estimate=cost(1),
         name="window",
-    )(place, own, near, swapped, far, frames)
+    )(place, own, near, swapped, far, frames, later)
 
 
 def hold_kernel(value, *refs):
@@ -511,11 +522,11 @@
     )(place, rates, received, token)
 
 
-def read_out(place, intervals, skip_gain, received, drives, kernels, frames):
+def read_out(place, intervals, skip_gain, received, early, late, kernels, frames):
     return pl.pallas_call(
         readout_kernel,
         out_shape=jax.ShapeDtypeStruct((FRAMES, CHANS, WIDE, CH), BF16),
-        in_specs=[in_smem(), anywhere(), in_vmem(), in_vmem(), anywhere()]
+        in_specs=[in_smem(), anywhere(), in_vmem(), in_vmem(), anywhere(), anywhere()]
         + [in_vmem()] * CHANS
         + [anywhere()],
         out_specs=anywhere(),
@@ -536,7 +547,7 @@
         compiler_params=pltpu.CompilerParams(vmem_limit_bytes=52 << 20),
         cost_estimate=cost(6),
         name="read_out",
-    )(place, intervals, skip_gain, received, drives, *kernels, frames)
+    )(place, intervals, skip_gain, received, early, late, *kernels, frames)
 
 
 def around(value):
@@ -581,15 +592,17 @@
     message = drive(intervals, rates, kernel_t, frames)
     arrived = lax.all_to_all(message, "z", 0, 0)
     out_near, out_far = around(hold(out_own, (in_near, in_far)))
-    drives, done = window(place, kernel_t, in_near, swap(in_near), in_far, frames)
+    pieces = (kernel_t, in_near, swap(in_near), in_far)
+    early, done = window(0, EARLY, place, *pieces, frames, place)
     onward, done = relay(place, rates, arrived, done)
+    late, _ = window(EARLY, FRAMES - EARLY, place, *pieces, frames, done)
     out_near = after(out_near, done)
     received = lax.all_to_all(onward, ("x", "chan"), 0, 0)
     received = after(received, place, 2)
     out_far = after(out_far, done, 2)
     kernels = (out_own, out_near, swap(out_near), out_far)
     skip = skip_gain.reshape(1, CH)
-    return read_out(place, intervals, skip, received, drives, kernels, frames)
+    return read_out(place, intervals, skip, received, early, late, kernels, frames)
 
 
 def solution(mesh):

time: 52.5 us -> 52.2 us (level)
  waiting for transfers between devices: 8.37 us -> 5.37 us
  Pallas kernels: 21.1 us -> 23.5 us
    all_to_all x1, waiting for transfers between devices: 8.35 us -> 4.79 us  [local(): received = lax.all_to_all(onward, ('x', 'chan'), 0, 0)]
    pallas_call x1 -> x2, Pallas kernels: 6.9 us -> 9.26 us  [window(): pl.pallas_call(functools.partial(window_kernel, begin, size), out_shape=[...]
    all_to_all x1, waiting for transfers between devices: 0.01 us -> 0.56 us  [local(): arrived = lax.all_to_all(message, 'z', 0, 0)]
  transfers between devices with their start and end apart: 8 -> 8, of which waited for: 1 -> 2; matrix products, arithmetic and copies ran while one was open for 0% -> 0% of each run, Pallas kernels for 28% -> 33%
where the time goes in v12:
time: 52.2 us; the launch traced here: 51.6 us
  Pallas kernels  23.5 us (45%)
  starting transfers between devices  21.7 us (42%)
  waiting for transfers between devices  5.37 us (10%)
  local copies, waits for them, and re-layouts  0.85 us (2%)
    pallas_call x2, Pallas kernels, window(): pl.pallas_call(functools.partial(window_kernel, begin, size), out_shape=[...  9.26 us
    all_to_all x1, starting transfers between devices, local(): arrived = lax.all_to_all(message, 'z', 0, 0)  8.58 us
    pallas_call x1, Pallas kernels, drive(): pl.pallas_call(drive_kernel, out_shape=jax.ShapeDtypeStruct((ZS, ROWS //...  6.42 us
    pallas_call x1, Pallas kernels, read_out(): pl.pallas_call(readout_kernel, out_shape=jax.ShapeDtypeStruct((FRAMES, CH...  6.26 us
    all_to_all x1, starting transfers between devices, local(): received = lax.all_to_all(onward, ('x', 'chan'), 0, 0)  5.53 us
    ppermute x2, starting transfers between devices, around(): lax.ppermute(value, 'chan', far)  5.12 us
    all_to_all x1, waiting for transfers between devices, local(): received = lax.all_to_all(onward, ('x', 'chan'), 0, 0)  4.79 us
    ppermute x2, starting transfers between devices, around(): lax.ppermute(value, ('chan', 'clip'), near)  2.25 us
  transfers between devices with their start and end apart: 8, of which 2 were waited for; matrix products, arithmetic and copies ran while one was open for 0% of the time, Pallas kernels for 33%

profile of v12, /device:TPU:32, one launch (start us, length us, event | category | flops | bytes accessed | tf_op | source)
XLA Modules:
  0.0 51.6 jit_solution(9954244281884473186)
XLA Ops:
  0.0 3.2 %collective-permute-start.2 = (bf16[9,64,256]{2,1,0:T(8,128)(2,1)}, bf16[9,64,256]{2,1,0:T(8,128)(2,1)S(1)}, u32[]{:S(2)}, u32[]{:S(2)}) collective-permute-start(bf16[9,64,256]{2,1,0:T(8,128)(2,1)} %bitcast.10), channel_id=1, source_target_pairs={{0,4},{2,6},{4,0},{6,2},{1,5},{3,7},{5,1},{7,3},{8,12},{10,14},{12... | collective-permute-start | bytes 884744 | tf_op jit(solution)/shard_map/ppermute | solution.py:560
  3.2 0.7 %collective-permute-start = (bf16[9,64,256]{2,1,0:T(8,128)(2,1)}, bf16[9,64,256]{2,1,0:T(8,128)(2,1)S(1)}, u32[]{:S(2)}, u32[]{:S(2)}) collective-permute-start(bf16[9,64,256]{2,1,0:T(8,128)(2,1)} %bitcast.11), channel_id=1, source_target_pairs={{0,2},{1,7},{2,4},{3,1},{4,6},{5,3},{6,0},{7,5},{8,10},{9,15},{10,... | collective-permute-start | bytes 884744 | tf_op jit(solution)/shard_map/ppermute | solution.py:560
  3.9 6.4 %drive.1 = bf16[8,9,16,128]{3,2,1,0:T(8,128)(2,1)} custom-call(f32[32]{0:T(128)} %intervals_far.3, f32[1,64]{1,0:T(1,128)} %bitcast.18, bf16[9,64,256]{2,1,0:T(8,128)(2,1)} %bitcast.12, bf16[32,16,16,256]{3,2,1,0:T(8,128)(2,1)} %frames.7), custom_call_target="tpu_custom_call" | custom-call | flops 8800000000 | bytes 1048576 | tf_op jit(solution)/shard_map/drive/pallas_call | solution.py:445
  10.3 8.6 %all-to-all-start = ((bf16[8,9,16,128]{3,2,1,0:T(8,128)(2,1)}), bf16[8,9,16,128]{3,2,1,0:T(8,128)(2,1)S(1)}, u32[]{:S(2)}, u32[]{:S(2)}) async-start(bf16[8,9,16,128]{3,2,1,0:T(8,128)(2,1)} %drive.1), calls=%async_computation | async-start | bytes 589824 | tf_op jit(solution)/shard_map/all_to_all | solution.py:593
  18.9 0.0 copy-start.1
  18.9 0.0 copy-start
  18.9 0.0 collective-permute-done.refs_1_.near.refs_0_
  18.9 0.1 collective-permute-start.1
  19.0 0.0 collective-permute-done.2.refs_0_
  19.0 0.8 %copy-done.1 = bf16[3,3,64,256]{3,2,1,0:T(8,128)(2,1)S(1)} copy-done((bf16[3,3,64,256]{3,2,1,0:T(8,128)(2,1)S(1)}, bf16[3,3,64,256]{3,2,1,0:T(8,128)(2,1)}, u32[]{:S(2)}) %copy-start.1) | copy-done | bytes 294936
  19.8 0.0 copy-start.3
  19.8 0.1 hold.1
  19.9 1.9 %collective-permute-start.5 = (bf16[9,64,256]{2,1,0:T(8,128)(2,1)S(1)}, bf16[9,64,256]{2,1,0:T(8,128)(2,1)S(1)}, u32[]{:S(2)}, u32[]{:S(2)}) collective-permute-start(bf16[9,64,256]{2,1,0:T(8,128)(2,1)S(1)} %hold.1), channel_id=1, source_target_pairs={{0,4},{2,6},{4,0},{6,2},{1,5},{3,7},{5,1},{7,3},{8,12},{10,14},{12... | collective-permute-start | bytes 884744 | tf_op jit(solution)/shard_map/ppermute | solution.py:560
  21.8 1.6 %collective-permute-start.3 = (bf16[9,64,256]{2,1,0:T(8,128)(2,1)S(1)}, bf16[9,64,256]{2,1,0:T(8,128)(2,1)S(1)}, u32[]{:S(2)}, u32[]{:S(2)}) collective-permute-start(bf16[9,64,256]{2,1,0:T(8,128)(2,1)S(1)} %hold.1), channel_id=1, source_target_pairs={{0,2},{1,7},{2,4},{3,1},{4,6},{5,3},{6,0},{7,5},{8,10},{9,15},{10,... | collective-permute-start | bytes 884744 | tf_op jit(solution)/shard_map/ppermute | solution.py:560
  23.4 0.1 pad_add_fusion.place._.refs_1_
  23.5 0.0 collective-permute-done.1.swapped
  23.5 0.0 copy-done
  23.5 5.8 %window.2 = (bf16[24,6,16,256]{3,2,1,0:T(8,128)(2,1)}, f32[8,128]{1,0:T(8,128)S(1)}) custom-call(s32[4]{0:T(128)S(1)} %pad_add_fusion.place._.refs_1_, bf16[9,64,256]{2,1,0:T(8,128)(2,1)S(1)} %bitcast.13, bf16[9,64,256]{2,1,0:T(8,128)(2,1)S(1)} %collective-permute-done.refs_1_.near.refs_0_, bf16[9,64,256]{2,1,0:T(8,128)(2,1)S(1)} %collective-permute-done.1.swapped, ...), custom_call_target="tpu_custom_call" | custom-call | flops 1100000000 | bytes 1048576 | tf_op jit(solution)/shard_map/window/pallas_call | solution.py:469
  29.3 0.6 %all-to-all-done.received = bf16[8,9,16,128]{3,2,1,0:T(8,128)(2,1)S(1)} async-done(((bf16[8,9,16,128]{3,2,1,0:T(8,128)(2,1)}), bf16[8,9,16,128]{3,2,1,0:T(8,128)(2,1)S(1)}, u32[]{:S(2)}, u32[]{:S(2)}) %all-to-all-start) | async-done | bytes 294944 | tf_op jit(solution)/shard_map/all_to_all | solution.py:593
  29.8 0.0 copy-done.3
  29.8 1.5 %relay.1 = (bf16[16,4,16,128]{3,2,1,0:T(8,128)(2,1)}, f32[8,128]{1,0:T(8,128)S(1)}) custom-call(s32[4]{0:T(128)S(1)} %pad_add_fusion.place._.refs_1_, f32[1,64]{1,0:T(1,128)S(1)} %bitcast.19, bf16[8,9,16,128]{3,2,1,0:T(8,128)(2,1)S(1)} %all-to-all-done.received, f32[8,128]{1,0:T(8,128)S(1)} %get-tuple-element.10.token), custom_call_target="tpu_custom_call" | custom-call | flops 1100000000 | bytes 1048576 | tf_op jit(solution)/shard_map/relay/pallas_call | solution.py:511
  31.3 5.5 %all-to-all-start.1 = ((bf16[16,4,16,128]{3,2,1,0:T(8,128)(2,1)}), bf16[16,4,16,128]{3,2,1,0:T(8,128)(2,1)S(1)}, u32[]{:S(2)}, u32[]{:S(2)}) async-start(bf16[16,4,16,128]{3,2,1,0:T(8,128)(2,1)} %get-tuple-element.11), calls=%async_computation.1 | async-start | bytes 524288 | tf_op jit(solution)/shard_map/all_to_all | solution.py:600
  36.8 0.0 collective-permute-done.3.refs_0_
  36.9 0.1 collective-permute-start.4
  37.0 0.0 collective-permute-done.5.refs_0_
  37.0 3.5 %window.3 = (bf16[8,6,16,256]{3,2,1,0:T(8,128)(2,1)S(1)}, f32[8,128]{1,0:T(8,128)}) custom-call(s32[4]{0:T(128)S(1)} %pad_add_fusion.place._.refs_1_, bf16[9,64,256]{2,1,0:T(8,128)(2,1)S(1)} %bitcast.14, bf16[9,64,256]{2,1,0:T(8,128)(2,1)S(1)} %collective-permute-done.refs_1_.near.refs_0_, bf16[9,64,256]{2,1,0:T(8,128)(2,1)S(1)} %collective-permute-done.1.swapped, ...), custom_call_target="tpu_custom_call" | custom-call | flops 1100000000 | bytes 1048576 | tf_op jit(solution)/shard_map/window/pallas_call | solution.py:469
  40.5 0.0 copy-start.2
  40.5 0.0 copy-start.4
  40.5 4.8 %all-to-all-done.1.refs_0_ = bf16[16,4,16,128]{3,2,1,0:T(8,128)(2,1)S(1)} async-done(((bf16[16,4,16,128]{3,2,1,0:T(8,128)(2,1)}), bf16[16,4,16,128]{3,2,1,0:T(8,128)(2,1)S(1)}, u32[]{:S(2)}, u32[]{:S(2)}) %all-to-all-start.1) | async-done | bytes 262176 | tf_op jit(solution)/shard_map/all_to_all | solution.py:600
  45.3 0.0 collective-permute-done.4.swapped
  45.3 0.0 copy-done.2
  45.3 0.0 copy-done.4
  45.3 6.3 %read_out.1 = bf16[32,4,16,256]{3,2,1,0:T(8,128)(2,1)} custom-call(s32[4]{0:T(128)S(1)} %pad_add_fusion.place._.refs_1_, f32[32]{0:T(128)S(1)} %copy-done.4, f32[1,256]{1,0:T(1,128)S(1)} %bitcast.17, bf16[16,4,16,128]{3,2,1,0:T(8,128)(2,1)S(1)} %after.5.received, bf16[24,6,16,256]{3,2,1,0:T(8,128)(2,1)} %get-tuple-element.12.early, ...), custom_call_target="tpu_custom_call" | custom-call | flops 6600000000 | bytes 1048576 | tf_op jit(solution)/shard_map/read_out/pallas_call | solution.py:526
  (4 shorter events, 0.0 us)
Async XLA Ops:
  0.0 19.0 %collective-permute-start.2 = (bf16[9,64,256]{2,1,0:T(8,128)(2,1)}, bf16[9,64,256]{2,1,0:T(8,128)(2,1)S(1)}, u32[]{:S(2)}, u32[]{:S(2)}) collective-permute-start(bf16[9,64,256]{2,1,0:T(8,128)(2,1)} %bitcast.10), channel_id=1, source_target_pairs={{0,4},{2,6},{4,0},{6,2},{1,5},{3,7},{5,1},{7,3},{8,12},{10,14},{12... | collective-permute-start | bytes 884744 | tf_op jit(solution)/shard_map/ppermute | solution.py:560
  3.2 15.7 %collective-permute-start = (bf16[9,64,256]{2,1,0:T(8,128)(2,1)}, bf16[9,64,256]{2,1,0:T(8,128)(2,1)S(1)}, u32[]{:S(2)}, u32[]{:S(2)}) collective-permute-start(bf16[9,64,256]{2,1,0:T(8,128)(2,1)} %bitcast.11), channel_id=1, source_target_pairs={{0,2},{1,7},{2,4},{3,1},{4,6},{5,3},{6,0},{7,5},{8,10},{9,15},{10,... | collective-permute-start | bytes 884744 | tf_op jit(solution)/shard_map/ppermute | solution.py:560
  10.3 19.5 %all-to-all-start = ((bf16[8,9,16,128]{3,2,1,0:T(8,128)(2,1)}), bf16[8,9,16,128]{3,2,1,0:T(8,128)(2,1)S(1)}, u32[]{:S(2)}, u32[]{:S(2)}) async-start(bf16[8,9,16,128]{3,2,1,0:T(8,128)(2,1)} %drive.1), calls=%async_computation | async-start | bytes 589824 | tf_op jit(solution)/shard_map/all_to_all | solution.py:593
  18.9 1.0 %copy-start.1 = (bf16[3,3,64,256]{3,2,1,0:T(8,128)(2,1)S(1)}, bf16[3,3,64,256]{3,2,1,0:T(8,128)(2,1)}, u32[]{:S(2)}) copy-start(bf16[3,3,64,256]{3,2,1,0:T(8,128)(2,1)} %param.10) | copy-start | bytes 884740
  18.9 4.6 %copy-start = (bf16[3,3,256,64]{2,3,1,0:T(8,128)(2,1)S(1)}, bf16[3,3,256,64]{2,3,1,0:T(8,128)(2,1)}, u32[]{:S(2)}) copy-start(bf16[3,3,256,64]{2,3,1,0:T(8,128)(2,1)} %param.9) | copy-start | bytes 884740
  18.9 4.6 %collective-permute-start.1 = (bf16[9,64,256]{2,1,0:T(8,128)(2,1)S(1)}, bf16[9,64,256]{2,1,0:T(8,128)(2,1)S(1)}, u32[]{:S(2)}, u32[]{:S(2)}) collective-permute-start(bf16[9,64,256]{2,1,0:T(8,128)(2,1)S(1)} %collective-permute-done.refs_1_.near.refs_0_), channel_id=1, source_target_pairs={{0,1},{1,0},{2,3},{3,2},{4,5},{5,4},{6,7},{7,6},{8,9},{9,8},{10,11... | collective-permute-start | bytes 884744 | tf_op jit(solution)/shard_map/ppermute | solution.py:581
  19.8 10.0 %copy-start.3 = (f32[64]{0:T(128)S(1)}, f32[64]{0:T(128)}, u32[]{:S(2)}) copy-start(f32[64]{0:T(128)} %param.8) | copy-start | bytes 772
  19.9 17.0 %collective-permute-start.5 = (bf16[9,64,256]{2,1,0:T(8,128)(2,1)S(1)}, bf16[9,64,256]{2,1,0:T(8,128)(2,1)S(1)}, u32[]{:S(2)}, u32[]{:S(2)}) collective-permute-start(bf16[9,64,256]{2,1,0:T(8,128)(2,1)S(1)} %hold.1), channel_id=1, source_target_pairs={{0,4},{2,6},{4,0},{6,2},{1,5},{3,7},{5,1},{7,3},{8,12},{10,14},{12... | collective-permute-start | bytes 884744 | tf_op jit(solution)/shard_map/ppermute | solution.py:560
  21.8 15.0 %collective-permute-start.3 = (bf16[9,64,256]{2,1,0:T(8,128)(2,1)S(1)}, bf16[9,64,256]{2,1,0:T(8,128)(2,1)S(1)}, u32[]{:S(2)}, u32[]{:S(2)}) collective-permute-start(bf16[9,64,256]{2,1,0:T(8,128)(2,1)S(1)} %hold.1), channel_id=1, source_target_pairs={{0,2},{1,7},{2,4},{3,1},{4,6},{5,3},{6,0},{7,5},{8,10},{9,15},{10,... | collective-permute-start | bytes 884744 | tf_op jit(solution)/shard_map/ppermute | solution.py:560
  31.3 14.0 %all-to-all-start.1 = ((bf16[16,4,16,128]{3,2,1,0:T(8,128)(2,1)}), bf16[16,4,16,128]{3,2,1,0:T(8,128)(2,1)S(1)}, u32[]{:S(2)}, u32[]{:S(2)}) async-start(bf16[16,4,16,128]{3,2,1,0:T(8,128)(2,1)} %get-tuple-element.11), calls=%async_computation.1 | async-start | bytes 524288 | tf_op jit(solution)/shard_map/all_to_all | solution.py:600
  36.9 8.5 %collective-permute-start.4 = (bf16[9,64,256]{2,1,0:T(8,128)(2,1)S(1)}, bf16[9,64,256]{2,1,0:T(8,128)(2,1)S(1)}, u32[]{:S(2)}, u32[]{:S(2)}) collective-permute-start(bf16[9,64,256]{2,1,0:T(8,128)(2,1)S(1)} %after.6.near), channel_id=1, source_target_pairs={{0,1},{1,0},{2,3},{3,2},{4,5},{5,4},{6,7},{7,6},{8,9},{9,8},{10,11... | collective-permute-start | bytes 884744 | tf_op jit(solution)/shard_map/ppermute | solution.py:581
  40.5 4.8 %copy-start.2 = (f32[256]{0:T(256)S(1)}, f32[256]{0:T(256)}, u32[]{:S(2)}) copy-start(f32[256]{0:T(256)} %param.11) | copy-start | bytes 3076
  40.5 4.8 %copy-start.4 = (f32[32]{0:T(128)S(1)}, f32[32]{0:T(128)}, u32[]{:S(2)}) copy-start(f32[32]{0:T(128)} %intervals_far.3) | copy-start | bytes 388

commit v13 on v10

--- a/solution.py
+++ b/solution.py
@@ -532,7 +532,7 @@
     del refs
 
 
-def after(value, other, length=2):
+def after(value, other, length=0):
     return pl.pallas_call(
         after_kernel,
         out_shape=jax.ShapeDtypeStruct(value.shape, value.dtype),
@@ -556,13 +556,12 @@
     kernel_t = jnp.transpose(in_kernel.reshape(9, CH, OWN), (0, 2, 1))
     out_own = out_kernel.reshape(9, OWN, CH)
     near, out_near = neighbour(kernel_t), neighbour(out_own)
+    far = opposite(kernel_t)
     message = drive(intervals, rates, kernel_t, frames)
     arrived = lax.all_to_all(message, "z", 0, 0)
-    pieces = (kernel_t, near, swap(near), after(opposite(kernel_t), near))
-    out_swapped, out_far = swap(out_near), opposite(out_own)
-    drives, done = window(place, *pieces, frames, out_swapped)
-    out_far = after(out_far, done, 2)
-    out_pieces = (out_own, out_near, out_swapped, out_far)
+    pieces = (kernel_t, near, swap(near), after(far, near, 2))
+    out_pieces = (out_own, out_near, swap(out_near), neighbour(out_near))
+    drives, done = window(place, *pieces, frames, out_pieces[2])
     onward = relay(place, rates, arrived, done, out_pieces[3])
     received = lax.all_to_all(onward, ("x", "chan"), 0, 0)
     skip = skip_gain.reshape(1, CH)

time: 55.2 us -> 52.2 us (0.946)
  waiting for transfers between devices: 3.24 us -> 1.52 us
  starting transfers between devices: 16.2 us -> 14.8 us
    ppermute x2 -> x1, starting transfers between devices: 5.03 us -> 3.19 us  [opposite(): lax.ppermute(value, 'chan', [(c, (c + 2) % CHANS) for c in range(CHANS)])]
    ppermute x2, waiting for transfers between devices: 1.3 us -> 0.01 us  [swap(): return lax.ppermute(value, 'clip', [(0, 1), (1, 0)])]
    ppermute x2 -> x3, waiting for transfers between devices: 0.7 us -> 0.01 us  [neighbour(): return lax.ppermute(value, ('chan', 'clip'), route)]
    ppermute x2 -> x3, starting transfers between devices: 2.25 us -> 2.49 us  [neighbour(): return lax.ppermute(value, ('chan', 'clip'), route)]
  transfers between devices with their start and end apart: 7 -> 7, of which waited for: 4 -> 1; matrix products, arithmetic and copies ran while one was open for 0% -> 0% of each run, Pallas kernels for 24% -> 26%
where the time goes in v13:
time: 52.2 us; the launch traced here: 51.8 us
  Pallas kernels  20.3 us (39%)
  blocking collectives  14.9 us (29%)
  starting transfers between devices  14.8 us (28%)
  waiting for transfers between devices  1.52 us (3%)
    all_to_all x1, blocking collectives, local(): received = lax.all_to_all(onward, ('x', 'chan'), 0, 0)  14.9 us
    all_to_all x1, starting transfers between devices, local(): arrived = lax.all_to_all(message, 'z', 0, 0)  8.58 us
    pallas_call x1, Pallas kernels, window(): pl.pallas_call(window_kernel, out_shape=[jax.ShapeDtypeStruct((FRAMES, WI...  6.9 us
    pallas_call x1, Pallas kernels, drive(): pl.pallas_call(drive_kernel, out_shape=jax.ShapeDtypeStruct((ZS, ROWS //...  6.42 us
    pallas_call x1, Pallas kernels, read_out(): pl.pallas_call(readout_kernel, out_shape=jax.ShapeDtypeStruct((FRAMES, CH...  6.24 us
    ppermute x1, starting transfers between devices, opposite(): lax.ppermute(value, 'chan', [(c, (c + 2) % CHANS) for c in range(CHANS)])  3.19 us
    ppermute x3, starting transfers between devices, neighbour(): return lax.ppermute(value, ('chan', 'clip'), route)  2.49 us
    all_to_all x1, waiting for transfers between devices, local(): arrived = lax.all_to_all(message, 'z', 0, 0)  1.5 us
  transfers between devices with their start and end apart: 7, of which 1 were waited for; matrix products, arithmetic and copies ran while one was open for 0% of the time, Pallas kernels for 26%

profile of v13, /device:TPU:32, one launch (start us, length us, event | category | flops | bytes accessed | tf_op | source)
XLA Modules:
  0.0 51.8 jit_solution(16973750933517225947)
XLA Ops:
  0.0 3.2 %collective-permute-start.2 = (bf16[9,64,256]{2,1,0:T(8,128)(2,1)}, bf16[9,64,256]{2,1,0:T(8,128)(2,1)S(1)}, u32[]{:S(2)}, u32[]{:S(2)}) collective-permute-start(bf16[9,64,256]{2,1,0:T(8,128)(2,1)} %bitcast.10), channel_id=1, source_target_pairs={{0,4},{2,6},{4,0},{6,2},{1,5},{3,7},{5,1},{7,3},{8,12},{10,14},{12... | collective-permute-start | bytes 884744 | tf_op jit(solution)/shard_map/ppermute | solution.py:528
  3.2 0.7 %collective-permute-start = (bf16[9,64,256]{2,1,0:T(8,128)(2,1)}, bf16[9,64,256]{2,1,0:T(8,128)(2,1)S(1)}, u32[]{:S(2)}, u32[]{:S(2)}) collective-permute-start(bf16[9,64,256]{2,1,0:T(8,128)(2,1)} %bitcast.11), channel_id=1, source_target_pairs={{0,2},{1,7},{2,4},{3,1},{4,6},{5,3},{6,0},{7,5},{8,10},{9,15},{10,... | collective-permute-start | bytes 884744 | tf_op jit(solution)/shard_map/ppermute | solution.py:524
  3.9 0.0 collective-permute-start.3
  3.9 6.4 %drive.1 = bf16[8,9,16,128]{3,2,1,0:T(8,128)(2,1)} custom-call(f32[32]{0:T(128)} %intervals_far.3, f32[1,64]{1,0:T(1,128)} %bitcast.17, bf16[9,64,256]{2,1,0:T(8,128)(2,1)} %bitcast.12, bf16[32,16,16,256]{3,2,1,0:T(8,128)(2,1)} %frames.5), custom_call_target="tpu_custom_call" | custom-call | flops 8800000000 | bytes 1048576 | tf_op jit(solution)/shard_map/drive/pallas_call | solution.py:434
  10.3 8.6 %all-to-all-start = ((bf16[8,9,16,128]{3,2,1,0:T(8,128)(2,1)}), bf16[8,9,16,128]{3,2,1,0:T(8,128)(2,1)S(1)}, u32[]{:S(2)}, u32[]{:S(2)}) async-start(bf16[8,9,16,128]{3,2,1,0:T(8,128)(2,1)} %drive.1), calls=%async_computation | async-start | bytes 589824 | tf_op jit(solution)/shard_map/all_to_all | solution.py:561
  18.9 0.0 copy-start
  18.9 0.0 collective-permute-done.refs_1_.near
  18.9 0.1 collective-permute-start.1
  19.0 0.0 collective-permute-done.3.near
  19.0 0.5 collective-permute-start.4
  19.5 0.1 pad_add_fusion.place
  19.6 1.8 %collective-permute-start.5 = (bf16[9,64,256]{2,1,0:T(8,128)(2,1)S(1)}, bf16[9,64,256]{2,1,0:T(8,128)(2,1)S(1)}, u32[]{:S(2)}, u32[]{:S(2)}) collective-permute-start(bf16[9,64,256]{2,1,0:T(8,128)(2,1)S(1)} %collective-permute-done.3.near), channel_id=1, source_target_pairs={{0,2},{1,7},{2,4},{3,1},{4,6},{5,3},{6,0},{7,5},{8,10},{9,15},{10,... | collective-permute-start | bytes 884744 | tf_op jit(solution)/shard_map/ppermute | solution.py:524
  21.4 0.0 collective-permute-done.2.refs_0_
  21.4 0.0 copy-start.3
  21.4 0.0 copy-start.1
  21.4 0.0 copy-start.2
  21.4 0.0 copy-start.4
  21.4 0.0 collective-permute-done.1.swapped
  21.4 0.0 collective-permute-done.4.later.swapped
  21.4 0.0 copy-done
  21.4 6.9 %window.1 = (bf16[32,6,16,256]{3,2,1,0:T(8,128)(2,1)}, f32[8,128]{1,0:T(8,128)S(1)}) custom-call(s32[4]{0:T(128)S(1)} %pad_add_fusion.place, bf16[9,64,256]{2,1,0:T(8,128)(2,1)S(1)} %bitcast.13, bf16[9,64,256]{2,1,0:T(8,128)(2,1)S(1)} %collective-permute-done.refs_1_.near, bf16[9,64,256]{2,1,0:T(8,128)(2,1)S(1)} %collective-permute-done.1.swapped, ...), custom_call_target="tpu_custom_call" | custom-call | flops 1100000000 | bytes 1048576 | tf_op jit(solution)/shard_map/window/pallas_call | solution.py:457
  28.4 1.5 %all-to-all-done.received = bf16[8,9,16,128]{3,2,1,0:T(8,128)(2,1)S(1)} async-done(((bf16[8,9,16,128]{3,2,1,0:T(8,128)(2,1)}), bf16[8,9,16,128]{3,2,1,0:T(8,128)(2,1)S(1)}, u32[]{:S(2)}, u32[]{:S(2)}) %all-to-all-start) | async-done | bytes 294944 | tf_op jit(solution)/shard_map/all_to_all | solution.py:561
  29.9 0.0 collective-permute-done.5.later.far
  29.9 0.0 copy-done.3
  29.9 0.8 %relay.1 = bf16[16,4,16,128]{3,2,1,0:T(8,128)(2,1)S(1)} custom-call(s32[4]{0:T(128)S(1)} %pad_add_fusion.place, f32[1,64]{1,0:T(1,128)S(1)} %bitcast.18, bf16[8,9,16,128]{3,2,1,0:T(8,128)(2,1)S(1)} %all-to-all-done.received, f32[8,128]{1,0:T(8,128)S(1)} %get-tuple-element.7.token, bf16[9,64,256]{2,1,0:T(8,128)(2,1)S(1)} %collective-permute-done.5.later.far), custom_call_target="tpu_custom_call" | custom-call | flops 1100000000 | bytes 1048576 | tf_op jit(solution)/shard_map/relay/pallas_call | solution.py:479
  30.6 14.9 %all_to_all.10.received = bf16[16,4,16,128]{3,2,1,0:T(8,128)(2,1)S(1)} all-to-all(bf16[16,4,16,128]{3,2,1,0:T(8,128)(2,1)S(1)} %relay.1), channel_id=1, replica_groups=mesh['x'=4,'z'=8,'chan'=4,'clip'=2] {'x','chan'}, dimensions={0} | all-to-all | bytes 524288 | tf_op jit(solution)/shard_map/all_to_all | solution.py:566
  45.5 0.0 copy-done.1
  45.5 0.0 copy-done.2
  45.5 0.0 copy-done.4
  45.5 6.2 %read_out.1 = bf16[32,4,16,256]{3,2,1,0:T(8,128)(2,1)} custom-call(s32[4]{0:T(128)S(1)} %pad_add_fusion.place, f32[32]{0:T(128)S(1)} %copy-done.4, f32[1,256]{1,0:T(1,128)S(1)} %bitcast.16, bf16[16,4,16,128]{3,2,1,0:T(8,128)(2,1)S(1)} %all_to_all.10.received, bf16[32,6,16,256]{3,2,1,0:T(8,128)(2,1)} %get-tuple-element.8.drives_far, ...), custom_call_target="tpu_custom_call" | custom-call | flops 6600000000 | bytes 1048576 | tf_op jit(solution)/shard_map/read_out/pallas_call | solution.py:491
  (1 shorter events, 0.0 us)
Async XLA Ops:
  0.0 21.4 %collective-permute-start.2 = (bf16[9,64,256]{2,1,0:T(8,128)(2,1)}, bf16[9,64,256]{2,1,0:T(8,128)(2,1)S(1)}, u32[]{:S(2)}, u32[]{:S(2)}) collective-permute-start(bf16[9,64,256]{2,1,0:T(8,128)(2,1)} %bitcast.10), channel_id=1, source_target_pairs={{0,4},{2,6},{4,0},{6,2},{1,5},{3,7},{5,1},{7,3},{8,12},{10,14},{12... | collective-permute-start | bytes 884744 | tf_op jit(solution)/shard_map/ppermute | solution.py:528
  3.2 15.7 %collective-permute-start = (bf16[9,64,256]{2,1,0:T(8,128)(2,1)}, bf16[9,64,256]{2,1,0:T(8,128)(2,1)S(1)}, u32[]{:S(2)}, u32[]{:S(2)}) collective-permute-start(bf16[9,64,256]{2,1,0:T(8,128)(2,1)} %bitcast.11), channel_id=1, source_target_pairs={{0,2},{1,7},{2,4},{3,1},{4,6},{5,3},{6,0},{7,5},{8,10},{9,15},{10,... | collective-permute-start | bytes 884744 | tf_op jit(solution)/shard_map/ppermute | solution.py:524
  3.9 15.2 %collective-permute-start.3 = (bf16[9,64,256]{2,1,0:T(8,128)(2,1)}, bf16[9,64,256]{2,1,0:T(8,128)(2,1)S(1)}, u32[]{:S(2)}, u32[]{:S(2)}) collective-permute-start(bf16[9,64,256]{2,1,0:T(8,128)(2,1)} %bitcast.14), channel_id=1, source_target_pairs={{0,2},{1,7},{2,4},{3,1},{4,6},{5,3},{6,0},{7,5},{8,10},{9,15},{10,... | collective-permute-start | bytes 884744 | tf_op jit(solution)/shard_map/ppermute | solution.py:524
  10.3 19.5 %all-to-all-start = ((bf16[8,9,16,128]{3,2,1,0:T(8,128)(2,1)}), bf16[8,9,16,128]{3,2,1,0:T(8,128)(2,1)S(1)}, u32[]{:S(2)}, u32[]{:S(2)}) async-start(bf16[8,9,16,128]{3,2,1,0:T(8,128)(2,1)} %drive.1), calls=%async_computation | async-start | bytes 589824 | tf_op jit(solution)/shard_map/all_to_all | solution.py:561
  18.9 2.5 %copy-start = (bf16[3,3,256,64]{2,3,1,0:T(8,128)(2,1)S(1)}, bf16[3,3,256,64]{2,3,1,0:T(8,128)(2,1)}, u32[]{:S(2)}) copy-start(bf16[3,3,256,64]{2,3,1,0:T(8,128)(2,1)} %param.9) | copy-start | bytes 884740
  18.9 2.5 %collective-permute-start.1 = (bf16[9,64,256]{2,1,0:T(8,128)(2,1)S(1)}, bf16[9,64,256]{2,1,0:T(8,128)(2,1)S(1)}, u32[]{:S(2)}, u32[]{:S(2)}) collective-permute-start(bf16[9,64,256]{2,1,0:T(8,128)(2,1)S(1)} %collective-permute-done.refs_1_.near), channel_id=1, source_target_pairs={{0,1},{1,0},{2,3},{3,2},{4,5},{5,4},{6,7},{7,6},{8,9},{9,8},{10,11... | collective-permute-start | bytes 884744 | tf_op jit(solution)/shard_map/ppermute | solution.py:549
  19.0 2.4 %collective-permute-start.4 = (bf16[9,64,256]{2,1,0:T(8,128)(2,1)S(1)}, bf16[9,64,256]{2,1,0:T(8,128)(2,1)S(1)}, u32[]{:S(2)}, u32[]{:S(2)}) collective-permute-start(bf16[9,64,256]{2,1,0:T(8,128)(2,1)S(1)} %collective-permute-done.3.near), channel_id=1, source_target_pairs={{0,1},{1,0},{2,3},{3,2},{4,5},{5,4},{6,7},{7,6},{8,9},{9,8},{10,11... | collective-permute-start | bytes 884744 | tf_op jit(solution)/shard_map/ppermute | solution.py:549
  19.6 10.3 %collective-permute-start.5 = (bf16[9,64,256]{2,1,0:T(8,128)(2,1)S(1)}, bf16[9,64,256]{2,1,0:T(8,128)(2,1)S(1)}, u32[]{:S(2)}, u32[]{:S(2)}) collective-permute-start(bf16[9,64,256]{2,1,0:T(8,128)(2,1)S(1)} %collective-permute-done.3.near), channel_id=1, source_target_pairs={{0,2},{1,7},{2,4},{3,1},{4,6},{5,3},{6,0},{7,5},{8,10},{9,15},{10,... | collective-permute-start | bytes 884744 | tf_op jit(solution)/shard_map/ppermute | solution.py:524
  21.4 8.5 %copy-start.3 = (f32[64]{0:T(128)S(1)}, f32[64]{0:T(128)}, u32[]{:S(2)}) copy-start(f32[64]{0:T(128)} %param.8) | copy-start | bytes 772
  21.4 24.1 %copy-start.1 = (bf16[3,3,64,256]{3,2,1,0:T(8,128)(2,1)S(1)}, bf16[3,3,64,256]{3,2,1,0:T(8,128)(2,1)}, u32[]{:S(2)}) copy-start(bf16[3,3,64,256]{3,2,1,0:T(8,128)(2,1)} %param.10) | copy-start | bytes 884740
  21.4 24.1 %copy-start.2 = (f32[256]{0:T(256)S(1)}, f32[256]{0:T(256)}, u32[]{:S(2)}) copy-start(f32[256]{0:T(256)} %param.11) | copy-start | bytes 3076
  21.4 24.1 %copy-start.4 = (f32[32]{0:T(128)S(1)}, f32[32]{0:T(128)}, u32[]{:S(2)}) copy-start(f32[32]{0:T(128)} %intervals_far.3) | copy-start | bytes 388

commit v14 on v13

--- a/solution.py
+++ b/solution.py
@@ -276,9 +276,9 @@
         mine = z == other
         before = jnp.where(mine, total, before)
         elapsed_before = jnp.where(mine, elapsed, elapsed_before)
-        spent = join3(received[other, ROWS // 2], 0)
+        spent = join3(received[ZS - 1 - other, ROWS // 2], 0)
         decay = jnp.exp(-spent * rate).reshape(1, 1, LANES)
-        total = decay * total + received[other, : ROWS // 2].astype(F32)
+        total = decay * total + received[ZS - 1 - other, : ROWS // 2].astype(F32)
         elapsed = elapsed + spent
 
     low = low_half((WIDE, LANES))
@@ -558,7 +558,8 @@
     near, out_near = neighbour(kernel_t), neighbour(out_own)
     far = opposite(kernel_t)
     message = drive(intervals, rates, kernel_t, frames)
-    arrived = lax.all_to_all(message, "z", 0, 0)
+    backwards = [list(reversed(range(ZS)))]
+    arrived = lax.all_to_all(message, "z", 0, 0, axis_index_groups=backwards)
     pieces = (kernel_t, near, swap(near), after(far, near, 2))
     out_pieces = (out_own, out_near, swap(out_near), neighbour(out_near))
     drives, done = window(place, *pieces, frames, out_pieces[2])

time: 52.2 us -> 51.9 us (level)
  waiting for transfers between devices: 1.52 us -> 0.02 us
  blocking collectives: 14.9 us -> 16 us
    all_to_all x1, waiting for transfers between devices: 1.5 us -> 0.01 us  [local(): arrived = lax.all_to_all(message, 'z', 0, 0, axis_index_groups=backwards)]
    all_to_all x1, blocking collectives: 14.9 us -> 16 us  [local(): received = lax.all_to_all(onward, ('x', 'chan'), 0, 0)]
  transfers between devices with their start and end apart: 7 -> 7, of which waited for: 1 -> 0; matrix products, arithmetic and copies ran while one was open for 0% -> 0% of each run, Pallas kernels for 26% -> 26%
where the time goes in v14:
time: 51.9 us; the launch traced here: 51.6 us
  Pallas kernels  20.3 us (39%)
  blocking collectives  16 us (31%)
  starting transfers between devices  15 us (29%)
    all_to_all x1, blocking collectives, local(): received = lax.all_to_all(onward, ('x', 'chan'), 0, 0)  16 us
    all_to_all x1, starting transfers between devices, local(): arrived = lax.all_to_all(message, 'z', 0, 0, axis_index_groups=backwards)  8.77 us
    pallas_call x1, Pallas kernels, window(): pl.pallas_call(window_kernel, out_shape=[jax.ShapeDtypeStruct((FRAMES, WI...  6.9 us
    pallas_call x1, Pallas kernels, drive(): pl.pallas_call(drive_kernel, out_shape=jax.ShapeDtypeStruct((ZS, ROWS //...  6.42 us
    pallas_call x1, Pallas kernels, read_out(): pl.pallas_call(readout_kernel, out_shape=jax.ShapeDtypeStruct((FRAMES, CH...  6.25 us
    ppermute x1, starting transfers between devices, opposite(): lax.ppermute(value, 'chan', [(c, (c + 2) % CHANS) for c in range(CHANS)])  3.19 us
    ppermute x3, starting transfers between devices, neighbour(): return lax.ppermute(value, ('chan', 'clip'), route)  2.49 us
  transfers between devices with their start and end apart: 7, of which 0 were waited for; matrix products, arithmetic and copies ran while one was open for 0% of the time, Pallas kernels for 26%

profile of v14, /device:TPU:32, one launch (start us, length us, event | category | flops | bytes accessed | tf_op | source)
XLA Modules:
  0.0 51.6 jit_solution(6766412021693532255)
XLA Ops:
  0.0 3.2 %collective-permute-start.2 = (bf16[9,64,256]{2,1,0:T(8,128)(2,1)}, bf16[9,64,256]{2,1,0:T(8,128)(2,1)S(1)}, u32[]{:S(2)}, u32[]{:S(2)}) collective-permute-start(bf16[9,64,256]{2,1,0:T(8,128)(2,1)} %bitcast.10), channel_id=1, source_target_pairs={{0,4},{2,6},{4,0},{6,2},{1,5},{3,7},{5,1},{7,3},{8,12},{10,14},{12... | collective-permute-start | bytes 884744 | tf_op jit(solution)/shard_map/ppermute | solution.py:528
  3.2 0.7 %collective-permute-start = (bf16[9,64,256]{2,1,0:T(8,128)(2,1)}, bf16[9,64,256]{2,1,0:T(8,128)(2,1)S(1)}, u32[]{:S(2)}, u32[]{:S(2)}) collective-permute-start(bf16[9,64,256]{2,1,0:T(8,128)(2,1)} %bitcast.11), channel_id=1, source_target_pairs={{0,2},{1,7},{2,4},{3,1},{4,6},{5,3},{6,0},{7,5},{8,10},{9,15},{10,... | collective-permute-start | bytes 884744 | tf_op jit(solution)/shard_map/ppermute | solution.py:524
  3.9 0.0 collective-permute-start.3
  3.9 6.4 %drive.1 = bf16[8,9,16,128]{3,2,1,0:T(8,128)(2,1)} custom-call(f32[32]{0:T(128)} %intervals_far.3, f32[1,64]{1,0:T(1,128)} %bitcast.17, bf16[9,64,256]{2,1,0:T(8,128)(2,1)} %bitcast.12, bf16[32,16,16,256]{3,2,1,0:T(8,128)(2,1)} %frames.5), custom_call_target="tpu_custom_call" | custom-call | flops 8800000000 | bytes 1048576 | tf_op jit(solution)/shard_map/drive/pallas_call | solution.py:434
  10.3 8.8 %all-to-all-start = ((bf16[8,9,16,128]{3,2,1,0:T(8,128)(2,1)}), bf16[8,9,16,128]{3,2,1,0:T(8,128)(2,1)S(1)}, u32[]{:S(2)}, u32[]{:S(2)}) async-start(bf16[8,9,16,128]{3,2,1,0:T(8,128)(2,1)} %drive.1), calls=%async_computation | async-start | bytes 589824 | tf_op jit(solution)/shard_map/all_to_all | solution.py:562
  19.1 0.0 copy-start
  19.1 0.0 collective-permute-done.refs_1_.near
  19.1 0.1 collective-permute-start.1
  19.2 0.0 collective-permute-done.3.near
  19.2 0.5 collective-permute-start.4
  19.7 0.1 pad_add_fusion.place
  19.8 1.8 %collective-permute-start.5 = (bf16[9,64,256]{2,1,0:T(8,128)(2,1)S(1)}, bf16[9,64,256]{2,1,0:T(8,128)(2,1)S(1)}, u32[]{:S(2)}, u32[]{:S(2)}) collective-permute-start(bf16[9,64,256]{2,1,0:T(8,128)(2,1)S(1)} %collective-permute-done.3.near), channel_id=1, source_target_pairs={{0,2},{1,7},{2,4},{3,1},{4,6},{5,3},{6,0},{7,5},{8,10},{9,15},{10,... | collective-permute-start | bytes 884744 | tf_op jit(solution)/shard_map/ppermute | solution.py:524
  21.6 0.0 collective-permute-done.2.refs_0_
  21.6 0.0 copy-start.3
  21.6 0.0 copy-start.1
  21.6 0.0 copy-start.2
  21.6 0.0 copy-start.4
  21.6 0.0 collective-permute-done.1.swapped
  21.6 0.0 collective-permute-done.4.later.swapped
  21.6 0.0 copy-done
  21.6 6.9 %window.1 = (bf16[32,6,16,256]{3,2,1,0:T(8,128)(2,1)}, f32[8,128]{1,0:T(8,128)S(1)}) custom-call(s32[4]{0:T(128)S(1)} %pad_add_fusion.place, bf16[9,64,256]{2,1,0:T(8,128)(2,1)S(1)} %bitcast.13, bf16[9,64,256]{2,1,0:T(8,128)(2,1)S(1)} %collective-permute-done.refs_1_.near, bf16[9,64,256]{2,1,0:T(8,128)(2,1)S(1)} %collective-permute-done.1.swapped, ...), custom_call_target="tpu_custom_call" | custom-call | flops 1100000000 | bytes 1048576 | tf_op jit(solution)/shard_map/window/pallas_call | solution.py:457
  28.5 0.0 all-to-all-done.received
  28.6 0.0 collective-permute-done.5.later.far
  28.6 0.0 copy-done.3
  28.6 0.8 %relay.1 = bf16[16,4,16,128]{3,2,1,0:T(8,128)(2,1)S(1)} custom-call(s32[4]{0:T(128)S(1)} %pad_add_fusion.place, f32[1,64]{1,0:T(1,128)S(1)} %bitcast.18, bf16[8,9,16,128]{3,2,1,0:T(8,128)(2,1)S(1)} %all-to-all-done.received, f32[8,128]{1,0:T(8,128)S(1)} %get-tuple-element.7.token, bf16[9,64,256]{2,1,0:T(8,128)(2,1)S(1)} %collective-permute-done.5.later.far), custom_call_target="tpu_custom_call" | custom-call | flops 1100000000 | bytes 1048576 | tf_op jit(solution)/shard_map/relay/pallas_call | solution.py:479
  29.4 16.0 %all_to_all.10.received = bf16[16,4,16,128]{3,2,1,0:T(8,128)(2,1)S(1)} all-to-all(bf16[16,4,16,128]{3,2,1,0:T(8,128)(2,1)S(1)} %relay.1), channel_id=1, replica_groups=mesh['x'=4,'z'=8,'chan'=4,'clip'=2] {'x','chan'}, dimensions={0} | all-to-all | bytes 524288 | tf_op jit(solution)/shard_map/all_to_all | solution.py:567
  45.4 0.0 copy-done.1
  45.4 0.0 copy-done.2
  45.4 0.0 copy-done.4
  45.4 6.2 %read_out.1 = bf16[32,4,16,256]{3,2,1,0:T(8,128)(2,1)} custom-call(s32[4]{0:T(128)S(1)} %pad_add_fusion.place, f32[32]{0:T(128)S(1)} %copy-done.4, f32[1,256]{1,0:T(1,128)S(1)} %bitcast.16, bf16[16,4,16,128]{3,2,1,0:T(8,128)(2,1)S(1)} %all_to_all.10.received, bf16[32,6,16,256]{3,2,1,0:T(8,128)(2,1)} %get-tuple-element.8.drives_far, ...), custom_call_target="tpu_custom_call" | custom-call | flops 6600000000 | bytes 1048576 | tf_op jit(solution)/shard_map/read_out/pallas_call | solution.py:491
  (1 shorter events, 0.0 us)
Async XLA Ops:
  0.0 21.6 %collective-permute-start.2 = (bf16[9,64,256]{2,1,0:T(8,128)(2,1)}, bf16[9,64,256]{2,1,0:T(8,128)(2,1)S(1)}, u32[]{:S(2)}, u32[]{:S(2)}) collective-permute-start(bf16[9,64,256]{2,1,0:T(8,128)(2,1)} %bitcast.10), channel_id=1, source_target_pairs={{0,4},{2,6},{4,0},{6,2},{1,5},{3,7},{5,1},{7,3},{8,12},{10,14},{12... | collective-permute-start | bytes 884744 | tf_op jit(solution)/shard_map/ppermute | solution.py:528
  3.2 15.9 %collective-permute-start = (bf16[9,64,256]{2,1,0:T(8,128)(2,1)}, bf16[9,64,256]{2,1,0:T(8,128)(2,1)S(1)}, u32[]{:S(2)}, u32[]{:S(2)}) collective-permute-start(bf16[9,64,256]{2,1,0:T(8,128)(2,1)} %bitcast.11), channel_id=1, source_target_pairs={{0,2},{1,7},{2,4},{3,1},{4,6},{5,3},{6,0},{7,5},{8,10},{9,15},{10,... | collective-permute-start | bytes 884744 | tf_op jit(solution)/shard_map/ppermute | solution.py:524
  3.9 15.3 %collective-permute-start.3 = (bf16[9,64,256]{2,1,0:T(8,128)(2,1)}, bf16[9,64,256]{2,1,0:T(8,128)(2,1)S(1)}, u32[]{:S(2)}, u32[]{:S(2)}) collective-permute-start(bf16[9,64,256]{2,1,0:T(8,128)(2,1)} %bitcast.14), channel_id=1, source_target_pairs={{0,2},{1,7},{2,4},{3,1},{4,6},{5,3},{6,0},{7,5},{8,10},{9,15},{10,... | collective-permute-start | bytes 884744 | tf_op jit(solution)/shard_map/ppermute | solution.py:524
  10.3 18.2 %all-to-all-start = ((bf16[8,9,16,128]{3,2,1,0:T(8,128)(2,1)}), bf16[8,9,16,128]{3,2,1,0:T(8,128)(2,1)S(1)}, u32[]{:S(2)}, u32[]{:S(2)}) async-start(bf16[8,9,16,128]{3,2,1,0:T(8,128)(2,1)} %drive.1), calls=%async_computation | async-start | bytes 589824 | tf_op jit(solution)/shard_map/all_to_all | solution.py:562
  19.1 2.5 %copy-start = (bf16[3,3,256,64]{2,3,1,0:T(8,128)(2,1)S(1)}, bf16[3,3,256,64]{2,3,1,0:T(8,128)(2,1)}, u32[]{:S(2)}) copy-start(bf16[3,3,256,64]{2,3,1,0:T(8,128)(2,1)} %param.9) | copy-start | bytes 884740
  19.1 2.5 %collective-permute-start.1 = (bf16[9,64,256]{2,1,0:T(8,128)(2,1)S(1)}, bf16[9,64,256]{2,1,0:T(8,128)(2,1)S(1)}, u32[]{:S(2)}, u32[]{:S(2)}) collective-permute-start(bf16[9,64,256]{2,1,0:T(8,128)(2,1)S(1)} %collective-permute-done.refs_1_.near), channel_id=1, source_target_pairs={{0,1},{1,0},{2,3},{3,2},{4,5},{5,4},{6,7},{7,6},{8,9},{9,8},{10,11... | collective-permute-start | bytes 884744 | tf_op jit(solution)/shard_map/ppermute | solution.py:549
  19.2 2.4 %collective-permute-start.4 = (bf16[9,64,256]{2,1,0:T(8,128)(2,1)S(1)}, bf16[9,64,256]{2,1,0:T(8,128)(2,1)S(1)}, u32[]{:S(2)}, u32[]{:S(2)}) collective-permute-start(bf16[9,64,256]{2,1,0:T(8,128)(2,1)S(1)} %collective-permute-done.3.near), channel_id=1, source_target_pairs={{0,1},{1,0},{2,3},{3,2},{4,5},{5,4},{6,7},{7,6},{8,9},{9,8},{10,11... | collective-permute-start | bytes 884744 | tf_op jit(solution)/shard_map/ppermute | solution.py:549
  19.8 8.8 %collective-permute-start.5 = (bf16[9,64,256]{2,1,0:T(8,128)(2,1)S(1)}, bf16[9,64,256]{2,1,0:T(8,128)(2,1)S(1)}, u32[]{:S(2)}, u32[]{:S(2)}) collective-permute-start(bf16[9,64,256]{2,1,0:T(8,128)(2,1)S(1)} %collective-permute-done.3.near), channel_id=1, source_target_pairs={{0,2},{1,7},{2,4},{3,1},{4,6},{5,3},{6,0},{7,5},{8,10},{9,15},{10,... | collective-permute-start | bytes 884744 | tf_op jit(solution)/shard_map/ppermute | solution.py:524
  21.6 7.0 %copy-start.3 = (f32[64]{0:T(128)S(1)}, f32[64]{0:T(128)}, u32[]{:S(2)}) copy-start(f32[64]{0:T(128)} %param.8) | copy-start | bytes 772
  21.6 23.8 %copy-start.1 = (bf16[3,3,64,256]{3,2,1,0:T(8,128)(2,1)S(1)}, bf16[3,3,64,256]{3,2,1,0:T(8,128)(2,1)}, u32[]{:S(2)}) copy-start(bf16[3,3,64,256]{3,2,1,0:T(8,128)(2,1)} %param.10) | copy-start | bytes 884740
  21.6 23.8 %copy-start.2 = (f32[256]{0:T(256)S(1)}, f32[256]{0:T(256)}, u32[]{:S(2)}) copy-start(f32[256]{0:T(256)} %param.11) | copy-start | bytes 3076
  21.6 23.8 %copy-start.4 = (f32[32]{0:T(128)S(1)}, f32[32]{0:T(128)}, u32[]{:S(2)}) copy-start(f32[32]{0:T(128)} %intervals_far.3) | copy-start | bytes 388

commit v15 on v14

--- a/solution.py
+++ b/solution.py
@@ -20,6 +20,7 @@
 ZS = 8
 XS = 4
 WINDOW = 6
+LAST = XS * CHANS - 1
 STEP = 4
 PIECES = ((0, 4), (4, 4), (8, 4), (12, 4))
 CHUNKS = len(PIECES)
@@ -304,9 +305,9 @@
             later = jnp.where(low, totals[here], totals[there]).astype(BF16)
             level = jnp.where(low, befores[here], befores[there]).astype(BF16)
             for to in range(XS):
-                message[to * CHANS + chan, q] = jnp.where(x == to, level, later)
+                message[LAST - to * CHANS - chan, q] = jnp.where(x == to, level, later)
         for to in range(XS):
-            message[to * CHANS + chan, WINDOW // 2] = extra
+            message[LAST - to * CHANS - chan, WINDOW // 2] = extra
 
 
 OUT_STEP = 8
@@ -348,12 +349,12 @@
     rates, entering = [], []
     for step in range(CHANS):
         source = lax.rem(chan + CHANS - step, CHANS)
-        level = received[x * CHANS + source]
+        level = received[LAST - x * CHANS - source]
         rate = join3(level[WINDOW // 2], 6)
         spent = join3(level[WINDOW // 2], 3)
         total = jnp.zeros((WINDOW // 2, WIDE, LANES), F32)
         for other in range(XS - 1):
-            earlier = received[other * CHANS + source]
+            earlier = received[LAST - other * CHANS - source]
             decay = jnp.exp(-join3(earlier[WINDOW // 2], 0) * rate).reshape(1, 1, LANES)
             added = decay * total + earlier[: WINDOW // 2].astype(F32)
             total = jnp.where(other < x, added, total)
@@ -564,7 +565,8 @@
     out_pieces = (out_own, out_near, swap(out_near), neighbour(out_near))
     drives, done = window(place, *pieces, frames, out_pieces[2])
     onward = relay(place, rates, arrived, done, out_pieces[3])
-    received = lax.all_to_all(onward, ("x", "chan"), 0, 0)
+    backwards = [list(reversed(range(XS * CHANS)))]
+    received = lax.all_to_all(onward, ("x", "chan"), 0, 0, axis_index_groups=backwards)
     skip = skip_gain.reshape(1, CH)
     return read_out(place, intervals, skip, received, drives, out_pieces, frames)
 

time: 51.9 us -> 49.5 us (0.954)
  blocking collectives: 16 us -> 13.6 us
    all_to_all x1, blocking collectives: 16 us -> 13.6 us  [local(): lax.all_to_all(onward, ('x', 'chan'), 0, 0, axis_index_groups=backwards)]
  transfers between devices with their start and end apart: 7 -> 7, of which waited for: 0 -> 0; matrix products, arithmetic and copies ran while one was open for 0% -> 0% of each run, Pallas kernels for 26% -> 27%
where the time goes in v15:
time: 49.5 us; the launch traced here: 49.2 us
  Pallas kernels  20.4 us (41%)
  starting transfers between devices  15 us (30%)
  blocking collectives  13.6 us (27%)
    all_to_all x1, blocking collectives, local(): lax.all_to_all(onward, ('x', 'chan'), 0, 0, axis_index_groups=backwards)  13.6 us
    all_to_all x1, starting transfers between devices, local(): arrived = lax.all_to_all(message, 'z', 0, 0, axis_index_groups=backwards)  8.77 us
    pallas_call x1, Pallas kernels, window(): pl.pallas_call(window_kernel, out_shape=[jax.ShapeDtypeStruct((FRAMES, WI...  6.9 us
    pallas_call x1, Pallas kernels, drive(): pl.pallas_call(drive_kernel, out_shape=jax.ShapeDtypeStruct((ZS, ROWS //...  6.42 us
    pallas_call x1, Pallas kernels, read_out(): pl.pallas_call(readout_kernel, out_shape=jax.ShapeDtypeStruct((FRAMES, CH...  6.26 us
    ppermute x1, starting transfers between devices, opposite(): lax.ppermute(value, 'chan', [(c, (c + 2) % CHANS) for c in range(CHANS)])  3.19 us
    ppermute x3, starting transfers between devices, neighbour(): return lax.ppermute(value, ('chan', 'clip'), route)  2.49 us
  transfers between devices with their start and end apart: 7, of which 0 were waited for; matrix products, arithmetic and copies ran while one was open for 0% of the time, Pallas kernels for 27%

profile of v15, /device:TPU:32, one launch (start us, length us, event | category | flops | bytes accessed | tf_op | source)
XLA Modules:
  0.0 49.2 jit_solution(16730514059452421218)
XLA Ops:
  0.0 3.2 %collective-permute-start.2 = (bf16[9,64,256]{2,1,0:T(8,128)(2,1)}, bf16[9,64,256]{2,1,0:T(8,128)(2,1)S(1)}, u32[]{:S(2)}, u32[]{:S(2)}) collective-permute-start(bf16[9,64,256]{2,1,0:T(8,128)(2,1)} %bitcast.10), channel_id=1, source_target_pairs={{0,4},{2,6},{4,0},{6,2},{1,5},{3,7},{5,1},{7,3},{8,12},{10,14},{12... | collective-permute-start | bytes 884744 | tf_op jit(solution)/shard_map/ppermute | solution.py:529
  3.2 0.7 %collective-permute-start = (bf16[9,64,256]{2,1,0:T(8,128)(2,1)}, bf16[9,64,256]{2,1,0:T(8,128)(2,1)S(1)}, u32[]{:S(2)}, u32[]{:S(2)}) collective-permute-start(bf16[9,64,256]{2,1,0:T(8,128)(2,1)} %bitcast.11), channel_id=1, source_target_pairs={{0,2},{1,7},{2,4},{3,1},{4,6},{5,3},{6,0},{7,5},{8,10},{9,15},{10,... | collective-permute-start | bytes 884744 | tf_op jit(solution)/shard_map/ppermute | solution.py:525
  3.9 0.0 collective-permute-start.3
  3.9 6.4 %drive.1 = bf16[8,9,16,128]{3,2,1,0:T(8,128)(2,1)} custom-call(f32[32]{0:T(128)} %intervals_far.3, f32[1,64]{1,0:T(1,128)} %bitcast.17, bf16[9,64,256]{2,1,0:T(8,128)(2,1)} %bitcast.12, bf16[32,16,16,256]{3,2,1,0:T(8,128)(2,1)} %frames.5), custom_call_target="tpu_custom_call" | custom-call | flops 8800000000 | bytes 1048576 | tf_op jit(solution)/shard_map/drive/pallas_call | solution.py:435
  10.3 8.8 %all-to-all-start = ((bf16[8,9,16,128]{3,2,1,0:T(8,128)(2,1)}), bf16[8,9,16,128]{3,2,1,0:T(8,128)(2,1)S(1)}, u32[]{:S(2)}, u32[]{:S(2)}) async-start(bf16[8,9,16,128]{3,2,1,0:T(8,128)(2,1)} %drive.1), calls=%async_computation | async-start | bytes 589824 | tf_op jit(solution)/shard_map/all_to_all | solution.py:563
  19.1 0.0 copy-start
  19.1 0.0 collective-permute-done.refs_1_.near
  19.1 0.1 collective-permute-start.1
  19.2 0.0 collective-permute-done.3.near
  19.2 0.5 collective-permute-start.4
  19.7 0.1 pad_add_fusion.place
  19.8 1.8 %collective-permute-start.5 = (bf16[9,64,256]{2,1,0:T(8,128)(2,1)S(1)}, bf16[9,64,256]{2,1,0:T(8,128)(2,1)S(1)}, u32[]{:S(2)}, u32[]{:S(2)}) collective-permute-start(bf16[9,64,256]{2,1,0:T(8,128)(2,1)S(1)} %collective-permute-done.3.near), channel_id=1, source_target_pairs={{0,2},{1,7},{2,4},{3,1},{4,6},{5,3},{6,0},{7,5},{8,10},{9,15},{10,... | collective-permute-start | bytes 884744 | tf_op jit(solution)/shard_map/ppermute | solution.py:525
  21.6 0.0 collective-permute-done.2.refs_0_
  21.6 0.0 copy-start.3
  21.6 0.0 copy-start.1
  21.6 0.0 copy-start.2
  21.6 0.0 copy-start.4
  21.6 0.0 collective-permute-done.1.swapped
  21.6 0.0 collective-permute-done.4.later.swapped
  21.6 0.0 copy-done
  21.6 6.9 %window.1 = (bf16[32,6,16,256]{3,2,1,0:T(8,128)(2,1)}, f32[8,128]{1,0:T(8,128)S(1)}) custom-call(s32[4]{0:T(128)S(1)} %pad_add_fusion.place, bf16[9,64,256]{2,1,0:T(8,128)(2,1)S(1)} %bitcast.13, bf16[9,64,256]{2,1,0:T(8,128)(2,1)S(1)} %collective-permute-done.refs_1_.near, bf16[9,64,256]{2,1,0:T(8,128)(2,1)S(1)} %collective-permute-done.1.swapped, ...), custom_call_target="tpu_custom_call" | custom-call | flops 1100000000 | bytes 1048576 | tf_op jit(solution)/shard_map/window/pallas_call | solution.py:458
  28.5 0.0 all-to-all-done.received
  28.6 0.0 collective-permute-done.5.later.far
  28.6 0.0 copy-done.3
  28.6 0.8 %relay.1 = bf16[16,4,16,128]{3,2,1,0:T(8,128)(2,1)S(1)} custom-call(s32[4]{0:T(128)S(1)} %pad_add_fusion.place, f32[1,64]{1,0:T(1,128)S(1)} %bitcast.18, bf16[8,9,16,128]{3,2,1,0:T(8,128)(2,1)S(1)} %all-to-all-done.received, f32[8,128]{1,0:T(8,128)S(1)} %get-tuple-element.7.token, bf16[9,64,256]{2,1,0:T(8,128)(2,1)S(1)} %collective-permute-done.5.later.far), custom_call_target="tpu_custom_call" | custom-call | flops 1100000000 | bytes 1048576 | tf_op jit(solution)/shard_map/relay/pallas_call | solution.py:480
  29.4 13.6 %all_to_all.10.received = bf16[16,4,16,128]{3,2,1,0:T(8,128)(2,1)S(1)} all-to-all(bf16[16,4,16,128]{3,2,1,0:T(8,128)(2,1)S(1)} %relay.1), channel_id=1, replica_groups={{198,196,194,192,134,132,130,128,70,68,66,64,6,4,2,0},{199,197,195,193,..., dimensions={0} | all-to-all | bytes 524288 | tf_op jit(solution)/shard_map/all_to_all | solution.py:569
  42.9 0.0 copy-done.1
  42.9 0.0 copy-done.2
  42.9 0.0 copy-done.4
  42.9 6.3 %read_out.1 = bf16[32,4,16,256]{3,2,1,0:T(8,128)(2,1)} custom-call(s32[4]{0:T(128)S(1)} %pad_add_fusion.place, f32[32]{0:T(128)S(1)} %copy-done.4, f32[1,256]{1,0:T(1,128)S(1)} %bitcast.16, bf16[16,4,16,128]{3,2,1,0:T(8,128)(2,1)S(1)} %all_to_all.10.received, bf16[32,6,16,256]{3,2,1,0:T(8,128)(2,1)} %get-tuple-element.8.drives_far, ...), custom_call_target="tpu_custom_call" | custom-call | flops 6600000000 | bytes 1048576 | tf_op jit(solution)/shard_map/read_out/pallas_call | solution.py:492
  (1 shorter events, 0.0 us)
Async XLA Ops:
  0.0 21.6 %collective-permute-start.2 = (bf16[9,64,256]{2,1,0:T(8,128)(2,1)}, bf16[9,64,256]{2,1,0:T(8,128)(2,1)S(1)}, u32[]{:S(2)}, u32[]{:S(2)}) collective-permute-start(bf16[9,64,256]{2,1,0:T(8,128)(2,1)} %bitcast.10), channel_id=1, source_target_pairs={{0,4},{2,6},{4,0},{6,2},{1,5},{3,7},{5,1},{7,3},{8,12},{10,14},{12... | collective-permute-start | bytes 884744 | tf_op jit(solution)/shard_map/ppermute | solution.py:529
  3.2 15.9 %collective-permute-start = (bf16[9,64,256]{2,1,0:T(8,128)(2,1)}, bf16[9,64,256]{2,1,0:T(8,128)(2,1)S(1)}, u32[]{:S(2)}, u32[]{:S(2)}) collective-permute-start(bf16[9,64,256]{2,1,0:T(8,128)(2,1)} %bitcast.11), channel_id=1, source_target_pairs={{0,2},{1,7},{2,4},{3,1},{4,6},{5,3},{6,0},{7,5},{8,10},{9,15},{10,... | collective-permute-start | bytes 884744 | tf_op jit(solution)/shard_map/ppermute | solution.py:525
  3.9 15.3 %collective-permute-start.3 = (bf16[9,64,256]{2,1,0:T(8,128)(2,1)}, bf16[9,64,256]{2,1,0:T(8,128)(2,1)S(1)}, u32[]{:S(2)}, u32[]{:S(2)}) collective-permute-start(bf16[9,64,256]{2,1,0:T(8,128)(2,1)} %bitcast.14), channel_id=1, source_target_pairs={{0,2},{1,7},{2,4},{3,1},{4,6},{5,3},{6,0},{7,5},{8,10},{9,15},{10,... | collective-permute-start | bytes 884744 | tf_op jit(solution)/shard_map/ppermute | solution.py:525
  10.3 18.2 %all-to-all-start = ((bf16[8,9,16,128]{3,2,1,0:T(8,128)(2,1)}), bf16[8,9,16,128]{3,2,1,0:T(8,128)(2,1)S(1)}, u32[]{:S(2)}, u32[]{:S(2)}) async-start(bf16[8,9,16,128]{3,2,1,0:T(8,128)(2,1)} %drive.1), calls=%async_computation | async-start | bytes 589824 | tf_op jit(solution)/shard_map/all_to_all | solution.py:563
  19.1 2.5 %copy-start = (bf16[3,3,256,64]{2,3,1,0:T(8,128)(2,1)S(1)}, bf16[3,3,256,64]{2,3,1,0:T(8,128)(2,1)}, u32[]{:S(2)}) copy-start(bf16[3,3,256,64]{2,3,1,0:T(8,128)(2,1)} %param.9) | copy-start | bytes 884740
  19.1 2.5 %collective-permute-start.1 = (bf16[9,64,256]{2,1,0:T(8,128)(2,1)S(1)}, bf16[9,64,256]{2,1,0:T(8,128)(2,1)S(1)}, u32[]{:S(2)}, u32[]{:S(2)}) collective-permute-start(bf16[9,64,256]{2,1,0:T(8,128)(2,1)S(1)} %collective-permute-done.refs_1_.near), channel_id=1, source_target_pairs={{0,1},{1,0},{2,3},{3,2},{4,5},{5,4},{6,7},{7,6},{8,9},{9,8},{10,11... | collective-permute-start | bytes 884744 | tf_op jit(solution)/shard_map/ppermute | solution.py:550
  19.2 2.4 %collective-permute-start.4 = (bf16[9,64,256]{2,1,0:T(8,128)(2,1)S(1)}, bf16[9,64,256]{2,1,0:T(8,128)(2,1)S(1)}, u32[]{:S(2)}, u32[]{:S(2)}) collective-permute-start(bf16[9,64,256]{2,1,0:T(8,128)(2,1)S(1)} %collective-permute-done.3.near), channel_id=1, source_target_pairs={{0,1},{1,0},{2,3},{3,2},{4,5},{5,4},{6,7},{7,6},{8,9},{9,8},{10,11... | collective-permute-start | bytes 884744 | tf_op jit(solution)/shard_map/ppermute | solution.py:550
  19.8 8.8 %collective-permute-start.5 = (bf16[9,64,256]{2,1,0:T(8,128)(2,1)S(1)}, bf16[9,64,256]{2,1,0:T(8,128)(2,1)S(1)}, u32[]{:S(2)}, u32[]{:S(2)}) collective-permute-start(bf16[9,64,256]{2,1,0:T(8,128)(2,1)S(1)} %collective-permute-done.3.near), channel_id=1, source_target_pairs={{0,2},{1,7},{2,4},{3,1},{4,6},{5,3},{6,0},{7,5},{8,10},{9,15},{10,... | collective-permute-start | bytes 884744 | tf_op jit(solution)/shard_map/ppermute | solution.py:525
  21.6 7.0 %copy-start.3 = (f32[64]{0:T(128)S(1)}, f32[64]{0:T(128)}, u32[]{:S(2)}) copy-start(f32[64]{0:T(128)} %param.8) | copy-start | bytes 772
  21.6 21.4 %copy-start.1 = (bf16[3,3,64,256]{3,2,1,0:T(8,128)(2,1)S(1)}, bf16[3,3,64,256]{3,2,1,0:T(8,128)(2,1)}, u32[]{:S(2)}) copy-start(bf16[3,3,64,256]{3,2,1,0:T(8,128)(2,1)} %param.10) | copy-start | bytes 884740
  21.6 21.4 %copy-start.2 = (f32[256]{0:T(256)S(1)}, f32[256]{0:T(256)}, u32[]{:S(2)}) copy-start(f32[256]{0:T(256)} %param.11) | copy-start | bytes 3076
  21.6 21.3 %copy-start.4 = (f32[32]{0:T(128)S(1)}, f32[32]{0:T(128)}, u32[]{:S(2)}) copy-start(f32[32]{0:T(128)} %intervals_far.3) | copy-start | bytes 388

commit v16 on v12

--- a/solution.py
+++ b/solution.py
@@ -20,6 +20,7 @@
 ZS = 8
 XS = 4
 WINDOW = 6
+LAST = XS * CHANS - 1
 STEP = 4
 PIECES = ((0, 4), (4, 4), (8, 4), (12, 4))
 CHUNKS = len(PIECES)
@@ -279,9 +280,9 @@
         mine = z == other
         before = jnp.where(mine, total, before)
         elapsed_before = jnp.where(mine, elapsed, elapsed_before)
-        spent = join3(received[other, ROWS // 2], 0)
+        spent = join3(received[ZS - 1 - other, ROWS // 2], 0)
         decay = jnp.exp(-spent * rate).reshape(1, 1, LANES)
-        total = decay * total + received[other, : ROWS // 2].astype(F32)
+        total = decay * total + received[ZS - 1 - other, : ROWS // 2].astype(F32)
         elapsed = elapsed + spent
 
     low = low_half((WIDE, LANES))
@@ -307,9 +308,9 @@
             later = jnp.where(low, totals[here], totals[there]).astype(BF16)
             level = jnp.where(low, befores[here], befores[there]).astype(BF16)
             for to in range(XS):
-                message[to * CHANS + chan, q] = jnp.where(x == to, level, later)
+                message[LAST - to * CHANS - chan, q] = jnp.where(x == to, level, later)
         for to in range(XS):
-            message[to * CHANS + chan, WINDOW // 2] = extra
+            message[LAST - to * CHANS - chan, WINDOW // 2] = extra
 
 
 OUT_STEP = 8
@@ -359,12 +360,12 @@
     rates, entering = [], []
     for step in range(CHANS):
         source = lax.rem(chan + CHANS - step, CHANS)
-        level = received[x * CHANS + source]
+        level = received[LAST - x * CHANS - source]
         rate = join3(level[WINDOW // 2], 6)
         spent = join3(level[WINDOW // 2], 3)
         total = jnp.zeros((WINDOW // 2, WIDE, LANES), F32)
         for other in range(XS - 1):
-            earlier = received[other * CHANS + source]
+            earlier = received[LAST - other * CHANS - source]
             decay = jnp.exp(-join3(earlier[WINDOW // 2], 0) * rate).reshape(1, 1, LANES)
             added = decay * total + earlier[: WINDOW // 2].astype(F32)
             total = jnp.where(other < x, added, total)
@@ -590,14 +591,16 @@
     in_near, in_far = around(kernel_t)
     in_far = after(in_far, in_near, 2)
     message = drive(intervals, rates, kernel_t, frames)
-    arrived = lax.all_to_all(message, "z", 0, 0)
+    backwards = [list(reversed(range(ZS)))]
+    arrived = lax.all_to_all(message, "z", 0, 0, axis_index_groups=backwards)
     out_near, out_far = around(hold(out_own, (in_near, in_far)))
     pieces = (kernel_t, in_near, swap(in_near), in_far)
     early, done = window(0, EARLY, place, *pieces, frames, place)
     onward, done = relay(place, rates, arrived, done)
     late, _ = window(EARLY, FRAMES - EARLY, place, *pieces, frames, done)
     out_near = after(out_near, done)
-    received = lax.all_to_all(onward, ("x", "chan"), 0, 0)
+    backwards = [list(reversed(range(XS * CHANS)))]
+    received = lax.all_to_all(onward, ("x", "chan"), 0, 0, axis_index_groups=backwards)
     received = after(received, place, 2)
     out_far = after(out_far, done, 2)
     kernels = (out_own, out_near, swap(out_near), out_far)

time: 52.2 us -> 51.4 us (0.985)
  the two profiles are of different devices: /device:TPU:32 before, /device:TPU:1 now
where the time goes in v16:
time: 51.4 us; the launch traced here: 51 us
  starting transfers between devices  26.7 us (52%)
  Pallas kernels  23.5 us (46%)
  local copies, waits for them, and re-layouts  0.65 us (1%)
    pallas_call x2, Pallas kernels, window(): pl.pallas_call(functools.partial(window_kernel, begin, size), out_shape=[...  9.26 us
    all_to_all x1, starting transfers between devices, local(): arrived = lax.all_to_all(message, 'z', 0, 0, axis_index_groups=backwards)  8.96 us
    all_to_all x1, starting transfers between devices, local(): lax.all_to_all(onward, ('x', 'chan'), 0, 0, axis_index_groups=backwards)  7.01 us
    pallas_call x1, Pallas kernels, drive(): pl.pallas_call(drive_kernel, out_shape=jax.ShapeDtypeStruct((ZS, ROWS //...  6.42 us
    pallas_call x1, Pallas kernels, read_out(): pl.pallas_call(readout_kernel, out_shape=jax.ShapeDtypeStruct((FRAMES, CH...  6.25 us
    ppermute x2, starting transfers between devices, around(): lax.ppermute(value, 'chan', far)  5.39 us
    ppermute x2, starting transfers between devices, swap(): return lax.ppermute(value, 'clip', [(0, 1), (1, 0)])  3.34 us
    ppermute x2, starting transfers between devices, around(): lax.ppermute(value, ('chan', 'clip'), near)  2.01 us
  transfers between devices with their start and end apart: 8, of which 0 were waited for; matrix products, arithmetic and copies ran while one was open for 0% of the time, Pallas kernels for 34%

profile of v16, /device:TPU:1, one launch (start us, length us, event | category | flops | bytes accessed | tf_op | source)
XLA Modules:
  0.0 51.0 jit_solution(5668937050145511395)
XLA Ops:
  0.0 3.7 %collective-permute-start.2 = (bf16[9,64,256]{2,1,0:T(8,128)(2,1)}, bf16[9,64,256]{2,1,0:T(8,128)(2,1)S(1)}, u32[]{:S(2)}, u32[]{:S(2)}) collective-permute-start(bf16[9,64,256]{2,1,0:T(8,128)(2,1)} %bitcast.10), channel_id=1, source_target_pairs={{0,4},{2,6},{4,0},{6,2},{1,5},{3,7},{5,1},{7,3},{8,12},{10,14},{12... | collective-permute-start | bytes 884744 | tf_op jit(solution)/shard_map/ppermute | solution.py:561
  3.7 0.8 %collective-permute-start = (bf16[9,64,256]{2,1,0:T(8,128)(2,1)}, bf16[9,64,256]{2,1,0:T(8,128)(2,1)S(1)}, u32[]{:S(2)}, u32[]{:S(2)}) collective-permute-start(bf16[9,64,256]{2,1,0:T(8,128)(2,1)} %bitcast.11), channel_id=1, source_target_pairs={{0,2},{1,7},{2,4},{3,1},{4,6},{5,3},{6,0},{7,5},{8,10},{9,15},{10,... | collective-permute-start | bytes 884744 | tf_op jit(solution)/shard_map/ppermute | solution.py:561
  4.5 6.4 %drive.1 = bf16[8,9,16,128]{3,2,1,0:T(8,128)(2,1)} custom-call(f32[32]{0:T(128)} %intervals_far.3, f32[1,64]{1,0:T(1,128)} %bitcast.18, bf16[9,64,256]{2,1,0:T(8,128)(2,1)} %bitcast.12, bf16[32,16,16,256]{3,2,1,0:T(8,128)(2,1)} %frames.7), custom_call_target="tpu_custom_call" | custom-call | flops 8800000000 | bytes 1048576 | tf_op jit(solution)/shard_map/drive/pallas_call | solution.py:446
  10.9 9.0 %all-to-all-start = ((bf16[8,9,16,128]{3,2,1,0:T(8,128)(2,1)}), bf16[8,9,16,128]{3,2,1,0:T(8,128)(2,1)S(1)}, u32[]{:S(2)}, u32[]{:S(2)}) async-start(bf16[8,9,16,128]{3,2,1,0:T(8,128)(2,1)} %drive.1), calls=%async_computation | async-start | bytes 589824 | tf_op jit(solution)/shard_map/all_to_all | solution.py:595
  19.9 0.0 copy-start.1
  19.9 0.0 copy-start
  19.9 0.0 collective-permute-done.refs_1_.near.refs_0_
  19.9 1.2 %collective-permute-start.1 = (bf16[9,64,256]{2,1,0:T(8,128)(2,1)S(1)}, bf16[9,64,256]{2,1,0:T(8,128)(2,1)S(1)}, u32[]{:S(2)}, u32[]{:S(2)}) collective-permute-start(bf16[9,64,256]{2,1,0:T(8,128)(2,1)S(1)} %collective-permute-done.refs_1_.near.refs_0_), channel_id=1, source_target_pairs={{0,1},{1,0},{2,3},{3,2},{4,5},{5,4},{6,7},{7,6},{8,9},{9,8},{10,11... | collective-permute-start | bytes 884744 | tf_op jit(solution)/shard_map/ppermute | solution.py:582
  21.1 0.0 collective-permute-done.2.refs_0_
  21.1 0.0 copy-done.1
  21.1 0.0 copy-start.3
  21.1 0.1 hold.1
  21.2 1.6 %collective-permute-start.5 = (bf16[9,64,256]{2,1,0:T(8,128)(2,1)S(1)}, bf16[9,64,256]{2,1,0:T(8,128)(2,1)S(1)}, u32[]{:S(2)}, u32[]{:S(2)}) collective-permute-start(bf16[9,64,256]{2,1,0:T(8,128)(2,1)S(1)} %hold.1), channel_id=1, source_target_pairs={{0,4},{2,6},{4,0},{6,2},{1,5},{3,7},{5,1},{7,3},{8,12},{10,14},{12... | collective-permute-start | bytes 884744 | tf_op jit(solution)/shard_map/ppermute | solution.py:561
  22.9 1.2 %collective-permute-start.3 = (bf16[9,64,256]{2,1,0:T(8,128)(2,1)S(1)}, bf16[9,64,256]{2,1,0:T(8,128)(2,1)S(1)}, u32[]{:S(2)}, u32[]{:S(2)}) collective-permute-start(bf16[9,64,256]{2,1,0:T(8,128)(2,1)S(1)} %hold.1), channel_id=1, source_target_pairs={{0,2},{1,7},{2,4},{3,1},{4,6},{5,3},{6,0},{7,5},{8,10},{9,15},{10,... | collective-permute-start | bytes 884744 | tf_op jit(solution)/shard_map/ppermute | solution.py:561
  24.1 0.1 pad_add_fusion.place._.refs_1_
  24.2 0.0 collective-permute-done.1.swapped
  24.2 0.0 copy-done
  24.2 5.8 %window.2 = (bf16[24,6,16,256]{3,2,1,0:T(8,128)(2,1)}, f32[8,128]{1,0:T(8,128)S(1)}) custom-call(s32[4]{0:T(128)S(1)} %pad_add_fusion.place._.refs_1_, bf16[9,64,256]{2,1,0:T(8,128)(2,1)S(1)} %bitcast.13, bf16[9,64,256]{2,1,0:T(8,128)(2,1)S(1)} %collective-permute-done.refs_1_.near.refs_0_, bf16[9,64,256]{2,1,0:T(8,128)(2,1)S(1)} %collective-permute-done.1.swapped, ...), custom_call_target="tpu_custom_call" | custom-call | flops 1100000000 | bytes 1048576 | tf_op jit(solution)/shard_map/window/pallas_call | solution.py:470
  30.0 0.0 all-to-all-done.received
  30.0 0.0 copy-done.3
  30.0 1.5 %relay.1 = (bf16[16,4,16,128]{3,2,1,0:T(8,128)(2,1)}, f32[8,128]{1,0:T(8,128)S(1)}) custom-call(s32[4]{0:T(128)S(1)} %pad_add_fusion.place._.refs_1_, f32[1,64]{1,0:T(1,128)S(1)} %bitcast.19, bf16[8,9,16,128]{3,2,1,0:T(8,128)(2,1)S(1)} %all-to-all-done.received, f32[8,128]{1,0:T(8,128)S(1)} %get-tuple-element.10.token), custom_call_target="tpu_custom_call" | custom-call | flops 1100000000 | bytes 1048576 | tf_op jit(solution)/shard_map/relay/pallas_call | solution.py:512
  31.5 7.0 %all-to-all-start.1 = ((bf16[16,4,16,128]{3,2,1,0:T(8,128)(2,1)}), bf16[16,4,16,128]{3,2,1,0:T(8,128)(2,1)S(1)}, u32[]{:S(2)}, u32[]{:S(2)}) async-start(bf16[16,4,16,128]{3,2,1,0:T(8,128)(2,1)} %get-tuple-element.11), calls=%async_computation.1 | async-start | bytes 524288 | tf_op jit(solution)/shard_map/all_to_all | solution.py:603
  38.5 0.0 collective-permute-done.3.refs_0_
  38.5 2.1 %collective-permute-start.4 = (bf16[9,64,256]{2,1,0:T(8,128)(2,1)S(1)}, bf16[9,64,256]{2,1,0:T(8,128)(2,1)S(1)}, u32[]{:S(2)}, u32[]{:S(2)}) collective-permute-start(bf16[9,64,256]{2,1,0:T(8,128)(2,1)S(1)} %after.6.near), channel_id=1, source_target_pairs={{0,1},{1,0},{2,3},{3,2},{4,5},{5,4},{6,7},{7,6},{8,9},{9,8},{10,11... | collective-permute-start | bytes 884744 | tf_op jit(solution)/shard_map/ppermute | solution.py:582
  40.6 0.0 collective-permute-done.5.refs_0_
  40.6 3.5 %window.3 = (bf16[8,6,16,256]{3,2,1,0:T(8,128)(2,1)S(1)}, f32[8,128]{1,0:T(8,128)}) custom-call(s32[4]{0:T(128)S(1)} %pad_add_fusion.place._.refs_1_, bf16[9,64,256]{2,1,0:T(8,128)(2,1)S(1)} %bitcast.14, bf16[9,64,256]{2,1,0:T(8,128)(2,1)S(1)} %collective-permute-done.refs_1_.near.refs_0_, bf16[9,64,256]{2,1,0:T(8,128)(2,1)S(1)} %collective-permute-done.1.swapped, ...), custom_call_target="tpu_custom_call" | custom-call | flops 1100000000 | bytes 1048576 | tf_op jit(solution)/shard_map/window/pallas_call | solution.py:470
  44.1 0.0 copy-start.2
  44.1 0.0 copy-start.4
  44.1 0.0 all-to-all-done.1.refs_0_
  44.2 0.0 collective-permute-done.4.swapped
  44.2 0.6 %copy-done.2 = f32[256]{0:T(256)S(1)} copy-done((f32[256]{0:T(256)S(1)}, f32[256]{0:T(256)}, u32[]{:S(2)}) %copy-start.2) | copy-done | bytes 1048
  44.8 0.0 copy-done.4
  44.8 6.3 %read_out.1 = bf16[32,4,16,256]{3,2,1,0:T(8,128)(2,1)} custom-call(s32[4]{0:T(128)S(1)} %pad_add_fusion.place._.refs_1_, f32[32]{0:T(128)S(1)} %copy-done.4, f32[1,256]{1,0:T(1,128)S(1)} %bitcast.17, bf16[16,4,16,128]{3,2,1,0:T(8,128)(2,1)S(1)} %after.5.received, bf16[24,6,16,256]{3,2,1,0:T(8,128)(2,1)} %get-tuple-element.12.early, ...), custom_call_target="tpu_custom_call" | custom-call | flops 6600000000 | bytes 1048576 | tf_op jit(solution)/shard_map/read_out/pallas_call | solution.py:527
  (4 shorter events, 0.0 us)
Async XLA Ops:
  0.0 21.1 %collective-permute-start.2 = (bf16[9,64,256]{2,1,0:T(8,128)(2,1)}, bf16[9,64,256]{2,1,0:T(8,128)(2,1)S(1)}, u32[]{:S(2)}, u32[]{:S(2)}) collective-permute-start(bf16[9,64,256]{2,1,0:T(8,128)(2,1)} %bitcast.10), channel_id=1, source_target_pairs={{0,4},{2,6},{4,0},{6,2},{1,5},{3,7},{5,1},{7,3},{8,12},{10,14},{12... | collective-permute-start | bytes 884744 | tf_op jit(solution)/shard_map/ppermute | solution.py:561
  3.7 16.2 %collective-permute-start = (bf16[9,64,256]{2,1,0:T(8,128)(2,1)}, bf16[9,64,256]{2,1,0:T(8,128)(2,1)S(1)}, u32[]{:S(2)}, u32[]{:S(2)}) collective-permute-start(bf16[9,64,256]{2,1,0:T(8,128)(2,1)} %bitcast.11), channel_id=1, source_target_pairs={{0,2},{1,7},{2,4},{3,1},{4,6},{5,3},{6,0},{7,5},{8,10},{9,15},{10,... | collective-permute-start | bytes 884744 | tf_op jit(solution)/shard_map/ppermute | solution.py:561
  10.9 19.0 %all-to-all-start = ((bf16[8,9,16,128]{3,2,1,0:T(8,128)(2,1)}), bf16[8,9,16,128]{3,2,1,0:T(8,128)(2,1)S(1)}, u32[]{:S(2)}, u32[]{:S(2)}) async-start(bf16[8,9,16,128]{3,2,1,0:T(8,128)(2,1)} %drive.1), calls=%async_computation | async-start | bytes 589824 | tf_op jit(solution)/shard_map/all_to_all | solution.py:595
  19.9 1.2 %copy-start.1 = (bf16[3,3,64,256]{3,2,1,0:T(8,128)(2,1)S(1)}, bf16[3,3,64,256]{3,2,1,0:T(8,128)(2,1)}, u32[]{:S(2)}) copy-start(bf16[3,3,64,256]{3,2,1,0:T(8,128)(2,1)} %param.10) | copy-start | bytes 884740
  19.9 4.3 %copy-start = (bf16[3,3,256,64]{2,3,1,0:T(8,128)(2,1)S(1)}, bf16[3,3,256,64]{2,3,1,0:T(8,128)(2,1)}, u32[]{:S(2)}) copy-start(bf16[3,3,256,64]{2,3,1,0:T(8,128)(2,1)} %param.9) | copy-start | bytes 884740
  19.9 4.3 %collective-permute-start.1 = (bf16[9,64,256]{2,1,0:T(8,128)(2,1)S(1)}, bf16[9,64,256]{2,1,0:T(8,128)(2,1)S(1)}, u32[]{:S(2)}, u32[]{:S(2)}) collective-permute-start(bf16[9,64,256]{2,1,0:T(8,128)(2,1)S(1)} %collective-permute-done.refs_1_.near.refs_0_), channel_id=1, source_target_pairs={{0,1},{1,0},{2,3},{3,2},{4,5},{5,4},{6,7},{7,6},{8,9},{9,8},{10,11... | collective-permute-start | bytes 884744 | tf_op jit(solution)/shard_map/ppermute | solution.py:582
  21.1 8.8 %copy-start.3 = (f32[64]{0:T(128)S(1)}, f32[64]{0:T(128)}, u32[]{:S(2)}) copy-start(f32[64]{0:T(128)} %param.8) | copy-start | bytes 772
  21.2 19.4 %collective-permute-start.5 = (bf16[9,64,256]{2,1,0:T(8,128)(2,1)S(1)}, bf16[9,64,256]{2,1,0:T(8,128)(2,1)S(1)}, u32[]{:S(2)}, u32[]{:S(2)}) collective-permute-start(bf16[9,64,256]{2,1,0:T(8,128)(2,1)S(1)} %hold.1), channel_id=1, source_target_pairs={{0,4},{2,6},{4,0},{6,2},{1,5},{3,7},{5,1},{7,3},{8,12},{10,14},{12... | collective-permute-start | bytes 884744 | tf_op jit(solution)/shard_map/ppermute | solution.py:561
  22.9 15.6 %collective-permute-start.3 = (bf16[9,64,256]{2,1,0:T(8,128)(2,1)S(1)}, bf16[9,64,256]{2,1,0:T(8,128)(2,1)S(1)}, u32[]{:S(2)}, u32[]{:S(2)}) collective-permute-start(bf16[9,64,256]{2,1,0:T(8,128)(2,1)S(1)} %hold.1), channel_id=1, source_target_pairs={{0,2},{1,7},{2,4},{3,1},{4,6},{5,3},{6,0},{7,5},{8,10},{9,15},{10,... | collective-permute-start | bytes 884744 | tf_op jit(solution)/shard_map/ppermute | solution.py:561
  31.5 12.7 %all-to-all-start.1 = ((bf16[16,4,16,128]{3,2,1,0:T(8,128)(2,1)}), bf16[16,4,16,128]{3,2,1,0:T(8,128)(2,1)S(1)}, u32[]{:S(2)}, u32[]{:S(2)}) async-start(bf16[16,4,16,128]{3,2,1,0:T(8,128)(2,1)} %get-tuple-element.11), calls=%async_computation.1 | async-start | bytes 524288 | tf_op jit(solution)/shard_map/all_to_all | solution.py:603
  38.5 5.7 %collective-permute-start.4 = (bf16[9,64,256]{2,1,0:T(8,128)(2,1)S(1)}, bf16[9,64,256]{2,1,0:T(8,128)(2,1)S(1)}, u32[]{:S(2)}, u32[]{:S(2)}) collective-permute-start(bf16[9,64,256]{2,1,0:T(8,128)(2,1)S(1)} %after.6.near), channel_id=1, source_target_pairs={{0,1},{1,0},{2,3},{3,2},{4,5},{5,4},{6,7},{7,6},{8,9},{9,8},{10,11... | collective-permute-start | bytes 884744 | tf_op jit(solution)/shard_map/ppermute | solution.py:582
  44.1 0.7 %copy-start.2 = (f32[256]{0:T(256)S(1)}, f32[256]{0:T(256)}, u32[]{:S(2)}) copy-start(f32[256]{0:T(256)} %param.11) | copy-start | bytes 3076
  44.1 0.7 %copy-start.4 = (f32[32]{0:T(128)S(1)}, f32[32]{0:T(128)}, u32[]{:S(2)}) copy-start(f32[32]{0:T(128)} %intervals_far.3) | copy-start | bytes 388

commit v17 on v15

--- a/solution.py
+++ b/solution.py
@@ -21,6 +21,7 @@
 XS = 4
 WINDOW = 6
 LAST = XS * CHANS - 1
+TURN = (6, 7, 0, 1, 5, 4, 3, 2)
 STEP = 4
 PIECES = ((0, 4), (4, 4), (8, 4), (12, 4))
 CHUNKS = len(PIECES)
@@ -277,9 +278,9 @@
         mine = z == other
         before = jnp.where(mine, total, before)
         elapsed_before = jnp.where(mine, elapsed, elapsed_before)
-        spent = join3(received[ZS - 1 - other, ROWS // 2], 0)
+        spent = join3(received[TURN.index(other), ROWS // 2], 0)
         decay = jnp.exp(-spent * rate).reshape(1, 1, LANES)
-        total = decay * total + received[ZS - 1 - other, : ROWS // 2].astype(F32)
+        total = decay * total + received[TURN.index(other), : ROWS // 2].astype(F32)
         elapsed = elapsed + spent
 
     low = low_half((WIDE, LANES))
@@ -559,7 +560,7 @@
     near, out_near = neighbour(kernel_t), neighbour(out_own)
     far = opposite(kernel_t)
     message = drive(intervals, rates, kernel_t, frames)
-    backwards = [list(reversed(range(ZS)))]
+    backwards = [list(TURN)]
     arrived = lax.all_to_all(message, "z", 0, 0, axis_index_groups=backwards)
     pieces = (kernel_t, near, swap(near), after(far, near, 2))
     out_pieces = (out_own, out_near, swap(out_near), neighbour(out_near))

time: 49.5 us -> 49.9 us (level)
  starting transfers between devices: 15 us -> 15.5 us
where the time goes in v17:
time: 49.9 us; the launch traced here: 49.6 us
  Pallas kernels  20.3 us (41%)
  starting transfers between devices  15.5 us (31%)
  blocking collectives  13.6 us (27%)
    all_to_all x1, blocking collectives, local(): lax.all_to_all(onward, ('x', 'chan'), 0, 0, axis_index_groups=backwards)  13.6 us
    all_to_all x1, starting transfers between devices, local(): arrived = lax.all_to_all(message, 'z', 0, 0, axis_index_groups=backwards)  9.19 us
    pallas_call x1, Pallas kernels, window(): pl.pallas_call(window_kernel, out_shape=[jax.ShapeDtypeStruct((FRAMES, WI...  6.9 us
    pallas_call x1, Pallas kernels, drive(): pl.pallas_call(drive_kernel, out_shape=jax.ShapeDtypeStruct((ZS, ROWS //...  6.42 us
    pallas_call x1, Pallas kernels, read_out(): pl.pallas_call(readout_kernel, out_shape=jax.ShapeDtypeStruct((FRAMES, CH...  6.25 us
    ppermute x1, starting transfers between devices, opposite(): lax.ppermute(value, 'chan', [(c, (c + 2) % CHANS) for c in range(CHANS)])  3.19 us
    ppermute x3, starting transfers between devices, neighbour(): return lax.ppermute(value, ('chan', 'clip'), route)  2.49 us
  transfers between devices with their start and end apart: 7, of which 0 were waited for; matrix products, arithmetic and copies ran while one was open for 0% of the time, Pallas kernels for 27%

profile of v17, /device:TPU:32, one launch (start us, length us, event | category | flops | bytes accessed | tf_op | source)
XLA Modules:
  0.0 49.6 jit_solution(15261574215655999915)
XLA Ops:
  0.0 3.2 %collective-permute-start.2 = (bf16[9,64,256]{2,1,0:T(8,128)(2,1)}, bf16[9,64,256]{2,1,0:T(8,128)(2,1)S(1)}, u32[]{:S(2)}, u32[]{:S(2)}) collective-permute-start(bf16[9,64,256]{2,1,0:T(8,128)(2,1)} %bitcast.10), channel_id=1, source_target_pairs={{0,4},{2,6},{4,0},{6,2},{1,5},{3,7},{5,1},{7,3},{8,12},{10,14},{12... | collective-permute-start | bytes 884744 | tf_op jit(solution)/shard_map/ppermute | solution.py:530
  3.2 0.7 %collective-permute-start = (bf16[9,64,256]{2,1,0:T(8,128)(2,1)}, bf16[9,64,256]{2,1,0:T(8,128)(2,1)S(1)}, u32[]{:S(2)}, u32[]{:S(2)}) collective-permute-start(bf16[9,64,256]{2,1,0:T(8,128)(2,1)} %bitcast.11), channel_id=1, source_target_pairs={{0,2},{1,7},{2,4},{3,1},{4,6},{5,3},{6,0},{7,5},{8,10},{9,15},{10,... | collective-permute-start | bytes 884744 | tf_op jit(solution)/shard_map/ppermute | solution.py:526
  3.9 0.0 collective-permute-start.3
  3.9 6.4 %drive.1 = bf16[8,9,16,128]{3,2,1,0:T(8,128)(2,1)} custom-call(f32[32]{0:T(128)} %intervals_far.3, f32[1,64]{1,0:T(1,128)} %bitcast.17, bf16[9,64,256]{2,1,0:T(8,128)(2,1)} %bitcast.12, bf16[32,16,16,256]{3,2,1,0:T(8,128)(2,1)} %frames.5), custom_call_target="tpu_custom_call" | custom-call | flops 8800000000 | bytes 1048576 | tf_op jit(solution)/shard_map/drive/pallas_call | solution.py:436
  10.3 9.2 %all-to-all-start = ((bf16[8,9,16,128]{3,2,1,0:T(8,128)(2,1)}), bf16[8,9,16,128]{3,2,1,0:T(8,128)(2,1)S(1)}, u32[]{:S(2)}, u32[]{:S(2)}) async-start(bf16[8,9,16,128]{3,2,1,0:T(8,128)(2,1)} %drive.1), calls=%async_computation | async-start | bytes 589824 | tf_op jit(solution)/shard_map/all_to_all | solution.py:564
  19.5 0.0 copy-start
  19.5 0.0 collective-permute-done.refs_1_.near
  19.5 0.1 collective-permute-start.1
  19.6 0.0 collective-permute-done.3.near
  19.6 0.5 collective-permute-start.4
  20.1 0.1 pad_add_fusion.place
  20.2 1.8 %collective-permute-start.5 = (bf16[9,64,256]{2,1,0:T(8,128)(2,1)S(1)}, bf16[9,64,256]{2,1,0:T(8,128)(2,1)S(1)}, u32[]{:S(2)}, u32[]{:S(2)}) collective-permute-start(bf16[9,64,256]{2,1,0:T(8,128)(2,1)S(1)} %collective-permute-done.3.near), channel_id=1, source_target_pairs={{0,2},{1,7},{2,4},{3,1},{4,6},{5,3},{6,0},{7,5},{8,10},{9,15},{10,... | collective-permute-start | bytes 884744 | tf_op jit(solution)/shard_map/ppermute | solution.py:526
  22.0 0.0 collective-permute-done.2.refs_0_
  22.0 0.0 copy-start.3
  22.0 0.0 copy-start.1
  22.0 0.0 copy-start.2
  22.0 0.0 copy-start.4
  22.0 0.0 collective-permute-done.1.swapped
  22.0 0.0 collective-permute-done.4.later.swapped
  22.0 0.0 copy-done
  22.1 6.9 %window.1 = (bf16[32,6,16,256]{3,2,1,0:T(8,128)(2,1)}, f32[8,128]{1,0:T(8,128)S(1)}) custom-call(s32[4]{0:T(128)S(1)} %pad_add_fusion.place, bf16[9,64,256]{2,1,0:T(8,128)(2,1)S(1)} %bitcast.13, bf16[9,64,256]{2,1,0:T(8,128)(2,1)S(1)} %collective-permute-done.refs_1_.near, bf16[9,64,256]{2,1,0:T(8,128)(2,1)S(1)} %collective-permute-done.1.swapped, ...), custom_call_target="tpu_custom_call" | custom-call | flops 1100000000 | bytes 1048576 | tf_op jit(solution)/shard_map/window/pallas_call | solution.py:459
  29.0 0.0 all-to-all-done.received
  29.0 0.0 collective-permute-done.5.later.far
  29.0 0.0 copy-done.3
  29.0 0.8 %relay.1 = bf16[16,4,16,128]{3,2,1,0:T(8,128)(2,1)S(1)} custom-call(s32[4]{0:T(128)S(1)} %pad_add_fusion.place, f32[1,64]{1,0:T(1,128)S(1)} %bitcast.18, bf16[8,9,16,128]{3,2,1,0:T(8,128)(2,1)S(1)} %all-to-all-done.received, f32[8,128]{1,0:T(8,128)S(1)} %get-tuple-element.7.token, bf16[9,64,256]{2,1,0:T(8,128)(2,1)S(1)} %collective-permute-done.5.later.far), custom_call_target="tpu_custom_call" | custom-call | flops 1100000000 | bytes 1048576 | tf_op jit(solution)/shard_map/relay/pallas_call | solution.py:481
  29.8 13.6 %all_to_all.10.received = bf16[16,4,16,128]{3,2,1,0:T(8,128)(2,1)S(1)} all-to-all(bf16[16,4,16,128]{3,2,1,0:T(8,128)(2,1)S(1)} %relay.1), channel_id=1, replica_groups={{198,196,194,192,134,132,130,128,70,68,66,64,6,4,2,0},{199,197,195,193,..., dimensions={0} | all-to-all | bytes 524288 | tf_op jit(solution)/shard_map/all_to_all | solution.py:570
  43.4 0.0 copy-done.1
  43.4 0.0 copy-done.2
  43.4 0.0 copy-done.4
  43.4 6.3 %read_out.1 = bf16[32,4,16,256]{3,2,1,0:T(8,128)(2,1)} custom-call(s32[4]{0:T(128)S(1)} %pad_add_fusion.place, f32[32]{0:T(128)S(1)} %copy-done.4, f32[1,256]{1,0:T(1,128)S(1)} %bitcast.16, bf16[16,4,16,128]{3,2,1,0:T(8,128)(2,1)S(1)} %all_to_all.10.received, bf16[32,6,16,256]{3,2,1,0:T(8,128)(2,1)} %get-tuple-element.8.drives_far, ...), custom_call_target="tpu_custom_call" | custom-call | flops 6600000000 | bytes 1048576 | tf_op jit(solution)/shard_map/read_out/pallas_call | solution.py:493
  (1 shorter events, 0.0 us)
Async XLA Ops:
  0.0 22.0 %collective-permute-start.2 = (bf16[9,64,256]{2,1,0:T(8,128)(2,1)}, bf16[9,64,256]{2,1,0:T(8,128)(2,1)S(1)}, u32[]{:S(2)}, u32[]{:S(2)}) collective-permute-start(bf16[9,64,256]{2,1,0:T(8,128)(2,1)} %bitcast.10), channel_id=1, source_target_pairs={{0,4},{2,6},{4,0},{6,2},{1,5},{3,7},{5,1},{7,3},{8,12},{10,14},{12... | collective-permute-start | bytes 884744 | tf_op jit(solution)/shard_map/ppermute | solution.py:530
  3.2 16.3 %collective-permute-start = (bf16[9,64,256]{2,1,0:T(8,128)(2,1)}, bf16[9,64,256]{2,1,0:T(8,128)(2,1)S(1)}, u32[]{:S(2)}, u32[]{:S(2)}) collective-permute-start(bf16[9,64,256]{2,1,0:T(8,128)(2,1)} %bitcast.11), channel_id=1, source_target_pairs={{0,2},{1,7},{2,4},{3,1},{4,6},{5,3},{6,0},{7,5},{8,10},{9,15},{10,... | collective-permute-start | bytes 884744 | tf_op jit(solution)/shard_map/ppermute | solution.py:526
  3.9 15.8 %collective-permute-start.3 = (bf16[9,64,256]{2,1,0:T(8,128)(2,1)}, bf16[9,64,256]{2,1,0:T(8,128)(2,1)S(1)}, u32[]{:S(2)}, u32[]{:S(2)}) collective-permute-start(bf16[9,64,256]{2,1,0:T(8,128)(2,1)} %bitcast.14), channel_id=1, source_target_pairs={{0,2},{1,7},{2,4},{3,1},{4,6},{5,3},{6,0},{7,5},{8,10},{9,15},{10,... | collective-permute-start | bytes 884744 | tf_op jit(solution)/shard_map/ppermute | solution.py:526
  10.3 18.6 %all-to-all-start = ((bf16[8,9,16,128]{3,2,1,0:T(8,128)(2,1)}), bf16[8,9,16,128]{3,2,1,0:T(8,128)(2,1)S(1)}, u32[]{:S(2)}, u32[]{:S(2)}) async-start(bf16[8,9,16,128]{3,2,1,0:T(8,128)(2,1)} %drive.1), calls=%async_computation | async-start | bytes 589824 | tf_op jit(solution)/shard_map/all_to_all | solution.py:564
  19.5 2.5 %copy-start = (bf16[3,3,256,64]{2,3,1,0:T(8,128)(2,1)S(1)}, bf16[3,3,256,64]{2,3,1,0:T(8,128)(2,1)}, u32[]{:S(2)}) copy-start(bf16[3,3,256,64]{2,3,1,0:T(8,128)(2,1)} %param.9) | copy-start | bytes 884740
  19.5 2.5 %collective-permute-start.1 = (bf16[9,64,256]{2,1,0:T(8,128)(2,1)S(1)}, bf16[9,64,256]{2,1,0:T(8,128)(2,1)S(1)}, u32[]{:S(2)}, u32[]{:S(2)}) collective-permute-start(bf16[9,64,256]{2,1,0:T(8,128)(2,1)S(1)} %collective-permute-done.refs_1_.near), channel_id=1, source_target_pairs={{0,1},{1,0},{2,3},{3,2},{4,5},{5,4},{6,7},{7,6},{8,9},{9,8},{10,11... | collective-permute-start | bytes 884744 | tf_op jit(solution)/shard_map/ppermute | solution.py:551
  19.6 2.4 %collective-permute-start.4 = (bf16[9,64,256]{2,1,0:T(8,128)(2,1)S(1)}, bf16[9,64,256]{2,1,0:T(8,128)(2,1)S(1)}, u32[]{:S(2)}, u32[]{:S(2)}) collective-permute-start(bf16[9,64,256]{2,1,0:T(8,128)(2,1)S(1)} %collective-permute-done.3.near), channel_id=1, source_target_pairs={{0,1},{1,0},{2,3},{3,2},{4,5},{5,4},{6,7},{7,6},{8,9},{9,8},{10,11... | collective-permute-start | bytes 884744 | tf_op jit(solution)/shard_map/ppermute | solution.py:551
  20.2 8.8 %collective-permute-start.5 = (bf16[9,64,256]{2,1,0:T(8,128)(2,1)S(1)}, bf16[9,64,256]{2,1,0:T(8,128)(2,1)S(1)}, u32[]{:S(2)}, u32[]{:S(2)}) collective-permute-start(bf16[9,64,256]{2,1,0:T(8,128)(2,1)S(1)} %collective-permute-done.3.near), channel_id=1, source_target_pairs={{0,2},{1,7},{2,4},{3,1},{4,6},{5,3},{6,0},{7,5},{8,10},{9,15},{10,... | collective-permute-start | bytes 884744 | tf_op jit(solution)/shard_map/ppermute | solution.py:526
  22.0 7.0 %copy-start.3 = (f32[64]{0:T(128)S(1)}, f32[64]{0:T(128)}, u32[]{:S(2)}) copy-start(f32[64]{0:T(128)} %param.8) | copy-start | bytes 772
  22.0 21.4 %copy-start.1 = (bf16[3,3,64,256]{3,2,1,0:T(8,128)(2,1)S(1)}, bf16[3,3,64,256]{3,2,1,0:T(8,128)(2,1)}, u32[]{:S(2)}) copy-start(bf16[3,3,64,256]{3,2,1,0:T(8,128)(2,1)} %param.10) | copy-start | bytes 884740
  22.0 21.4 %copy-start.2 = (f32[256]{0:T(256)S(1)}, f32[256]{0:T(256)}, u32[]{:S(2)}) copy-start(f32[256]{0:T(256)} %param.11) | copy-start | bytes 3076
  22.0 21.4 %copy-start.4 = (f32[32]{0:T(128)S(1)}, f32[32]{0:T(128)}, u32[]{:S(2)}) copy-start(f32[32]{0:T(128)} %intervals_far.3) | copy-start | bytes 388
